TPU v7x, 512 devices: a whole 4x8x8 slice. The times are simulated.
512 devices in a mesh: dp: 32 (over z, x), fsdp: 16 (over y, core).
Axes of the slice: x: 4, y: 8, z: 8, core: 2. Of those that a mesh axis runs over, the one named last changes fastest.
Arguments:
- attended: bfloat16 [2048, 16384], P(None, 'dp'), may hold values from -6 to 6
- residual: bfloat16 [3200, 16384], P('fsdp', 'dp'), may hold values from -6 to 6
- grad_out: bfloat16 [3200, 12288], P('fsdp', 'dp'), may hold values from -10 to 10
- out_weight: bfloat16 [3200, 2048], P('fsdp'), may hold values from -0.125 to 0.125
- layer_scale: float32 [3200], P('fsdp'), may hold values from 0.1 to 1.9
- frames: int32 [32], replicated, may hold values from 0 to 2, as said below
- partner: int32 [32], replicated, may hold values from 0 to 31, as said below
- moved_tiles: int32 [32], replicated, may hold values from 0 to 16, as said below
- owner_slot: int32 [16], replicated, may hold values from 0 to 15, each once
Outputs:
- layer_out: bfloat16 [3200, 12288], P('fsdp', 'dp')
- input_grad: bfloat16 [2048, 16384], P('fsdp', 'dp')
- scale_grad: float32 [3200], P('fsdp')
- ortho_update: bfloat16 [3200, 16, 128], P(None, 'fsdp')
Inputs may be any that keep to these rules, and one draw needn't show every extreme that they name: In each pair of partners one replica holds 2 frames and the other at most half of 2. partner[partner[i]] = i and partner[i] != i. Replica i sends the last moved_tiles[i] tiles of 16 patches of its live slots to partner[i]; only the replica of a pair that holds 2 frames sends; after the moves every replica holds at most 24 tiles, and some pair holds exactly 24 tiles on both sides. `owner_slot`: each slot once.
All inputs are finite; a program needn't handle non-finite values.
Results may differ from a plain program's by a relative error of at most 0.022.
Values may be sent and summed in bfloat16 or wider, within the bound.
No kernel may reach another device: no remote copies, remote signals or barrier semaphores. Data moves between devices by JAX's collectives and lax.ppermute only.
A program may use at most 64 MiB of HBM per device.

v0:
```python
import math

import jax
import jax.numpy as jnp
from jax import lax
from jax.sharding import PartitionSpec as P

D = 3200
HD = 128
FRAME = 256
TILE = 16
ITERS = 5
CAP_ROWS = 512
MOVE_ROWS = 256
BAL_ROWS = 384


coeff_linear = 3.4445
coeff_square = -4.775
coeff_cubic = 2.0315
EPSILON = 1e-07


def positions(shape, dimension):
    return lax.broadcasted_iota(jnp.int32, shape, dimension)


def pad_along(values, before, after, dimension):
    widths = [(0, 0)] * values.ndim
    widths[dimension] = (before, after)
    return jnp.pad(values, widths)


def send_window(rows, live, sent, dimension):
    begin = jnp.maximum(live - MOVE_ROWS, 0)
    window = lax.dynamic_slice_in_dim(rows, begin, MOVE_ROWS, dimension)
    chosen = positions(window.shape, dimension) >= MOVE_ROWS - sent
    return jnp.where(chosen, window, jnp.zeros_like(window))


def place_received(own_rows, received, kept, incoming, dimension):
    own_part = lax.slice_in_dim(own_rows, 0, BAL_ROWS, axis=dimension)
    own_part = jnp.where(
        positions(own_part.shape, dimension) < kept, own_part, jnp.zeros_like(own_part)
    )
    padded = pad_along(received, BAL_ROWS, BAL_ROWS, dimension)
    begin = BAL_ROWS + MOVE_ROWS - incoming - kept
    return own_part + lax.dynamic_slice_in_dim(padded, begin, BAL_ROWS, dimension)


def return_window(balanced, kept, incoming, dimension):
    padded = pad_along(balanced, MOVE_ROWS, MOVE_ROWS, dimension)
    window = lax.dynamic_slice_in_dim(padded, kept + incoming, MOVE_ROWS, dimension)
    chosen = positions(window.shape, dimension) >= MOVE_ROWS - incoming
    return jnp.where(chosen, window, jnp.zeros_like(window))


def place_returned(balanced, returned, live, kept, dimension):
    own_part = pad_along(balanced, 0, CAP_ROWS - BAL_ROWS, dimension)
    own_part = jnp.where(
        positions(own_part.shape, dimension) < kept, own_part, jnp.zeros_like(own_part)
    )
    padded = pad_along(returned, CAP_ROWS, CAP_ROWS, dimension)
    begin = CAP_ROWS + MOVE_ROWS - live
    return own_part + lax.dynamic_slice_in_dim(padded, begin, CAP_ROWS, dimension)


def slots_first(window, senders):
    return window.T.reshape(senders, MOVE_ROWS // senders, window.shape[0])


def features_first(pieces):
    return pieces.reshape(MOVE_ROWS, pieces.shape[2]).T


def route_tiles(attended_win, residual_win, partner):
    senders = lax.axis_size("dp")
    attended_rows = slots_first(attended_win, senders)
    residual_rows = slots_first(residual_win, senders)
    for section_index in range(2):
        attended_rows, residual_rows = (
            lax.all_to_all(attended_rows, "dp", split_axis=0, concat_axis=0, tiled=True),
            lax.all_to_all(residual_rows, "dp", split_axis=0, concat_axis=0, tiled=True),
        )
        if section_index == 0:
            attended_rows = jnp.take(attended_rows, partner, axis=0)
            residual_rows = jnp.take(residual_rows, partner, axis=0)
    return (features_first(attended_rows), features_first(residual_rows))


def return_tiles(gradient_win, partner):
    senders = lax.axis_size("dp")
    gradient_rows = slots_first(gradient_win, senders)
    for section_index in range(2):
        gradient_rows = lax.all_to_all(gradient_rows, "dp", split_axis=0, concat_axis=0, tiled=True)
        if section_index == 0:
            gradient_rows = jnp.take(gradient_rows, partner, axis=0)
    return features_first(gradient_rows)


def gram_of(iterate):
    return jnp.einsum("dph,dpk->phk", iterate, iterate, precision=lax.Precision.HIGHEST)


def ortho_step(iterate, gram_matrix):
    highest = lax.Precision.HIGHEST
    square = jnp.einsum("phk,pkl->phl", gram_matrix, gram_matrix, precision=highest)
    polynomial = coeff_square * gram_matrix + coeff_cubic * square
    return coeff_linear * iterate + jnp.einsum(
        "dph,phk->dpk", iterate, polynomial, precision=highest
    )


def body(
    attended, residual, grad_out, out_weight, layer_scale, frames, partner, moved_tiles, owner_slot
):
    replica = lax.axis_index("dp")
    live_rows = frames * FRAME
    sent_rows = moved_tiles * TILE
    kept_rows = live_rows - sent_rows
    incoming = jnp.take(sent_rows, partner)
    my_live = live_rows[replica]
    my_sent = sent_rows[replica]
    my_kept = kept_rows[replica]
    my_incoming = incoming[replica]
    residual_win = send_window(residual, my_live, my_sent, 1)
    got_attended, got_residual = route_tiles(
        send_window(attended, my_live, my_sent, 1), residual_win, partner
    )
    attended_here = place_received(attended, got_attended, my_kept, my_incoming, 1)
    residual_here = place_received(residual, got_residual, my_kept, my_incoming, 1)
    projected = jnp.dot(out_weight, attended_here, preferred_element_type=jnp.float32)
    gains = layer_scale[:, None]
    layer_out = (residual_here.astype(jnp.float32) + gains * projected).astype(jnp.bfloat16)
    scaled = (grad_out.astype(jnp.float32) * gains).astype(jnp.bfloat16)
    inverse_root = 1.0 / math.sqrt(lax.axis_size("dp") * grad_out.shape[1])
    scale_part = jnp.sum(grad_out.astype(jnp.float32) * projected, axis=1) * inverse_root
    input_bal = lax.psum_scatter(
        lax.dot_general(
            out_weight, scaled, (((0,), (0,)), ((), ())), preferred_element_type=jnp.float32
        ).astype(jnp.bfloat16),
        "fsdp",
        scatter_dimension=0,
        tiled=True,
    )
    grad_part = lax.dot_general(
        scaled, attended_here, (((1,), (1,)), ((), ())), preferred_element_type=jnp.float32
    )
    returned = return_tiles(return_window(input_bal, my_kept, my_incoming, 1), partner)
    input_grad = place_returned(input_bal, returned, my_live, my_kept, 1)
    head_count = owner_slot.shape[0]
    inverse = (
        jnp.zeros((head_count,), jnp.int32)
        .at[owner_slot]
        .set(jnp.arange(head_count, dtype=jnp.int32))
    )
    slot_grad = jnp.take(grad_part.reshape(grad_part.shape[0], head_count, HD), inverse, axis=1)
    outgoing, scale_grad = lax.psum((slot_grad, scale_part), "dp")
    owned = lax.all_to_all(outgoing, "fsdp", split_axis=1, concat_axis=0, tiled=True)
    squares = jnp.sum(owned * owned, axis=(0, 2))
    iterate = owned / (jnp.sqrt(squares) + EPSILON)[None, :, None]
    for sweep in range(ITERS):
        iterate = ortho_step(iterate, gram_of(iterate))
    ortho_update = (0.2 * math.sqrt(D) * iterate).astype(jnp.bfloat16)
    return (layer_out, input_grad, scale_grad, ortho_update)


def solution(mesh):
    placed = (
        P(None, "dp"),
        P("fsdp", "dp"),
        P("fsdp", "dp"),
        P("fsdp", None),
        P("fsdp"),
        P(),
        P(),
        P(),
        P(),
    )
    return jax.shard_map(
        body,
        mesh=mesh,
        in_specs=placed,
        out_specs=(P("fsdp", "dp"), P("fsdp", "dp"), P("fsdp"), P(None, "fsdp", None)),
        check_vma=False,
    )
```

profile of v0, /device:TPU:8, one launch (start us, length us, event | category | flops | bytes accessed | tf_op | source)
XLA Modules:
  0.0 383.7 jit_solution(17020048814661135641)
XLA Ops:
  8.0 0.8 broadcast_multiply_fusion.3
  11.2 1.7 constant_dynamic-slice_fusion
  13.6 1.1 select_bitcast_fusion.1
  14.7 13.3 %all-to-all-start.2 = ((bf16[32,8,2048]{2,1,0:T(8,128)(2,1)}), bf16[32,8,2048]{2,1,0:T(8,128)(2,1)S(1)}, u32[]{:S(2)}, u32[]{:S(2)}) async-start(bf16[32,8,2048]{2,1,0:T(8,128)(2,1)} %select_bitcast_fusion.1), calls=%async_computation.2 | async-start | bytes 2097152 | tf_op jit(solution)/shard_map/all_to_all | solution.py:82
  28.1 1.6 fusion.7
  29.7 1.6 copy.32
  31.4 0.7 gather_fusion.1
  32.1 24.0 %all-to-all-done.2 = bf16[32,8,2048]{2,1,0:T(8,128)(2,1)S(1)} async-done(((bf16[32,8,2048]{2,1,0:T(8,128)(2,1)}), bf16[32,8,2048]{2,1,0:T(8,128)(2,1)S(1)}, u32[]{:S(2)}, u32[]{:S(2)}) %all-to-all-start.2) | async-done | bytes 1048608 | tf_op jit(solution)/shard_map/all_to_all | solution.py:82
  56.7 1.1 broadcast_select_fusion
  57.9 5.5 %all-to-all-start.3 = ((bf16[32,8,2048]{2,1,0:T(8,128)(2,1)}), bf16[32,8,2048]{2,1,0:T(8,128)(2,1)S(1)}, u32[]{:S(2)}, u32[]{:S(2)}) async-start(bf16[32,8,2048]{2,1,0:T(8,128)(2,1)} %broadcast_select_fusion), calls=%async_computation.3 | async-start | bytes 2097152 | tf_op jit(solution)/shard_map/all_to_all | solution.py:82
  66.0 1.7 copy.35
  69.0 21.4 %all-to-all-done.3 = bf16[32,8,2048]{2,1,0:T(8,128)(2,1)S(1)} async-done(((bf16[32,8,2048]{2,1,0:T(8,128)(2,1)}), bf16[32,8,2048]{2,1,0:T(8,128)(2,1)S(1)}, u32[]{:S(2)}, u32[]{:S(2)}) %all-to-all-start.3) | async-done | bytes 1048608 | tf_op jit(solution)/shard_map/all_to_all | solution.py:82
  90.4 2.7 convolution_bitcast_fusion.5
  93.3 1.8 gather_fusion.4
  95.1 2.8 select_bitcast_fusion
  97.9 0.9 copy-done.5
  99.0 0.8 select_bitcast_fusion.2
  99.8 5.6 %all-to-all-start = ((bf16[32,8,200]{2,1,0:T(8,128)(2,1)}), bf16[32,8,200]{2,1,0:T(8,128)(2,1)S(1)}, u32[]{:S(2)}, u32[]{:S(2)}) async-start(bf16[32,8,200]{2,1,0:T(8,128)(2,1)} %select_bitcast_fusion.2), calls=%async_computation | async-start | bytes 262144 | tf_op jit(solution)/shard_map/all_to_all | solution.py:83
  107.3 8.6 %all-to-all-done = bf16[32,8,200]{2,1,0:T(8,128)(2,1)S(1)} async-done(((bf16[32,8,200]{2,1,0:T(8,128)(2,1)}), bf16[32,8,200]{2,1,0:T(8,128)(2,1)S(1)}, u32[]{:S(2)}, u32[]{:S(2)}) %all-to-all-start) | async-done | bytes 102432 | tf_op jit(solution)/shard_map/all_to_all | solution.py:83
  116.5 1.0 copy.33
  117.5 0.8 fusion.36
  118.3 3.9 %all-to-all-start.4 = ((bf16[32,8,128]{2,1,0:T(8,128)(2,1)}), bf16[32,8,128]{2,1,0:T(8,128)(2,1)S(1)}, u32[]{:S(2)}, u32[]{:S(2)}) async-start(bf16[32,8,128]{2,1,0:T(8,128)(2,1)} %fusion.36), calls=%async_computation.4 | async-start | bytes 131072 | tf_op jit(solution)/shard_map/all_to_all | solution.py:95
  122.2 0.8 broadcast_select_fusion.1
  122.9 9.8 %all-to-all-done.4 = bf16[32,8,128]{2,1,0:T(8,128)(2,1)S(1)} async-done(((bf16[32,8,128]{2,1,0:T(8,128)(2,1)}), bf16[32,8,128]{2,1,0:T(8,128)(2,1)S(1)}, u32[]{:S(2)}, u32[]{:S(2)}) %all-to-all-start.4) | async-done | bytes 65568 | tf_op jit(solution)/shard_map/all_to_all | solution.py:95
  132.8 3.9 %all-to-all-start.1 = ((bf16[32,8,200]{2,1,0:T(8,128)(2,1)}), bf16[32,8,200]{2,1,0:T(8,128)(2,1)S(1)}, u32[]{:S(2)}, u32[]{:S(2)}) async-start(bf16[32,8,200]{2,1,0:T(8,128)(2,1)} %broadcast_select_fusion.1), calls=%async_computation.1 | async-start | bytes 262144 | tf_op jit(solution)/shard_map/all_to_all | solution.py:83
  137.3 9.9 %all-to-all-done.1 = bf16[32,8,200]{2,1,0:T(8,128)(2,1)S(1)} async-done(((bf16[32,8,200]{2,1,0:T(8,128)(2,1)}), bf16[32,8,200]{2,1,0:T(8,128)(2,1)S(1)}, u32[]{:S(2)}, u32[]{:S(2)}) %all-to-all-start.1) | async-done | bytes 102432 | tf_op jit(solution)/shard_map/all_to_all | solution.py:83
  147.2 13.7 %all_to_all.39 = bf16[32,8,128]{2,1,0:T(8,128)(2,1)} all-to-all(bf16[32,8,128]{2,1,0:T(8,128)(2,1)S(1)} %broadcast_select_fusion.2), channel_id=1, replica_groups=mesh['dp'=32,'fsdp'=16] {'dp'}, dimensions={0} | all-to-all | bytes 131072 | tf_op jit(solution)/shard_map/all_to_all | solution.py:95
  160.8 99.0 %all-reduce.7.cloned.1.call-done = f32[200,16,128]{2,0,1:T(8,128)} async-done(((f32[200,16,128]{2,0,1:T(8,128)}), f32[200,16,128]{2,0,1:T(8,128)}) %all-reduce.7.cloned.1.call-update) | async-done | bytes 1638416 | tf_op jit(solution)/shard_map/psum | solution.py:158
  259.8 7.3 %all-to-all-start.6 = ((f32[200,16,128]{2,0,1:T(8,128)}), f32[200,16,128]{2,0,1:T(8,128)S(1)}, u32[]{:S(2)}, u32[]{:S(2)}) async-start(f32[200,16,128]{2,0,1:T(8,128)} %all-reduce.7.cloned.1.call-done), calls=%async_computation.6 | async-start | bytes 3276800 | tf_op jit(solution)/shard_map/all_to_all | solution.py:159
  269.0 1.7 copy.25
  270.7 1.7 fusion.34
  272.4 1.7 copy.30
  274.0 3.4 fusion.32
  277.5 72.4 %psum.14 = f32[200]{0:T(256)} all-reduce(f32[200]{0:T(256)S(1)} %broadcast_multiply_fusion.1), channel_id=1, replica_groups=mesh['dp'=32,'fsdp'=16] {'dp'}, use_global_device_ids=true, to_apply=%region_2.3 | all-reduce | flops 200 | bytes 1600 | tf_op jit(solution)/shard_map/psum | solution.py:158
  349.9 1.0 multiply_reduce_fusion
  351.6 1.9 broadcast_multiply_fusion
  353.5 2.8 copy.29
  356.3 2.7 fusion.23
  359.3 1.6 fusion.5
  361.0 1.6 fusion.20
  362.8 1.6 fusion.4
  364.4 1.6 fusion.17
  366.2 1.6 fusion.3
  367.8 1.8 fusion.14
  369.9 1.6 fusion.2
  371.5 1.6 fusion.11
  373.3 1.7 fusion.6
  375.0 1.3 copy.31
  (56 shorter events, 8.4 us)
Async XLA Ops:
  8.0 20.1 %copy-start = (bf16[200,2048]{1,0:T(8,128)(2,1)S(1)}, bf16[200,2048]{1,0:T(8,128)(2,1)}, u32[]{:S(2)}) copy-start(bf16[200,2048]{1,0:T(8,128)(2,1)} %param.12) | copy-start | bytes 2457604
  13.6 14.5 %copy-start.6 = (f32[200]{0:T(256)S(1)}, f32[200]{0:T(256)}, u32[]{:S(2)}) copy-start(f32[200]{0:T(256)} %param.13) | copy-start | bytes 2404
  14.7 41.4 %all-to-all-start.2 = ((bf16[32,8,2048]{2,1,0:T(8,128)(2,1)}), bf16[32,8,2048]{2,1,0:T(8,128)(2,1)S(1)}, u32[]{:S(2)}, u32[]{:S(2)}) async-start(bf16[32,8,2048]{2,1,0:T(8,128)(2,1)} %select_bitcast_fusion.1), calls=%async_computation.2 | async-start | bytes 2097152 | tf_op jit(solution)/shard_map/all_to_all | solution.py:82
  28.0 88.5 %reduce-scatter.4.cloned.1.call-start = ((), (), s32[]{:S(2)}) async-start(), calls=%async_computation.9 | async-start | bytes 1671168
  29.7 1.6 copy-start.7
  57.9 32.5 %all-to-all-start.3 = ((bf16[32,8,2048]{2,1,0:T(8,128)(2,1)}), bf16[32,8,2048]{2,1,0:T(8,128)(2,1)S(1)}, u32[]{:S(2)}, u32[]{:S(2)}) async-start(bf16[32,8,2048]{2,1,0:T(8,128)(2,1)} %broadcast_select_fusion), calls=%async_computation.3 | async-start | bytes 2097152 | tf_op jit(solution)/shard_map/all_to_all | solution.py:82
  63.4 2.6 slice-start
  63.4 196.4 %all-reduce.7.cloned.1.call-start = ((), (), s32[]{:S(2)}) async-start(), calls=%async_computation.8 | async-start | bytes 3276800 | tf_op jit(solution)/shard_map/psum | solution.py:158
  63.5 4.2 %copy-start.8 = (s32[16]{0:T(128)S(1)}, s32[16]{0:T(128)}, u32[]{:S(2)}) copy-start(s32[16]{0:T(128)} %param.17) | copy-start | bytes 196
  97.9 0.9 copy-start.5
  99.8 16.2 %all-to-all-start = ((bf16[32,8,200]{2,1,0:T(8,128)(2,1)}), bf16[32,8,200]{2,1,0:T(8,128)(2,1)S(1)}, u32[]{:S(2)}, u32[]{:S(2)}) async-start(bf16[32,8,200]{2,1,0:T(8,128)(2,1)} %select_bitcast_fusion.2), calls=%async_computation | async-start | bytes 262144 | tf_op jit(solution)/shard_map/all_to_all | solution.py:83
  117.5 142.3 %copy-start.3 = (bf16[128,384]{0,1:T(8,128)(2,1)}, bf16[128,384]{0,1:T(8,128)(2,1)S(1)}, u32[]{:S(2)}) copy-start(bf16[128,384]{0,1:T(8,128)(2,1)S(1)} %copy.33) | copy-start | bytes 294916
  118.3 14.4 %all-to-all-start.4 = ((bf16[32,8,128]{2,1,0:T(8,128)(2,1)}), bf16[32,8,128]{2,1,0:T(8,128)(2,1)S(1)}, u32[]{:S(2)}, u32[]{:S(2)}) async-start(bf16[32,8,128]{2,1,0:T(8,128)(2,1)} %fusion.36), calls=%async_computation.4 | async-start | bytes 131072 | tf_op jit(solution)/shard_map/all_to_all | solution.py:95
  132.8 14.4 %all-to-all-start.1 = ((bf16[32,8,200]{2,1,0:T(8,128)(2,1)}), bf16[32,8,200]{2,1,0:T(8,128)(2,1)S(1)}, u32[]{:S(2)}, u32[]{:S(2)}) async-start(bf16[32,8,200]{2,1,0:T(8,128)(2,1)} %broadcast_select_fusion.1), calls=%async_computation.1 | async-start | bytes 262144 | tf_op jit(solution)/shard_map/all_to_all | solution.py:83
  147.2 112.6 %copy-start.4 = (bf16[32,8,200]{2,1,0:T(8,128)(2,1)}, bf16[32,8,200]{2,1,0:T(8,128)(2,1)S(1)}, u32[]{:S(2)}) copy-start(bf16[32,8,200]{2,1,0:T(8,128)(2,1)S(1)} %all-to-all-done.1) | copy-start | bytes 307204
  259.8 90.1 %all-to-all-start.6 = ((f32[200,16,128]{2,0,1:T(8,128)}), f32[200,16,128]{2,0,1:T(8,128)S(1)}, u32[]{:S(2)}, u32[]{:S(2)}) async-start(f32[200,16,128]{2,0,1:T(8,128)} %all-reduce.7.cloned.1.call-done), calls=%async_computation.6 | async-start | bytes 3276800 | tf_op jit(solution)/shard_map/all_to_all | solution.py:159
  353.5 2.8 copy-start.1
  356.3 3.0 copy-start.2
Sparse Core Ops, SparseCore 0:
  31.7 59.2 reduce-scatter.3
Sparse Core Ops, SparseCore 1:
  98.0 161.8 all-reduce.6
where the time goes:
time: 385 us; the launch traced here: 384 us
  waiting for transfers between devices  173 us (45%)
  blocking collectives  86.1 us (22%)
  starting transfers between devices  39.6 us (10%)
  matrix products  26.3 us (7%)
  local copies, waits for them, and re-layouts  22.6 us (6%)
  between operations  22.4 us (6%)
  other arithmetic  14.2 us (4%)
    psum x1, waiting for transfers between devices, body(): outgoing, scale_grad = lax.psum((slot_grad, scale_part), 'dp')  99 us
    psum x1, blocking collectives, body(): outgoing, scale_grad = lax.psum((slot_grad, scale_part), 'dp')  72.4 us
    all_to_all x2, waiting for transfers between devices, route_tiles(): lax.all_to_all(attended_rows, 'dp', split_axis=0, concat_axis=0, tiled=True)  45.4 us
    all_to_all x2, starting transfers between devices, route_tiles(): lax.all_to_all(attended_rows, 'dp', split_axis=0, concat_axis=0, tiled=True)  18.9 us
    all_to_all x2, waiting for transfers between devices, route_tiles(): lax.all_to_all(residual_rows, 'dp', split_axis=0, concat_axis=0, tiled=True)  18.4 us
    all_to_all x1, blocking collectives, return_tiles(): lax.all_to_all(gradient_rows, 'dp', split_axis=0, concat_axis=0, tiled=True)  13.7 us
    all_to_all x1, waiting for transfers between devices, return_tiles(): lax.all_to_all(gradient_rows, 'dp', split_axis=0, concat_axis=0, tiled=True)  9.81 us
    all_to_all x2, starting transfers between devices, route_tiles(): lax.all_to_all(residual_rows, 'dp', split_axis=0, concat_axis=0, tiled=True)  9.47 us
  transfers between devices with their start and end apart: 8, of which 6 were waited for; matrix products, arithmetic and copies ran while one was open for 8% of the time, Pallas kernels for 0%

commit v1 on v0

v1 whole, which is shorter than its diff:
```python
import math

import jax
import jax.numpy as jnp
from jax import lax
from jax.experimental import pallas as pl
from jax.experimental.pallas import tpu as pltpu
from jax.sharding import PartitionSpec as P

D = 3200
HEADS = 16
HD = 128
FRAME = 256
TILE = 16
ITERS = 5
A = 2048
CAP_ROWS = 512
MOVE_ROWS = 256
BAL_ROWS = 384
N_DP = 32
N_FSDP = 16

ROWS = D // N_FSDP
SHARE = HD // N_DP
WIDE = 3456
PAD_ROWS = 256
CHIPS = N_FSDP // 2

coeff_linear = 3.4445
coeff_square = -4.775
coeff_cubic = 2.0315
EPSILON = 1e-07
INVERSE_ROOT = 1.0 / math.sqrt(N_DP * BAL_ROWS)

bf16 = jnp.bfloat16
f32 = jnp.float32

ROWS_BY_COLS = (((0,), (0,)), ((), ()))
COLS_BY_COLS = (((1,), (1,)), ((), ()))


def positions(shape, dimension):
    return lax.broadcasted_iota(jnp.int32, shape, dimension)


def dot(a, b, dims=(((1,), (0,)), ((), ()))):
    return lax.dot_general(a, b, dims, preferred_element_type=f32)


def same(size):
    return positions((size, size), 0) == positions((size, size), 1)


def to_column(row):
    size = row.shape[1]
    return jnp.sum(jnp.where(same(size), row, 0.0), axis=1, keepdims=True)


def to_row(column):
    size = column.shape[0]
    return jnp.sum(jnp.where(same(size), column, 0.0), axis=0, keepdims=True)


def my_counts(index_ref, frames_ref, partner_ref, moved_ref):
    replica = index_ref[0]
    mate = partner_ref[replica]
    kept = frames_ref[replica] * FRAME - moved_ref[replica] * TILE
    incoming = moved_ref[mate] * TILE
    holds_two = (frames_ref[replica] > frames_ref[mate]).astype(jnp.int32)
    return kept, incoming, holds_two


def light_places(kept, incoming):
    bal_col = positions((BAL_ROWS, MOVE_ROWS), 0)
    win_col = positions((BAL_ROWS, MOVE_ROWS), 1)
    hit = bal_col == win_col + (kept + incoming - MOVE_ROWS)
    hit = hit & (win_col >= MOVE_ROWS - incoming)
    return jnp.where(hit, 1.0, 0.0).astype(bf16)


def project_kernel(
    index_ref, frames_ref, partner_ref, moved_ref,
    attended_ref, residual_ref, grad_ref, weight_ref, scale_ref,
    projected_ref, layer_ref, window_ref,
):
    kept, incoming, holds_two = my_counts(index_ref, frames_ref, partner_ref, moved_ref)
    gains = to_column(scale_ref[...])
    projected = dot(weight_ref[...], attended_ref[...])
    projected_ref[...] = projected
    layer = (residual_ref[...].astype(f32) + gains * projected).astype(bf16)
    layer_ref[...] = layer
    grad_win = dot(grad_ref[...], light_places(kept, incoming))
    layer_win = layer[:, MOVE_ROWS:].astype(f32)
    window = jnp.where(holds_two == 1, layer_win, grad_win).astype(bf16)
    window_ref[pl.ds(0, ROWS), :] = window
    window_ref[pl.ds(ROWS, PAD_ROWS - ROWS), :] = jnp.zeros(
        (PAD_ROWS - ROWS, MOVE_ROWS), bf16
    )


def weight_grad_kernel(
    index_ref, frames_ref, partner_ref, moved_ref, slot_ref,
    attended_ref, grad_ref, got_ref, projected_ref, scale_ref,
    scaled_ref, pieces_ref,
    head_of, wide,
):
    kept, incoming, holds_two = my_counts(index_ref, frames_ref, partner_ref, moved_ref)
    for head in range(HEADS):
        head_of[slot_ref[head]] = head
    own = grad_ref[...].astype(f32)
    own = jnp.concatenate([own, jnp.zeros((ROWS, CAP_ROWS - BAL_ROWS), f32)], axis=1)
    got = got_ref[pl.ds(0, ROWS), :].astype(f32)
    got = jnp.where(holds_two == 1, got, 0.0)
    got = jnp.concatenate([jnp.zeros((ROWS, CAP_ROWS - MOVE_ROWS), f32), got], axis=1)
    grad = jnp.where(positions((ROWS, CAP_ROWS), 1) < kept, own, got)
    scaled = (grad * to_column(scale_ref[...])).astype(bf16)
    scaled_ref[...] = scaled
    part = jnp.sum(grad * projected_ref[...], axis=1, keepdims=True) * INVERSE_ROOT
    part = to_row(part)
    high = part.astype(bf16).astype(f32)
    low = part - high
    wide[:, pl.ds(D, WIDE - D)] = jnp.zeros((HD, WIDE - D), f32)
    for slot in range(HEADS):
        first = pl.multiple_of(head_of[slot] * HD, HD)
        wide[:, pl.ds(slot * ROWS, ROWS)] = dot(
            attended_ref[pl.ds(first, HD), :], scaled, COLS_BY_COLS
        )
    for piece in range(N_DP):
        pieces_ref[piece] = wide[pl.ds(piece * SHARE, SHARE), :].astype(bf16)
        pieces_ref[piece, pl.ds(0, 2), pl.ds(D, ROWS)] = jnp.concatenate(
            [high, low], axis=0
        ).astype(bf16)


def input_kernel(
    index_ref, frames_ref, partner_ref, moved_ref,
    weight_ref, scaled_ref, layer_ref, got_ref,
    layer_out_ref, mine_ref, theirs_ref,
):
    kept, incoming, holds_two = my_counts(index_ref, frames_ref, partner_ref, moved_ref)
    core = index_ref[1]
    scaled = scaled_ref[...]
    for chip in range(CHIPS):
        first = pl.multiple_of((2 * chip + core) * HD, HD)
        mine_ref[chip] = dot(weight_ref[:, pl.ds(first, HD)], scaled, ROWS_BY_COLS).astype(bf16)
        first = pl.multiple_of((2 * chip + 1 - core) * HD, HD)
        theirs_ref[chip] = dot(weight_ref[:, pl.ds(first, HD)], scaled, ROWS_BY_COLS).astype(bf16)
    received = dot(got_ref[pl.ds(0, ROWS), :], light_places(kept, incoming), COLS_BY_COLS)
    own = layer_ref[:, pl.ds(0, BAL_ROWS)].astype(f32)
    keep = positions((ROWS, BAL_ROWS), 1) < kept
    layer_out_ref[...] = jnp.where(keep, own, received).astype(bf16)


def slots_kernel(pieces_ref, by_slot_ref, scale_grad_ref):
    total = pieces_ref[0].astype(f32)
    for piece in range(1, N_DP):
        total = total + pieces_ref[piece].astype(f32)
    for slot in range(HEADS):
        by_slot_ref[slot] = total[:, slot * ROWS : (slot + 1) * ROWS].astype(bf16)
    scale_grad_ref[...] = total[0:1, D : D + ROWS] + total[1:2, D : D + ROWS]


def spread_kernel(owned_ref, copies_ref, joined):
    for block in range(N_FSDP):
        joined[:, pl.ds(block * ROWS, ROWS)] = owned_ref[block].astype(f32)
    whole = joined[...].astype(bf16)
    for piece in range(N_DP):
        copies_ref[piece] = whole


def ortho_kernel(pieces_ref, out_ref, joined):
    def mul(a, b):
        return jnp.dot(a, b, precision=lax.Precision.HIGHEST, preferred_element_type=f32)

    for piece in range(N_DP):
        joined[pl.ds(piece * SHARE, SHARE), :] = pieces_ref[piece].astype(f32)
    grad = joined[...].astype(bf16)
    gram = dot(grad, grad, COLS_BY_COLS)
    eye = jnp.where(same(HD), 1.0, 0.0).astype(f32)
    squares = jnp.sum(jnp.sum(gram * eye, axis=1, keepdims=True), axis=0, keepdims=True)
    norm = jnp.sqrt(squares) + EPSILON
    gram = gram / norm / norm
    total = None
    for sweep in range(ITERS):
        step = coeff_linear * eye + coeff_square * gram + coeff_cubic * mul(gram, gram)
        total = step if total is None else mul(total, step)
        if sweep < ITERS - 1:
            gram = mul(mul(step, gram), step)
    total = total * (0.2 * math.sqrt(D) / norm)
    high = total.astype(bf16)
    low = (total - high.astype(f32)).astype(bf16)
    out = dot(grad, high, ROWS_BY_COLS) + dot(grad, low, ROWS_BY_COLS)
    out_ref[...] = out.astype(bf16)


def call(kernel, name, scalars, arrays, outs, scratch=()):
    smem = pl.BlockSpec(memory_space=pltpu.SMEM)
    vmem = pl.BlockSpec(memory_space=pltpu.VMEM)
    return pl.pallas_call(
        kernel,
        out_shape=[jax.ShapeDtypeStruct(shape, dtype) for shape, dtype in outs],
        in_specs=[smem] * len(scalars) + [vmem] * len(arrays),
        out_specs=[vmem] * len(outs),
        scratch_shapes=list(scratch),
        compiler_params=pltpu.CompilerParams(vmem_limit_bytes=40 * 1024 * 1024),
        name=name,
    )(*scalars, *arrays)


def exchange(pieces, axis, groups=None):
    return lax.all_to_all(
        pieces, axis, split_axis=0, concat_axis=0, tiled=True, axis_index_groups=groups
    )


def body(
    attended, residual, grad_out, out_weight, layer_scale, frames, partner, moved_tiles, owner_slot
):
    index = jnp.stack([lax.axis_index("dp"), lax.axis_index("fsdp") % 2])
    counts = (index, frames, partner, moved_tiles)
    scale_row = layer_scale[None, :]

    projected, layer_own, window = call(
        project_kernel, "project", counts,
        (attended, residual, grad_out, out_weight, scale_row),
        [((ROWS, CAP_ROWS), f32), ((ROWS, CAP_ROWS), bf16), ((PAD_ROWS, MOVE_ROWS), bf16)],
    )
    pieces = exchange(window.reshape(N_DP, PAD_ROWS // N_DP, MOVE_ROWS), "dp")
    pieces = exchange(jnp.take(pieces, partner, axis=0), "dp")
    got = pieces.reshape(PAD_ROWS, MOVE_ROWS)

    scaled, pieces = call(
        weight_grad_kernel, "weight_grad", (*counts, owner_slot),
        (attended, grad_out, got, projected, scale_row),
        [((ROWS, CAP_ROWS), bf16), ((N_DP, SHARE, WIDE), bf16)],
        [pltpu.SMEM((HEADS,), jnp.int32), pltpu.VMEM((HD, WIDE), f32)],
    )
    pieces = exchange(pieces, "dp")

    layer_out, mine, theirs = call(
        input_kernel, "input_grad", counts,
        (out_weight, scaled, layer_own, got),
        [((ROWS, BAL_ROWS), bf16)] + [((CHIPS, HD, CAP_ROWS), bf16)] * 2,
    )
    theirs = lax.ppermute(theirs, "fsdp", [(i, i ^ 1) for i in range(N_FSDP)])
    mine = (mine.astype(f32) + theirs.astype(f32)).astype(bf16)
    cores = [[2 * chip + core for chip in range(CHIPS)] for core in range(2)]
    mine = exchange(mine, "fsdp", cores)
    input_grad = jnp.sum(mine.astype(f32), axis=0).astype(bf16)

    by_slot, scale_grad = call(
        slots_kernel, "slots", (), (pieces,),
        [((HEADS, SHARE, ROWS), bf16), ((1, ROWS), f32)],
    )
    owned = exchange(by_slot, "fsdp")
    (copies,) = call(
        spread_kernel, "spread", (), (owned,),
        [((N_DP, SHARE, D), bf16)],
        [pltpu.VMEM((SHARE, D), f32)],
    )
    whole = exchange(copies, "dp")
    (ortho_update,) = call(
        ortho_kernel, "ortho", (), (whole,), [((D, HD), bf16)], [pltpu.VMEM((HD, D), f32)]
    )
    return (layer_out, input_grad, scale_grad.reshape(ROWS), ortho_update[:, None, :])


def solution(mesh):
    placed = (
        P(None, "dp"),
        P("fsdp", "dp"),
        P("fsdp", "dp"),
        P("fsdp", None),
        P("fsdp"),
        P(),
        P(),
        P(),
        P(),
    )
    return jax.shard_map(
        body,
        mesh=mesh,
        in_specs=placed,
        out_specs=(P("fsdp", "dp"), P("fsdp", "dp"), P("fsdp"), P(None, "fsdp", None)),
        check_vma=False,
    )
```

time: 385 us -> 164 us (0.43)
  the two profiles are of different devices: /device:TPU:8 before, /device:TPU:1 now
where the time goes in v1:
time: 164 us; the launch traced here: 162 us
  waiting for transfers between devices  77 us (47%)
  starting transfers between devices  43.3 us (26%)
  Pallas kernels  13.5 us (8%)
  blocking collectives  12.6 us (8%)
  local copies, waits for them, and re-layouts  12.1 us (7%)
  other arithmetic  2.3 us (1%)
    all_to_all x5, waiting for transfers between devices, exchange(): lax.all_to_all(pieces, axis, split_axis=0, concat_axis=0, tiled=True, axi...  76.9 us
    all_to_all x5, starting transfers between devices, exchange(): lax.all_to_all(pieces, axis, split_axis=0, concat_axis=0, tiled=True, axi...  38 us
    pallas_call x6, Pallas kernels, call(): pl.pallas_call(kernel, out_shape=[jax.ShapeDtypeStruct(shape, dtype) for...  13.5 us
    all_to_all x1, blocking collectives, exchange(): lax.all_to_all(pieces, axis, split_axis=0, concat_axis=0, tiled=True, axi...  12.6 us
    unnamed x42, local copies, waits for them, and re-layouts  11.5 us
    ppermute x1, starting transfers between devices, body(): theirs = lax.ppermute(theirs, 'fsdp', [(i, i ^ 1) for i in range(N_FSDP)])  5.23 us
  transfers between devices with their start and end apart: 6, of which 5 were waited for; matrix products, arithmetic and copies ran while one was open for 1% of the time, Pallas kernels for 3%

profile of v1, /device:TPU:1, one launch (start us, length us, event | category | flops | bytes accessed | tf_op | source)
XLA Modules:
  0.0 161.6 jit_solution(5608245813018107698)
XLA Ops:
  0.6 0.0 copy-start.15
  0.7 0.1 pad_add_fusion.index_ref
  0.7 1.6 copy-done
  2.3 1.1 copy-done.2
  3.5 0.9 copy-done.5
  4.4 0.9 copy-done.9
  5.3 0.7 copy-done.12
  6.0 0.7 copy-done.14
  6.6 0.7 copy-done.16
  7.3 0.7 copy-done.18
  8.0 0.0 copy-start.19
  8.0 0.0 copy-start.20
  8.0 1.9 %project.1 = (f32[200,512]{1,0:T(8,128)S(1)}, bf16[200,512]{1,0:T(8,128)(2,1)S(1)}, bf16[256,256]{1,0:T(8,128)(2,1)}) custom-call(s32[2]{0:T(128)S(1)} %pad_add_fusion.index_ref, s32[32]{0:T(128)S(1)} %copy-done.12, s32[32]{0:T(128)S(1)} %copy-done.14, s32[32]{0:T(128)S(1)} %copy-done.16, bf16[2048,512]{1,0:T(8,128)(2,1)S(1)} %copy-done, ...), custom_call_target="tpu_custom_call" | custom-call | tf_op jit(solution)/shard_map/project/pallas_call | solution.py:199
  9.9 0.7 copy-done.7
  10.6 13.7 %all-to-all-start = ((bf16[32,8,256]{2,1,0:T(8,128)(2,1)}), bf16[32,8,256]{2,1,0:T(8,128)(2,1)S(1)}, u32[]{:S(2)}, u32[]{:S(2)}) async-start(bf16[32,8,256]{2,1,0:T(8,128)(2,1)} %bitcast.3), calls=%async_computation | async-start | bytes 262144 | tf_op jit(solution)/shard_map/all_to_all | solution.py:211
  24.4 0.0 copy-done.15
  24.4 9.3 %all-to-all-done = bf16[32,8,256]{2,1,0:T(8,128)(2,1)S(1)} async-done(((bf16[32,8,256]{2,1,0:T(8,128)(2,1)}), bf16[32,8,256]{2,1,0:T(8,128)(2,1)S(1)}, u32[]{:S(2)}, u32[]{:S(2)}) %all-to-all-start) | async-done | bytes 131104 | tf_op jit(solution)/shard_map/all_to_all | solution.py:211
  33.7 0.6 gather_fusion
  34.3 0.1 broadcast_select_fusion
  34.4 12.6 %all_to_all.30 = bf16[32,8,256]{2,1,0:T(8,128)(2,1)S(1)} all-to-all(bf16[32,8,256]{2,1,0:T(8,128)(2,1)S(1)} %broadcast_select_fusion), channel_id=1, replica_groups=mesh['dp'=32,'fsdp'=16] {'dp'}, dimensions={0} | all-to-all | bytes 262144 | tf_op jit(solution)/shard_map/all_to_all | solution.py:211
  47.0 0.0 copy-done.1
  47.0 0.0 copy-done.6
  47.0 0.0 copy-done.13
  47.0 0.0 copy-done.17
  47.1 0.0 copy-start.8
  47.1 1.0 copy-done.8
  48.1 2.2 %weight_grad.1 = (bf16[200,512]{1,0:T(8,128)(2,1)S(1)}, bf16[32,4,3456]{2,1,0:T(4,128)(2,1)S(1)}) custom-call(s32[2]{0:T(128)S(1)} %pad_add_fusion.index_ref, s32[32]{0:T(128)S(1)} %copy-done.13, s32[32]{0:T(128)S(1)} %copy-done.15, s32[32]{0:T(128)S(1)} %copy-done.17, s32[16]{0:T(128)S(1)} %copy-done.20, bf16[2048,512]{1,0:T(8,128)(2,1)S(1)} %copy-done.1, ...), custom_call_target="tpu_custom_call" | custom-call | tf_op jit(solution)/shard_map/weight_grad/pallas_call | solution.py:199
  50.3 0.0 copy-start.4
  50.3 0.9 copy-done.4
  51.2 0.7 copy-done.10
  51.9 3.9 %all-to-all-start.3 = ((bf16[32,4,3456]{2,1,0:T(4,128)(2,1)}), bf16[32,4,3456]{2,1,0:T(4,128)(2,1)S(1)}, u32[]{:S(2)}, u32[]{:S(2)}) async-start(bf16[32,4,3456]{2,1,0:T(4,128)(2,1)} %copy-done.4), calls=%async_computation.3 | async-start | bytes 1769472 | tf_op jit(solution)/shard_map/all_to_all | solution.py:211
  55.8 0.0 copy-start.11
  55.8 0.9 copy-done.11
  56.8 2.4 %input_grad.1 = (bf16[200,384]{1,0:T(8,128)(2,1)}, bf16[8,128,512]{2,1,0:T(8,128)(2,1)S(1)}, bf16[8,128,512]{2,1,0:T(8,128)(2,1)}) custom-call(s32[2]{0:T(128)S(1)} %pad_add_fusion.index_ref, s32[32]{0:T(128)S(1)} %copy-done.13, s32[32]{0:T(128)S(1)} %copy-done.15, s32[32]{0:T(128)S(1)} %copy-done.17, bf16[200,2048]{1,0:T(8,128)(2,1)S(1)} %copy-done.3, ...), custom_call_target="tpu_custom_call" | custom-call | tf_op jit(solution)/shard_map/input_grad/pallas_call | solution.py:199
  59.1 5.2 %collective-permute-start = (bf16[8,128,512]{2,1,0:T(8,128)(2,1)}, bf16[8,128,512]{2,1,0:T(8,128)(2,1)S(1)}, u32[]{:S(2)}, u32[]{:S(2)}) collective-permute-start(bf16[8,128,512]{2,1,0:T(8,128)(2,1)} %get-tuple-element.20), channel_id=1, source_target_pairs={{0,1},{1,0},{2,3},{3,2},{4,5},{5,4},{6,7},{7,6},{8,9},{9,8},{10,11... | collective-permute-start | bytes 3145736 | tf_op jit(solution)/shard_map/ppermute | solution.py:245
  64.4 12.5 %all-to-all-done.3.pieces_ref = bf16[32,4,3456]{2,1,0:T(4,128)(2,1)S(1)} async-done(((bf16[32,4,3456]{2,1,0:T(4,128)(2,1)}), bf16[32,4,3456]{2,1,0:T(4,128)(2,1)S(1)}, u32[]{:S(2)}, u32[]{:S(2)}) %all-to-all-start.3) | async-done | bytes 884768 | tf_op jit(solution)/shard_map/all_to_all | solution.py:211
  76.9 0.8 slots.1
  77.7 12.0 %all-to-all-start.4 = ((bf16[16,4,200]{2,1,0:T(4,128)(2,1)}), bf16[16,4,200]{2,1,0:T(4,128)(2,1)S(1)}, u32[]{:S(2)}, u32[]{:S(2)}) async-start(bf16[16,4,200]{2,1,0:T(4,128)(2,1)} %get-tuple-element.23), calls=%async_computation.4 | async-start | bytes 65536 | tf_op jit(solution)/shard_map/all_to_all | solution.py:211
  89.7 0.0 collective-permute-done
  89.7 1.3 add_convert_fusion
  91.0 6.1 %all-to-all-done.4.owned_ref = bf16[16,4,200]{2,1,0:T(4,128)(2,1)S(1)} async-done(((bf16[16,4,200]{2,1,0:T(4,128)(2,1)}), bf16[16,4,200]{2,1,0:T(4,128)(2,1)S(1)}, u32[]{:S(2)}, u32[]{:S(2)}) %all-to-all-start.4) | async-done | bytes 25632 | tf_op jit(solution)/shard_map/all_to_all | solution.py:211
  97.1 3.6 %all-to-all-start.2 = ((bf16[8,128,512]{2,1,0:T(8,128)(2,1)}), bf16[8,128,512]{2,1,0:T(8,128)(2,1)S(1)}, u32[]{:S(2)}, u32[]{:S(2)}) async-start(bf16[8,128,512]{2,1,0:T(8,128)(2,1)} %add_convert_fusion), calls=%async_computation.2 | async-start | bytes 2097152 | tf_op jit(solution)/shard_map/all_to_all | solution.py:211
  100.7 1.0 spread.1
  101.7 28.2 %all-to-all-done.2 = bf16[8,128,512]{2,1,0:T(8,128)(2,1)S(1)} async-done(((bf16[8,128,512]{2,1,0:T(8,128)(2,1)}), bf16[8,128,512]{2,1,0:T(8,128)(2,1)S(1)}, u32[]{:S(2)}, u32[]{:S(2)}) %all-to-all-start.2) | async-done | bytes 1048608 | tf_op jit(solution)/shard_map/all_to_all | solution.py:211
  129.9 4.8 %all-to-all-start.5 = ((bf16[32,4,3200]{2,1,0:T(4,128)(2,1)}), bf16[32,4,3200]{2,1,0:T(4,128)(2,1)S(1)}, u32[]{:S(2)}, u32[]{:S(2)}) async-start(bf16[32,4,3200]{2,1,0:T(4,128)(2,1)} %spread.1), calls=%async_computation.5 | async-start | bytes 1638400 | tf_op jit(solution)/shard_map/all_to_all | solution.py:211
  134.7 0.8 reduce_sum.12
  135.5 20.9 %all-to-all-done.5.pieces_ref = bf16[32,4,3200]{2,1,0:T(4,128)(2,1)S(1)} async-done(((bf16[32,4,3200]{2,1,0:T(4,128)(2,1)}), bf16[32,4,3200]{2,1,0:T(4,128)(2,1)S(1)}, u32[]{:S(2)}, u32[]{:S(2)}) %all-to-all-start.5) | async-done | bytes 819232 | tf_op jit(solution)/shard_map/all_to_all | solution.py:211
  156.4 5.2 %ortho.1 = bf16[3200,128]{1,0:T(8,128)(2,1)} custom-call(bf16[32,4,3200]{2,1,0:T(4,128)(2,1)S(1)} %all-to-all-done.5.pieces_ref), custom_call_target="tpu_custom_call" | custom-call | tf_op jit(solution)/shard_map/ortho/pallas_call | solution.py:199
  (21 shorter events, 0.0 us)
Async XLA Ops:
  0.6 23.7 %copy-start.15 = (s32[32]{0:T(128)S(1)}, s32[32]{0:T(128)}, u32[]{:S(2)}) copy-start(s32[32]{0:T(128)} %partner_ref.5) | copy-start | bytes 388
  0.7 1.6 copy-start
  2.3 1.1 copy-start.2
  3.5 0.9 copy-start.5
  4.4 0.9 copy-start.9
  5.3 0.7 copy-start.12
  6.0 0.7 copy-start.14
  6.6 0.7 copy-start.16
  7.3 0.7 copy-start.18
  8.0 39.1 %copy-start.1 = (bf16[2048,512]{1,0:T(8,128)(2,1)S(1)}, bf16[2048,512]{1,0:T(8,128)(2,1)}, u32[]{:S(2)}) copy-start(bf16[2048,512]{1,0:T(8,128)(2,1)} %attended_ref.3) | copy-start | bytes 6291460
  8.0 39.1 %copy-start.6 = (bf16[200,384]{1,0:T(8,128)(2,1)S(1)}, bf16[200,384]{1,0:T(8,128)(2,1)}, u32[]{:S(2)}) copy-start(bf16[200,384]{1,0:T(8,128)(2,1)} %grad_ref.3) | copy-start | bytes 460804
  8.0 39.1 %copy-start.13 = (s32[32]{0:T(128)S(1)}, s32[32]{0:T(128)}, u32[]{:S(2)}) copy-start(s32[32]{0:T(128)} %frames_ref.5) | copy-start | bytes 388
  8.0 39.1 %copy-start.17 = (s32[32]{0:T(128)S(1)}, s32[32]{0:T(128)}, u32[]{:S(2)}) copy-start(s32[32]{0:T(128)} %moved_ref.5) | copy-start | bytes 388
  8.0 39.1 %copy-start.19 = (f32[200]{0:T(256)S(1)}, f32[200]{0:T(256)}, u32[]{:S(2)}) copy-start(f32[200]{0:T(256)} %param.13) | copy-start | bytes 2404
  8.0 39.1 %copy-start.20 = (s32[16]{0:T(128)S(1)}, s32[16]{0:T(128)}, u32[]{:S(2)}) copy-start(s32[16]{0:T(128)} %slot_ref.1) | copy-start | bytes 196
  9.9 0.8 copy-start.7
  10.6 23.1 %all-to-all-start = ((bf16[32,8,256]{2,1,0:T(8,128)(2,1)}), bf16[32,8,256]{2,1,0:T(8,128)(2,1)S(1)}, u32[]{:S(2)}, u32[]{:S(2)}) async-start(bf16[32,8,256]{2,1,0:T(8,128)(2,1)} %bitcast.3), calls=%async_computation | async-start | bytes 262144 | tf_op jit(solution)/shard_map/all_to_all | solution.py:211
  47.1 1.0 copy-start.8
  48.1 7.7 %copy-start.3 = (bf16[200,2048]{1,0:T(8,128)(2,1)S(1)}, bf16[200,2048]{1,0:T(8,128)(2,1)}, u32[]{:S(2)}) copy-start(bf16[200,2048]{1,0:T(8,128)(2,1)} %weight_ref.3) | copy-start | bytes 2457604
  50.3 0.9 copy-start.4
  51.2 0.7 copy-start.10
  51.9 25.0 %all-to-all-start.3 = ((bf16[32,4,3456]{2,1,0:T(4,128)(2,1)}), bf16[32,4,3456]{2,1,0:T(4,128)(2,1)S(1)}, u32[]{:S(2)}, u32[]{:S(2)}) async-start(bf16[32,4,3456]{2,1,0:T(4,128)(2,1)} %copy-done.4), calls=%async_computation.3 | async-start | bytes 1769472 | tf_op jit(solution)/shard_map/all_to_all | solution.py:211
  55.8 0.9 copy-start.11
  59.1 30.6 %collective-permute-start = (bf16[8,128,512]{2,1,0:T(8,128)(2,1)}, bf16[8,128,512]{2,1,0:T(8,128)(2,1)S(1)}, u32[]{:S(2)}, u32[]{:S(2)}) collective-permute-start(bf16[8,128,512]{2,1,0:T(8,128)(2,1)} %get-tuple-element.20), channel_id=1, source_target_pairs={{0,1},{1,0},{2,3},{3,2},{4,5},{5,4},{6,7},{7,6},{8,9},{9,8},{10,11... | collective-permute-start | bytes 3145736 | tf_op jit(solution)/shard_map/ppermute | solution.py:245
  77.7 19.4 %all-to-all-start.4 = ((bf16[16,4,200]{2,1,0:T(4,128)(2,1)}), bf16[16,4,200]{2,1,0:T(4,128)(2,1)S(1)}, u32[]{:S(2)}, u32[]{:S(2)}) async-start(bf16[16,4,200]{2,1,0:T(4,128)(2,1)} %get-tuple-element.23), calls=%async_computation.4 | async-start | bytes 65536 | tf_op jit(solution)/shard_map/all_to_all | solution.py:211
  97.1 32.8 %all-to-all-start.2 = ((bf16[8,128,512]{2,1,0:T(8,128)(2,1)}), bf16[8,128,512]{2,1,0:T(8,128)(2,1)S(1)}, u32[]{:S(2)}, u32[]{:S(2)}) async-start(bf16[8,128,512]{2,1,0:T(8,128)(2,1)} %add_convert_fusion), calls=%async_computation.2 | async-start | bytes 2097152 | tf_op jit(solution)/shard_map/all_to_all | solution.py:211
  129.9 26.5 %all-to-all-start.5 = ((bf16[32,4,3200]{2,1,0:T(4,128)(2,1)}), bf16[32,4,3200]{2,1,0:T(4,128)(2,1)S(1)}, u32[]{:S(2)}, u32[]{:S(2)}) async-start(bf16[32,4,3200]{2,1,0:T(4,128)(2,1)} %spread.1), calls=%async_computation.5 | async-start | bytes 1638400 | tf_op jit(solution)/shard_map/all_to_all | solution.py:211

commit v2 on v1

v2 whole, which is shorter than its diff:
```python
import math

import jax
import jax.numpy as jnp
from jax import lax
from jax.experimental import pallas as pl
from jax.experimental.pallas import tpu as pltpu
from jax.sharding import Mesh, PartitionSpec as P

D = 3200
HEADS = 16
HD = 128
FRAME = 256
TILE = 16
ITERS = 5
A = 2048
CAP_ROWS = 512
MOVE_ROWS = 256
BAL_ROWS = 384
N_DP = 32
N_FSDP = 16

NZ, NX, NY, NC = 8, 4, 8, 2
ROWS = D // N_FSDP
BY_X = HD // NX
BY_ZX = BY_X // NZ
WIDE = D + HD
PAD_ROWS = 256
CHUNK = 512

coeff_linear = 3.4445
coeff_square = -4.775
coeff_cubic = 2.0315
EPSILON = 1e-07
INVERSE_ROOT = 1.0 / math.sqrt(N_DP * BAL_ROWS)

bf16 = jnp.bfloat16
f32 = jnp.float32

ROWS_BY_COLS = (((0,), (0,)), ((), ()))
COLS_BY_COLS = (((1,), (1,)), ((), ()))


def positions(shape, dimension):
    return lax.broadcasted_iota(jnp.int32, shape, dimension)


def dot(a, b, dims=(((1,), (0,)), ((), ()))):
    return lax.dot_general(a, b, dims, preferred_element_type=f32)


def same(size):
    return positions((size, size), 0) == positions((size, size), 1)


def to_column(row):
    size = row.shape[1]
    return jnp.sum(jnp.where(same(size), row, 0.0), axis=1, keepdims=True)


def to_row(column):
    size = column.shape[0]
    return jnp.sum(jnp.where(same(size), column, 0.0), axis=0, keepdims=True)


def my_counts(frames_ref, partner_ref, moved_ref):
    replica = lax.axis_index("z") * NX + lax.axis_index("x")
    mate = partner_ref[replica]
    kept = frames_ref[replica] * FRAME - moved_ref[replica] * TILE
    incoming = moved_ref[mate] * TILE
    holds_two = (frames_ref[replica] > frames_ref[mate]).astype(jnp.int32)
    return kept, incoming, holds_two


def light_places(kept, incoming):
    bal_col = positions((BAL_ROWS, MOVE_ROWS), 0)
    win_col = positions((BAL_ROWS, MOVE_ROWS), 1)
    hit = bal_col == win_col + (kept + incoming - MOVE_ROWS)
    hit = hit & (win_col >= MOVE_ROWS - incoming)
    return jnp.where(hit, 1.0, 0.0).astype(bf16)


def start(sems, *pairs):
    copies = [pltpu.make_async_copy(a, b, sems.at[i]) for i, (a, b) in enumerate(pairs)]
    for copy in copies:
        copy.start()
    return copies


def wait(copies):
    for copy in copies:
        copy.wait()


def project_kernel(
    frames_hbm, partner_hbm, moved_hbm,
    attended_hbm, residual_hbm, grad_hbm, weight_hbm, scale_hbm,
    projected_hbm, layer_hbm, window_hbm,
    frames_ref, partner_ref, moved_ref,
    attended_ref, residual_ref, grad_ref, weight_ref, scale_ref,
    projected_ref, layer_ref, window_ref,
    small_sems, attended_sems, weight_sems, out_sems,
):
    small = start(
        small_sems,
        (frames_hbm, frames_ref),
        (partner_hbm, partner_ref),
        (moved_hbm, moved_ref),
        (scale_hbm, scale_ref),
        (grad_hbm, grad_ref),
        (residual_hbm, residual_ref),
    )
    cuts = [pl.ds(first, CHUNK) for first in range(0, A, CHUNK)]
    attended = start(
        attended_sems, *[(attended_hbm.at[cut, :], attended_ref.at[cut, :]) for cut in cuts]
    )
    weight = start(
        weight_sems, *[(weight_hbm.at[:, cut], weight_ref.at[:, cut]) for cut in cuts]
    )
    wait(small[:5])
    kept, incoming, holds_two = my_counts(frames_ref, partner_ref, moved_ref)
    gains = to_column(scale_ref[...])
    grad_win = dot(grad_ref[...], light_places(kept, incoming))
    window_ref[pl.ds(ROWS, PAD_ROWS - ROWS), :] = jnp.zeros(
        (PAD_ROWS - ROWS, MOVE_ROWS), bf16
    )
    projected = None
    for index, cut in enumerate(cuts):
        attended[index].wait()
        weight[index].wait()
        part = dot(weight_ref[:, cut], attended_ref[cut, :])
        projected = part if projected is None else projected + part
    small[5].wait()
    layer = (residual_ref[...].astype(f32) + gains * projected).astype(bf16)
    layer_win = layer[:, MOVE_ROWS:].astype(f32)
    window_ref[pl.ds(0, ROWS), :] = jnp.where(holds_two == 1, layer_win, grad_win).astype(bf16)
    out = start(out_sems, (window_ref, window_hbm))
    projected_ref[...] = projected
    layer_ref[...] = layer
    out += start(
        out_sems.at[pl.ds(1, 2)], (projected_ref, projected_hbm), (layer_ref, layer_hbm)
    )
    wait(out)


def weight_grad_kernel(
    frames_ref, partner_ref, moved_ref, slot_ref,
    attended_ref, grad_ref, scale_ref, got_ref, projected_hbm,
    scaled_hbm, pieces_hbm,
    head_of, wide, projected_ref, scaled_ref, pieces_ref, sems,
):
    (fetch,) = start(sems, (projected_hbm, projected_ref))
    kept, incoming, holds_two = my_counts(frames_ref, partner_ref, moved_ref)
    for head in range(HEADS):
        head_of[slot_ref[head]] = head
    own = grad_ref[...].astype(f32)
    own = jnp.concatenate([own, jnp.zeros((ROWS, CAP_ROWS - BAL_ROWS), f32)], axis=1)
    got = got_ref[pl.ds(0, ROWS), :].astype(f32)
    got = jnp.where(holds_two == 1, got, 0.0)
    got = jnp.concatenate([jnp.zeros((ROWS, CAP_ROWS - MOVE_ROWS), f32), got], axis=1)
    grad = jnp.where(positions((ROWS, CAP_ROWS), 1) < kept, own, got)
    scaled = (grad * to_column(scale_ref[...])).astype(bf16)
    scaled_ref[...] = scaled
    (store,) = start(sems.at[pl.ds(1, 1)], (scaled_ref, scaled_hbm))
    for slot in range(HEADS):
        first = pl.multiple_of(head_of[slot] * HD, HD)
        wide[:, pl.ds(slot * ROWS, ROWS)] = dot(
            attended_ref[pl.ds(first, HD), :], scaled, COLS_BY_COLS
        )
    fetch.wait()
    part = jnp.sum(grad * projected_ref[...], axis=1, keepdims=True) * INVERSE_ROOT
    part = to_row(part)
    high = part.astype(bf16).astype(f32)
    low = part - high
    rest = ROWS - HD
    zeros = jnp.zeros((1, HD - rest), f32)
    lines = [
        high[:, :HD],
        jnp.concatenate([high[:, HD:], zeros], axis=1),
        low[:, :HD],
        jnp.concatenate([low[:, HD:], zeros], axis=1),
        jnp.zeros((BY_X - 4, HD), f32),
    ]
    lines = jnp.concatenate(lines, axis=0).astype(bf16)
    stores = [store]
    for x in range(NX):
        pieces_ref[x, :, pl.ds(0, D)] = wide[pl.ds(x * BY_X, BY_X), :].astype(bf16)
        pieces_ref[x, :, pl.ds(D, HD)] = lines
        stores += start(sems.at[pl.ds(2 + x, 1)], (pieces_ref.at[x], pieces_hbm.at[x]))
    wait(stores)


def input_kernel(
    frames_ref, partner_ref, moved_ref,
    weight_ref, got_ref, scaled_hbm, layer_hbm,
    even_ref, odd_ref, layer_out_ref,
    scaled_ref, layer_ref, sems,
):
    fetch = start(sems, (scaled_hbm, scaled_ref), (layer_hbm, layer_ref))
    kept, incoming, holds_two = my_counts(frames_ref, partner_ref, moved_ref)
    block = lax.axis_index("y") * NC + lax.axis_index("c")
    fetch[0].wait()
    scaled = scaled_ref[...]
    for index, other in enumerate(EVEN):
        for ref, partner in ((even_ref, other), (odd_ref, other + 1)):
            first = pl.multiple_of((block ^ partner) * HD, HD)
            part = dot(weight_ref[:, pl.ds(first, HD)], scaled, ROWS_BY_COLS)
            ref[pl.ds(index * HD, HD), :] = part.astype(bf16)
    fetch[1].wait()
    received = dot(got_ref[pl.ds(0, ROWS), :], light_places(kept, incoming), COLS_BY_COLS)
    own = layer_ref[:, pl.ds(0, BAL_ROWS)].astype(f32)
    keep = positions((ROWS, BAL_ROWS), 1) < kept
    layer_out_ref[...] = jnp.where(keep, own, received).astype(bf16)


def slots_kernel(pieces_ref, by_slot_ref, scale_ref):
    total = pieces_ref[0].astype(f32)
    for x in range(1, NX):
        total = total + pieces_ref[x].astype(f32)
    for slot in range(HEADS):
        part = total[:, slot * ROWS : (slot + 1) * ROWS]
        for z in range(NZ):
            by_slot_ref[z * HEADS + slot] = part[z * BY_ZX : (z + 1) * BY_ZX, :].astype(bf16)
    lines = total[0:2, D:] + total[2:4, D:]
    high = lines.astype(bf16).astype(f32)
    scale_ref[...] = jnp.concatenate([high, lines - high], axis=0).astype(bf16)


def spread_kernel(owned_ref, scale_ref, copies_hbm, joined, whole, sems):
    for block in range(N_FSDP):
        total = owned_ref[block].astype(f32)
        for z in range(1, NZ):
            total = total + owned_ref[z * N_FSDP + block].astype(f32)
        joined[:, pl.ds(block * ROWS, ROWS)] = total
    joined[:, pl.ds(D, HD)] = scale_ref[...].astype(f32)
    whole[...] = joined[...].astype(bf16)
    wait(start(sems, *[(whole, copies_hbm.at[z]) for z in range(NZ)]))


def join_kernel(pieces_ref, copies_hbm, scale_grad_ref, joined, whole, sems):
    for z in range(NZ):
        joined[pl.ds(z * BY_ZX, BY_ZX), :] = pieces_ref[z, :, pl.ds(0, D)].astype(f32)
    whole[...] = joined[...].astype(bf16)
    copies = start(sems, *[(whole, copies_hbm.at[x]) for x in range(NX)])
    lines = pieces_ref[0, :, pl.ds(D, HD)].astype(f32)
    for z in range(1, NZ):
        lines = lines + pieces_ref[z, :, pl.ds(D, HD)].astype(f32)
    lines = lines[0:2, :] + lines[2:4, :]
    scale_grad_ref[...] = jnp.concatenate([lines[0:1, :], lines[1:2, : ROWS - HD]], axis=1)
    wait(copies)


def ortho_kernel(grad_ref, out_ref):
    def mul(a, b):
        return jnp.dot(a, b, precision=lax.Precision.HIGHEST, preferred_element_type=f32)

    grad = grad_ref[...]
    gram = dot(grad, grad, COLS_BY_COLS)
    eye = jnp.where(same(HD), 1.0, 0.0).astype(f32)
    squares = jnp.sum(jnp.sum(gram * eye, axis=1, keepdims=True), axis=0, keepdims=True)
    norm = jnp.sqrt(squares) + EPSILON
    gram = gram / norm / norm
    total = None
    for sweep in range(ITERS):
        step = coeff_linear * eye + coeff_square * gram + coeff_cubic * mul(gram, gram)
        total = step if total is None else mul(total, step)
        if sweep < ITERS - 1:
            gram = mul(mul(step, gram), step)
    total = total * (0.2 * math.sqrt(D) / norm)
    high = total.astype(bf16)
    low = (total - high.astype(f32)).astype(bf16)
    out = dot(grad, high, ROWS_BY_COLS) + dot(grad, low, ROWS_BY_COLS)
    out_ref[...] = out.astype(bf16)


S, V, H = pltpu.SMEM, pltpu.VMEM, pltpu.HBM


def call(kernel, name, places, arrays, outs, scratch=()):
    arrays = [
        pltpu.with_memory_space_constraint(array, H) if place is H else array
        for array, place in zip(arrays, places)
    ]
    return pl.pallas_call(
        kernel,
        out_shape=[
            H(shape, dtype) if place is H else jax.ShapeDtypeStruct(shape, dtype)
            for shape, dtype, place in outs
        ],
        in_specs=[pl.BlockSpec(memory_space=place) for place in places],
        out_specs=[pl.BlockSpec(memory_space=place) for shape, dtype, place in outs],
        scratch_shapes=list(scratch),
        compiler_params=pltpu.CompilerParams(vmem_limit_bytes=32 * 1024 * 1024),
        name=name,
    )(*arrays)


def exchange(pieces, axes):
    return lax.all_to_all(pieces, axes, split_axis=0, concat_axis=0, tiled=True)


def crossed(array, axis, size, bit):
    return lax.ppermute(array, axis, [(i, i ^ bit) for i in range(size)])


def add(a, b):
    return (a.astype(f32) + b.astype(f32)).astype(bf16)


EVEN = (0, 8, 4, 12, 2, 10, 6, 14)


def sum_blocks(even, odd):
    left = add(even, crossed(odd, "c", NC, 1))
    for bit in (1, 2, 4):
        half = left.shape[0] // 2
        left = add(left[:half], crossed(left[half:], "y", NY, bit))
    return left


def body(
    attended, residual, grad_out, out_weight, layer_scale, frames, partner, moved_tiles, owner_slot
):
    scale_row = layer_scale[None, :]
    ints = pltpu.SMEM((N_DP,), jnp.int32)
    dma = pltpu.SemaphoreType.DMA

    projected, layer_own, window = call(
        project_kernel, "project", [H] * 8,
        (frames, partner, moved_tiles, attended, residual, grad_out, out_weight, scale_row),
        [((ROWS, CAP_ROWS), f32, H), ((ROWS, CAP_ROWS), bf16, H), ((PAD_ROWS, MOVE_ROWS), bf16, H)],
        [
            ints, ints, ints,
            V((A, CAP_ROWS), bf16), V((ROWS, CAP_ROWS), bf16), V((ROWS, BAL_ROWS), bf16),
            V((ROWS, A), bf16), V((1, ROWS), f32),
            V((ROWS, CAP_ROWS), f32), V((ROWS, CAP_ROWS), bf16), V((PAD_ROWS, MOVE_ROWS), bf16),
            dma((6,)), dma((A // CHUNK,)), dma((A // CHUNK,)), dma((3,)),
        ],
    )
    pieces = exchange(window.reshape(N_DP, PAD_ROWS // N_DP, MOVE_ROWS), ("z", "x"))
    pieces = exchange(jnp.take(pieces, partner, axis=0), ("z", "x"))
    got = pieces.reshape(PAD_ROWS, MOVE_ROWS)

    scaled, pieces = call(
        weight_grad_kernel, "weight_grad", [S] * 4 + [V] * 4 + [H],
        (frames, partner, moved_tiles, owner_slot, attended, grad_out, scale_row, got, projected),
        [((ROWS, CAP_ROWS), bf16, H), ((NX, BY_X, WIDE), bf16, H)],
        [
            pltpu.SMEM((HEADS,), jnp.int32), V((HD, D), f32),
            V((ROWS, CAP_ROWS), f32), V((ROWS, CAP_ROWS), bf16),
            V((NX, BY_X, WIDE), bf16), dma((2 + NX,)),
        ],
    )
    pieces = exchange(pieces, "x")

    half = ((A // 2, CAP_ROWS), bf16, V)
    even, odd, layer_out = call(
        input_kernel, "input_grad", [S] * 3 + [V] * 2 + [H] * 2,
        (frames, partner, moved_tiles, out_weight, got, scaled, layer_own),
        [half, half, ((ROWS, BAL_ROWS), bf16, V)],
        [V((ROWS, CAP_ROWS), bf16), V((ROWS, CAP_ROWS), bf16), dma((2,))],
    )
    input_grad = sum_blocks(even, odd)

    by_slot, scale_lines = call(
        slots_kernel, "slots", [V], (pieces,),
        [((NZ * HEADS, BY_ZX, ROWS), bf16, V), ((4, HD), bf16, V)],
    )
    owned = exchange(by_slot, ("z", "y", "c"))
    (copies,) = call(
        spread_kernel, "spread", [V] * 2, (owned, scale_lines),
        [((NZ, BY_ZX, WIDE), bf16, H)],
        [V((BY_ZX, WIDE), f32), V((BY_ZX, WIDE), bf16), dma((NZ,))],
    )
    copies, scale_grad = call(
        join_kernel, "join", [V], (exchange(copies, "z"),),
        [((NX, BY_X, D), bf16, H), ((1, ROWS), f32, V)],
        [V((BY_X, D), f32), V((BY_X, D), bf16), dma((NX,))],
    )
    whole = exchange(copies, "x").reshape(HD, D)
    (ortho_update,) = call(ortho_kernel, "ortho", [V], (whole,), [((D, HD), bf16, V)])
    return (layer_out, input_grad, scale_grad.reshape(ROWS), ortho_update[:, None, :])


def solution(mesh):
    chips = Mesh(mesh.devices.reshape(NZ, NX, NY, NC), ("z", "x", "y", "c"))
    dp, fsdp = ("z", "x"), ("y", "c")
    placed = (
        P(None, dp),
        P(fsdp, dp),
        P(fsdp, dp),
        P(fsdp, None),
        P(fsdp),
        P(),
        P(),
        P(),
        P(),
    )
    return jax.shard_map(
        body,
        mesh=chips,
        in_specs=placed,
        out_specs=(P(fsdp, dp), P(fsdp, dp), P(fsdp), P(None, fsdp, None)),
        check_vma=False,
    )
```

time: 164 us -> 134 us (0.82)
  waiting for transfers between devices: 77 us -> 33 us
  blocking collectives: 12.6 us -> 37.4 us
  local copies, waits for them, and re-layouts: 12.1 us -> 2.46 us
  starting transfers between devices: 43.3 us -> 37.5 us
  Pallas kernels: 13.5 us -> 18.3 us
    all_to_all x5 -> x4, waiting for transfers between devices: 76.9 us -> 25 us  [exchange(): return lax.all_to_all(pieces, axes, split_axis=0, concat_axis=0, tiled=True)]
    all_to_all x1 -> x2, blocking collectives: 12.6 us -> 37.4 us  [exchange(): return lax.all_to_all(pieces, axes, split_axis=0, concat_axis=0, tiled=True)]
    all_to_all x5 -> x4, starting transfers between devices: 38 us -> 24.3 us  [exchange(): return lax.all_to_all(pieces, axes, split_axis=0, concat_axis=0, tiled=True)]
    unnamed x42 -> x18, local copies, waits for them, and re-layouts: 11.5 us -> 1.03 us
    ppermute x1 -> x4, starting transfers between devices: 5.23 us -> 13.2 us  [crossed(): return lax.ppermute(array, axis, [(i, i ^ bit) for i in range(size)])]
    ppermute x1 -> x4, waiting for transfers between devices: 0.01 us -> 7.94 us  [crossed(): return lax.ppermute(array, axis, [(i, i ^ bit) for i in range(size)])]
    pallas_call x6 -> x7, Pallas kernels: 13.5 us -> 18.3 us  [call(): pl.pallas_call(kernel, out_shape=[H(shape, dtype) if place is H else jax....]
  transfers between devices with their start and end apart: 6 -> 8, of which waited for: 5 -> 6; matrix products, arithmetic and copies ran while one was open for 1% -> 2% of each run, Pallas kernels for 3% -> 2%
where the time goes in v2:
time: 134 us; the launch traced here: 132 us
  starting transfers between devices  37.5 us (28%)
  blocking collectives  37.4 us (28%)
  waiting for transfers between devices  33 us (25%)
  Pallas kernels  18.3 us (14%)
  other arithmetic  2.52 us (2%)
  local copies, waits for them, and re-layouts  2.46 us (2%)
    all_to_all x2, blocking collectives, exchange(): return lax.all_to_all(pieces, axes, split_axis=0, concat_axis=0, tiled=True)  37.4 us
    all_to_all x4, waiting for transfers between devices, exchange(): return lax.all_to_all(pieces, axes, split_axis=0, concat_axis=0, tiled=True)  25 us
    all_to_all x4, starting transfers between devices, exchange(): return lax.all_to_all(pieces, axes, split_axis=0, concat_axis=0, tiled=True)  24.3 us
    pallas_call x7, Pallas kernels, call(): pl.pallas_call(kernel, out_shape=[H(shape, dtype) if place is H else jax....  18.3 us
    ppermute x4, starting transfers between devices, crossed(): return lax.ppermute(array, axis, [(i, i ^ bit) for i in range(size)])  13.2 us
    ppermute x4, waiting for transfers between devices, crossed(): return lax.ppermute(array, axis, [(i, i ^ bit) for i in range(size)])  7.94 us
  transfers between devices with their start and end apart: 8, of which 6 were waited for; matrix products, arithmetic and copies ran while one was open for 2% of the time, Pallas kernels for 2%

profile of v2, /device:TPU:1, one launch (start us, length us, event | category | flops | bytes accessed | tf_op | source)
XLA Modules:
  0.0 132.0 jit_solution(8660743116987316397)
XLA Ops:
  0.6 0.0 copy-start.4
  0.6 0.0 copy-start
  0.7 0.0 copy-start.2
  0.7 0.0 copy-start.3
  0.7 0.0 copy-start.5
  0.7 0.0 copy-start.6
  0.7 0.0 copy-start.7
  0.7 3.6 %project.1 = (f32[200,512]{1,0:T(8,128)}, bf16[200,512]{1,0:T(8,128)(2,1)}, bf16[256,256]{1,0:T(8,128)(2,1)}) custom-call(s32[32]{0:T(128)} %frames_ref.3, s32[32]{0:T(128)} %partner_ref.3, s32[32]{0:T(128)} %moved_ref.3, bf16[2048,512]{1,0:T(8,128)(2,1)} %attended_ref.1, bf16[200,512]{1,0:T(8,128)(2,1)} %residual_hbm.1, bf16[200,384]{1,0:T(8,128)(2,1)} %grad_ref.1, ...), custom_call_target="tpu_custom_call" | custom-call | tf_op jit(solution)/shard_map/project/pallas_call | solution.py:284
  4.3 0.0 copy-start.1
  4.3 13.9 %all-to-all-start = ((bf16[32,8,256]{2,1,0:T(8,128)(2,1)}), bf16[32,8,256]{2,1,0:T(8,128)(2,1)S(1)}, u32[]{:S(2)}, u32[]{:S(2)}) async-start(bf16[32,8,256]{2,1,0:T(8,128)(2,1)} %bitcast.12), calls=%async_computation | async-start | bytes 262144 | tf_op jit(solution)/shard_map/all_to_all | solution.py:299
  18.2 0.0 copy-done.4
  18.2 9.3 %all-to-all-done = bf16[32,8,256]{2,1,0:T(8,128)(2,1)S(1)} async-done(((bf16[32,8,256]{2,1,0:T(8,128)(2,1)}), bf16[32,8,256]{2,1,0:T(8,128)(2,1)S(1)}, u32[]{:S(2)}, u32[]{:S(2)}) %all-to-all-start) | async-done | bytes 131104 | tf_op jit(solution)/shard_map/all_to_all | solution.py:299
  27.5 0.6 gather_fusion
  28.1 0.1 broadcast_select_fusion
  28.2 12.6 %all_to_all.30 = bf16[32,8,256]{2,1,0:T(8,128)(2,1)S(1)} all-to-all(bf16[32,8,256]{2,1,0:T(8,128)(2,1)S(1)} %broadcast_select_fusion), channel_id=1, replica_groups=mesh['z'=8,'x'=4,'y'=8,'c'=2] {'z','x'}, dimensions={0} | all-to-all | bytes 262144 | tf_op jit(solution)/shard_map/all_to_all | solution.py:299
  40.8 0.0 copy-done
  40.8 0.0 copy-done.2
  40.8 0.0 copy-done.3
  40.8 0.0 copy-done.5
  40.8 0.0 copy-done.6
  40.9 0.0 copy-done.7
  40.9 3.5 %weight_grad.1 = (bf16[200,512]{1,0:T(8,128)(2,1)}, bf16[4,32,3328]{2,1,0:T(8,128)(2,1)}) custom-call(s32[32]{0:T(128)S(1)} %copy-done.3, s32[32]{0:T(128)S(1)} %copy-done.4, s32[32]{0:T(128)S(1)} %copy-done.5, s32[16]{0:T(128)S(1)} %copy-done.7, bf16[2048,512]{1,0:T(8,128)(2,1)S(1)} %copy-done, bf16[200,384]{1,0:T(8,128)(2,1)S(1)} %copy-done.2, ...), custom_call_target="tpu_custom_call" | custom-call | tf_op jit(solution)/shard_map/weight_grad/pallas_call | solution.py:284
  44.4 3.4 %input_grad.1 = (bf16[1024,512]{1,0:T(8,128)(2,1)S(1)}, bf16[1024,512]{1,0:T(8,128)(2,1)}, bf16[200,384]{1,0:T(8,128)(2,1)}) custom-call(s32[32]{0:T(128)S(1)} %copy-done.3, s32[32]{0:T(128)S(1)} %copy-done.4, s32[32]{0:T(128)S(1)} %copy-done.5, bf16[200,2048]{1,0:T(8,128)(2,1)S(1)} %copy-done.1, bf16[256,256]{1,0:T(8,128)(2,1)S(1)} %bitcast.8, ...), custom_call_target="tpu_custom_call" | custom-call | tf_op jit(solution)/shard_map/input_grad/pallas_call | solution.py:284
  47.8 5.2 %collective-permute-start = (bf16[1024,512]{1,0:T(8,128)(2,1)}, bf16[1024,512]{1,0:T(8,128)(2,1)S(1)}, u32[]{:S(2)}, u32[]{:S(2)}) collective-permute-start(bf16[1024,512]{1,0:T(8,128)(2,1)} %get-tuple-element.22), channel_id=1, source_target_pairs={{0,1},{1,0},{2,3},{3,2},{4,5},{5,4},{6,7},{7,6},{8,9},{9,8},{10,11... | collective-permute-start | bytes 3145736 | tf_op jit(solution)/shard_map/ppermute | solution.py:303
  53.0 3.5 %all-to-all-start.2 = ((bf16[4,32,3328]{2,1,0:T(8,128)(2,1)}), bf16[4,32,3328]{2,1,0:T(8,128)(2,1)S(1)}, u32[]{:S(2)}, u32[]{:S(2)}) async-start(bf16[4,32,3328]{2,1,0:T(8,128)(2,1)} %get-tuple-element.23), calls=%async_computation.2 | async-start | bytes 1703936 | tf_op jit(solution)/shard_map/all_to_all | solution.py:299
  56.5 0.0 collective-permute-done
  56.6 1.0 copy-done.8
  57.6 1.5 %add_convert_fusion = bf16[1024,512]{1,0:T(8,128)(2,1)S(1)} fusion(bf16[1024,512]{1,0:T(8,128)(2,1)} %copy-done.8, bf16[1024,512]{1,0:T(8,128)(2,1)S(1)} %get-tuple-element.21), kind=kLoop, calls=%fused_computation.1 | loop fusion | flops 2097152 | bytes 3145728 | tf_op jit(solution)/shard_map/convert_element_type | solution.py:307
  59.1 0.8 slice.27
  59.9 3.2 %collective-permute-start.1 = (bf16[512,512]{1,0:T(8,128)(2,1)}, bf16[512,512]{1,0:T(8,128)(2,1)S(1)}, u32[]{:S(2)}, u32[]{:S(2)}) collective-permute-start(bf16[512,512]{1,0:T(8,128)(2,1)} %slice.27), channel_id=1, source_target_pairs={{0,2},{2,0},{4,6},{6,4},{8,10},{10,8},{12,14},{14,12},{1,3},{3,1},... | collective-permute-start | bytes 1572872 | tf_op jit(solution)/shard_map/ppermute | solution.py:303
  63.1 6.6 %all-to-all-done.2.pieces_ref = bf16[4,32,3328]{2,1,0:T(8,128)(2,1)S(1)} async-done(((bf16[4,32,3328]{2,1,0:T(8,128)(2,1)}), bf16[4,32,3328]{2,1,0:T(8,128)(2,1)S(1)}, u32[]{:S(2)}, u32[]{:S(2)}) %all-to-all-start.2) | async-done | bytes 852000 | tf_op jit(solution)/shard_map/all_to_all | solution.py:299
  69.7 0.2 slots.1
  69.9 24.8 %all_to_all.31.owned_ref = bf16[128,4,200]{2,1,0:T(4,128)(2,1)S(1)} all-to-all(bf16[128,4,200]{2,1,0:T(4,128)(2,1)S(1)} %get-tuple-element.24), channel_id=1, replica_groups=mesh['z'=8,'x'=4,'y'=8,'c'=2] {'z','y','c'}, dimensions={0} | all-to-all | bytes 409600 | tf_op jit(solution)/shard_map/all_to_all | solution.py:299
  94.6 0.9 spread.1
  95.5 3.4 %all-to-all-start.4 = ((bf16[8,4,3328]{2,1,0:T(4,128)(2,1)}), bf16[8,4,3328]{2,1,0:T(4,128)(2,1)S(1)}, u32[]{:S(2)}, u32[]{:S(2)}) async-start(bf16[8,4,3328]{2,1,0:T(4,128)(2,1)} %spread.1), calls=%async_computation.4 | async-start | bytes 425984 | tf_op jit(solution)/shard_map/all_to_all | solution.py:299
  98.9 0.0 collective-permute-done.1
  98.9 0.1 add_convert_fusion.1
  99.1 2.0 %collective-permute-start.2 = (bf16[256,512]{1,0:T(8,128)(2,1)S(1)}, bf16[256,512]{1,0:T(8,128)(2,1)S(1)}, u32[]{:S(2)}, u32[]{:S(2)}) collective-permute-start(bf16[256,512]{1,0:T(8,128)(2,1)S(1)} %slice.29), channel_id=1, source_target_pairs={{0,4},{2,6},{4,0},{6,2},{8,12},{10,14},{12,8},{14,10},{1,5},{3,7},... | collective-permute-start | bytes 786440 | tf_op jit(solution)/shard_map/ppermute | solution.py:303
  101.1 8.7 %all-to-all-done.4.pieces_ref = bf16[8,4,3328]{2,1,0:T(4,128)(2,1)S(1)} async-done(((bf16[8,4,3328]{2,1,0:T(4,128)(2,1)}), bf16[8,4,3328]{2,1,0:T(4,128)(2,1)S(1)}, u32[]{:S(2)}, u32[]{:S(2)}) %all-to-all-start.4) | async-done | bytes 213024 | tf_op jit(solution)/shard_map/all_to_all | solution.py:299
  109.9 1.5 %join.1 = (bf16[4,32,3200]{2,1,0:T(8,128)(2,1)}, f32[1,200]{1,0:T(1,128)}) custom-call(bf16[8,4,3328]{2,1,0:T(4,128)(2,1)S(1)} %all-to-all-done.4.pieces_ref), custom_call_target="tpu_custom_call" | custom-call | tf_op jit(solution)/shard_map/join/pallas_call | solution.py:284
  111.4 3.5 %all-to-all-start.5 = ((bf16[4,32,3200]{2,1,0:T(8,128)(2,1)}), bf16[4,32,3200]{2,1,0:T(8,128)(2,1)S(1)}, u32[]{:S(2)}, u32[]{:S(2)}) async-start(bf16[4,32,3200]{2,1,0:T(8,128)(2,1)} %get-tuple-element.27), calls=%async_computation.5 | async-start | bytes 1638400 | tf_op jit(solution)/shard_map/all_to_all | solution.py:299
  114.9 0.5 collective-permute-done.2
  115.5 0.1 add_convert_fusion.2
  115.6 2.8 %collective-permute-start.3 = (bf16[128,512]{1,0:T(8,128)(2,1)S(1)}, bf16[128,512]{1,0:T(8,128)(2,1)S(1)}, u32[]{:S(2)}, u32[]{:S(2)}) collective-permute-start(bf16[128,512]{1,0:T(8,128)(2,1)S(1)} %slice.31), channel_id=1, source_target_pairs={{0,8},{2,10},{4,12},{6,14},{8,0},{10,2},{12,4},{14,6},{1,9},{3,11}... | collective-permute-start | bytes 393224 | tf_op jit(solution)/shard_map/ppermute | solution.py:303
  118.4 7.4 %collective-permute-done.3 = bf16[128,512]{1,0:T(8,128)(2,1)S(1)} collective-permute-done((bf16[128,512]{1,0:T(8,128)(2,1)S(1)}, bf16[128,512]{1,0:T(8,128)(2,1)S(1)}, u32[]{:S(2)}, u32[]{:S(2)}) %collective-permute-start.3) | collective-permute-done | bytes 131104 | tf_op jit(solution)/shard_map/ppermute | solution.py:303
  125.8 0.7 add_convert_fusion.3
  126.5 0.4 all-to-all-done.5
  126.9 5.2 %ortho.1 = bf16[3200,128]{1,0:T(8,128)(2,1)} custom-call(bf16[128,3200]{1,0:T(8,128)(2,1)S(1)} %bitcast.6), custom_call_target="tpu_custom_call" | custom-call | tf_op jit(solution)/shard_map/ortho/pallas_call | solution.py:284
  (7 shorter events, 0.1 us)
Async XLA Ops:
  0.6 17.5 %copy-start.4 = (s32[32]{0:T(128)S(1)}, s32[32]{0:T(128)}, u32[]{:S(2)}) copy-start(s32[32]{0:T(128)} %partner_ref.3) | copy-start | bytes 388
  0.6 40.2 %copy-start = (bf16[2048,512]{1,0:T(8,128)(2,1)S(1)}, bf16[2048,512]{1,0:T(8,128)(2,1)}, u32[]{:S(2)}) copy-start(bf16[2048,512]{1,0:T(8,128)(2,1)} %attended_ref.1) | copy-start | bytes 6291460
  0.7 40.2 %copy-start.2 = (bf16[200,384]{1,0:T(8,128)(2,1)S(1)}, bf16[200,384]{1,0:T(8,128)(2,1)}, u32[]{:S(2)}) copy-start(bf16[200,384]{1,0:T(8,128)(2,1)} %grad_ref.1) | copy-start | bytes 460804
  0.7 40.2 %copy-start.3 = (s32[32]{0:T(128)S(1)}, s32[32]{0:T(128)}, u32[]{:S(2)}) copy-start(s32[32]{0:T(128)} %frames_ref.3) | copy-start | bytes 388
  0.7 40.2 %copy-start.5 = (s32[32]{0:T(128)S(1)}, s32[32]{0:T(128)}, u32[]{:S(2)}) copy-start(s32[32]{0:T(128)} %moved_ref.3) | copy-start | bytes 388
  0.7 40.2 %copy-start.6 = (f32[200]{0:T(256)S(1)}, f32[200]{0:T(256)}, u32[]{:S(2)}) copy-start(f32[200]{0:T(256)} %param.13) | copy-start | bytes 2404
  0.7 40.2 %copy-start.7 = (s32[16]{0:T(128)S(1)}, s32[16]{0:T(128)}, u32[]{:S(2)}) copy-start(s32[16]{0:T(128)} %slot_ref.1) | copy-start | bytes 196
  4.3 40.1 %copy-start.1 = (bf16[200,2048]{1,0:T(8,128)(2,1)S(1)}, bf16[200,2048]{1,0:T(8,128)(2,1)}, u32[]{:S(2)}) copy-start(bf16[200,2048]{1,0:T(8,128)(2,1)} %weight_ref.1) | copy-start | bytes 2457604
  4.3 23.2 %all-to-all-start = ((bf16[32,8,256]{2,1,0:T(8,128)(2,1)}), bf16[32,8,256]{2,1,0:T(8,128)(2,1)S(1)}, u32[]{:S(2)}, u32[]{:S(2)}) async-start(bf16[32,8,256]{2,1,0:T(8,128)(2,1)} %bitcast.12), calls=%async_computation | async-start | bytes 262144 | tf_op jit(solution)/shard_map/all_to_all | solution.py:299
  47.8 8.8 %collective-permute-start = (bf16[1024,512]{1,0:T(8,128)(2,1)}, bf16[1024,512]{1,0:T(8,128)(2,1)S(1)}, u32[]{:S(2)}, u32[]{:S(2)}) collective-permute-start(bf16[1024,512]{1,0:T(8,128)(2,1)} %get-tuple-element.22), channel_id=1, source_target_pairs={{0,1},{1,0},{2,3},{3,2},{4,5},{5,4},{6,7},{7,6},{8,9},{9,8},{10,11... | collective-permute-start | bytes 3145736 | tf_op jit(solution)/shard_map/ppermute | solution.py:303
  53.0 16.6 %all-to-all-start.2 = ((bf16[4,32,3328]{2,1,0:T(8,128)(2,1)}), bf16[4,32,3328]{2,1,0:T(8,128)(2,1)S(1)}, u32[]{:S(2)}, u32[]{:S(2)}) async-start(bf16[4,32,3328]{2,1,0:T(8,128)(2,1)} %get-tuple-element.23), calls=%async_computation.2 | async-start | bytes 1703936 | tf_op jit(solution)/shard_map/all_to_all | solution.py:299
  56.5 1.0 copy-start.8
  59.9 39.0 %collective-permute-start.1 = (bf16[512,512]{1,0:T(8,128)(2,1)}, bf16[512,512]{1,0:T(8,128)(2,1)S(1)}, u32[]{:S(2)}, u32[]{:S(2)}) collective-permute-start(bf16[512,512]{1,0:T(8,128)(2,1)} %slice.27), channel_id=1, source_target_pairs={{0,2},{2,0},{4,6},{6,4},{8,10},{10,8},{12,14},{14,12},{1,3},{3,1},... | collective-permute-start | bytes 1572872 | tf_op jit(solution)/shard_map/ppermute | solution.py:303
  95.5 14.4 %all-to-all-start.4 = ((bf16[8,4,3328]{2,1,0:T(4,128)(2,1)}), bf16[8,4,3328]{2,1,0:T(4,128)(2,1)S(1)}, u32[]{:S(2)}, u32[]{:S(2)}) async-start(bf16[8,4,3328]{2,1,0:T(4,128)(2,1)} %spread.1), calls=%async_computation.4 | async-start | bytes 425984 | tf_op jit(solution)/shard_map/all_to_all | solution.py:299
  99.1 16.4 %collective-permute-start.2 = (bf16[256,512]{1,0:T(8,128)(2,1)S(1)}, bf16[256,512]{1,0:T(8,128)(2,1)S(1)}, u32[]{:S(2)}, u32[]{:S(2)}) collective-permute-start(bf16[256,512]{1,0:T(8,128)(2,1)S(1)} %slice.29), channel_id=1, source_target_pairs={{0,4},{2,6},{4,0},{6,2},{8,12},{10,14},{12,8},{14,10},{1,5},{3,7},... | collective-permute-start | bytes 786440 | tf_op jit(solution)/shard_map/ppermute | solution.py:303
  111.4 15.4 %all-to-all-start.5 = ((bf16[4,32,3200]{2,1,0:T(8,128)(2,1)}), bf16[4,32,3200]{2,1,0:T(8,128)(2,1)S(1)}, u32[]{:S(2)}, u32[]{:S(2)}) async-start(bf16[4,32,3200]{2,1,0:T(8,128)(2,1)} %get-tuple-element.27), calls=%async_computation.5 | async-start | bytes 1638400 | tf_op jit(solution)/shard_map/all_to_all | solution.py:299
  115.6 10.2 %collective-permute-start.3 = (bf16[128,512]{1,0:T(8,128)(2,1)S(1)}, bf16[128,512]{1,0:T(8,128)(2,1)S(1)}, u32[]{:S(2)}, u32[]{:S(2)}) collective-permute-start(bf16[128,512]{1,0:T(8,128)(2,1)S(1)} %slice.31), channel_id=1, source_target_pairs={{0,8},{2,10},{4,12},{6,14},{8,0},{10,2},{12,4},{14,6},{1,9},{3,11}... | collective-permute-start | bytes 393224 | tf_op jit(solution)/shard_map/ppermute | solution.py:303

commit v3 on v2

--- a/solution.py
+++ b/solution.py
@@ -23,7 +23,7 @@
 NZ, NX, NY, NC = 8, 4, 8, 2
 ROWS = D // N_FSDP
 BY_X = HD // NX
-BY_ZX = BY_X // NZ
+SHARE = HD // N_DP
 WIDE = D + HD
 PAD_ROWS = 256
 CHUNK = 512
@@ -172,21 +172,20 @@
     part = to_row(part)
     high = part.astype(bf16).astype(f32)
     low = part - high
-    rest = ROWS - HD
-    zeros = jnp.zeros((1, HD - rest), f32)
+    zeros = jnp.zeros((1, 2 * HD - ROWS), f32)
     lines = [
         high[:, :HD],
         jnp.concatenate([high[:, HD:], zeros], axis=1),
         low[:, :HD],
         jnp.concatenate([low[:, HD:], zeros], axis=1),
-        jnp.zeros((BY_X - 4, HD), f32),
     ]
-    lines = jnp.concatenate(lines, axis=0).astype(bf16)
+    wide[:, pl.ds(D, HD)] = jnp.concatenate(lines * N_DP, axis=0)
     stores = [store]
-    for x in range(NX):
-        pieces_ref[x, :, pl.ds(0, D)] = wide[pl.ds(x * BY_X, BY_X), :].astype(bf16)
-        pieces_ref[x, :, pl.ds(D, HD)] = lines
-        stores += start(sems.at[pl.ds(2 + x, 1)], (pieces_ref.at[x], pieces_hbm.at[x]))
+    for z in range(NZ):
+        for x in range(NX):
+            pieces_ref[z * NX + x] = wide[pl.ds((x * NZ + z) * SHARE, SHARE), :].astype(bf16)
+        cut = pl.ds(z * NX, NX)
+        stores += start(sems.at[pl.ds(2 + z, 1)], (pieces_ref.at[cut], pieces_hbm.at[cut]))
     wait(stores)
 
 
@@ -213,41 +212,29 @@
     layer_out_ref[...] = jnp.where(keep, own, received).astype(bf16)
 
 
-def slots_kernel(pieces_ref, by_slot_ref, scale_ref):
+def slots_kernel(pieces_ref, copies_hbm, scale_grad_ref, by_slot, sems):
     total = pieces_ref[0].astype(f32)
-    for x in range(1, NX):
-        total = total + pieces_ref[x].astype(f32)
+    for piece in range(1, N_DP):
+        total = total + pieces_ref[piece].astype(f32)
     for slot in range(HEADS):
-        part = total[:, slot * ROWS : (slot + 1) * ROWS]
-        for z in range(NZ):
-            by_slot_ref[z * HEADS + slot] = part[z * BY_ZX : (z + 1) * BY_ZX, :].astype(bf16)
+        by_slot[slot] = total[:, slot * ROWS : (slot + 1) * ROWS].astype(bf16)
+    copies = [
+        (by_slot, copies_hbm.at[pl.ds(z * HEADS, HEADS)]) for z in range(NZ)
+    ]
+    copies = start(sems, *copies)
     lines = total[0:2, D:] + total[2:4, D:]
-    high = lines.astype(bf16).astype(f32)
-    scale_ref[...] = jnp.concatenate([high, lines - high], axis=0).astype(bf16)
-
-
-def spread_kernel(owned_ref, scale_ref, copies_hbm, joined, whole, sems):
-    for block in range(N_FSDP):
-        total = owned_ref[block].astype(f32)
-        for z in range(1, NZ):
-            total = total + owned_ref[z * N_FSDP + block].astype(f32)
-        joined[:, pl.ds(block * ROWS, ROWS)] = total
-    joined[:, pl.ds(D, HD)] = scale_ref[...].astype(f32)
-    whole[...] = joined[...].astype(bf16)
-    wait(start(sems, *[(whole, copies_hbm.at[z]) for z in range(NZ)]))
-
-
-def join_kernel(pieces_ref, copies_hbm, scale_grad_ref, joined, whole, sems):
-    for z in range(NZ):
-        joined[pl.ds(z * BY_ZX, BY_ZX), :] = pieces_ref[z, :, pl.ds(0, D)].astype(f32)
-    whole[...] = joined[...].astype(bf16)
-    copies = start(sems, *[(whole, copies_hbm.at[x]) for x in range(NX)])
-    lines = pieces_ref[0, :, pl.ds(D, HD)].astype(f32)
-    for z in range(1, NZ):
-        lines = lines + pieces_ref[z, :, pl.ds(D, HD)].astype(f32)
-    lines = lines[0:2, :] + lines[2:4, :]
     scale_grad_ref[...] = jnp.concatenate([lines[0:1, :], lines[1:2, : ROWS - HD]], axis=1)
     wait(copies)
+
+
+def join_kernel(owned_ref, copies_hbm, joined, whole, sems):
+    for z in range(NZ):
+        for block in range(N_FSDP):
+            joined[pl.ds(z * SHARE, SHARE), pl.ds(block * ROWS, ROWS)] = owned_ref[
+                z * N_FSDP + block
+            ].astype(f32)
+    whole[...] = joined[...].astype(bf16)
+    wait(start(sems, *[(whole, copies_hbm.at[x]) for x in range(NX)]))
 
 
 def ortho_kernel(grad_ref, out_ref):
@@ -274,9 +261,10 @@
 
 
 S, V, H = pltpu.SMEM, pltpu.VMEM, pltpu.HBM
-
-
-def call(kernel, name, places, arrays, outs, scratch=()):
+FREE = pl.CostEstimate(flops=0, bytes_accessed=0, transcendentals=0)
+
+
+def call(kernel, name, places, arrays, outs, scratch=(), cost=None):
     arrays = [
         pltpu.with_memory_space_constraint(array, H) if place is H else array
         for array, place in zip(arrays, places)
@@ -292,6 +280,7 @@
         scratch_shapes=list(scratch),
         compiler_params=pltpu.CompilerParams(vmem_limit_bytes=32 * 1024 * 1024),
         name=name,
+        cost_estimate=cost,
     )(*arrays)
 
 
@@ -303,19 +292,23 @@
     return lax.ppermute(array, axis, [(i, i ^ bit) for i in range(size)])
 
 
-def add(a, b):
-    return (a.astype(f32) + b.astype(f32)).astype(bf16)
-
-
 EVEN = (0, 8, 4, 12, 2, 10, 6, 14)
 
 
-def sum_blocks(even, odd):
-    left = add(even, crossed(odd, "c", NC, 1))
-    for bit in (1, 2, 4):
-        half = left.shape[0] // 2
-        left = add(left[:half], crossed(left[half:], "y", NY, bit))
-    return left
+def add_kernel(left_ref, other_ref, *out_refs):
+    rows = left_ref.shape[0] // len(out_refs)
+    for index, out_ref in enumerate(out_refs):
+        cut = pl.ds(index * rows, rows)
+        total = left_ref[cut, :].astype(f32) + other_ref[cut, :].astype(f32)
+        out_ref[...] = total.astype(bf16)
+
+
+def add(left, other, parts):
+    rows = left.shape[0] // parts
+    return call(
+        add_kernel, "add", [V] * 2, (left, other),
+        [((rows, CAP_ROWS), bf16, V)] * parts, cost=FREE,
+    )
 
 
 def body(
@@ -344,14 +337,14 @@
     scaled, pieces = call(
         weight_grad_kernel, "weight_grad", [S] * 4 + [V] * 4 + [H],
         (frames, partner, moved_tiles, owner_slot, attended, grad_out, scale_row, got, projected),
-        [((ROWS, CAP_ROWS), bf16, H), ((NX, BY_X, WIDE), bf16, H)],
+        [((ROWS, CAP_ROWS), bf16, H), ((N_DP, SHARE, WIDE), bf16, H)],
         [
-            pltpu.SMEM((HEADS,), jnp.int32), V((HD, D), f32),
+            pltpu.SMEM((HEADS,), jnp.int32), V((HD, WIDE), f32),
             V((ROWS, CAP_ROWS), f32), V((ROWS, CAP_ROWS), bf16),
-            V((NX, BY_X, WIDE), bf16), dma((2 + NX,)),
+            V((N_DP, SHARE, WIDE), bf16), dma((2 + NZ,)),
         ],
     )
-    pieces = exchange(pieces, "x")
+    summed = exchange(pieces, ("z", "x"))
 
     half = ((A // 2, CAP_ROWS), bf16, V)
     even, odd, layer_out = call(
@@ -359,26 +352,29 @@
         (frames, partner, moved_tiles, out_weight, got, scaled, layer_own),
         [half, half, ((ROWS, BAL_ROWS), bf16, V)],
         [V((ROWS, CAP_ROWS), bf16), V((ROWS, CAP_ROWS), bf16), dma((2,))],
-    )
-    input_grad = sum_blocks(even, odd)
-
-    by_slot, scale_lines = call(
-        slots_kernel, "slots", [V], (pieces,),
-        [((NZ * HEADS, BY_ZX, ROWS), bf16, V), ((4, HD), bf16, V)],
-    )
-    owned = exchange(by_slot, ("z", "y", "c"))
+        FREE,
+    )
+    left, other = add(even, crossed(odd, "c", NC, 1), 2)
+    summed, _ = lax.optimization_barrier((summed, left))
+    copies, scale_grad = call(
+        slots_kernel, "slots", [V], (summed,),
+        [((NZ * HEADS, SHARE, ROWS), bf16, H), ((1, ROWS), f32, V)],
+        [V((HEADS, SHARE, ROWS), bf16), dma((NZ,))],
+    )
+    owned = exchange(copies, ("z", "y", "c"))
+    left, other = add(left, crossed(other, "y", NY, 1), 2)
+    left, other = add(left, crossed(other, "y", NY, 2), 2)
+    owned, _ = lax.optimization_barrier((owned, left))
     (copies,) = call(
-        spread_kernel, "spread", [V] * 2, (owned, scale_lines),
-        [((NZ, BY_ZX, WIDE), bf16, H)],
-        [V((BY_ZX, WIDE), f32), V((BY_ZX, WIDE), bf16), dma((NZ,))],
-    )
-    copies, scale_grad = call(
-        join_kernel, "join", [V], (exchange(copies, "z"),),
-        [((NX, BY_X, D), bf16, H), ((1, ROWS), f32, V)],
+        join_kernel, "join", [V], (owned,),
+        [((NX, BY_X, D), bf16, H)],
         [V((BY_X, D), f32), V((BY_X, D), bf16), dma((NX,))],
     )
+    other = crossed(other, "y", NY, 4)
     whole = exchange(copies, "x").reshape(HD, D)
     (ortho_update,) = call(ortho_kernel, "ortho", [V], (whole,), [((D, HD), bf16, V)])
+    left, other, ortho_update = lax.optimization_barrier((left, other, ortho_update))
+    (input_grad,) = add(left, other, 1)
     return (layer_out, input_grad, scale_grad.reshape(ROWS), ortho_update[:, None, :])
 
 

time: 134 us -> 128 us (0.955)
  blocking collectives: 37.4 us -> 12.6 us
  starting transfers between devices: 37.5 us -> 54.4 us
  waiting for transfers between devices: 33 us -> 38.9 us
  other arithmetic: 2.52 us -> 0.12 us
  local copies, waits for them, and re-layouts: 2.46 us -> 0.6 us
    all_to_all x2 -> x1, blocking collectives: 37.4 us -> 12.6 us  [exchange(): return lax.all_to_all(pieces, axes, split_axis=0, concat_axis=0, tiled=True)]
    all_to_all x4, starting transfers between devices: 24.3 us -> 36.4 us  [exchange(): return lax.all_to_all(pieces, axes, split_axis=0, concat_axis=0, tiled=True)]
    ppermute x4, waiting for transfers between devices: 7.94 us -> 17.2 us  [crossed(): return lax.ppermute(array, axis, [(i, i ^ bit) for i in range(size)])]
    ppermute x4, starting transfers between devices: 13.2 us -> 18 us  [crossed(): return lax.ppermute(array, axis, [(i, i ^ bit) for i in range(size)])]
    all_to_all x4, waiting for transfers between devices: 25 us -> 21.7 us  [exchange(): return lax.all_to_all(pieces, axes, split_axis=0, concat_axis=0, tiled=True)]
    convert_element_type x4 -> x0, other arithmetic: 2.4 us -> none  [add(): return (a.astype(f32) + b.astype(f32)).astype(bf16)]
    pallas_call x7 -> x10, Pallas kernels: 18.3 us -> 19.3 us  [call(): pl.pallas_call(kernel, out_shape=[H(shape, dtype) if place is H else jax....]
  transfers between devices with their start and end apart: 8 -> 8, of which waited for: 6 -> 5; matrix products, arithmetic and copies ran while one was open for 2% -> 0% of each run, Pallas kernels for 2% -> 8%
where the time goes in v3:
time: 128 us; the launch traced here: 127 us
  starting transfers between devices  54.4 us (42%)
  waiting for transfers between devices  38.9 us (30%)
  Pallas kernels  19.3 us (15%)
  blocking collectives  12.6 us (10%)
    all_to_all x4, starting transfers between devices, exchange(): return lax.all_to_all(pieces, axes, split_axis=0, concat_axis=0, tiled=True)  36.4 us
    all_to_all x4, waiting for transfers between devices, exchange(): return lax.all_to_all(pieces, axes, split_axis=0, concat_axis=0, tiled=True)  21.7 us
    pallas_call x10, Pallas kernels, call(): pl.pallas_call(kernel, out_shape=[H(shape, dtype) if place is H else jax....  19.3 us
    ppermute x4, starting transfers between devices, crossed(): return lax.ppermute(array, axis, [(i, i ^ bit) for i in range(size)])  18 us
    ppermute x4, waiting for transfers between devices, crossed(): return lax.ppermute(array, axis, [(i, i ^ bit) for i in range(size)])  17.2 us
    all_to_all x1, blocking collectives, exchange(): return lax.all_to_all(pieces, axes, split_axis=0, concat_axis=0, tiled=True)  12.6 us
  transfers between devices with their start and end apart: 8, of which 5 were waited for; matrix products, arithmetic and copies ran while one was open for 0% of the time, Pallas kernels for 8%

profile of v3, /device:TPU:1, one launch (start us, length us, event | category | flops | bytes accessed | tf_op | source)
XLA Modules:
  0.0 126.9 jit_solution(7244719432158161292)
XLA Ops:
  0.6 0.0 copy-start.4
  0.6 0.0 copy-start
  0.7 0.0 copy-start.2
  0.7 0.0 copy-start.3
  0.7 0.0 copy-start.5
  0.7 0.0 copy-start.6
  0.7 0.0 copy-start.7
  0.7 3.6 %project.1 = (f32[200,512]{1,0:T(8,128)}, bf16[200,512]{1,0:T(8,128)(2,1)}, bf16[256,256]{1,0:T(8,128)(2,1)}) custom-call(s32[32]{0:T(128)} %frames_ref.3, s32[32]{0:T(128)} %partner_ref.3, s32[32]{0:T(128)} %moved_ref.3, bf16[2048,512]{1,0:T(8,128)(2,1)} %attended_ref.1, bf16[200,512]{1,0:T(8,128)(2,1)} %residual_hbm.1, bf16[200,384]{1,0:T(8,128)(2,1)} %grad_ref.1, ...), custom_call_target="tpu_custom_call" | custom-call | tf_op jit(solution)/shard_map/project/pallas_call | solution.py:272
  4.3 13.7 %all-to-all-start = ((bf16[32,8,256]{2,1,0:T(8,128)(2,1)}), bf16[32,8,256]{2,1,0:T(8,128)(2,1)S(1)}, u32[]{:S(2)}, u32[]{:S(2)}) async-start(bf16[32,8,256]{2,1,0:T(8,128)(2,1)} %bitcast.12), calls=%async_computation | async-start | bytes 262144 | tf_op jit(solution)/shard_map/all_to_all | solution.py:288
  18.0 0.0 copy-done.4
  18.1 9.3 %all-to-all-done = bf16[32,8,256]{2,1,0:T(8,128)(2,1)S(1)} async-done(((bf16[32,8,256]{2,1,0:T(8,128)(2,1)}), bf16[32,8,256]{2,1,0:T(8,128)(2,1)S(1)}, u32[]{:S(2)}, u32[]{:S(2)}) %all-to-all-start) | async-done | bytes 131104 | tf_op jit(solution)/shard_map/all_to_all | solution.py:288
  27.4 0.6 gather_fusion
  27.9 0.1 broadcast_select_fusion
  28.0 12.6 %all_to_all.25 = bf16[32,8,256]{2,1,0:T(8,128)(2,1)S(1)} all-to-all(bf16[32,8,256]{2,1,0:T(8,128)(2,1)S(1)} %broadcast_select_fusion), channel_id=1, replica_groups=mesh['z'=8,'x'=4,'y'=8,'c'=2] {'z','x'}, dimensions={0} | all-to-all | bytes 262144 | tf_op jit(solution)/shard_map/all_to_all | solution.py:288
  40.7 0.0 copy-done
  40.7 0.0 copy-done.2
  40.7 0.0 copy-done.3
  40.7 0.0 copy-done.5
  40.7 0.0 copy-done.6
  40.7 0.0 copy-done.7
  40.7 0.0 copy-start.1
  40.7 3.6 %weight_grad.1 = (bf16[200,512]{1,0:T(8,128)(2,1)}, bf16[32,4,3328]{2,1,0:T(4,128)(2,1)}) custom-call(s32[32]{0:T(128)S(1)} %copy-done.3, s32[32]{0:T(128)S(1)} %copy-done.4, s32[32]{0:T(128)S(1)} %copy-done.5, s32[16]{0:T(128)S(1)} %copy-done.7, bf16[2048,512]{1,0:T(8,128)(2,1)S(1)} %copy-done, bf16[200,384]{1,0:T(8,128)(2,1)S(1)} %copy-done.2, ...), custom_call_target="tpu_custom_call" | custom-call | tf_op jit(solution)/shard_map/weight_grad/pallas_call | solution.py:272
  44.3 3.9 %all-to-all-start.2 = ((bf16[32,4,3328]{2,1,0:T(4,128)(2,1)}), bf16[32,4,3328]{2,1,0:T(4,128)(2,1)S(1)}, u32[]{:S(2)}, u32[]{:S(2)}) async-start(bf16[32,4,3328]{2,1,0:T(4,128)(2,1)} %get-tuple-element.38), calls=%async_computation.2 | async-start | bytes 1703936 | tf_op jit(solution)/shard_map/all_to_all | solution.py:288
  48.2 0.0 copy-done.1
  48.3 3.2 %input_grad.1 = (bf16[1024,512]{1,0:T(8,128)(2,1)S(1)}, bf16[1024,512]{1,0:T(8,128)(2,1)S(1)}, bf16[200,384]{1,0:T(8,128)(2,1)}) custom-call(s32[32]{0:T(128)S(1)} %copy-done.3, s32[32]{0:T(128)S(1)} %copy-done.4, s32[32]{0:T(128)S(1)} %copy-done.5, bf16[200,2048]{1,0:T(8,128)(2,1)S(1)} %copy-done.1, bf16[256,256]{1,0:T(8,128)(2,1)S(1)} %bitcast.8, ...), custom_call_target="tpu_custom_call" | custom-call | tf_op jit(solution)/shard_map/input_grad/pallas_call | solution.py:272
  51.5 5.3 %collective-permute-start = (bf16[1024,512]{1,0:T(8,128)(2,1)S(1)}, bf16[1024,512]{1,0:T(8,128)(2,1)S(1)}, u32[]{:S(2)}, u32[]{:S(2)}) collective-permute-start(bf16[1024,512]{1,0:T(8,128)(2,1)S(1)} %get-tuple-element.31), channel_id=1, source_target_pairs={{0,1},{1,0},{2,3},{3,2},{4,5},{5,4},{6,7},{7,6},{8,9},{9,8},{10,11... | collective-permute-start | bytes 3145736 | tf_op jit(solution)/shard_map/ppermute | solution.py:292
  56.7 2.3 %collective-permute-done.other_ref = bf16[1024,512]{1,0:T(8,128)(2,1)S(1)} collective-permute-done((bf16[1024,512]{1,0:T(8,128)(2,1)S(1)}, bf16[1024,512]{1,0:T(8,128)(2,1)S(1)}, u32[]{:S(2)}, u32[]{:S(2)}) %collective-permute-start) | collective-permute-done | bytes 1048608 | tf_op jit(solution)/shard_map/ppermute | solution.py:292
  59.0 0.2 add.20
  59.3 3.2 %collective-permute-start.1 = (bf16[512,512]{1,0:T(8,128)(2,1)S(1)}, bf16[512,512]{1,0:T(8,128)(2,1)S(1)}, u32[]{:S(2)}, u32[]{:S(2)}) collective-permute-start(bf16[512,512]{1,0:T(8,128)(2,1)S(1)} %get-tuple-element.33), channel_id=1, source_target_pairs={{0,2},{2,0},{4,6},{6,4},{8,10},{10,8},{12,14},{14,12},{1,3},{3,1},... | collective-permute-start | bytes 1572872 | tf_op jit(solution)/shard_map/ppermute | solution.py:292
  62.4 6.1 %all-to-all-done.2.pieces_ref = bf16[32,4,3328]{2,1,0:T(4,128)(2,1)S(1)} async-done(((bf16[32,4,3328]{2,1,0:T(4,128)(2,1)}), bf16[32,4,3328]{2,1,0:T(4,128)(2,1)S(1)}, u32[]{:S(2)}, u32[]{:S(2)}) %all-to-all-start.2) | async-done | bytes 852000 | tf_op jit(solution)/shard_map/all_to_all | solution.py:288
  68.5 1.5 %slots.1 = (bf16[128,4,200]{2,1,0:T(4,128)(2,1)}, f32[1,200]{1,0:T(1,128)}) custom-call(bf16[32,4,3328]{2,1,0:T(4,128)(2,1)S(1)} %all-to-all-done.2.pieces_ref), custom_call_target="tpu_custom_call" | custom-call | tf_op jit(solution)/shard_map/slots/pallas_call | solution.py:272
  70.0 15.2 %all-to-all-start.3 = ((bf16[128,4,200]{2,1,0:T(4,128)(2,1)}), bf16[128,4,200]{2,1,0:T(4,128)(2,1)S(1)}, u32[]{:S(2)}, u32[]{:S(2)}) async-start(bf16[128,4,200]{2,1,0:T(4,128)(2,1)} %get-tuple-element.40), calls=%async_computation.3 | async-start | bytes 524288 | tf_op jit(solution)/shard_map/all_to_all | solution.py:288
  85.3 0.0 collective-permute-done.1.other_ref
  85.3 0.1 add.21
  85.4 4.2 %collective-permute-start.2 = (bf16[256,512]{1,0:T(8,128)(2,1)S(1)}, bf16[256,512]{1,0:T(8,128)(2,1)S(1)}, u32[]{:S(2)}, u32[]{:S(2)}) collective-permute-start(bf16[256,512]{1,0:T(8,128)(2,1)S(1)} %get-tuple-element.35), channel_id=1, source_target_pairs={{0,4},{2,6},{4,0},{6,2},{8,12},{10,14},{12,8},{14,10},{1,5},{3,7},... | collective-permute-start | bytes 786440 | tf_op jit(solution)/shard_map/ppermute | solution.py:292
  89.6 14.9 %collective-permute-done.2.other_ref = bf16[256,512]{1,0:T(8,128)(2,1)S(1)} collective-permute-done((bf16[256,512]{1,0:T(8,128)(2,1)S(1)}, bf16[256,512]{1,0:T(8,128)(2,1)S(1)}, u32[]{:S(2)}, u32[]{:S(2)}) %collective-permute-start.2) | collective-permute-done | bytes 262176 | tf_op jit(solution)/shard_map/ppermute | solution.py:292
  104.5 0.1 add.22
  104.6 0.0 all-to-all-done.3.owned_ref
  104.6 1.2 join.1
  105.7 3.5 %all-to-all-start.4 = ((bf16[4,32,3200]{2,1,0:T(8,128)(2,1)}), bf16[4,32,3200]{2,1,0:T(8,128)(2,1)S(1)}, u32[]{:S(2)}, u32[]{:S(2)}) async-start(bf16[4,32,3200]{2,1,0:T(8,128)(2,1)} %join.1), calls=%async_computation.4 | async-start | bytes 1638400 | tf_op jit(solution)/shard_map/all_to_all | solution.py:288
  109.3 5.4 %collective-permute-start.3 = (bf16[128,512]{1,0:T(8,128)(2,1)S(1)}, bf16[128,512]{1,0:T(8,128)(2,1)S(1)}, u32[]{:S(2)}, u32[]{:S(2)}) collective-permute-start(bf16[128,512]{1,0:T(8,128)(2,1)S(1)} %get-tuple-element.37), channel_id=1, source_target_pairs={{0,8},{2,10},{4,12},{6,14},{8,0},{10,2},{12,4},{14,6},{1,9},{3,11}... | collective-permute-start | bytes 393224 | tf_op jit(solution)/shard_map/ppermute | solution.py:292
  114.7 6.4 %all-to-all-done.4 = bf16[4,32,3200]{2,1,0:T(8,128)(2,1)S(1)} async-done(((bf16[4,32,3200]{2,1,0:T(8,128)(2,1)}), bf16[4,32,3200]{2,1,0:T(8,128)(2,1)S(1)}, u32[]{:S(2)}, u32[]{:S(2)}) %all-to-all-start.4) | async-done | bytes 819232 | tf_op jit(solution)/shard_map/all_to_all | solution.py:288
  121.1 5.2 %ortho.1 = bf16[3200,128]{1,0:T(8,128)(2,1)} custom-call(bf16[128,3200]{1,0:T(8,128)(2,1)S(1)} %bitcast.6), custom_call_target="tpu_custom_call" | custom-call | tf_op jit(solution)/shard_map/ortho/pallas_call | solution.py:272
  126.2 0.0 collective-permute-done.3.other_ref
  126.2 0.7 add.23
  (3 shorter events, 0.0 us)
Async XLA Ops:
  0.6 17.4 %copy-start.4 = (s32[32]{0:T(128)S(1)}, s32[32]{0:T(128)}, u32[]{:S(2)}) copy-start(s32[32]{0:T(128)} %partner_ref.3) | copy-start | bytes 388
  0.6 40.1 %copy-start = (bf16[2048,512]{1,0:T(8,128)(2,1)S(1)}, bf16[2048,512]{1,0:T(8,128)(2,1)}, u32[]{:S(2)}) copy-start(bf16[2048,512]{1,0:T(8,128)(2,1)} %attended_ref.1) | copy-start | bytes 6291460
  0.7 40.0 %copy-start.2 = (bf16[200,384]{1,0:T(8,128)(2,1)S(1)}, bf16[200,384]{1,0:T(8,128)(2,1)}, u32[]{:S(2)}) copy-start(bf16[200,384]{1,0:T(8,128)(2,1)} %grad_ref.1) | copy-start | bytes 460804
  0.7 40.0 %copy-start.3 = (s32[32]{0:T(128)S(1)}, s32[32]{0:T(128)}, u32[]{:S(2)}) copy-start(s32[32]{0:T(128)} %frames_ref.3) | copy-start | bytes 388
  0.7 40.0 %copy-start.5 = (s32[32]{0:T(128)S(1)}, s32[32]{0:T(128)}, u32[]{:S(2)}) copy-start(s32[32]{0:T(128)} %moved_ref.3) | copy-start | bytes 388
  0.7 40.0 %copy-start.6 = (f32[200]{0:T(256)S(1)}, f32[200]{0:T(256)}, u32[]{:S(2)}) copy-start(f32[200]{0:T(256)} %param.13) | copy-start | bytes 2404
  0.7 40.0 %copy-start.7 = (s32[16]{0:T(128)S(1)}, s32[16]{0:T(128)}, u32[]{:S(2)}) copy-start(s32[16]{0:T(128)} %slot_ref.1) | copy-start | bytes 196
  4.3 23.1 %all-to-all-start = ((bf16[32,8,256]{2,1,0:T(8,128)(2,1)}), bf16[32,8,256]{2,1,0:T(8,128)(2,1)S(1)}, u32[]{:S(2)}, u32[]{:S(2)}) async-start(bf16[32,8,256]{2,1,0:T(8,128)(2,1)} %bitcast.12), calls=%async_computation | async-start | bytes 262144 | tf_op jit(solution)/shard_map/all_to_all | solution.py:288
  40.7 7.5 %copy-start.1 = (bf16[200,2048]{1,0:T(8,128)(2,1)S(1)}, bf16[200,2048]{1,0:T(8,128)(2,1)}, u32[]{:S(2)}) copy-start(bf16[200,2048]{1,0:T(8,128)(2,1)} %weight_ref.1) | copy-start | bytes 2457604
  44.3 24.2 %all-to-all-start.2 = ((bf16[32,4,3328]{2,1,0:T(4,128)(2,1)}), bf16[32,4,3328]{2,1,0:T(4,128)(2,1)S(1)}, u32[]{:S(2)}, u32[]{:S(2)}) async-start(bf16[32,4,3328]{2,1,0:T(4,128)(2,1)} %get-tuple-element.38), calls=%async_computation.2 | async-start | bytes 1703936 | tf_op jit(solution)/shard_map/all_to_all | solution.py:288
  51.5 7.5 %collective-permute-start = (bf16[1024,512]{1,0:T(8,128)(2,1)S(1)}, bf16[1024,512]{1,0:T(8,128)(2,1)S(1)}, u32[]{:S(2)}, u32[]{:S(2)}) collective-permute-start(bf16[1024,512]{1,0:T(8,128)(2,1)S(1)} %get-tuple-element.31), channel_id=1, source_target_pairs={{0,1},{1,0},{2,3},{3,2},{4,5},{5,4},{6,7},{7,6},{8,9},{9,8},{10,11... | collective-permute-start | bytes 3145736 | tf_op jit(solution)/shard_map/ppermute | solution.py:292
  59.3 26.0 %collective-permute-start.1 = (bf16[512,512]{1,0:T(8,128)(2,1)S(1)}, bf16[512,512]{1,0:T(8,128)(2,1)S(1)}, u32[]{:S(2)}, u32[]{:S(2)}) collective-permute-start(bf16[512,512]{1,0:T(8,128)(2,1)S(1)} %get-tuple-element.33), channel_id=1, source_target_pairs={{0,2},{2,0},{4,6},{6,4},{8,10},{10,8},{12,14},{14,12},{1,3},{3,1},... | collective-permute-start | bytes 1572872 | tf_op jit(solution)/shard_map/ppermute | solution.py:292
  70.0 34.5 %all-to-all-start.3 = ((bf16[128,4,200]{2,1,0:T(4,128)(2,1)}), bf16[128,4,200]{2,1,0:T(4,128)(2,1)S(1)}, u32[]{:S(2)}, u32[]{:S(2)}) async-start(bf16[128,4,200]{2,1,0:T(4,128)(2,1)} %get-tuple-element.40), calls=%async_computation.3 | async-start | bytes 524288 | tf_op jit(solution)/shard_map/all_to_all | solution.py:288
  85.4 19.1 %collective-permute-start.2 = (bf16[256,512]{1,0:T(8,128)(2,1)S(1)}, bf16[256,512]{1,0:T(8,128)(2,1)S(1)}, u32[]{:S(2)}, u32[]{:S(2)}) collective-permute-start(bf16[256,512]{1,0:T(8,128)(2,1)S(1)} %get-tuple-element.35), channel_id=1, source_target_pairs={{0,4},{2,6},{4,0},{6,2},{8,12},{10,14},{12,8},{14,10},{1,5},{3,7},... | collective-permute-start | bytes 786440 | tf_op jit(solution)/shard_map/ppermute | solution.py:292
  105.7 15.3 %all-to-all-start.4 = ((bf16[4,32,3200]{2,1,0:T(8,128)(2,1)}), bf16[4,32,3200]{2,1,0:T(8,128)(2,1)S(1)}, u32[]{:S(2)}, u32[]{:S(2)}) async-start(bf16[4,32,3200]{2,1,0:T(8,128)(2,1)} %join.1), calls=%async_computation.4 | async-start | bytes 1638400 | tf_op jit(solution)/shard_map/all_to_all | solution.py:288
  109.3 17.0 %collective-permute-start.3 = (bf16[128,512]{1,0:T(8,128)(2,1)S(1)}, bf16[128,512]{1,0:T(8,128)(2,1)S(1)}, u32[]{:S(2)}, u32[]{:S(2)}) collective-permute-start(bf16[128,512]{1,0:T(8,128)(2,1)S(1)} %get-tuple-element.37), channel_id=1, source_target_pairs={{0,8},{2,10},{4,12},{6,14},{8,0},{10,2},{12,4},{14,6},{1,9},{3,11}... | collective-permute-start | bytes 393224 | tf_op jit(solution)/shard_map/ppermute | solution.py:292

commit v4 on v3

--- a/solution.py
+++ b/solution.py
@@ -1,3 +1,4 @@
+import functools
 import math
 
 import jax
@@ -24,7 +25,8 @@
 ROWS = D // N_FSDP
 BY_X = HD // NX
 SHARE = HD // N_DP
-WIDE = D + HD
+HALF = D // NC
+WIDE = 14 * HD
 PAD_ROWS = 256
 CHUNK = 512
 
@@ -162,11 +164,12 @@
     scaled = (grad * to_column(scale_ref[...])).astype(bf16)
     scaled_ref[...] = scaled
     (store,) = start(sems.at[pl.ds(1, 1)], (scaled_ref, scaled_hbm))
-    for slot in range(HEADS):
-        first = pl.multiple_of(head_of[slot] * HD, HD)
-        wide[:, pl.ds(slot * ROWS, ROWS)] = dot(
-            attended_ref[pl.ds(first, HD), :], scaled, COLS_BY_COLS
-        )
+    for y in range(NY):
+        for c in range(NC):
+            first = pl.multiple_of(head_of[y * NC + c] * HD, HD)
+            wide[c, :, pl.ds(y * ROWS, ROWS)] = dot(
+                attended_ref[pl.ds(first, HD), :], scaled, COLS_BY_COLS
+            )
     fetch.wait()
     part = jnp.sum(grad * projected_ref[...], axis=1, keepdims=True) * INVERSE_ROOT
     part = to_row(part)
@@ -179,12 +182,17 @@
         low[:, :HD],
         jnp.concatenate([low[:, HD:], zeros], axis=1),
     ]
-    wide[:, pl.ds(D, HD)] = jnp.concatenate(lines * N_DP, axis=0)
+    lines = jnp.concatenate(lines * N_DP, axis=0)
+    for c in range(NC):
+        wide[c, :, pl.ds(HALF, WIDE - HD - HALF)] = jnp.zeros((HD, WIDE - HD - HALF), f32)
+        wide[c, :, pl.ds(WIDE - HD, HD)] = lines
     stores = [store]
     for z in range(NZ):
         for x in range(NX):
-            pieces_ref[z * NX + x] = wide[pl.ds((x * NZ + z) * SHARE, SHARE), :].astype(bf16)
-        cut = pl.ds(z * NX, NX)
+            cut = pl.ds((x * NZ + z) * SHARE, SHARE)
+            for c in range(NC):
+                pieces_ref[(z * NX + x) * NC + c] = wide[c, cut, :].astype(bf16)
+        cut = pl.ds(z * NX * NC, NX * NC)
         stores += start(sems.at[pl.ds(2 + z, 1)], (pieces_ref.at[cut], pieces_hbm.at[cut]))
     wait(stores)
 
@@ -213,25 +221,28 @@
 
 
 def slots_kernel(pieces_ref, copies_hbm, scale_grad_ref, by_slot, sems):
-    total = pieces_ref[0].astype(f32)
-    for piece in range(1, N_DP):
-        total = total + pieces_ref[piece].astype(f32)
-    for slot in range(HEADS):
-        by_slot[slot] = total[:, slot * ROWS : (slot + 1) * ROWS].astype(bf16)
-    copies = [
-        (by_slot, copies_hbm.at[pl.ds(z * HEADS, HEADS)]) for z in range(NZ)
-    ]
+    totals = []
+    for c in range(NC):
+        total = pieces_ref[c].astype(f32)
+        for replica in range(1, N_DP):
+            total = total + pieces_ref[replica * NC + c].astype(f32)
+        totals.append(total)
+    for y in range(NY):
+        both = [total[:, y * ROWS : (y + 1) * ROWS] for total in totals]
+        by_slot[y] = jnp.concatenate(both, axis=1).astype(bf16)
+    copies = [(by_slot, copies_hbm.at[pl.ds(z * NY, NY)]) for z in range(NZ)]
     copies = start(sems, *copies)
-    lines = total[0:2, D:] + total[2:4, D:]
+    lines = [total[0:2, WIDE - HD :] + total[2:4, WIDE - HD :] for total in totals]
+    lines = jnp.where(lax.axis_index("c") == 0, lines[0], lines[1])
     scale_grad_ref[...] = jnp.concatenate([lines[0:1, :], lines[1:2, : ROWS - HD]], axis=1)
     wait(copies)
 
 
 def join_kernel(owned_ref, copies_hbm, joined, whole, sems):
     for z in range(NZ):
-        for block in range(N_FSDP):
-            joined[pl.ds(z * SHARE, SHARE), pl.ds(block * ROWS, ROWS)] = owned_ref[
-                z * N_FSDP + block
+        for y in range(NY):
+            joined[pl.ds(z * SHARE, SHARE), pl.ds(y * NC * ROWS, NC * ROWS)] = owned_ref[
+                z * NY + y
             ].astype(f32)
     whole[...] = joined[...].astype(bf16)
     wait(start(sems, *[(whole, copies_hbm.at[x]) for x in range(NX)]))
@@ -295,18 +306,21 @@
 EVEN = (0, 8, 4, 12, 2, 10, 6, 14)
 
 
-def add_kernel(left_ref, other_ref, *out_refs):
-    rows = left_ref.shape[0] // len(out_refs)
+def add_kernel(*refs, parts):
+    in_refs, out_refs = refs[:-parts], refs[-parts:]
+    rows = in_refs[0].shape[0] // parts
     for index, out_ref in enumerate(out_refs):
         cut = pl.ds(index * rows, rows)
-        total = left_ref[cut, :].astype(f32) + other_ref[cut, :].astype(f32)
+        total = in_refs[0][cut, :].astype(f32)
+        for ref in in_refs[1:]:
+            total = total + ref[cut, :].astype(f32)
         out_ref[...] = total.astype(bf16)
 
 
-def add(left, other, parts):
-    rows = left.shape[0] // parts
+def add(arrays, parts):
+    rows = arrays[0].shape[0] // parts
     return call(
-        add_kernel, "add", [V] * 2, (left, other),
+        functools.partial(add_kernel, parts=parts), "add", [V] * len(arrays), arrays,
         [((rows, CAP_ROWS), bf16, V)] * parts, cost=FREE,
     )
 
@@ -337,14 +351,14 @@
     scaled, pieces = call(
         weight_grad_kernel, "weight_grad", [S] * 4 + [V] * 4 + [H],
         (frames, partner, moved_tiles, owner_slot, attended, grad_out, scale_row, got, projected),
-        [((ROWS, CAP_ROWS), bf16, H), ((N_DP, SHARE, WIDE), bf16, H)],
+        [((ROWS, CAP_ROWS), bf16, H), ((N_DP * NC, SHARE, WIDE), bf16, H)],
         [
-            pltpu.SMEM((HEADS,), jnp.int32), V((HD, WIDE), f32),
+            pltpu.SMEM((HEADS,), jnp.int32), V((NC, HD, WIDE), f32),
             V((ROWS, CAP_ROWS), f32), V((ROWS, CAP_ROWS), bf16),
-            V((N_DP, SHARE, WIDE), bf16), dma((2 + NZ,)),
+            V((N_DP * NC, SHARE, WIDE), bf16), dma((2 + NZ,)),
         ],
     )
-    summed = exchange(pieces, ("z", "x"))
+    summed = exchange(pieces, ("z", "x", "c"))
 
     half = ((A // 2, CAP_ROWS), bf16, V)
     even, odd, layer_out = call(
@@ -354,27 +368,26 @@
         [V((ROWS, CAP_ROWS), bf16), V((ROWS, CAP_ROWS), bf16), dma((2,))],
         FREE,
     )
-    left, other = add(even, crossed(odd, "c", NC, 1), 2)
+    left, other = add((even, crossed(odd, "c", NC, 1)), 2)
     summed, _ = lax.optimization_barrier((summed, left))
     copies, scale_grad = call(
         slots_kernel, "slots", [V], (summed,),
-        [((NZ * HEADS, SHARE, ROWS), bf16, H), ((1, ROWS), f32, V)],
-        [V((HEADS, SHARE, ROWS), bf16), dma((NZ,))],
-    )
-    owned = exchange(copies, ("z", "y", "c"))
-    left, other = add(left, crossed(other, "y", NY, 1), 2)
-    left, other = add(left, crossed(other, "y", NY, 2), 2)
+        [((NZ * NY, SHARE, NC * ROWS), bf16, H), ((1, ROWS), f32, V)],
+        [V((NY, SHARE, NC * ROWS), bf16), dma((NZ,))],
+    )
+    owned = exchange(copies, ("z", "y"))
+    left, *others = add((left, crossed(other, "y", NY, 1)), 4)
     owned, _ = lax.optimization_barrier((owned, left))
+    others = [crossed(other, "y", NY, step) for other, step in zip(others, (4, 2, 6))]
     (copies,) = call(
         join_kernel, "join", [V], (owned,),
         [((NX, BY_X, D), bf16, H)],
         [V((BY_X, D), f32), V((BY_X, D), bf16), dma((NX,))],
     )
-    other = crossed(other, "y", NY, 4)
     whole = exchange(copies, "x").reshape(HD, D)
     (ortho_update,) = call(ortho_kernel, "ortho", [V], (whole,), [((D, HD), bf16, V)])
-    left, other, ortho_update = lax.optimization_barrier((left, other, ortho_update))
-    (input_grad,) = add(left, other, 1)
+    left, others, ortho_update = lax.optimization_barrier((left, others, ortho_update))
+    (input_grad,) = add((left, *others), 1)
     return (layer_out, input_grad, scale_grad.reshape(ROWS), ortho_update[:, None, :])
 
 

time: 128 us -> 128 us (level)
  starting transfers between devices: 54.4 us -> 52.2 us
  waiting for transfers between devices: 38.9 us -> 40.5 us
    all_to_all x4, waiting for transfers between devices: 21.7 us -> 35.8 us  [exchange(): return lax.all_to_all(pieces, axes, split_axis=0, concat_axis=0, tiled=True)]
    ppermute x4 -> x5, waiting for transfers between devices: 17.2 us -> 4.73 us  [crossed(): return lax.ppermute(array, axis, [(i, i ^ bit) for i in range(size)])]
    ppermute x4 -> x5, starting transfers between devices: 18 us -> 17 us  [crossed(): return lax.ppermute(array, axis, [(i, i ^ bit) for i in range(size)])]
    pallas_call x10 -> x9, Pallas kernels: 19.3 us -> 19.4 us  [call(): pl.pallas_call(kernel, out_shape=[H(shape, dtype) if place is H else jax....]
  transfers between devices with their start and end apart: 8 -> 9, of which waited for: 5 -> 5; matrix products, arithmetic and copies ran while one was open for 0% -> 0% of each run, Pallas kernels for 8% -> 8%
where the time goes in v4:
time: 128 us; the launch traced here: 126 us
  starting transfers between devices  52.2 us (41%)
  waiting for transfers between devices  40.5 us (32%)
  Pallas kernels  19.4 us (15%)
  blocking collectives  12.6 us (10%)
    all_to_all x4, waiting for transfers between devices, exchange(): return lax.all_to_all(pieces, axes, split_axis=0, concat_axis=0, tiled=True)  35.8 us
    all_to_all x4, starting transfers between devices, exchange(): return lax.all_to_all(pieces, axes, split_axis=0, concat_axis=0, tiled=True)  35.2 us
    pallas_call x9, Pallas kernels, call(): pl.pallas_call(kernel, out_shape=[H(shape, dtype) if place is H else jax....  19.4 us
    ppermute x5, starting transfers between devices, crossed(): return lax.ppermute(array, axis, [(i, i ^ bit) for i in range(size)])  17 us
    all_to_all x1, blocking collectives, exchange(): return lax.all_to_all(pieces, axes, split_axis=0, concat_axis=0, tiled=True)  12.6 us
    ppermute x5, waiting for transfers between devices, crossed(): return lax.ppermute(array, axis, [(i, i ^ bit) for i in range(size)])  4.73 us
  transfers between devices with their start and end apart: 9, of which 5 were waited for; matrix products, arithmetic and copies ran while one was open for 0% of the time, Pallas kernels for 8%

profile of v4, /device:TPU:1, one launch (start us, length us, event | category | flops | bytes accessed | tf_op | source)
XLA Modules:
  0.0 126.4 jit_solution(14091105685399907441)
XLA Ops:
  0.6 0.0 copy-start.4
  0.6 0.0 copy-start
  0.7 0.0 copy-start.2
  0.7 0.0 copy-start.3
  0.7 0.0 copy-start.5
  0.7 0.0 copy-start.6
  0.7 0.0 copy-start.7
  0.7 3.6 %project.1 = (f32[200,512]{1,0:T(8,128)}, bf16[200,512]{1,0:T(8,128)(2,1)}, bf16[256,256]{1,0:T(8,128)(2,1)}) custom-call(s32[32]{0:T(128)} %frames_ref.3, s32[32]{0:T(128)} %partner_ref.3, s32[32]{0:T(128)} %moved_ref.3, bf16[2048,512]{1,0:T(8,128)(2,1)} %attended_ref.1, bf16[200,512]{1,0:T(8,128)(2,1)} %residual_hbm.1, bf16[200,384]{1,0:T(8,128)(2,1)} %grad_ref.1, ...), custom_call_target="tpu_custom_call" | custom-call | tf_op jit(solution)/shard_map/project/pallas_call | solution.py:283
  4.3 13.7 %all-to-all-start = ((bf16[32,8,256]{2,1,0:T(8,128)(2,1)}), bf16[32,8,256]{2,1,0:T(8,128)(2,1)S(1)}, u32[]{:S(2)}, u32[]{:S(2)}) async-start(bf16[32,8,256]{2,1,0:T(8,128)(2,1)} %bitcast.12), calls=%async_computation | async-start | bytes 262144 | tf_op jit(solution)/shard_map/all_to_all | solution.py:299
  18.0 0.0 copy-done.4
  18.1 9.3 %all-to-all-done = bf16[32,8,256]{2,1,0:T(8,128)(2,1)S(1)} async-done(((bf16[32,8,256]{2,1,0:T(8,128)(2,1)}), bf16[32,8,256]{2,1,0:T(8,128)(2,1)S(1)}, u32[]{:S(2)}, u32[]{:S(2)}) %all-to-all-start) | async-done | bytes 131104 | tf_op jit(solution)/shard_map/all_to_all | solution.py:299
  27.4 0.6 gather_fusion
  27.9 0.1 broadcast_select_fusion
  28.1 12.6 %all_to_all.25 = bf16[32,8,256]{2,1,0:T(8,128)(2,1)S(1)} all-to-all(bf16[32,8,256]{2,1,0:T(8,128)(2,1)S(1)} %broadcast_select_fusion), channel_id=1, replica_groups=mesh['z'=8,'x'=4,'y'=8,'c'=2] {'z','x'}, dimensions={0} | all-to-all | bytes 262144 | tf_op jit(solution)/shard_map/all_to_all | solution.py:299
  40.7 0.0 copy-done
  40.7 0.0 copy-done.2
  40.7 0.0 copy-done.3
  40.7 0.0 copy-done.5
  40.7 0.0 copy-done.6
  40.7 0.0 copy-done.7
  40.7 0.0 copy-start.1
  40.8 3.7 %weight_grad.1 = (bf16[200,512]{1,0:T(8,128)(2,1)}, bf16[64,4,1792]{2,1,0:T(4,128)(2,1)}) custom-call(s32[32]{0:T(128)S(1)} %copy-done.3, s32[32]{0:T(128)S(1)} %copy-done.4, s32[32]{0:T(128)S(1)} %copy-done.5, s32[16]{0:T(128)S(1)} %copy-done.7, bf16[2048,512]{1,0:T(8,128)(2,1)S(1)} %copy-done, bf16[200,384]{1,0:T(8,128)(2,1)S(1)} %copy-done.2, ...), custom_call_target="tpu_custom_call" | custom-call | tf_op jit(solution)/shard_map/weight_grad/pallas_call | solution.py:283
  44.4 7.4 %all-to-all-start.2 = ((bf16[64,4,1792]{2,1,0:T(4,128)(2,1)}), bf16[64,4,1792]{2,1,0:T(4,128)(2,1)S(1)}, u32[]{:S(2)}, u32[]{:S(2)}) async-start(bf16[64,4,1792]{2,1,0:T(4,128)(2,1)} %get-tuple-element.40), calls=%async_computation.2 | async-start | bytes 1835008 | tf_op jit(solution)/shard_map/all_to_all | solution.py:299
  51.8 0.0 copy-done.1
  51.9 3.2 %input_grad.1 = (bf16[1024,512]{1,0:T(8,128)(2,1)S(1)}, bf16[1024,512]{1,0:T(8,128)(2,1)S(1)}, bf16[200,384]{1,0:T(8,128)(2,1)}) custom-call(s32[32]{0:T(128)S(1)} %copy-done.3, s32[32]{0:T(128)S(1)} %copy-done.4, s32[32]{0:T(128)S(1)} %copy-done.5, bf16[200,2048]{1,0:T(8,128)(2,1)S(1)} %copy-done.1, bf16[256,256]{1,0:T(8,128)(2,1)S(1)} %bitcast.8, ...), custom_call_target="tpu_custom_call" | custom-call | tf_op jit(solution)/shard_map/input_grad/pallas_call | solution.py:283
  55.1 2.5 %collective-permute-start = (bf16[1024,512]{1,0:T(8,128)(2,1)S(1)}, bf16[1024,512]{1,0:T(8,128)(2,1)S(1)}, u32[]{:S(2)}, u32[]{:S(2)}) collective-permute-start(bf16[1024,512]{1,0:T(8,128)(2,1)S(1)} %get-tuple-element.33), channel_id=1, source_target_pairs={{0,1},{1,0},{2,3},{3,2},{4,5},{5,4},{6,7},{7,6},{8,9},{9,8},{10,11... | collective-permute-start | bytes 3145736 | tf_op jit(solution)/shard_map/ppermute | solution.py:303
  57.6 2.3 %collective-permute-done.refs_1_ = bf16[1024,512]{1,0:T(8,128)(2,1)S(1)} collective-permute-done((bf16[1024,512]{1,0:T(8,128)(2,1)S(1)}, bf16[1024,512]{1,0:T(8,128)(2,1)S(1)}, u32[]{:S(2)}, u32[]{:S(2)}) %collective-permute-start) | collective-permute-done | bytes 1048608 | tf_op jit(solution)/shard_map/ppermute | solution.py:303
  59.8 0.2 add.19
  60.1 3.2 %collective-permute-start.1 = (bf16[512,512]{1,0:T(8,128)(2,1)S(1)}, bf16[512,512]{1,0:T(8,128)(2,1)S(1)}, u32[]{:S(2)}, u32[]{:S(2)}) collective-permute-start(bf16[512,512]{1,0:T(8,128)(2,1)S(1)} %get-tuple-element.35), channel_id=1, source_target_pairs={{0,2},{2,0},{4,6},{6,4},{8,10},{10,8},{12,14},{14,12},{1,3},{3,1},... | collective-permute-start | bytes 1572872 | tf_op jit(solution)/shard_map/ppermute | solution.py:303
  63.3 14.0 %all-to-all-done.2.pieces_ref = bf16[64,4,1792]{2,1,0:T(4,128)(2,1)S(1)} async-done(((bf16[64,4,1792]{2,1,0:T(4,128)(2,1)}), bf16[64,4,1792]{2,1,0:T(4,128)(2,1)S(1)}, u32[]{:S(2)}, u32[]{:S(2)}) %all-to-all-start.2) | async-done | bytes 917536 | tf_op jit(solution)/shard_map/all_to_all | solution.py:299
  77.3 1.5 %slots.1 = (bf16[64,4,400]{2,1,0:T(4,128)(2,1)}, f32[1,200]{1,0:T(1,128)}) custom-call(bf16[64,4,1792]{2,1,0:T(4,128)(2,1)S(1)} %all-to-all-done.2.pieces_ref), custom_call_target="tpu_custom_call" | custom-call | tf_op jit(solution)/shard_map/slots/pallas_call | solution.py:283
  78.8 10.5 %all-to-all-start.3 = ((bf16[64,4,400]{2,1,0:T(4,128)(2,1)}), bf16[64,4,400]{2,1,0:T(4,128)(2,1)S(1)}, u32[]{:S(2)}, u32[]{:S(2)}) async-start(bf16[64,4,400]{2,1,0:T(4,128)(2,1)} %get-tuple-element.42), calls=%async_computation.3 | async-start | bytes 524288 | tf_op jit(solution)/shard_map/all_to_all | solution.py:299
  89.3 0.0 collective-permute-done.1.refs_1_
  89.4 0.1 add.20
  89.5 12.5 %all-to-all-done.3.owned_ref = bf16[64,4,400]{2,1,0:T(4,128)(2,1)S(1)} async-done(((bf16[64,4,400]{2,1,0:T(4,128)(2,1)}), bf16[64,4,400]{2,1,0:T(4,128)(2,1)S(1)}, u32[]{:S(2)}, u32[]{:S(2)}) %all-to-all-start.3) | async-done | bytes 204832 | tf_op jit(solution)/shard_map/all_to_all | solution.py:299
  102.0 1.1 join.1
  103.1 3.5 %all-to-all-start.4 = ((bf16[4,32,3200]{2,1,0:T(8,128)(2,1)}), bf16[4,32,3200]{2,1,0:T(8,128)(2,1)S(1)}, u32[]{:S(2)}, u32[]{:S(2)}) async-start(bf16[4,32,3200]{2,1,0:T(8,128)(2,1)} %join.1), calls=%async_computation.4 | async-start | bytes 1638400 | tf_op jit(solution)/shard_map/all_to_all | solution.py:299
  106.7 4.3 %collective-permute-start.2 = (bf16[128,512]{1,0:T(8,128)(2,1)S(1)}, bf16[128,512]{1,0:T(8,128)(2,1)S(1)}, u32[]{:S(2)}, u32[]{:S(2)}) collective-permute-start(bf16[128,512]{1,0:T(8,128)(2,1)S(1)} %get-tuple-element.37), channel_id=1, source_target_pairs={{0,8},{2,10},{4,12},{6,14},{8,0},{10,2},{12,4},{14,6},{1,9},{3,11}... | collective-permute-start | bytes 393224 | tf_op jit(solution)/shard_map/ppermute | solution.py:303
  111.0 2.9 %collective-permute-start.3 = (bf16[128,512]{1,0:T(8,128)(2,1)S(1)}, bf16[128,512]{1,0:T(8,128)(2,1)S(1)}, u32[]{:S(2)}, u32[]{:S(2)}) collective-permute-start(bf16[128,512]{1,0:T(8,128)(2,1)S(1)} %get-tuple-element.38), channel_id=1, source_target_pairs={{0,4},{2,6},{4,0},{6,2},{8,12},{10,14},{12,8},{14,10},{1,5},{3,7},... | collective-permute-start | bytes 393224 | tf_op jit(solution)/shard_map/ppermute | solution.py:303
  113.8 4.2 %collective-permute-start.4 = (bf16[128,512]{1,0:T(8,128)(2,1)S(1)}, bf16[128,512]{1,0:T(8,128)(2,1)S(1)}, u32[]{:S(2)}, u32[]{:S(2)}) collective-permute-start(bf16[128,512]{1,0:T(8,128)(2,1)S(1)} %get-tuple-element.39), channel_id=1, source_target_pairs={{0,12},{2,14},{4,8},{6,10},{8,4},{10,6},{12,0},{14,2},{1,13},{3,15... | collective-permute-start | bytes 393224 | tf_op jit(solution)/shard_map/ppermute | solution.py:303
  118.1 0.0 all-to-all-done.4
  118.1 5.2 %ortho.1 = bf16[3200,128]{1,0:T(8,128)(2,1)} custom-call(bf16[128,3200]{1,0:T(8,128)(2,1)S(1)} %bitcast.6), custom_call_target="tpu_custom_call" | custom-call | tf_op jit(solution)/shard_map/ortho/pallas_call | solution.py:283
  123.2 0.0 collective-permute-done.2.refs_1_
  123.2 2.5 %collective-permute-done.3.refs_2_ = bf16[128,512]{1,0:T(8,128)(2,1)S(1)} collective-permute-done((bf16[128,512]{1,0:T(8,128)(2,1)S(1)}, bf16[128,512]{1,0:T(8,128)(2,1)S(1)}, u32[]{:S(2)}, u32[]{:S(2)}) %collective-permute-start.3) | collective-permute-done | bytes 131104 | tf_op jit(solution)/shard_map/ppermute | solution.py:303
  125.7 0.0 collective-permute-done.4.refs_3_
  125.7 0.7 add.21
  (3 shorter events, 0.0 us)
Async XLA Ops:
  0.6 17.4 %copy-start.4 = (s32[32]{0:T(128)S(1)}, s32[32]{0:T(128)}, u32[]{:S(2)}) copy-start(s32[32]{0:T(128)} %partner_ref.3) | copy-start | bytes 388
  0.6 40.1 %copy-start = (bf16[2048,512]{1,0:T(8,128)(2,1)S(1)}, bf16[2048,512]{1,0:T(8,128)(2,1)}, u32[]{:S(2)}) copy-start(bf16[2048,512]{1,0:T(8,128)(2,1)} %attended_ref.1) | copy-start | bytes 6291460
  0.7 40.0 %copy-start.2 = (bf16[200,384]{1,0:T(8,128)(2,1)S(1)}, bf16[200,384]{1,0:T(8,128)(2,1)}, u32[]{:S(2)}) copy-start(bf16[200,384]{1,0:T(8,128)(2,1)} %grad_ref.1) | copy-start | bytes 460804
  0.7 40.0 %copy-start.3 = (s32[32]{0:T(128)S(1)}, s32[32]{0:T(128)}, u32[]{:S(2)}) copy-start(s32[32]{0:T(128)} %frames_ref.3) | copy-start | bytes 388
  0.7 40.0 %copy-start.5 = (s32[32]{0:T(128)S(1)}, s32[32]{0:T(128)}, u32[]{:S(2)}) copy-start(s32[32]{0:T(128)} %moved_ref.3) | copy-start | bytes 388
  0.7 40.0 %copy-start.6 = (f32[200]{0:T(256)S(1)}, f32[200]{0:T(256)}, u32[]{:S(2)}) copy-start(f32[200]{0:T(256)} %param.13) | copy-start | bytes 2404
  0.7 40.0 %copy-start.7 = (s32[16]{0:T(128)S(1)}, s32[16]{0:T(128)}, u32[]{:S(2)}) copy-start(s32[16]{0:T(128)} %slot_ref.1) | copy-start | bytes 196
  4.3 23.1 %all-to-all-start = ((bf16[32,8,256]{2,1,0:T(8,128)(2,1)}), bf16[32,8,256]{2,1,0:T(8,128)(2,1)S(1)}, u32[]{:S(2)}, u32[]{:S(2)}) async-start(bf16[32,8,256]{2,1,0:T(8,128)(2,1)} %bitcast.12), calls=%async_computation | async-start | bytes 262144 | tf_op jit(solution)/shard_map/all_to_all | solution.py:299
  40.7 11.1 %copy-start.1 = (bf16[200,2048]{1,0:T(8,128)(2,1)S(1)}, bf16[200,2048]{1,0:T(8,128)(2,1)}, u32[]{:S(2)}) copy-start(bf16[200,2048]{1,0:T(8,128)(2,1)} %weight_ref.1) | copy-start | bytes 2457604
  44.4 32.8 %all-to-all-start.2 = ((bf16[64,4,1792]{2,1,0:T(4,128)(2,1)}), bf16[64,4,1792]{2,1,0:T(4,128)(2,1)S(1)}, u32[]{:S(2)}, u32[]{:S(2)}) async-start(bf16[64,4,1792]{2,1,0:T(4,128)(2,1)} %get-tuple-element.40), calls=%async_computation.2 | async-start | bytes 1835008 | tf_op jit(solution)/shard_map/all_to_all | solution.py:299
  55.1 4.7 %collective-permute-start = (bf16[1024,512]{1,0:T(8,128)(2,1)S(1)}, bf16[1024,512]{1,0:T(8,128)(2,1)S(1)}, u32[]{:S(2)}, u32[]{:S(2)}) collective-permute-start(bf16[1024,512]{1,0:T(8,128)(2,1)S(1)} %get-tuple-element.33), channel_id=1, source_target_pairs={{0,1},{1,0},{2,3},{3,2},{4,5},{5,4},{6,7},{7,6},{8,9},{9,8},{10,11... | collective-permute-start | bytes 3145736 | tf_op jit(solution)/shard_map/ppermute | solution.py:303
  60.1 29.3 %collective-permute-start.1 = (bf16[512,512]{1,0:T(8,128)(2,1)S(1)}, bf16[512,512]{1,0:T(8,128)(2,1)S(1)}, u32[]{:S(2)}, u32[]{:S(2)}) collective-permute-start(bf16[512,512]{1,0:T(8,128)(2,1)S(1)} %get-tuple-element.35), channel_id=1, source_target_pairs={{0,2},{2,0},{4,6},{6,4},{8,10},{10,8},{12,14},{14,12},{1,3},{3,1},... | collective-permute-start | bytes 1572872 | tf_op jit(solution)/shard_map/ppermute | solution.py:303
  78.8 23.2 %all-to-all-start.3 = ((bf16[64,4,400]{2,1,0:T(4,128)(2,1)}), bf16[64,4,400]{2,1,0:T(4,128)(2,1)S(1)}, u32[]{:S(2)}, u32[]{:S(2)}) async-start(bf16[64,4,400]{2,1,0:T(4,128)(2,1)} %get-tuple-element.42), calls=%async_computation.3 | async-start | bytes 524288 | tf_op jit(solution)/shard_map/all_to_all | solution.py:299
  103.1 14.9 %all-to-all-start.4 = ((bf16[4,32,3200]{2,1,0:T(8,128)(2,1)}), bf16[4,32,3200]{2,1,0:T(8,128)(2,1)S(1)}, u32[]{:S(2)}, u32[]{:S(2)}) async-start(bf16[4,32,3200]{2,1,0:T(8,128)(2,1)} %join.1), calls=%async_computation.4 | async-start | bytes 1638400 | tf_op jit(solution)/shard_map/all_to_all | solution.py:299
  106.7 16.6 %collective-permute-start.2 = (bf16[128,512]{1,0:T(8,128)(2,1)S(1)}, bf16[128,512]{1,0:T(8,128)(2,1)S(1)}, u32[]{:S(2)}, u32[]{:S(2)}) collective-permute-start(bf16[128,512]{1,0:T(8,128)(2,1)S(1)} %get-tuple-element.37), channel_id=1, source_target_pairs={{0,8},{2,10},{4,12},{6,14},{8,0},{10,2},{12,4},{14,6},{1,9},{3,11}... | collective-permute-start | bytes 393224 | tf_op jit(solution)/shard_map/ppermute | solution.py:303
  111.0 14.8 %collective-permute-start.3 = (bf16[128,512]{1,0:T(8,128)(2,1)S(1)}, bf16[128,512]{1,0:T(8,128)(2,1)S(1)}, u32[]{:S(2)}, u32[]{:S(2)}) collective-permute-start(bf16[128,512]{1,0:T(8,128)(2,1)S(1)} %get-tuple-element.38), channel_id=1, source_target_pairs={{0,4},{2,6},{4,0},{6,2},{8,12},{10,14},{12,8},{14,10},{1,5},{3,7},... | collective-permute-start | bytes 393224 | tf_op jit(solution)/shard_map/ppermute | solution.py:303
  113.8 11.9 %collective-permute-start.4 = (bf16[128,512]{1,0:T(8,128)(2,1)S(1)}, bf16[128,512]{1,0:T(8,128)(2,1)S(1)}, u32[]{:S(2)}, u32[]{:S(2)}) collective-permute-start(bf16[128,512]{1,0:T(8,128)(2,1)S(1)} %get-tuple-element.39), channel_id=1, source_target_pairs={{0,12},{2,14},{4,8},{6,10},{8,4},{10,6},{12,0},{14,2},{1,13},{3,15... | collective-permute-start | bytes 393224 | tf_op jit(solution)/shard_map/ppermute | solution.py:303

commit v5 on v3

--- a/solution.py
+++ b/solution.py
@@ -1,3 +1,4 @@
+import functools
 import math
 
 import jax
@@ -27,6 +28,7 @@
 WIDE = D + HD
 PAD_ROWS = 256
 CHUNK = 512
+PARTS = 5
 
 coeff_linear = 3.4445
 coeff_square = -4.775
@@ -147,7 +149,7 @@
     frames_ref, partner_ref, moved_ref, slot_ref,
     attended_ref, grad_ref, scale_ref, got_ref, projected_hbm,
     scaled_hbm, pieces_hbm,
-    head_of, wide, projected_ref, scaled_ref, pieces_ref, sems,
+    head_of, product, wide, projected_ref, scaled_ref, pieces_ref, sems,
 ):
     (fetch,) = start(sems, (projected_hbm, projected_ref))
     kept, incoming, holds_two = my_counts(frames_ref, partner_ref, moved_ref)
@@ -162,11 +164,10 @@
     scaled = (grad * to_column(scale_ref[...])).astype(bf16)
     scaled_ref[...] = scaled
     (store,) = start(sems.at[pl.ds(1, 1)], (scaled_ref, scaled_hbm))
+    product[...] = dot(attended_ref[...], scaled, COLS_BY_COLS)
     for slot in range(HEADS):
         first = pl.multiple_of(head_of[slot] * HD, HD)
-        wide[:, pl.ds(slot * ROWS, ROWS)] = dot(
-            attended_ref[pl.ds(first, HD), :], scaled, COLS_BY_COLS
-        )
+        wide[:, pl.ds(slot * ROWS, ROWS)] = product[pl.ds(first, HD), :]
     fetch.wait()
     part = jnp.sum(grad * projected_ref[...], axis=1, keepdims=True) * INVERSE_ROOT
     part = to_row(part)
@@ -237,10 +238,21 @@
     wait(start(sems, *[(whole, copies_hbm.at[x]) for x in range(NX)]))
 
 
-def ortho_kernel(grad_ref, out_ref):
-    def mul(a, b):
-        return jnp.dot(a, b, precision=lax.Precision.HIGHEST, preferred_element_type=f32)
-
+def split(values):
+    high = values.astype(bf16)
+    return high, (values - high.astype(f32)).astype(bf16)
+
+
+def mul(a, b):
+    a_high, a_low = split(a)
+    b_high, b_low = split(b)
+    return dot(
+        jnp.concatenate([a_high, a_high, a_low], axis=1),
+        jnp.concatenate([b_high, b_low, b_high], axis=0),
+    )
+
+
+def ortho_kernel(grad_ref, out_hbm, out_ref, sems):
     grad = grad_ref[...]
     gram = dot(grad, grad, COLS_BY_COLS)
     eye = jnp.where(same(HD), 1.0, 0.0).astype(f32)
@@ -253,11 +265,14 @@
         total = step if total is None else mul(total, step)
         if sweep < ITERS - 1:
             gram = mul(mul(step, gram), step)
-    total = total * (0.2 * math.sqrt(D) / norm)
-    high = total.astype(bf16)
-    low = (total - high.astype(f32)).astype(bf16)
-    out = dot(grad, high, ROWS_BY_COLS) + dot(grad, low, ROWS_BY_COLS)
-    out_ref[...] = out.astype(bf16)
+    total = jnp.concatenate(split(total * (0.2 * math.sqrt(D) / norm)), axis=1)
+    stores = []
+    for index, first in enumerate(range(0, D, D // PARTS)):
+        cut = pl.ds(first, D // PARTS)
+        out = dot(grad_ref[:, cut], total, ROWS_BY_COLS)
+        out_ref[cut, :] = (out[:, :HD] + out[:, HD:]).astype(bf16)
+        stores += start(sems.at[pl.ds(index, 1)], (out_ref.at[cut, :], out_hbm.at[cut, :]))
+    wait(stores)
 
 
 S, V, H = pltpu.SMEM, pltpu.VMEM, pltpu.HBM
@@ -295,18 +310,21 @@
 EVEN = (0, 8, 4, 12, 2, 10, 6, 14)
 
 
-def add_kernel(left_ref, other_ref, *out_refs):
-    rows = left_ref.shape[0] // len(out_refs)
+def add_kernel(*refs, parts):
+    in_refs, out_refs = refs[:-parts], refs[-parts:]
+    rows = in_refs[0].shape[0] // parts
     for index, out_ref in enumerate(out_refs):
         cut = pl.ds(index * rows, rows)
-        total = left_ref[cut, :].astype(f32) + other_ref[cut, :].astype(f32)
+        total = in_refs[0][cut, :].astype(f32)
+        for ref in in_refs[1:]:
+            total = total + ref[cut, :].astype(f32)
         out_ref[...] = total.astype(bf16)
 
 
-def add(left, other, parts):
-    rows = left.shape[0] // parts
+def add(arrays, parts):
+    rows = arrays[0].shape[0] // parts
     return call(
-        add_kernel, "add", [V] * 2, (left, other),
+        functools.partial(add_kernel, parts=parts), "add", [V] * len(arrays), arrays,
         [((rows, CAP_ROWS), bf16, V)] * parts, cost=FREE,
     )
 
@@ -339,7 +357,7 @@
         (frames, partner, moved_tiles, owner_slot, attended, grad_out, scale_row, got, projected),
         [((ROWS, CAP_ROWS), bf16, H), ((N_DP, SHARE, WIDE), bf16, H)],
         [
-            pltpu.SMEM((HEADS,), jnp.int32), V((HD, WIDE), f32),
+            pltpu.SMEM((HEADS,), jnp.int32), V((A, ROWS), f32), V((HD, WIDE), f32),
             V((ROWS, CAP_ROWS), f32), V((ROWS, CAP_ROWS), bf16),
             V((N_DP, SHARE, WIDE), bf16), dma((2 + NZ,)),
         ],
@@ -354,7 +372,7 @@
         [V((ROWS, CAP_ROWS), bf16), V((ROWS, CAP_ROWS), bf16), dma((2,))],
         FREE,
     )
-    left, other = add(even, crossed(odd, "c", NC, 1), 2)
+    left, other = add((even, crossed(odd, "c", NC, 1)), 2)
     summed, _ = lax.optimization_barrier((summed, left))
     copies, scale_grad = call(
         slots_kernel, "slots", [V], (summed,),
@@ -362,19 +380,21 @@
         [V((HEADS, SHARE, ROWS), bf16), dma((NZ,))],
     )
     owned = exchange(copies, ("z", "y", "c"))
-    left, other = add(left, crossed(other, "y", NY, 1), 2)
-    left, other = add(left, crossed(other, "y", NY, 2), 2)
+    left, *others = add((left, crossed(other, "y", NY, 1)), 4)
     owned, _ = lax.optimization_barrier((owned, left))
+    others = [crossed(other, "y", NY, step) for other, step in zip(others, (4, 2, 6))]
     (copies,) = call(
         join_kernel, "join", [V], (owned,),
         [((NX, BY_X, D), bf16, H)],
         [V((BY_X, D), f32), V((BY_X, D), bf16), dma((NX,))],
     )
-    other = crossed(other, "y", NY, 4)
     whole = exchange(copies, "x").reshape(HD, D)
-    (ortho_update,) = call(ortho_kernel, "ortho", [V], (whole,), [((D, HD), bf16, V)])
-    left, other, ortho_update = lax.optimization_barrier((left, other, ortho_update))
-    (input_grad,) = add(left, other, 1)
+    (ortho_update,) = call(
+        ortho_kernel, "ortho", [V], (whole,), [((D, HD), bf16, H)],
+        [V((D, HD), bf16), dma((PARTS,))],
+    )
+    left, others, ortho_update = lax.optimization_barrier((left, others, ortho_update))
+    (input_grad,) = add((left, *others), 1)
     return (layer_out, input_grad, scale_grad.reshape(ROWS), ortho_update[:, None, :])
 
 

time: 128 us -> 125 us (0.977)
  waiting for transfers between devices: 38.9 us -> 34.1 us
  starting transfers between devices: 54.4 us -> 56.1 us
    ppermute x4 -> x5, waiting for transfers between devices: 17.2 us -> 2.67 us  [crossed(): return lax.ppermute(array, axis, [(i, i ^ bit) for i in range(size)])]
    all_to_all x4, waiting for transfers between devices: 21.7 us -> 31.5 us  [exchange(): return lax.all_to_all(pieces, axes, split_axis=0, concat_axis=0, tiled=True)]
    ppermute x4 -> x5, starting transfers between devices: 18 us -> 19.8 us  [crossed(): return lax.ppermute(array, axis, [(i, i ^ bit) for i in range(size)])]
    pallas_call x10 -> x9, Pallas kernels: 19.3 us -> 18.8 us  [call(): pl.pallas_call(kernel, out_shape=[H(shape, dtype) if place is H else jax....]
  transfers between devices with their start and end apart: 8 -> 9, of which waited for: 5 -> 6; matrix products, arithmetic and copies ran while one was open for 0% -> 0% of each run, Pallas kernels for 8% -> 8%
where the time goes in v5:
time: 125 us; the launch traced here: 123 us
  starting transfers between devices  56.1 us (45%)
  waiting for transfers between devices  34.1 us (27%)
  Pallas kernels  18.8 us (15%)
  blocking collectives  12.6 us (10%)
    all_to_all x4, starting transfers between devices, exchange(): return lax.all_to_all(pieces, axes, split_axis=0, concat_axis=0, tiled=True)  36.3 us
    all_to_all x4, waiting for transfers between devices, exchange(): return lax.all_to_all(pieces, axes, split_axis=0, concat_axis=0, tiled=True)  31.5 us
    ppermute x5, starting transfers between devices, crossed(): return lax.ppermute(array, axis, [(i, i ^ bit) for i in range(size)])  19.8 us
    pallas_call x9, Pallas kernels, call(): pl.pallas_call(kernel, out_shape=[H(shape, dtype) if place is H else jax....  18.8 us
    all_to_all x1, blocking collectives, exchange(): return lax.all_to_all(pieces, axes, split_axis=0, concat_axis=0, tiled=True)  12.6 us
    ppermute x5, waiting for transfers between devices, crossed(): return lax.ppermute(array, axis, [(i, i ^ bit) for i in range(size)])  2.67 us
  transfers between devices with their start and end apart: 9, of which 6 were waited for; matrix products, arithmetic and copies ran while one was open for 0% of the time, Pallas kernels for 8%

profile of v5, /device:TPU:1, one launch (start us, length us, event | category | flops | bytes accessed | tf_op | source)
XLA Modules:
  0.0 123.4 jit_solution(18095374172242055775)
XLA Ops:
  0.6 0.0 copy-start.4
  0.6 0.0 copy-start
  0.7 0.0 copy-start.2
  0.7 0.0 copy-start.3
  0.7 0.0 copy-start.5
  0.7 0.0 copy-start.6
  0.7 0.0 copy-start.7
  0.7 3.6 %project.1 = (f32[200,512]{1,0:T(8,128)}, bf16[200,512]{1,0:T(8,128)(2,1)}, bf16[256,256]{1,0:T(8,128)(2,1)}) custom-call(s32[32]{0:T(128)} %frames_ref.3, s32[32]{0:T(128)} %partner_ref.3, s32[32]{0:T(128)} %moved_ref.3, bf16[2048,512]{1,0:T(8,128)(2,1)} %attended_ref.1, bf16[200,512]{1,0:T(8,128)(2,1)} %residual_hbm.1, bf16[200,384]{1,0:T(8,128)(2,1)} %grad_ref.1, ...), custom_call_target="tpu_custom_call" | custom-call | tf_op jit(solution)/shard_map/project/pallas_call | solution.py:287
  4.3 13.7 %all-to-all-start = ((bf16[32,8,256]{2,1,0:T(8,128)(2,1)}), bf16[32,8,256]{2,1,0:T(8,128)(2,1)S(1)}, u32[]{:S(2)}, u32[]{:S(2)}) async-start(bf16[32,8,256]{2,1,0:T(8,128)(2,1)} %bitcast.12), calls=%async_computation | async-start | bytes 262144 | tf_op jit(solution)/shard_map/all_to_all | solution.py:303
  18.0 0.0 copy-done.4
  18.1 9.3 %all-to-all-done = bf16[32,8,256]{2,1,0:T(8,128)(2,1)S(1)} async-done(((bf16[32,8,256]{2,1,0:T(8,128)(2,1)}), bf16[32,8,256]{2,1,0:T(8,128)(2,1)S(1)}, u32[]{:S(2)}, u32[]{:S(2)}) %all-to-all-start) | async-done | bytes 131104 | tf_op jit(solution)/shard_map/all_to_all | solution.py:303
  27.4 0.6 gather_fusion
  27.9 0.1 broadcast_select_fusion
  28.0 12.6 %all_to_all.25 = bf16[32,8,256]{2,1,0:T(8,128)(2,1)S(1)} all-to-all(bf16[32,8,256]{2,1,0:T(8,128)(2,1)S(1)} %broadcast_select_fusion), channel_id=1, replica_groups=mesh['z'=8,'x'=4,'y'=8,'c'=2] {'z','x'}, dimensions={0} | all-to-all | bytes 262144 | tf_op jit(solution)/shard_map/all_to_all | solution.py:303
  40.7 0.0 copy-done
  40.7 0.0 copy-done.2
  40.7 0.0 copy-done.3
  40.7 0.0 copy-done.5
  40.7 0.0 copy-done.6
  40.7 0.0 copy-done.7
  40.7 0.0 copy-start.1
  40.7 3.9 %weight_grad.1 = (bf16[200,512]{1,0:T(8,128)(2,1)}, bf16[32,4,3328]{2,1,0:T(4,128)(2,1)}) custom-call(s32[32]{0:T(128)S(1)} %copy-done.3, s32[32]{0:T(128)S(1)} %copy-done.4, s32[32]{0:T(128)S(1)} %copy-done.5, s32[16]{0:T(128)S(1)} %copy-done.7, bf16[2048,512]{1,0:T(8,128)(2,1)S(1)} %copy-done, bf16[200,384]{1,0:T(8,128)(2,1)S(1)} %copy-done.2, ...), custom_call_target="tpu_custom_call" | custom-call | tf_op jit(solution)/shard_map/weight_grad/pallas_call | solution.py:287
  44.7 3.9 %all-to-all-start.2 = ((bf16[32,4,3328]{2,1,0:T(4,128)(2,1)}), bf16[32,4,3328]{2,1,0:T(4,128)(2,1)S(1)}, u32[]{:S(2)}, u32[]{:S(2)}) async-start(bf16[32,4,3328]{2,1,0:T(4,128)(2,1)} %get-tuple-element.40), calls=%async_computation.2 | async-start | bytes 1703936 | tf_op jit(solution)/shard_map/all_to_all | solution.py:303
  48.6 0.0 copy-done.1
  48.6 3.2 %input_grad.1 = (bf16[1024,512]{1,0:T(8,128)(2,1)S(1)}, bf16[1024,512]{1,0:T(8,128)(2,1)S(1)}, bf16[200,384]{1,0:T(8,128)(2,1)}) custom-call(s32[32]{0:T(128)S(1)} %copy-done.3, s32[32]{0:T(128)S(1)} %copy-done.4, s32[32]{0:T(128)S(1)} %copy-done.5, bf16[200,2048]{1,0:T(8,128)(2,1)S(1)} %copy-done.1, bf16[256,256]{1,0:T(8,128)(2,1)S(1)} %bitcast.8, ...), custom_call_target="tpu_custom_call" | custom-call | tf_op jit(solution)/shard_map/input_grad/pallas_call | solution.py:287
  51.9 5.2 %collective-permute-start = (bf16[1024,512]{1,0:T(8,128)(2,1)S(1)}, bf16[1024,512]{1,0:T(8,128)(2,1)S(1)}, u32[]{:S(2)}, u32[]{:S(2)}) collective-permute-start(bf16[1024,512]{1,0:T(8,128)(2,1)S(1)} %get-tuple-element.33), channel_id=1, source_target_pairs={{0,1},{1,0},{2,3},{3,2},{4,5},{5,4},{6,7},{7,6},{8,9},{9,8},{10,11... | collective-permute-start | bytes 3145736 | tf_op jit(solution)/shard_map/ppermute | solution.py:307
  57.1 2.3 %collective-permute-done.refs_1_ = bf16[1024,512]{1,0:T(8,128)(2,1)S(1)} collective-permute-done((bf16[1024,512]{1,0:T(8,128)(2,1)S(1)}, bf16[1024,512]{1,0:T(8,128)(2,1)S(1)}, u32[]{:S(2)}, u32[]{:S(2)}) %collective-permute-start) | collective-permute-done | bytes 1048608 | tf_op jit(solution)/shard_map/ppermute | solution.py:307
  59.4 0.2 add.19
  59.6 3.2 %collective-permute-start.1 = (bf16[512,512]{1,0:T(8,128)(2,1)S(1)}, bf16[512,512]{1,0:T(8,128)(2,1)S(1)}, u32[]{:S(2)}, u32[]{:S(2)}) collective-permute-start(bf16[512,512]{1,0:T(8,128)(2,1)S(1)} %get-tuple-element.35), channel_id=1, source_target_pairs={{0,2},{2,0},{4,6},{6,4},{8,10},{10,8},{12,14},{14,12},{1,3},{3,1},... | collective-permute-start | bytes 1572872 | tf_op jit(solution)/shard_map/ppermute | solution.py:307
  62.8 6.1 %all-to-all-done.2.pieces_ref = bf16[32,4,3328]{2,1,0:T(4,128)(2,1)S(1)} async-done(((bf16[32,4,3328]{2,1,0:T(4,128)(2,1)}), bf16[32,4,3328]{2,1,0:T(4,128)(2,1)S(1)}, u32[]{:S(2)}, u32[]{:S(2)}) %all-to-all-start.2) | async-done | bytes 852000 | tf_op jit(solution)/shard_map/all_to_all | solution.py:303
  68.9 1.5 %slots.1 = (bf16[128,4,200]{2,1,0:T(4,128)(2,1)}, f32[1,200]{1,0:T(1,128)}) custom-call(bf16[32,4,3328]{2,1,0:T(4,128)(2,1)S(1)} %all-to-all-done.2.pieces_ref), custom_call_target="tpu_custom_call" | custom-call | tf_op jit(solution)/shard_map/slots/pallas_call | solution.py:287
  70.5 15.2 %all-to-all-start.3 = ((bf16[128,4,200]{2,1,0:T(4,128)(2,1)}), bf16[128,4,200]{2,1,0:T(4,128)(2,1)S(1)}, u32[]{:S(2)}, u32[]{:S(2)}) async-start(bf16[128,4,200]{2,1,0:T(4,128)(2,1)} %get-tuple-element.42), calls=%async_computation.3 | async-start | bytes 524288 | tf_op jit(solution)/shard_map/all_to_all | solution.py:303
  85.6 0.0 collective-permute-done.1.refs_1_
  85.7 0.1 add.20
  85.8 15.1 %all-to-all-done.3.owned_ref = bf16[128,4,200]{2,1,0:T(4,128)(2,1)S(1)} async-done(((bf16[128,4,200]{2,1,0:T(4,128)(2,1)}), bf16[128,4,200]{2,1,0:T(4,128)(2,1)S(1)}, u32[]{:S(2)}, u32[]{:S(2)}) %all-to-all-start.3) | async-done | bytes 204832 | tf_op jit(solution)/shard_map/all_to_all | solution.py:303
  100.9 1.2 join.1
  102.1 3.5 %all-to-all-start.4 = ((bf16[4,32,3200]{2,1,0:T(8,128)(2,1)}), bf16[4,32,3200]{2,1,0:T(8,128)(2,1)S(1)}, u32[]{:S(2)}, u32[]{:S(2)}) async-start(bf16[4,32,3200]{2,1,0:T(8,128)(2,1)} %join.1), calls=%async_computation.4 | async-start | bytes 1638400 | tf_op jit(solution)/shard_map/all_to_all | solution.py:303
  105.6 3.4 %collective-permute-start.2 = (bf16[128,512]{1,0:T(8,128)(2,1)S(1)}, bf16[128,512]{1,0:T(8,128)(2,1)S(1)}, u32[]{:S(2)}, u32[]{:S(2)}) collective-permute-start(bf16[128,512]{1,0:T(8,128)(2,1)S(1)} %get-tuple-element.37), channel_id=1, source_target_pairs={{0,8},{2,10},{4,12},{6,14},{8,0},{10,2},{12,4},{14,6},{1,9},{3,11}... | collective-permute-start | bytes 393224 | tf_op jit(solution)/shard_map/ppermute | solution.py:307
  109.0 2.8 %collective-permute-start.3 = (bf16[128,512]{1,0:T(8,128)(2,1)S(1)}, bf16[128,512]{1,0:T(8,128)(2,1)S(1)}, u32[]{:S(2)}, u32[]{:S(2)}) collective-permute-start(bf16[128,512]{1,0:T(8,128)(2,1)S(1)} %get-tuple-element.38), channel_id=1, source_target_pairs={{0,4},{2,6},{4,0},{6,2},{8,12},{10,14},{12,8},{14,10},{1,5},{3,7},... | collective-permute-start | bytes 393224 | tf_op jit(solution)/shard_map/ppermute | solution.py:307
  111.9 5.1 %collective-permute-start.4 = (bf16[128,512]{1,0:T(8,128)(2,1)S(1)}, bf16[128,512]{1,0:T(8,128)(2,1)S(1)}, u32[]{:S(2)}, u32[]{:S(2)}) collective-permute-start(bf16[128,512]{1,0:T(8,128)(2,1)S(1)} %get-tuple-element.39), channel_id=1, source_target_pairs={{0,12},{2,14},{4,8},{6,10},{8,4},{10,6},{12,0},{14,2},{1,13},{3,15... | collective-permute-start | bytes 393224 | tf_op jit(solution)/shard_map/ppermute | solution.py:307
  117.0 0.9 all-to-all-done.4
  117.9 4.4 %ortho.1 = bf16[3200,128]{1,0:T(8,128)(2,1)} custom-call(bf16[128,3200]{1,0:T(8,128)(2,1)S(1)} %bitcast.6), custom_call_target="tpu_custom_call" | custom-call | tf_op jit(solution)/shard_map/ortho/pallas_call | solution.py:287
  122.3 0.0 collective-permute-done.2.refs_1_
  122.3 0.4 collective-permute-done.3.refs_2_
  122.7 0.0 collective-permute-done.4.refs_3_
  122.7 0.7 add.21
  (3 shorter events, 0.0 us)
Async XLA Ops:
  0.6 17.4 %copy-start.4 = (s32[32]{0:T(128)S(1)}, s32[32]{0:T(128)}, u32[]{:S(2)}) copy-start(s32[32]{0:T(128)} %partner_ref.3) | copy-start | bytes 388
  0.6 40.1 %copy-start = (bf16[2048,512]{1,0:T(8,128)(2,1)S(1)}, bf16[2048,512]{1,0:T(8,128)(2,1)}, u32[]{:S(2)}) copy-start(bf16[2048,512]{1,0:T(8,128)(2,1)} %attended_ref.1) | copy-start | bytes 6291460
  0.7 40.0 %copy-start.2 = (bf16[200,384]{1,0:T(8,128)(2,1)S(1)}, bf16[200,384]{1,0:T(8,128)(2,1)}, u32[]{:S(2)}) copy-start(bf16[200,384]{1,0:T(8,128)(2,1)} %grad_ref.1) | copy-start | bytes 460804
  0.7 40.0 %copy-start.3 = (s32[32]{0:T(128)S(1)}, s32[32]{0:T(128)}, u32[]{:S(2)}) copy-start(s32[32]{0:T(128)} %frames_ref.3) | copy-start | bytes 388
  0.7 40.0 %copy-start.5 = (s32[32]{0:T(128)S(1)}, s32[32]{0:T(128)}, u32[]{:S(2)}) copy-start(s32[32]{0:T(128)} %moved_ref.3) | copy-start | bytes 388
  0.7 40.0 %copy-start.6 = (f32[200]{0:T(256)S(1)}, f32[200]{0:T(256)}, u32[]{:S(2)}) copy-start(f32[200]{0:T(256)} %param.13) | copy-start | bytes 2404
  0.7 40.0 %copy-start.7 = (s32[16]{0:T(128)S(1)}, s32[16]{0:T(128)}, u32[]{:S(2)}) copy-start(s32[16]{0:T(128)} %slot_ref.1) | copy-start | bytes 196
  4.3 23.1 %all-to-all-start = ((bf16[32,8,256]{2,1,0:T(8,128)(2,1)}), bf16[32,8,256]{2,1,0:T(8,128)(2,1)S(1)}, u32[]{:S(2)}, u32[]{:S(2)}) async-start(bf16[32,8,256]{2,1,0:T(8,128)(2,1)} %bitcast.12), calls=%async_computation | async-start | bytes 262144 | tf_op jit(solution)/shard_map/all_to_all | solution.py:303
  40.7 7.9 %copy-start.1 = (bf16[200,2048]{1,0:T(8,128)(2,1)S(1)}, bf16[200,2048]{1,0:T(8,128)(2,1)}, u32[]{:S(2)}) copy-start(bf16[200,2048]{1,0:T(8,128)(2,1)} %weight_ref.1) | copy-start | bytes 2457604
  44.7 24.2 %all-to-all-start.2 = ((bf16[32,4,3328]{2,1,0:T(4,128)(2,1)}), bf16[32,4,3328]{2,1,0:T(4,128)(2,1)S(1)}, u32[]{:S(2)}, u32[]{:S(2)}) async-start(bf16[32,4,3328]{2,1,0:T(4,128)(2,1)} %get-tuple-element.40), calls=%async_computation.2 | async-start | bytes 1703936 | tf_op jit(solution)/shard_map/all_to_all | solution.py:303
  51.9 7.5 %collective-permute-start = (bf16[1024,512]{1,0:T(8,128)(2,1)S(1)}, bf16[1024,512]{1,0:T(8,128)(2,1)S(1)}, u32[]{:S(2)}, u32[]{:S(2)}) collective-permute-start(bf16[1024,512]{1,0:T(8,128)(2,1)S(1)} %get-tuple-element.33), channel_id=1, source_target_pairs={{0,1},{1,0},{2,3},{3,2},{4,5},{5,4},{6,7},{7,6},{8,9},{9,8},{10,11... | collective-permute-start | bytes 3145736 | tf_op jit(solution)/shard_map/ppermute | solution.py:307
  59.6 26.0 %collective-permute-start.1 = (bf16[512,512]{1,0:T(8,128)(2,1)S(1)}, bf16[512,512]{1,0:T(8,128)(2,1)S(1)}, u32[]{:S(2)}, u32[]{:S(2)}) collective-permute-start(bf16[512,512]{1,0:T(8,128)(2,1)S(1)} %get-tuple-element.35), channel_id=1, source_target_pairs={{0,2},{2,0},{4,6},{6,4},{8,10},{10,8},{12,14},{14,12},{1,3},{3,1},... | collective-permute-start | bytes 1572872 | tf_op jit(solution)/shard_map/ppermute | solution.py:307
  70.5 30.4 %all-to-all-start.3 = ((bf16[128,4,200]{2,1,0:T(4,128)(2,1)}), bf16[128,4,200]{2,1,0:T(4,128)(2,1)S(1)}, u32[]{:S(2)}, u32[]{:S(2)}) async-start(bf16[128,4,200]{2,1,0:T(4,128)(2,1)} %get-tuple-element.42), calls=%async_computation.3 | async-start | bytes 524288 | tf_op jit(solution)/shard_map/all_to_all | solution.py:303
  102.1 15.9 %all-to-all-start.4 = ((bf16[4,32,3200]{2,1,0:T(8,128)(2,1)}), bf16[4,32,3200]{2,1,0:T(8,128)(2,1)S(1)}, u32[]{:S(2)}, u32[]{:S(2)}) async-start(bf16[4,32,3200]{2,1,0:T(8,128)(2,1)} %join.1), calls=%async_computation.4 | async-start | bytes 1638400 | tf_op jit(solution)/shard_map/all_to_all | solution.py:303
  105.6 16.7 %collective-permute-start.2 = (bf16[128,512]{1,0:T(8,128)(2,1)S(1)}, bf16[128,512]{1,0:T(8,128)(2,1)S(1)}, u32[]{:S(2)}, u32[]{:S(2)}) collective-permute-start(bf16[128,512]{1,0:T(8,128)(2,1)S(1)} %get-tuple-element.37), channel_id=1, source_target_pairs={{0,8},{2,10},{4,12},{6,14},{8,0},{10,2},{12,4},{14,6},{1,9},{3,11}... | collective-permute-start | bytes 393224 | tf_op jit(solution)/shard_map/ppermute | solution.py:307
  109.0 13.7 %collective-permute-start.3 = (bf16[128,512]{1,0:T(8,128)(2,1)S(1)}, bf16[128,512]{1,0:T(8,128)(2,1)S(1)}, u32[]{:S(2)}, u32[]{:S(2)}) collective-permute-start(bf16[128,512]{1,0:T(8,128)(2,1)S(1)} %get-tuple-element.38), channel_id=1, source_target_pairs={{0,4},{2,6},{4,0},{6,2},{8,12},{10,14},{12,8},{14,10},{1,5},{3,7},... | collective-permute-start | bytes 393224 | tf_op jit(solution)/shard_map/ppermute | solution.py:307
  111.9 10.8 %collective-permute-start.4 = (bf16[128,512]{1,0:T(8,128)(2,1)S(1)}, bf16[128,512]{1,0:T(8,128)(2,1)S(1)}, u32[]{:S(2)}, u32[]{:S(2)}) collective-permute-start(bf16[128,512]{1,0:T(8,128)(2,1)S(1)} %get-tuple-element.39), channel_id=1, source_target_pairs={{0,12},{2,14},{4,8},{6,10},{8,4},{10,6},{12,0},{14,2},{1,13},{3,15... | collective-permute-start | bytes 393224 | tf_op jit(solution)/shard_map/ppermute | solution.py:307

commit v6 on v5

--- a/solution.py
+++ b/solution.py
@@ -27,6 +27,8 @@
 SHARE = HD // N_DP
 WIDE = D + HD
 PAD_ROWS = 256
+EARLY = CAP_ROWS - MOVE_ROWS
+LATE = MOVE_ROWS
 CHUNK = 512
 PARTS = 5
 
@@ -94,7 +96,7 @@
         copy.wait()
 
 
-def project_kernel(
+def window_kernel(
     frames_hbm, partner_hbm, moved_hbm,
     attended_hbm, residual_hbm, grad_hbm, weight_hbm, scale_hbm,
     projected_hbm, layer_hbm, window_hbm,
@@ -103,6 +105,14 @@
     projected_ref, layer_ref, window_ref,
     small_sems, attended_sems, weight_sems, out_sems,
 ):
+    late = pl.ds(EARLY, LATE)
+    cuts = [pl.ds(first, CHUNK) for first in range(0, A, CHUNK)]
+    attended = start(
+        attended_sems, *[(attended_hbm.at[cut, late], attended_ref.at[cut, :]) for cut in cuts]
+    )
+    weight = start(
+        weight_sems, *[(weight_hbm.at[:, cut], weight_ref.at[:, cut]) for cut in cuts]
+    )
     small = start(
         small_sems,
         (frames_hbm, frames_ref),
@@ -110,14 +120,7 @@
         (moved_hbm, moved_ref),
         (scale_hbm, scale_ref),
         (grad_hbm, grad_ref),
-        (residual_hbm, residual_ref),
-    )
-    cuts = [pl.ds(first, CHUNK) for first in range(0, A, CHUNK)]
-    attended = start(
-        attended_sems, *[(attended_hbm.at[cut, :], attended_ref.at[cut, :]) for cut in cuts]
-    )
-    weight = start(
-        weight_sems, *[(weight_hbm.at[:, cut], weight_ref.at[:, cut]) for cut in cuts]
+        (residual_hbm.at[:, late], residual_ref),
     )
     wait(small[:5])
     kept, incoming, holds_two = my_counts(frames_ref, partner_ref, moved_ref)
@@ -134,8 +137,8 @@
         projected = part if projected is None else projected + part
     small[5].wait()
     layer = (residual_ref[...].astype(f32) + gains * projected).astype(bf16)
-    layer_win = layer[:, MOVE_ROWS:].astype(f32)
-    window_ref[pl.ds(0, ROWS), :] = jnp.where(holds_two == 1, layer_win, grad_win).astype(bf16)
+    window = jnp.where(holds_two == 1, layer.astype(f32), grad_win)
+    window_ref[pl.ds(0, ROWS), :] = window.astype(bf16)
     out = start(out_sems, (window_ref, window_hbm))
     projected_ref[...] = projected
     layer_ref[...] = layer
@@ -145,32 +148,61 @@
     wait(out)
 
 
+def by_slots(attended_ref, columns, scaled, slot_ref, head_of, wide):
+    for head in range(HEADS):
+        head_of[slot_ref[head]] = head
+    for slot in range(HEADS):
+        first = pl.multiple_of(head_of[slot] * HD, HD)
+        wide[:, pl.ds(slot * ROWS, ROWS)] = dot(
+            attended_ref[pl.ds(first, HD), columns], scaled, COLS_BY_COLS
+        )
+
+
+def early_kernel(
+    frames_ref, partner_ref, moved_ref, slot_ref,
+    attended_ref, residual_ref, grad_ref, weight_ref, scale_ref,
+    layer_hbm, scaled_hbm, wide_hbm, part_ref,
+    head_of, layer_ref, scaled_ref, wide_ref, sems,
+):
+    early = pl.ds(0, EARLY)
+    kept, incoming, holds_two = my_counts(frames_ref, partner_ref, moved_ref)
+    gains = to_column(scale_ref[...])
+    projected = dot(weight_ref[...], attended_ref[:, early])
+    layer_ref[...] = (residual_ref[:, early].astype(f32) + gains * projected).astype(bf16)
+    stores = start(sems, (layer_ref, layer_hbm))
+    keep = positions((ROWS, EARLY), 1) < kept
+    grad = jnp.where(keep, grad_ref[:, early].astype(f32), 0.0)
+    scaled = (grad * gains).astype(bf16)
+    scaled_ref[...] = scaled
+    stores += start(sems.at[pl.ds(1, 1)], (scaled_ref, scaled_hbm))
+    by_slots(attended_ref, early, scaled, slot_ref, head_of, wide_ref)
+    stores += start(sems.at[pl.ds(2, 1)], (wide_ref, wide_hbm))
+    part_ref[...] = to_row(jnp.sum(grad * projected, axis=1, keepdims=True))
+    wait(stores)
+
+
 def weight_grad_kernel(
     frames_ref, partner_ref, moved_ref, slot_ref,
-    attended_ref, grad_ref, scale_ref, got_ref, projected_hbm,
+    attended_ref, grad_ref, scale_ref, got_ref, part_ref, early_hbm, projected_hbm,
     scaled_hbm, pieces_hbm,
-    head_of, product, wide, projected_ref, scaled_ref, pieces_ref, sems,
+    head_of, wide, early_ref, projected_ref, scaled_ref, pieces_ref, sems,
 ):
-    (fetch,) = start(sems, (projected_hbm, projected_ref))
+    fetch = start(
+        sems.at[pl.ds(1 + NZ, 2)], (early_hbm, early_ref), (projected_hbm, projected_ref)
+    )
     kept, incoming, holds_two = my_counts(frames_ref, partner_ref, moved_ref)
-    for head in range(HEADS):
-        head_of[slot_ref[head]] = head
-    own = grad_ref[...].astype(f32)
+    own = grad_ref[:, pl.ds(EARLY, BAL_ROWS - EARLY)].astype(f32)
     own = jnp.concatenate([own, jnp.zeros((ROWS, CAP_ROWS - BAL_ROWS), f32)], axis=1)
     got = got_ref[pl.ds(0, ROWS), :].astype(f32)
     got = jnp.where(holds_two == 1, got, 0.0)
-    got = jnp.concatenate([jnp.zeros((ROWS, CAP_ROWS - MOVE_ROWS), f32), got], axis=1)
-    grad = jnp.where(positions((ROWS, CAP_ROWS), 1) < kept, own, got)
+    grad = jnp.where(positions((ROWS, LATE), 1) < kept - EARLY, own, got)
     scaled = (grad * to_column(scale_ref[...])).astype(bf16)
     scaled_ref[...] = scaled
-    (store,) = start(sems.at[pl.ds(1, 1)], (scaled_ref, scaled_hbm))
-    product[...] = dot(attended_ref[...], scaled, COLS_BY_COLS)
-    for slot in range(HEADS):
-        first = pl.multiple_of(head_of[slot] * HD, HD)
-        wide[:, pl.ds(slot * ROWS, ROWS)] = product[pl.ds(first, HD), :]
-    fetch.wait()
-    part = jnp.sum(grad * projected_ref[...], axis=1, keepdims=True) * INVERSE_ROOT
-    part = to_row(part)
+    stores = start(sems, (scaled_ref, scaled_hbm))
+    by_slots(attended_ref, pl.ds(EARLY, LATE), scaled, slot_ref, head_of, wide)
+    wait(fetch)
+    part = to_row(jnp.sum(grad * projected_ref[...], axis=1, keepdims=True))
+    part = (part + part_ref[...]) * INVERSE_ROOT
     high = part.astype(bf16).astype(f32)
     low = part - high
     zeros = jnp.zeros((1, 2 * HD - ROWS), f32)
@@ -180,33 +212,41 @@
         low[:, :HD],
         jnp.concatenate([low[:, HD:], zeros], axis=1),
     ]
-    wide[:, pl.ds(D, HD)] = jnp.concatenate(lines * N_DP, axis=0)
-    stores = [store]
+    lines = jnp.concatenate(lines, axis=0).astype(bf16)
     for z in range(NZ):
         for x in range(NX):
-            pieces_ref[z * NX + x] = wide[pl.ds((x * NZ + z) * SHARE, SHARE), :].astype(bf16)
+            cut = pl.ds((x * NZ + z) * SHARE, SHARE)
+            pieces_ref[z * NX + x, :, pl.ds(0, D)] = (wide[cut, :] + early_ref[cut, :]).astype(bf16)
+            pieces_ref[z * NX + x, :, pl.ds(D, HD)] = lines
         cut = pl.ds(z * NX, NX)
-        stores += start(sems.at[pl.ds(2 + z, 1)], (pieces_ref.at[cut], pieces_hbm.at[cut]))
+        stores += start(sems.at[pl.ds(1 + z, 1)], (pieces_ref.at[cut], pieces_hbm.at[cut]))
     wait(stores)
 
 
 def input_kernel(
     frames_ref, partner_ref, moved_ref,
-    weight_ref, got_ref, scaled_hbm, layer_hbm,
+    weight_ref, got_ref, scaled_early_hbm, scaled_late_hbm, layer_early_hbm, layer_late_hbm,
     even_ref, odd_ref, layer_out_ref,
     scaled_ref, layer_ref, sems,
 ):
-    fetch = start(sems, (scaled_hbm, scaled_ref), (layer_hbm, layer_ref))
+    early, late = pl.ds(0, EARLY), pl.ds(EARLY, LATE)
+    fetch = start(
+        sems,
+        (scaled_early_hbm, scaled_ref.at[:, early]),
+        (scaled_late_hbm, scaled_ref.at[:, late]),
+        (layer_early_hbm, layer_ref.at[:, early]),
+        (layer_late_hbm, layer_ref.at[:, late]),
+    )
     kept, incoming, holds_two = my_counts(frames_ref, partner_ref, moved_ref)
     block = lax.axis_index("y") * NC + lax.axis_index("c")
-    fetch[0].wait()
+    wait(fetch[:2])
     scaled = scaled_ref[...]
     for index, other in enumerate(EVEN):
         for ref, partner in ((even_ref, other), (odd_ref, other + 1)):
             first = pl.multiple_of((block ^ partner) * HD, HD)
             part = dot(weight_ref[:, pl.ds(first, HD)], scaled, ROWS_BY_COLS)
             ref[pl.ds(index * HD, HD), :] = part.astype(bf16)
-    fetch[1].wait()
+    wait(fetch[2:])
     received = dot(got_ref[pl.ds(0, ROWS), :], light_places(kept, incoming), COLS_BY_COLS)
     own = layer_ref[:, pl.ds(0, BAL_ROWS)].astype(f32)
     keep = positions((ROWS, BAL_ROWS), 1) < kept
@@ -336,15 +376,16 @@
     ints = pltpu.SMEM((N_DP,), jnp.int32)
     dma = pltpu.SemaphoreType.DMA
 
-    projected, layer_own, window = call(
-        project_kernel, "project", [H] * 8,
+    late = (ROWS, LATE)
+    projected, layer_late, window = call(
+        window_kernel, "window", [H] * 8,
         (frames, partner, moved_tiles, attended, residual, grad_out, out_weight, scale_row),
-        [((ROWS, CAP_ROWS), f32, H), ((ROWS, CAP_ROWS), bf16, H), ((PAD_ROWS, MOVE_ROWS), bf16, H)],
+        [(late, f32, H), (late, bf16, H), ((PAD_ROWS, MOVE_ROWS), bf16, H)],
         [
             ints, ints, ints,
-            V((A, CAP_ROWS), bf16), V((ROWS, CAP_ROWS), bf16), V((ROWS, BAL_ROWS), bf16),
+            V((A, LATE), bf16), V(late, bf16), V((ROWS, BAL_ROWS), bf16),
             V((ROWS, A), bf16), V((1, ROWS), f32),
-            V((ROWS, CAP_ROWS), f32), V((ROWS, CAP_ROWS), bf16), V((PAD_ROWS, MOVE_ROWS), bf16),
+            V(late, f32), V(late, bf16), V((PAD_ROWS, MOVE_ROWS), bf16),
             dma((6,)), dma((A // CHUNK,)), dma((A // CHUNK,)), dma((3,)),
         ],
     )
@@ -352,24 +393,38 @@
     pieces = exchange(jnp.take(pieces, partner, axis=0), ("z", "x"))
     got = pieces.reshape(PAD_ROWS, MOVE_ROWS)
 
-    scaled, pieces = call(
-        weight_grad_kernel, "weight_grad", [S] * 4 + [V] * 4 + [H],
-        (frames, partner, moved_tiles, owner_slot, attended, grad_out, scale_row, got, projected),
-        [((ROWS, CAP_ROWS), bf16, H), ((N_DP, SHARE, WIDE), bf16, H)],
+    early = (ROWS, EARLY)
+    heads = pltpu.SMEM((HEADS,), jnp.int32)
+    layer_early, scaled_early, wide, part = call(
+        early_kernel, "early", [S] * 4 + [V] * 5,
+        (frames, partner, moved_tiles, owner_slot, attended, residual, grad_out, out_weight, scale_row),
+        [(early, bf16, H), (early, bf16, H), ((HD, D), f32, H), ((1, ROWS), f32, V)],
+        [heads, V(early, bf16), V(early, bf16), V((HD, D), f32), dma((3,))],
+        FREE,
+    )
+    scaled_late, pieces = call(
+        weight_grad_kernel, "weight_grad", [S] * 4 + [V] * 5 + [H] * 2,
+        (
+            frames, partner, moved_tiles, owner_slot,
+            attended, grad_out, scale_row, got, part, wide, projected,
+        ),
+        [(late, bf16, H), ((N_DP, SHARE, WIDE), bf16, H)],
         [
-            pltpu.SMEM((HEADS,), jnp.int32), V((A, ROWS), f32), V((HD, WIDE), f32),
-            V((ROWS, CAP_ROWS), f32), V((ROWS, CAP_ROWS), bf16),
-            V((N_DP, SHARE, WIDE), bf16), dma((2 + NZ,)),
+            heads, V((HD, D), f32), V((HD, D), f32), V(late, f32), V(late, bf16),
+            V((N_DP, SHARE, WIDE), bf16), dma((3 + NZ,)),
         ],
     )
     summed = exchange(pieces, ("z", "x"))
 
     half = ((A // 2, CAP_ROWS), bf16, V)
     even, odd, layer_out = call(
-        input_kernel, "input_grad", [S] * 3 + [V] * 2 + [H] * 2,
-        (frames, partner, moved_tiles, out_weight, got, scaled, layer_own),
+        input_kernel, "input_grad", [S] * 3 + [V] * 2 + [H] * 4,
+        (
+            frames, partner, moved_tiles, out_weight, got,
+            scaled_early, scaled_late, layer_early, layer_late,
+        ),
         [half, half, ((ROWS, BAL_ROWS), bf16, V)],
-        [V((ROWS, CAP_ROWS), bf16), V((ROWS, CAP_ROWS), bf16), dma((2,))],
+        [V((ROWS, CAP_ROWS), bf16), V((ROWS, CAP_ROWS), bf16), dma((4,))],
         FREE,
     )
     left, other = add((even, crossed(odd, "c", NC, 1)), 2)
@@ -381,20 +436,20 @@
     )
     owned = exchange(copies, ("z", "y", "c"))
     left, *others = add((left, crossed(other, "y", NY, 1)), 4)
-    owned, _ = lax.optimization_barrier((owned, left))
     others = [crossed(other, "y", NY, step) for other, step in zip(others, (4, 2, 6))]
+    owned, _ = lax.optimization_barrier((owned, others[:2]))
     (copies,) = call(
         join_kernel, "join", [V], (owned,),
         [((NX, BY_X, D), bf16, H)],
         [V((BY_X, D), f32), V((BY_X, D), bf16), dma((NX,))],
     )
     whole = exchange(copies, "x").reshape(HD, D)
+    (input_grad,) = add((left, *others), 1)
+    whole, _ = lax.optimization_barrier((whole, input_grad))
     (ortho_update,) = call(
         ortho_kernel, "ortho", [V], (whole,), [((D, HD), bf16, H)],
         [V((D, HD), bf16), dma((PARTS,))],
     )
-    left, others, ortho_update = lax.optimization_barrier((left, others, ortho_update))
-    (input_grad,) = add((left, *others), 1)
     return (layer_out, input_grad, scale_grad.reshape(ROWS), ortho_update[:, None, :])
 
 

time: 125 us -> 131 us (1.048); the launches traced: 123 us -> 131 us
  blocking collectives: 12.6 us -> 0 us
  waiting for transfers between devices: 34.1 us -> 45.6 us
  starting transfers between devices: 56.1 us -> 59.8 us
  Pallas kernels: 18.8 us -> 21.5 us
  other arithmetic: 0.12 us -> 1.68 us
    ppermute x5, waiting for transfers between devices: 2.67 us -> 20.9 us  [crossed(): return lax.ppermute(array, axis, [(i, i ^ bit) for i in range(size)])]
    all_to_all x1 -> x0, blocking collectives: 12.6 us -> none  [exchange(): return lax.all_to_all(pieces, axes, split_axis=0, concat_axis=0, tiled=True)]
    all_to_all x4 -> x5, waiting for transfers between devices: 31.5 us -> 24.7 us  [exchange(): return lax.all_to_all(pieces, axes, split_axis=0, concat_axis=0, tiled=True)]
    all_to_all x4 -> x5, starting transfers between devices: 36.3 us -> 40.1 us  [exchange(): return lax.all_to_all(pieces, axes, split_axis=0, concat_axis=0, tiled=True)]
    pallas_call x9 -> x10, Pallas kernels: 18.8 us -> 21.5 us  [call(): pl.pallas_call(kernel, out_shape=[H(shape, dtype) if place is H else jax....]
    select_n x2, other arithmetic: 0.11 us -> 1.67 us  [body(): pieces = exchange(jnp.take(pieces, partner, axis=0), ('z', 'x'))]
  transfers between devices with their start and end apart: 9 -> 10, of which waited for: 6 -> 8; matrix products, arithmetic and copies ran while one was open for 0% -> 0% of each run, Pallas kernels for 8% -> 7%
where the time goes in v6:
time: 131 us
  starting transfers between devices  59.8 us (46%)
  waiting for transfers between devices  45.6 us (35%)
  Pallas kernels  21.5 us (16%)
  other arithmetic  1.68 us (1%)
    all_to_all x5, starting transfers between devices, exchange(): return lax.all_to_all(pieces, axes, split_axis=0, concat_axis=0, tiled=True)  40.1 us
    all_to_all x5, waiting for transfers between devices, exchange(): return lax.all_to_all(pieces, axes, split_axis=0, concat_axis=0, tiled=True)  24.7 us
    pallas_call x10, Pallas kernels, call(): pl.pallas_call(kernel, out_shape=[H(shape, dtype) if place is H else jax....  21.5 us
    ppermute x5, waiting for transfers between devices, crossed(): return lax.ppermute(array, axis, [(i, i ^ bit) for i in range(size)])  20.9 us
    ppermute x5, starting transfers between devices, crossed(): return lax.ppermute(array, axis, [(i, i ^ bit) for i in range(size)])  19.7 us
  transfers between devices with their start and end apart: 10, of which 8 were waited for; matrix products, arithmetic and copies ran while one was open for 0% of the time, Pallas kernels for 7%

profile of v6, /device:TPU:1, one launch (start us, length us, event | category | flops | bytes accessed | tf_op | source)
XLA Modules:
  0.0 130.8 jit_solution(12077466095910938037)
XLA Ops:
  0.6 0.0 copy-start.6
  0.6 0.0 copy-start
  0.7 0.0 copy-start.1
  0.7 0.0 copy-start.2
  0.7 0.0 copy-start.3
  0.7 0.0 copy-start.4
  0.7 0.0 copy-start.5
  0.7 0.0 copy-start.7
  0.7 0.0 copy-start.8
  0.7 3.5 %window.1 = (f32[200,256]{1,0:T(8,128)}, bf16[200,256]{1,0:T(8,128)(2,1)}, bf16[256,256]{1,0:T(8,128)(2,1)}) custom-call(s32[32]{0:T(128)} %frames_ref.5, s32[32]{0:T(128)} %partner_ref.5, s32[32]{0:T(128)} %moved_ref.5, bf16[2048,512]{1,0:T(8,128)(2,1)} %attended_ref.3, bf16[200,512]{1,0:T(8,128)(2,1)} %residual_ref.1, bf16[200,384]{1,0:T(8,128)(2,1)} %grad_ref.3, ...), custom_call_target="tpu_custom_call" | custom-call | tf_op jit(solution)/shard_map/window/pallas_call | solution.py:327
  4.2 13.7 %all-to-all-start = ((bf16[32,8,256]{2,1,0:T(8,128)(2,1)}), bf16[32,8,256]{2,1,0:T(8,128)(2,1)S(1)}, u32[]{:S(2)}, u32[]{:S(2)}) async-start(bf16[32,8,256]{2,1,0:T(8,128)(2,1)} %bitcast.13), calls=%async_computation | async-start | bytes 262144 | tf_op jit(solution)/shard_map/all_to_all | solution.py:343
  18.0 9.3 %all-to-all-done = bf16[32,8,256]{2,1,0:T(8,128)(2,1)S(1)} async-done(((bf16[32,8,256]{2,1,0:T(8,128)(2,1)}), bf16[32,8,256]{2,1,0:T(8,128)(2,1)S(1)}, u32[]{:S(2)}, u32[]{:S(2)}) %all-to-all-start) | async-done | bytes 131104 | tf_op jit(solution)/shard_map/all_to_all | solution.py:343
  27.3 1.2 gather_fusion
  28.5 1.7 %broadcast_select_fusion = bf16[32,8,256]{2,1,0:T(8,128)(2,1)} fusion(bf16[32,8,256]{2,1,0:T(8,128)(2,1)} %gather_fusion, pred[32]{0:T(512)(128)(4,1)S(1)} %compare_and_fusion), kind=kLoop, calls=%fused_computation.1 | loop fusion | flops 65536 | bytes 262176 | tf_op jit(solution)/shard_map/jit(_take)/select_n | solution.py:393
  30.2 3.9 %all-to-all-start.1 = ((bf16[32,8,256]{2,1,0:T(8,128)(2,1)}), bf16[32,8,256]{2,1,0:T(8,128)(2,1)S(1)}, u32[]{:S(2)}, u32[]{:S(2)}) async-start(bf16[32,8,256]{2,1,0:T(8,128)(2,1)} %broadcast_select_fusion), calls=%async_computation.1 | async-start | bytes 262144 | tf_op jit(solution)/shard_map/all_to_all | solution.py:343
  34.1 0.0 copy-done
  34.1 0.0 copy-done.1
  34.1 0.0 copy-done.2
  34.1 0.0 copy-done.3
  34.1 0.0 copy-done.4
  34.1 0.0 copy-done.5
  34.1 0.0 copy-done.7
  34.1 3.0 %early.1 = (bf16[200,256]{1,0:T(8,128)(2,1)}, bf16[200,256]{1,0:T(8,128)(2,1)}, f32[128,3200]{1,0:T(8,128)}, f32[1,200]{1,0:T(1,128)S(1)}) custom-call(s32[32]{0:T(128)S(1)} %copy-done.5, s32[32]{0:T(128)S(1)} %copy-done.6, s32[32]{0:T(128)S(1)} %copy-done.7, s32[16]{0:T(128)S(1)} %copy-done.8, bf16[2048,512]{1,0:T(8,128)(2,1)S(1)} %copy-done, ...), custom_call_target="tpu_custom_call" | custom-call | tf_op jit(solution)/shard_map/early/pallas_call | solution.py:327
  37.2 6.3 %all-to-all-done.1 = bf16[32,8,256]{2,1,0:T(8,128)(2,1)S(1)} async-done(((bf16[32,8,256]{2,1,0:T(8,128)(2,1)}), bf16[32,8,256]{2,1,0:T(8,128)(2,1)S(1)}, u32[]{:S(2)}, u32[]{:S(2)}) %all-to-all-start.1) | async-done | bytes 131104 | tf_op jit(solution)/shard_map/all_to_all | solution.py:343
  43.5 3.6 %weight_grad.1 = (bf16[200,256]{1,0:T(8,128)(2,1)}, bf16[32,4,3328]{2,1,0:T(4,128)(2,1)}) custom-call(s32[32]{0:T(128)S(1)} %copy-done.5, s32[32]{0:T(128)S(1)} %copy-done.6, s32[32]{0:T(128)S(1)} %copy-done.7, s32[16]{0:T(128)S(1)} %copy-done.8, bf16[2048,512]{1,0:T(8,128)(2,1)S(1)} %copy-done, bf16[200,384]{1,0:T(8,128)(2,1)S(1)} %copy-done.2, ...), custom_call_target="tpu_custom_call" | custom-call | tf_op jit(solution)/shard_map/weight_grad/pallas_call | solution.py:327
  47.0 3.9 %all-to-all-start.2 = ((bf16[32,4,3328]{2,1,0:T(4,128)(2,1)}), bf16[32,4,3328]{2,1,0:T(4,128)(2,1)S(1)}, u32[]{:S(2)}, u32[]{:S(2)}) async-start(bf16[32,4,3328]{2,1,0:T(4,128)(2,1)} %get-tuple-element.44), calls=%async_computation.2 | async-start | bytes 1703936 | tf_op jit(solution)/shard_map/all_to_all | solution.py:343
  51.0 3.2 %input_grad.1 = (bf16[1024,512]{1,0:T(8,128)(2,1)S(1)}, bf16[1024,512]{1,0:T(8,128)(2,1)S(1)}, bf16[200,384]{1,0:T(8,128)(2,1)}) custom-call(s32[32]{0:T(128)S(1)} %copy-done.5, s32[32]{0:T(128)S(1)} %copy-done.6, s32[32]{0:T(128)S(1)} %copy-done.7, bf16[200,2048]{1,0:T(8,128)(2,1)S(1)} %copy-done.1, bf16[256,256]{1,0:T(8,128)(2,1)S(1)} %bitcast.8, ...), custom_call_target="tpu_custom_call" | custom-call | tf_op jit(solution)/shard_map/input_grad/pallas_call | solution.py:327
  54.2 5.2 %collective-permute-start = (bf16[1024,512]{1,0:T(8,128)(2,1)S(1)}, bf16[1024,512]{1,0:T(8,128)(2,1)S(1)}, u32[]{:S(2)}, u32[]{:S(2)}) collective-permute-start(bf16[1024,512]{1,0:T(8,128)(2,1)S(1)} %get-tuple-element.37), channel_id=1, source_target_pairs={{0,1},{1,0},{2,3},{3,2},{4,5},{5,4},{6,7},{7,6},{8,9},{9,8},{10,11... | collective-permute-start | bytes 3145736 | tf_op jit(solution)/shard_map/ppermute | solution.py:347
  59.4 2.3 %collective-permute-done.refs_1_ = bf16[1024,512]{1,0:T(8,128)(2,1)S(1)} collective-permute-done((bf16[1024,512]{1,0:T(8,128)(2,1)S(1)}, bf16[1024,512]{1,0:T(8,128)(2,1)S(1)}, u32[]{:S(2)}, u32[]{:S(2)}) %collective-permute-start) | collective-permute-done | bytes 1048608 | tf_op jit(solution)/shard_map/ppermute | solution.py:347
  61.7 0.2 add.19
  61.9 3.2 %collective-permute-start.1 = (bf16[512,512]{1,0:T(8,128)(2,1)S(1)}, bf16[512,512]{1,0:T(8,128)(2,1)S(1)}, u32[]{:S(2)}, u32[]{:S(2)}) collective-permute-start(bf16[512,512]{1,0:T(8,128)(2,1)S(1)} %get-tuple-element.39), channel_id=1, source_target_pairs={{0,2},{2,0},{4,6},{6,4},{8,10},{10,8},{12,14},{14,12},{1,3},{3,1},... | collective-permute-start | bytes 1572872 | tf_op jit(solution)/shard_map/ppermute | solution.py:347
  65.1 6.2 %all-to-all-done.2.pieces_ref = bf16[32,4,3328]{2,1,0:T(4,128)(2,1)S(1)} async-done(((bf16[32,4,3328]{2,1,0:T(4,128)(2,1)}), bf16[32,4,3328]{2,1,0:T(4,128)(2,1)S(1)}, u32[]{:S(2)}, u32[]{:S(2)}) %all-to-all-start.2) | async-done | bytes 852000 | tf_op jit(solution)/shard_map/all_to_all | solution.py:343
  71.4 1.5 %slots.1 = (bf16[128,4,200]{2,1,0:T(4,128)(2,1)}, f32[1,200]{1,0:T(1,128)}) custom-call(bf16[32,4,3328]{2,1,0:T(4,128)(2,1)S(1)} %all-to-all-done.2.pieces_ref), custom_call_target="tpu_custom_call" | custom-call | tf_op jit(solution)/shard_map/slots/pallas_call | solution.py:327
  72.9 15.1 %all-to-all-start.3 = ((bf16[128,4,200]{2,1,0:T(4,128)(2,1)}), bf16[128,4,200]{2,1,0:T(4,128)(2,1)S(1)}, u32[]{:S(2)}, u32[]{:S(2)}) async-start(bf16[128,4,200]{2,1,0:T(4,128)(2,1)} %get-tuple-element.47), calls=%async_computation.3 | async-start | bytes 524288 | tf_op jit(solution)/shard_map/all_to_all | solution.py:343
  88.0 0.0 collective-permute-done.1.refs_1_
  88.0 0.1 add.20
  88.2 7.2 %collective-permute-start.2 = (bf16[128,512]{1,0:T(8,128)(2,1)S(1)}, bf16[128,512]{1,0:T(8,128)(2,1)S(1)}, u32[]{:S(2)}, u32[]{:S(2)}) collective-permute-start(bf16[128,512]{1,0:T(8,128)(2,1)S(1)} %get-tuple-element.41), channel_id=1, source_target_pairs={{0,8},{2,10},{4,12},{6,14},{8,0},{10,2},{12,4},{14,6},{1,9},{3,11}... | collective-permute-start | bytes 393224 | tf_op jit(solution)/shard_map/ppermute | solution.py:347
  95.4 2.2 %collective-permute-start.3 = (bf16[128,512]{1,0:T(8,128)(2,1)S(1)}, bf16[128,512]{1,0:T(8,128)(2,1)S(1)}, u32[]{:S(2)}, u32[]{:S(2)}) collective-permute-start(bf16[128,512]{1,0:T(8,128)(2,1)S(1)} %get-tuple-element.42), channel_id=1, source_target_pairs={{0,4},{2,6},{4,0},{6,2},{8,12},{10,14},{12,8},{14,10},{1,5},{3,7},... | collective-permute-start | bytes 393224 | tf_op jit(solution)/shard_map/ppermute | solution.py:347
  97.6 7.3 %collective-permute-done.2.refs_1_ = bf16[128,512]{1,0:T(8,128)(2,1)S(1)} collective-permute-done((bf16[128,512]{1,0:T(8,128)(2,1)S(1)}, bf16[128,512]{1,0:T(8,128)(2,1)S(1)}, u32[]{:S(2)}, u32[]{:S(2)}) %collective-permute-start.2) | collective-permute-done | bytes 131104 | tf_op jit(solution)/shard_map/ppermute | solution.py:347
  104.8 4.6 %collective-permute-done.3.refs_2_ = bf16[128,512]{1,0:T(8,128)(2,1)S(1)} collective-permute-done((bf16[128,512]{1,0:T(8,128)(2,1)S(1)}, bf16[128,512]{1,0:T(8,128)(2,1)S(1)}, u32[]{:S(2)}, u32[]{:S(2)}) %collective-permute-start.3) | collective-permute-done | bytes 131104 | tf_op jit(solution)/shard_map/ppermute | solution.py:347
  109.4 0.0 all-to-all-done.3.owned_ref
  109.4 1.2 join.1
  110.6 3.5 %all-to-all-start.4 = ((bf16[4,32,3200]{2,1,0:T(8,128)(2,1)}), bf16[4,32,3200]{2,1,0:T(8,128)(2,1)S(1)}, u32[]{:S(2)}, u32[]{:S(2)}) async-start(bf16[4,32,3200]{2,1,0:T(8,128)(2,1)} %join.1), calls=%async_computation.4 | async-start | bytes 1638400 | tf_op jit(solution)/shard_map/all_to_all | solution.py:343
  114.1 1.9 %collective-permute-start.4 = (bf16[128,512]{1,0:T(8,128)(2,1)S(1)}, bf16[128,512]{1,0:T(8,128)(2,1)S(1)}, u32[]{:S(2)}, u32[]{:S(2)}) collective-permute-start(bf16[128,512]{1,0:T(8,128)(2,1)S(1)} %get-tuple-element.43), channel_id=1, source_target_pairs={{0,12},{2,14},{4,8},{6,10},{8,4},{10,6},{12,0},{14,2},{1,13},{3,15... | collective-permute-start | bytes 393224 | tf_op jit(solution)/shard_map/ppermute | solution.py:347
  116.0 6.8 %collective-permute-done.4.refs_3_ = bf16[128,512]{1,0:T(8,128)(2,1)S(1)} collective-permute-done((bf16[128,512]{1,0:T(8,128)(2,1)S(1)}, bf16[128,512]{1,0:T(8,128)(2,1)S(1)}, u32[]{:S(2)}, u32[]{:S(2)}) %collective-permute-start.4) | collective-permute-done | bytes 131104 | tf_op jit(solution)/shard_map/ppermute | solution.py:347
  122.8 0.7 add.21
  123.5 2.9 %all-to-all-done.4 = bf16[4,32,3200]{2,1,0:T(8,128)(2,1)S(1)} async-done(((bf16[4,32,3200]{2,1,0:T(8,128)(2,1)}), bf16[4,32,3200]{2,1,0:T(8,128)(2,1)S(1)}, u32[]{:S(2)}, u32[]{:S(2)}) %all-to-all-start.4) | async-done | bytes 819232 | tf_op jit(solution)/shard_map/all_to_all | solution.py:343
  126.4 4.4 %ortho.1 = bf16[3200,128]{1,0:T(8,128)(2,1)} custom-call(bf16[128,3200]{1,0:T(8,128)(2,1)S(1)} %bitcast.6), custom_call_target="tpu_custom_call" | custom-call | tf_op jit(solution)/shard_map/ortho/pallas_call | solution.py:327
  (5 shorter events, 0.0 us)
Async XLA Ops:
  0.6 17.3 %copy-start.6 = (s32[32]{0:T(128)S(1)}, s32[32]{0:T(128)}, u32[]{:S(2)}) copy-start(s32[32]{0:T(128)} %partner_ref.5) | copy-start | bytes 388
  0.6 33.4 %copy-start = (bf16[2048,512]{1,0:T(8,128)(2,1)S(1)}, bf16[2048,512]{1,0:T(8,128)(2,1)}, u32[]{:S(2)}) copy-start(bf16[2048,512]{1,0:T(8,128)(2,1)} %attended_ref.3) | copy-start | bytes 6291460
  0.7 33.4 %copy-start.1 = (bf16[200,2048]{1,0:T(8,128)(2,1)S(1)}, bf16[200,2048]{1,0:T(8,128)(2,1)}, u32[]{:S(2)}) copy-start(bf16[200,2048]{1,0:T(8,128)(2,1)} %weight_ref.3) | copy-start | bytes 2457604
  0.7 33.4 %copy-start.2 = (bf16[200,384]{1,0:T(8,128)(2,1)S(1)}, bf16[200,384]{1,0:T(8,128)(2,1)}, u32[]{:S(2)}) copy-start(bf16[200,384]{1,0:T(8,128)(2,1)} %grad_ref.3) | copy-start | bytes 460804
  0.7 33.4 %copy-start.3 = (bf16[200,512]{1,0:T(8,128)(2,1)S(1)}, bf16[200,512]{1,0:T(8,128)(2,1)}, u32[]{:S(2)}) copy-start(bf16[200,512]{1,0:T(8,128)(2,1)} %residual_ref.1) | copy-start | bytes 614404
  0.7 33.4 %copy-start.4 = (f32[200]{0:T(256)S(1)}, f32[200]{0:T(256)}, u32[]{:S(2)}) copy-start(f32[200]{0:T(256)} %param.13) | copy-start | bytes 2404
  0.7 33.4 %copy-start.5 = (s32[32]{0:T(128)S(1)}, s32[32]{0:T(128)}, u32[]{:S(2)}) copy-start(s32[32]{0:T(128)} %frames_ref.5) | copy-start | bytes 388
  0.7 33.4 %copy-start.7 = (s32[32]{0:T(128)S(1)}, s32[32]{0:T(128)}, u32[]{:S(2)}) copy-start(s32[32]{0:T(128)} %moved_ref.5) | copy-start | bytes 388
  0.7 33.4 %copy-start.8 = (s32[16]{0:T(128)S(1)}, s32[16]{0:T(128)}, u32[]{:S(2)}) copy-start(s32[16]{0:T(128)} %slot_ref.3) | copy-start | bytes 196
  4.2 23.1 %all-to-all-start = ((bf16[32,8,256]{2,1,0:T(8,128)(2,1)}), bf16[32,8,256]{2,1,0:T(8,128)(2,1)S(1)}, u32[]{:S(2)}, u32[]{:S(2)}) async-start(bf16[32,8,256]{2,1,0:T(8,128)(2,1)} %bitcast.13), calls=%async_computation | async-start | bytes 262144 | tf_op jit(solution)/shard_map/all_to_all | solution.py:343
  30.2 13.3 %all-to-all-start.1 = ((bf16[32,8,256]{2,1,0:T(8,128)(2,1)}), bf16[32,8,256]{2,1,0:T(8,128)(2,1)S(1)}, u32[]{:S(2)}, u32[]{:S(2)}) async-start(bf16[32,8,256]{2,1,0:T(8,128)(2,1)} %broadcast_select_fusion), calls=%async_computation.1 | async-start | bytes 262144 | tf_op jit(solution)/shard_map/all_to_all | solution.py:343
  47.0 24.3 %all-to-all-start.2 = ((bf16[32,4,3328]{2,1,0:T(4,128)(2,1)}), bf16[32,4,3328]{2,1,0:T(4,128)(2,1)S(1)}, u32[]{:S(2)}, u32[]{:S(2)}) async-start(bf16[32,4,3328]{2,1,0:T(4,128)(2,1)} %get-tuple-element.44), calls=%async_computation.2 | async-start | bytes 1703936 | tf_op jit(solution)/shard_map/all_to_all | solution.py:343
  54.2 7.4 %collective-permute-start = (bf16[1024,512]{1,0:T(8,128)(2,1)S(1)}, bf16[1024,512]{1,0:T(8,128)(2,1)S(1)}, u32[]{:S(2)}, u32[]{:S(2)}) collective-permute-start(bf16[1024,512]{1,0:T(8,128)(2,1)S(1)} %get-tuple-element.37), channel_id=1, source_target_pairs={{0,1},{1,0},{2,3},{3,2},{4,5},{5,4},{6,7},{7,6},{8,9},{9,8},{10,11... | collective-permute-start | bytes 3145736 | tf_op jit(solution)/shard_map/ppermute | solution.py:347
  61.9 26.1 %collective-permute-start.1 = (bf16[512,512]{1,0:T(8,128)(2,1)S(1)}, bf16[512,512]{1,0:T(8,128)(2,1)S(1)}, u32[]{:S(2)}, u32[]{:S(2)}) collective-permute-start(bf16[512,512]{1,0:T(8,128)(2,1)S(1)} %get-tuple-element.39), channel_id=1, source_target_pairs={{0,2},{2,0},{4,6},{6,4},{8,10},{10,8},{12,14},{14,12},{1,3},{3,1},... | collective-permute-start | bytes 1572872 | tf_op jit(solution)/shard_map/ppermute | solution.py:347
  72.9 36.5 %all-to-all-start.3 = ((bf16[128,4,200]{2,1,0:T(4,128)(2,1)}), bf16[128,4,200]{2,1,0:T(4,128)(2,1)S(1)}, u32[]{:S(2)}, u32[]{:S(2)}) async-start(bf16[128,4,200]{2,1,0:T(4,128)(2,1)} %get-tuple-element.47), calls=%async_computation.3 | async-start | bytes 524288 | tf_op jit(solution)/shard_map/all_to_all | solution.py:343
  88.2 16.7 %collective-permute-start.2 = (bf16[128,512]{1,0:T(8,128)(2,1)S(1)}, bf16[128,512]{1,0:T(8,128)(2,1)S(1)}, u32[]{:S(2)}, u32[]{:S(2)}) collective-permute-start(bf16[128,512]{1,0:T(8,128)(2,1)S(1)} %get-tuple-element.41), channel_id=1, source_target_pairs={{0,8},{2,10},{4,12},{6,14},{8,0},{10,2},{12,4},{14,6},{1,9},{3,11}... | collective-permute-start | bytes 393224 | tf_op jit(solution)/shard_map/ppermute | solution.py:347
  95.4 14.0 %collective-permute-start.3 = (bf16[128,512]{1,0:T(8,128)(2,1)S(1)}, bf16[128,512]{1,0:T(8,128)(2,1)S(1)}, u32[]{:S(2)}, u32[]{:S(2)}) collective-permute-start(bf16[128,512]{1,0:T(8,128)(2,1)S(1)} %get-tuple-element.42), channel_id=1, source_target_pairs={{0,4},{2,6},{4,0},{6,2},{8,12},{10,14},{12,8},{14,10},{1,5},{3,7},... | collective-permute-start | bytes 393224 | tf_op jit(solution)/shard_map/ppermute | solution.py:347
  110.6 15.8 %all-to-all-start.4 = ((bf16[4,32,3200]{2,1,0:T(8,128)(2,1)}), bf16[4,32,3200]{2,1,0:T(8,128)(2,1)S(1)}, u32[]{:S(2)}, u32[]{:S(2)}) async-start(bf16[4,32,3200]{2,1,0:T(8,128)(2,1)} %join.1), calls=%async_computation.4 | async-start | bytes 1638400 | tf_op jit(solution)/shard_map/all_to_all | solution.py:343
  114.1 8.7 %collective-permute-start.4 = (bf16[128,512]{1,0:T(8,128)(2,1)S(1)}, bf16[128,512]{1,0:T(8,128)(2,1)S(1)}, u32[]{:S(2)}, u32[]{:S(2)}) collective-permute-start(bf16[128,512]{1,0:T(8,128)(2,1)S(1)} %get-tuple-element.43), channel_id=1, source_target_pairs={{0,12},{2,14},{4,8},{6,10},{8,4},{10,6},{12,0},{14,2},{1,13},{3,15... | collective-permute-start | bytes 393224 | tf_op jit(solution)/shard_map/ppermute | solution.py:347

commit v7 on v5

--- a/solution.py
+++ b/solution.py
@@ -97,10 +97,10 @@
 def project_kernel(
     frames_hbm, partner_hbm, moved_hbm,
     attended_hbm, residual_hbm, grad_hbm, weight_hbm, scale_hbm,
-    projected_hbm, layer_hbm, window_hbm,
+    projected_hbm, layer_hbm, window_ref,
     frames_ref, partner_ref, moved_ref,
     attended_ref, residual_ref, grad_ref, weight_ref, scale_ref,
-    projected_ref, layer_ref, window_ref,
+    projected_ref, layer_ref,
     small_sems, attended_sems, weight_sems, out_sems,
 ):
     small = start(
@@ -132,24 +132,34 @@
         weight[index].wait()
         part = dot(weight_ref[:, cut], attended_ref[cut, :])
         projected = part if projected is None else projected + part
+    projected_ref[...] = projected
+    out = start(out_sems, (projected_ref, projected_hbm))
     small[5].wait()
     layer = (residual_ref[...].astype(f32) + gains * projected).astype(bf16)
+    layer_ref[...] = layer
+    out += start(out_sems.at[pl.ds(1, 1)], (layer_ref, layer_hbm))
     layer_win = layer[:, MOVE_ROWS:].astype(f32)
     window_ref[pl.ds(0, ROWS), :] = jnp.where(holds_two == 1, layer_win, grad_win).astype(bf16)
-    out = start(out_sems, (window_ref, window_hbm))
-    projected_ref[...] = projected
-    layer_ref[...] = layer
-    out += start(
-        out_sems.at[pl.ds(1, 2)], (projected_ref, projected_hbm), (layer_ref, layer_hbm)
-    )
     wait(out)
+
+
+def forward_kernel(partner_ref, pieces_ref, out_ref):
+    for replica in range(N_DP):
+        out_ref[replica] = pieces_ref[partner_ref[replica]]
+
+
+def send_lanes(first, last, value, pieces_ref, pieces_hbm, sems):
+    lanes = pl.ds(first, last - first)
+    for piece in range(N_DP):
+        pieces_ref[piece, :, lanes] = value(piece, lanes)
+    return start(sems, (pieces_ref.at[:, :, lanes], pieces_hbm.at[:, :, lanes]))
 
 
 def weight_grad_kernel(
     frames_ref, partner_ref, moved_ref, slot_ref,
     attended_ref, grad_ref, scale_ref, got_ref, projected_hbm,
     scaled_hbm, pieces_hbm,
-    head_of, product, wide, projected_ref, scaled_ref, pieces_ref, sems,
+    head_of, wide, projected_ref, scaled_ref, pieces_ref, sems,
 ):
     (fetch,) = start(sems, (projected_hbm, projected_ref))
     kept, incoming, holds_two = my_counts(frames_ref, partner_ref, moved_ref)
@@ -164,10 +174,18 @@
     scaled = (grad * to_column(scale_ref[...])).astype(bf16)
     scaled_ref[...] = scaled
     (store,) = start(sems.at[pl.ds(1, 1)], (scaled_ref, scaled_hbm))
-    product[...] = dot(attended_ref[...], scaled, COLS_BY_COLS)
+    stores, done = [store], 0
     for slot in range(HEADS):
         first = pl.multiple_of(head_of[slot] * HD, HD)
-        wide[:, pl.ds(slot * ROWS, ROWS)] = product[pl.ds(first, HD), :]
+        wide[:, pl.ds(slot * ROWS, ROWS)] = dot(
+            attended_ref[pl.ds(first, HD), :], scaled, COLS_BY_COLS
+        )
+        if (slot + 1) % 4 == 0:
+            full = (slot + 1) * ROWS // HD * HD
+            stores += send_lanes(done, full, lambda piece, lanes: wide[
+                pl.ds((piece % NX * NZ + piece // NX) * SHARE, SHARE), lanes
+            ].astype(bf16), pieces_ref, pieces_hbm, sems.at[pl.ds(2 + slot // 4, 1)])
+            done = full
     fetch.wait()
     part = jnp.sum(grad * projected_ref[...], axis=1, keepdims=True) * INVERSE_ROOT
     part = to_row(part)
@@ -180,13 +198,10 @@
         low[:, :HD],
         jnp.concatenate([low[:, HD:], zeros], axis=1),
     ]
-    wide[:, pl.ds(D, HD)] = jnp.concatenate(lines * N_DP, axis=0)
-    stores = [store]
-    for z in range(NZ):
-        for x in range(NX):
-            pieces_ref[z * NX + x] = wide[pl.ds((x * NZ + z) * SHARE, SHARE), :].astype(bf16)
-        cut = pl.ds(z * NX, NX)
-        stores += start(sems.at[pl.ds(2 + z, 1)], (pieces_ref.at[cut], pieces_hbm.at[cut]))
+    lines = jnp.concatenate(lines, axis=0).astype(bf16)
+    stores += send_lanes(
+        D, WIDE, lambda piece, lanes: lines, pieces_ref, pieces_hbm, sems.at[pl.ds(6, 1)]
+    )
     wait(stores)
 
 
@@ -339,17 +354,21 @@
     projected, layer_own, window = call(
         project_kernel, "project", [H] * 8,
         (frames, partner, moved_tiles, attended, residual, grad_out, out_weight, scale_row),
-        [((ROWS, CAP_ROWS), f32, H), ((ROWS, CAP_ROWS), bf16, H), ((PAD_ROWS, MOVE_ROWS), bf16, H)],
+        [((ROWS, CAP_ROWS), f32, H), ((ROWS, CAP_ROWS), bf16, H), ((PAD_ROWS, MOVE_ROWS), bf16, V)],
         [
             ints, ints, ints,
             V((A, CAP_ROWS), bf16), V((ROWS, CAP_ROWS), bf16), V((ROWS, BAL_ROWS), bf16),
             V((ROWS, A), bf16), V((1, ROWS), f32),
-            V((ROWS, CAP_ROWS), f32), V((ROWS, CAP_ROWS), bf16), V((PAD_ROWS, MOVE_ROWS), bf16),
-            dma((6,)), dma((A // CHUNK,)), dma((A // CHUNK,)), dma((3,)),
+            V((ROWS, CAP_ROWS), f32), V((ROWS, CAP_ROWS), bf16),
+            dma((6,)), dma((A // CHUNK,)), dma((A // CHUNK,)), dma((2,)),
         ],
     )
     pieces = exchange(window.reshape(N_DP, PAD_ROWS // N_DP, MOVE_ROWS), ("z", "x"))
-    pieces = exchange(jnp.take(pieces, partner, axis=0), ("z", "x"))
+    (pieces,) = call(
+        forward_kernel, "forward", [S, V], (partner, pieces),
+        [((N_DP, PAD_ROWS // N_DP, MOVE_ROWS), bf16, V)],
+    )
+    pieces = exchange(pieces, ("z", "x"))
     got = pieces.reshape(PAD_ROWS, MOVE_ROWS)
 
     scaled, pieces = call(
@@ -357,9 +376,9 @@
         (frames, partner, moved_tiles, owner_slot, attended, grad_out, scale_row, got, projected),
         [((ROWS, CAP_ROWS), bf16, H), ((N_DP, SHARE, WIDE), bf16, H)],
         [
-            pltpu.SMEM((HEADS,), jnp.int32), V((A, ROWS), f32), V((HD, WIDE), f32),
+            pltpu.SMEM((HEADS,), jnp.int32), V((HD, D), f32),
             V((ROWS, CAP_ROWS), f32), V((ROWS, CAP_ROWS), bf16),
-            V((N_DP, SHARE, WIDE), bf16), dma((2 + NZ,)),
+            V((N_DP, SHARE, WIDE), bf16), dma((7,)),
         ],
     )
     summed = exchange(pieces, ("z", "x"))

time: 125 us -> 123 us (0.984)
  blocking collectives: 12.6 us -> 35.5 us
  starting transfers between devices: 56.1 us -> 42.5 us
  waiting for transfers between devices: 34.1 us -> 24.8 us
    all_to_all x1 -> x2, blocking collectives: 12.6 us -> 35.5 us  [exchange(): return lax.all_to_all(pieces, axes, split_axis=0, concat_axis=0, tiled=True)]
    all_to_all x4 -> x3, starting transfers between devices: 36.3 us -> 22.7 us  [exchange(): return lax.all_to_all(pieces, axes, split_axis=0, concat_axis=0, tiled=True)]
    all_to_all x4 -> x3, waiting for transfers between devices: 31.5 us -> 22.1 us  [exchange(): return lax.all_to_all(pieces, axes, split_axis=0, concat_axis=0, tiled=True)]
    pallas_call x9 -> x10, Pallas kernels: 18.8 us -> 18.5 us  [call(): pl.pallas_call(kernel, out_shape=[H(shape, dtype) if place is H else jax....]
  transfers between devices with their start and end apart: 9 -> 8, of which waited for: 6 -> 5; matrix products, arithmetic and copies ran while one was open for 0% -> 0% of each run, Pallas kernels for 8% -> 8%
where the time goes in v7:
time: 123 us; the launch traced here: 122 us
  starting transfers between devices  42.5 us (35%)
  blocking collectives  35.5 us (29%)
  waiting for transfers between devices  24.8 us (20%)
  Pallas kernels  18.5 us (15%)
    all_to_all x2, blocking collectives, exchange(): return lax.all_to_all(pieces, axes, split_axis=0, concat_axis=0, tiled=True)  35.5 us
    all_to_all x3, starting transfers between devices, exchange(): return lax.all_to_all(pieces, axes, split_axis=0, concat_axis=0, tiled=True)  22.7 us
    all_to_all x3, waiting for transfers between devices, exchange(): return lax.all_to_all(pieces, axes, split_axis=0, concat_axis=0, tiled=True)  22.1 us
    ppermute x5, starting transfers between devices, crossed(): return lax.ppermute(array, axis, [(i, i ^ bit) for i in range(size)])  19.8 us
    pallas_call x10, Pallas kernels, call(): pl.pallas_call(kernel, out_shape=[H(shape, dtype) if place is H else jax....  18.5 us
    ppermute x5, waiting for transfers between devices, crossed(): return lax.ppermute(array, axis, [(i, i ^ bit) for i in range(size)])  2.67 us
  transfers between devices with their start and end apart: 8, of which 5 were waited for; matrix products, arithmetic and copies ran while one was open for 0% of the time, Pallas kernels for 8%

profile of v7, /device:TPU:1, one launch (start us, length us, event | category | flops | bytes accessed | tf_op | source)
XLA Modules:
  0.0 122.2 jit_solution(11911006962982180714)
XLA Ops:
  0.6 0.0 copy-start.3
  0.6 0.0 copy-start.5
  0.7 0.0 copy-start.4
  0.7 0.0 copy-start.2
  0.7 0.0 copy-start
  0.7 0.0 copy-start.6
  0.7 0.0 copy-start.7
  0.7 3.6 %project.1 = (f32[200,512]{1,0:T(8,128)}, bf16[200,512]{1,0:T(8,128)(2,1)}, bf16[256,256]{1,0:T(8,128)(2,1)S(1)}) custom-call(s32[32]{0:T(128)} %frames_ref.3, s32[32]{0:T(128)} %partner_ref.5, s32[32]{0:T(128)} %moved_ref.3, bf16[2048,512]{1,0:T(8,128)(2,1)} %attended_ref.1, bf16[200,512]{1,0:T(8,128)(2,1)} %residual_hbm.1, bf16[200,384]{1,0:T(8,128)(2,1)} %grad_ref.1, ...), custom_call_target="tpu_custom_call" | custom-call | tf_op jit(solution)/shard_map/project/pallas_call | solution.py:302
  4.3 22.9 %all_to_all.25.pieces_ref = bf16[32,8,256]{2,1,0:T(8,128)(2,1)S(1)} all-to-all(bf16[32,8,256]{2,1,0:T(8,128)(2,1)S(1)} %bitcast.9), channel_id=1, replica_groups=mesh['z'=8,'x'=4,'y'=8,'c'=2] {'z','x'}, dimensions={0} | all-to-all | bytes 262144 | tf_op jit(solution)/shard_map/all_to_all | solution.py:318
  27.2 0.0 copy-done.3
  27.2 0.6 forward.1
  27.8 12.6 %all_to_all.26 = bf16[32,8,256]{2,1,0:T(8,128)(2,1)S(1)} all-to-all(bf16[32,8,256]{2,1,0:T(8,128)(2,1)S(1)} %forward.1), channel_id=1, replica_groups=mesh['z'=8,'x'=4,'y'=8,'c'=2] {'z','x'}, dimensions={0} | all-to-all | bytes 262144 | tf_op jit(solution)/shard_map/all_to_all | solution.py:318
  40.4 0.0 copy-done.5
  40.4 0.0 copy-done.4
  40.4 0.0 copy-done.2
  40.4 0.0 copy-done
  40.4 0.0 copy-done.6
  40.4 0.0 copy-done.7
  40.4 0.0 copy-start.1
  40.5 3.0 %weight_grad.1 = (bf16[200,512]{1,0:T(8,128)(2,1)}, bf16[32,4,3328]{2,1,0:T(4,128)(2,1)}) custom-call(s32[32]{0:T(128)S(1)} %copy-done.4, s32[32]{0:T(128)S(1)} %copy-done.3, s32[32]{0:T(128)S(1)} %copy-done.5, s32[16]{0:T(128)S(1)} %copy-done.7, bf16[2048,512]{1,0:T(8,128)(2,1)S(1)} %copy-done, bf16[200,384]{1,0:T(8,128)(2,1)S(1)} %copy-done.2, ...), custom_call_target="tpu_custom_call" | custom-call | tf_op jit(solution)/shard_map/weight_grad/pallas_call | solution.py:302
  43.5 3.9 %all-to-all-start.2 = ((bf16[32,4,3328]{2,1,0:T(4,128)(2,1)}), bf16[32,4,3328]{2,1,0:T(4,128)(2,1)S(1)}, u32[]{:S(2)}, u32[]{:S(2)}) async-start(bf16[32,4,3328]{2,1,0:T(4,128)(2,1)} %get-tuple-element.40), calls=%async_computation.2 | async-start | bytes 1703936 | tf_op jit(solution)/shard_map/all_to_all | solution.py:318
  47.4 0.0 copy-done.1
  47.4 3.2 %input_grad.1 = (bf16[1024,512]{1,0:T(8,128)(2,1)S(1)}, bf16[1024,512]{1,0:T(8,128)(2,1)S(1)}, bf16[200,384]{1,0:T(8,128)(2,1)}) custom-call(s32[32]{0:T(128)S(1)} %copy-done.4, s32[32]{0:T(128)S(1)} %copy-done.3, s32[32]{0:T(128)S(1)} %copy-done.5, bf16[200,2048]{1,0:T(8,128)(2,1)S(1)} %copy-done.1, bf16[256,256]{1,0:T(8,128)(2,1)S(1)} %bitcast.8, ...), custom_call_target="tpu_custom_call" | custom-call | tf_op jit(solution)/shard_map/input_grad/pallas_call | solution.py:302
  50.6 5.2 %collective-permute-start = (bf16[1024,512]{1,0:T(8,128)(2,1)S(1)}, bf16[1024,512]{1,0:T(8,128)(2,1)S(1)}, u32[]{:S(2)}, u32[]{:S(2)}) collective-permute-start(bf16[1024,512]{1,0:T(8,128)(2,1)S(1)} %get-tuple-element.33), channel_id=1, source_target_pairs={{0,1},{1,0},{2,3},{3,2},{4,5},{5,4},{6,7},{7,6},{8,9},{9,8},{10,11... | collective-permute-start | bytes 3145736 | tf_op jit(solution)/shard_map/ppermute | solution.py:322
  55.9 2.3 %collective-permute-done.refs_1_ = bf16[1024,512]{1,0:T(8,128)(2,1)S(1)} collective-permute-done((bf16[1024,512]{1,0:T(8,128)(2,1)S(1)}, bf16[1024,512]{1,0:T(8,128)(2,1)S(1)}, u32[]{:S(2)}, u32[]{:S(2)}) %collective-permute-start) | collective-permute-done | bytes 1048608 | tf_op jit(solution)/shard_map/ppermute | solution.py:322
  58.2 0.2 add.3
  58.4 3.2 %collective-permute-start.1 = (bf16[512,512]{1,0:T(8,128)(2,1)S(1)}, bf16[512,512]{1,0:T(8,128)(2,1)S(1)}, u32[]{:S(2)}, u32[]{:S(2)}) collective-permute-start(bf16[512,512]{1,0:T(8,128)(2,1)S(1)} %get-tuple-element.35), channel_id=1, source_target_pairs={{0,2},{2,0},{4,6},{6,4},{8,10},{10,8},{12,14},{14,12},{1,3},{3,1},... | collective-permute-start | bytes 1572872 | tf_op jit(solution)/shard_map/ppermute | solution.py:322
  61.6 6.1 %all-to-all-done.2.pieces_ref = bf16[32,4,3328]{2,1,0:T(4,128)(2,1)S(1)} async-done(((bf16[32,4,3328]{2,1,0:T(4,128)(2,1)}), bf16[32,4,3328]{2,1,0:T(4,128)(2,1)S(1)}, u32[]{:S(2)}, u32[]{:S(2)}) %all-to-all-start.2) | async-done | bytes 852000 | tf_op jit(solution)/shard_map/all_to_all | solution.py:318
  67.6 1.5 %slots.1 = (bf16[128,4,200]{2,1,0:T(4,128)(2,1)}, f32[1,200]{1,0:T(1,128)}) custom-call(bf16[32,4,3328]{2,1,0:T(4,128)(2,1)S(1)} %all-to-all-done.2.pieces_ref), custom_call_target="tpu_custom_call" | custom-call | tf_op jit(solution)/shard_map/slots/pallas_call | solution.py:302
  69.2 15.2 %all-to-all-start.3 = ((bf16[128,4,200]{2,1,0:T(4,128)(2,1)}), bf16[128,4,200]{2,1,0:T(4,128)(2,1)S(1)}, u32[]{:S(2)}, u32[]{:S(2)}) async-start(bf16[128,4,200]{2,1,0:T(4,128)(2,1)} %get-tuple-element.42), calls=%async_computation.3 | async-start | bytes 524288 | tf_op jit(solution)/shard_map/all_to_all | solution.py:318
  84.4 0.0 collective-permute-done.1.refs_1_
  84.4 0.1 add.4
  84.6 15.1 %all-to-all-done.3.owned_ref = bf16[128,4,200]{2,1,0:T(4,128)(2,1)S(1)} async-done(((bf16[128,4,200]{2,1,0:T(4,128)(2,1)}), bf16[128,4,200]{2,1,0:T(4,128)(2,1)S(1)}, u32[]{:S(2)}, u32[]{:S(2)}) %all-to-all-start.3) | async-done | bytes 204832 | tf_op jit(solution)/shard_map/all_to_all | solution.py:318
  99.7 1.2 join.1
  100.8 3.5 %all-to-all-start.4 = ((bf16[4,32,3200]{2,1,0:T(8,128)(2,1)}), bf16[4,32,3200]{2,1,0:T(8,128)(2,1)S(1)}, u32[]{:S(2)}, u32[]{:S(2)}) async-start(bf16[4,32,3200]{2,1,0:T(8,128)(2,1)} %join.1), calls=%async_computation.4 | async-start | bytes 1638400 | tf_op jit(solution)/shard_map/all_to_all | solution.py:318
  104.4 3.4 %collective-permute-start.2 = (bf16[128,512]{1,0:T(8,128)(2,1)S(1)}, bf16[128,512]{1,0:T(8,128)(2,1)S(1)}, u32[]{:S(2)}, u32[]{:S(2)}) collective-permute-start(bf16[128,512]{1,0:T(8,128)(2,1)S(1)} %get-tuple-element.37), channel_id=1, source_target_pairs={{0,8},{2,10},{4,12},{6,14},{8,0},{10,2},{12,4},{14,6},{1,9},{3,11}... | collective-permute-start | bytes 393224 | tf_op jit(solution)/shard_map/ppermute | solution.py:322
  107.8 2.8 %collective-permute-start.3 = (bf16[128,512]{1,0:T(8,128)(2,1)S(1)}, bf16[128,512]{1,0:T(8,128)(2,1)S(1)}, u32[]{:S(2)}, u32[]{:S(2)}) collective-permute-start(bf16[128,512]{1,0:T(8,128)(2,1)S(1)} %get-tuple-element.38), channel_id=1, source_target_pairs={{0,4},{2,6},{4,0},{6,2},{8,12},{10,14},{12,8},{14,10},{1,5},{3,7},... | collective-permute-start | bytes 393224 | tf_op jit(solution)/shard_map/ppermute | solution.py:322
  110.7 5.1 %collective-permute-start.4 = (bf16[128,512]{1,0:T(8,128)(2,1)S(1)}, bf16[128,512]{1,0:T(8,128)(2,1)S(1)}, u32[]{:S(2)}, u32[]{:S(2)}) collective-permute-start(bf16[128,512]{1,0:T(8,128)(2,1)S(1)} %get-tuple-element.39), channel_id=1, source_target_pairs={{0,12},{2,14},{4,8},{6,10},{8,4},{10,6},{12,0},{14,2},{1,13},{3,15... | collective-permute-start | bytes 393224 | tf_op jit(solution)/shard_map/ppermute | solution.py:322
  115.8 0.9 all-to-all-done.4
  116.7 4.4 %ortho.1 = bf16[3200,128]{1,0:T(8,128)(2,1)} custom-call(bf16[128,3200]{1,0:T(8,128)(2,1)S(1)} %bitcast.6), custom_call_target="tpu_custom_call" | custom-call | tf_op jit(solution)/shard_map/ortho/pallas_call | solution.py:302
  121.1 0.0 collective-permute-done.2.refs_1_
  121.1 0.4 collective-permute-done.3.refs_2_
  121.5 0.0 collective-permute-done.4.refs_3_
  121.5 0.7 add.5
Async XLA Ops:
  0.6 26.6 %copy-start.3 = (s32[32]{0:T(128)S(1)}, s32[32]{0:T(128)}, u32[]{:S(2)}) copy-start(s32[32]{0:T(128)} %partner_ref.5) | copy-start | bytes 388
  0.6 39.8 %copy-start.5 = (s32[32]{0:T(128)S(1)}, s32[32]{0:T(128)}, u32[]{:S(2)}) copy-start(s32[32]{0:T(128)} %moved_ref.3) | copy-start | bytes 388
  0.7 39.8 %copy-start.4 = (s32[32]{0:T(128)S(1)}, s32[32]{0:T(128)}, u32[]{:S(2)}) copy-start(s32[32]{0:T(128)} %frames_ref.3) | copy-start | bytes 388
  0.7 39.8 %copy-start.2 = (bf16[200,384]{1,0:T(8,128)(2,1)S(1)}, bf16[200,384]{1,0:T(8,128)(2,1)}, u32[]{:S(2)}) copy-start(bf16[200,384]{1,0:T(8,128)(2,1)} %grad_ref.1) | copy-start | bytes 460804
  0.7 39.7 %copy-start = (bf16[2048,512]{1,0:T(8,128)(2,1)S(1)}, bf16[2048,512]{1,0:T(8,128)(2,1)}, u32[]{:S(2)}) copy-start(bf16[2048,512]{1,0:T(8,128)(2,1)} %attended_ref.1) | copy-start | bytes 6291460
  0.7 39.7 %copy-start.6 = (f32[200]{0:T(256)S(1)}, f32[200]{0:T(256)}, u32[]{:S(2)}) copy-start(f32[200]{0:T(256)} %param.13) | copy-start | bytes 2404
  0.7 39.7 %copy-start.7 = (s32[16]{0:T(128)S(1)}, s32[16]{0:T(128)}, u32[]{:S(2)}) copy-start(s32[16]{0:T(128)} %slot_ref.1) | copy-start | bytes 196
  40.4 6.9 %copy-start.1 = (bf16[200,2048]{1,0:T(8,128)(2,1)S(1)}, bf16[200,2048]{1,0:T(8,128)(2,1)}, u32[]{:S(2)}) copy-start(bf16[200,2048]{1,0:T(8,128)(2,1)} %weight_ref.1) | copy-start | bytes 2457604
  43.5 24.2 %all-to-all-start.2 = ((bf16[32,4,3328]{2,1,0:T(4,128)(2,1)}), bf16[32,4,3328]{2,1,0:T(4,128)(2,1)S(1)}, u32[]{:S(2)}, u32[]{:S(2)}) async-start(bf16[32,4,3328]{2,1,0:T(4,128)(2,1)} %get-tuple-element.40), calls=%async_computation.2 | async-start | bytes 1703936 | tf_op jit(solution)/shard_map/all_to_all | solution.py:318
  50.6 7.5 %collective-permute-start = (bf16[1024,512]{1,0:T(8,128)(2,1)S(1)}, bf16[1024,512]{1,0:T(8,128)(2,1)S(1)}, u32[]{:S(2)}, u32[]{:S(2)}) collective-permute-start(bf16[1024,512]{1,0:T(8,128)(2,1)S(1)} %get-tuple-element.33), channel_id=1, source_target_pairs={{0,1},{1,0},{2,3},{3,2},{4,5},{5,4},{6,7},{7,6},{8,9},{9,8},{10,11... | collective-permute-start | bytes 3145736 | tf_op jit(solution)/shard_map/ppermute | solution.py:322
  58.4 26.0 %collective-permute-start.1 = (bf16[512,512]{1,0:T(8,128)(2,1)S(1)}, bf16[512,512]{1,0:T(8,128)(2,1)S(1)}, u32[]{:S(2)}, u32[]{:S(2)}) collective-permute-start(bf16[512,512]{1,0:T(8,128)(2,1)S(1)} %get-tuple-element.35), channel_id=1, source_target_pairs={{0,2},{2,0},{4,6},{6,4},{8,10},{10,8},{12,14},{14,12},{1,3},{3,1},... | collective-permute-start | bytes 1572872 | tf_op jit(solution)/shard_map/ppermute | solution.py:322
  69.2 30.5 %all-to-all-start.3 = ((bf16[128,4,200]{2,1,0:T(4,128)(2,1)}), bf16[128,4,200]{2,1,0:T(4,128)(2,1)S(1)}, u32[]{:S(2)}, u32[]{:S(2)}) async-start(bf16[128,4,200]{2,1,0:T(4,128)(2,1)} %get-tuple-element.42), calls=%async_computation.3 | async-start | bytes 524288 | tf_op jit(solution)/shard_map/all_to_all | solution.py:318
  100.8 15.9 %all-to-all-start.4 = ((bf16[4,32,3200]{2,1,0:T(8,128)(2,1)}), bf16[4,32,3200]{2,1,0:T(8,128)(2,1)S(1)}, u32[]{:S(2)}, u32[]{:S(2)}) async-start(bf16[4,32,3200]{2,1,0:T(8,128)(2,1)} %join.1), calls=%async_computation.4 | async-start | bytes 1638400 | tf_op jit(solution)/shard_map/all_to_all | solution.py:318
  104.4 16.7 %collective-permute-start.2 = (bf16[128,512]{1,0:T(8,128)(2,1)S(1)}, bf16[128,512]{1,0:T(8,128)(2,1)S(1)}, u32[]{:S(2)}, u32[]{:S(2)}) collective-permute-start(bf16[128,512]{1,0:T(8,128)(2,1)S(1)} %get-tuple-element.37), channel_id=1, source_target_pairs={{0,8},{2,10},{4,12},{6,14},{8,0},{10,2},{12,4},{14,6},{1,9},{3,11}... | collective-permute-start | bytes 393224 | tf_op jit(solution)/shard_map/ppermute | solution.py:322
  107.8 13.7 %collective-permute-start.3 = (bf16[128,512]{1,0:T(8,128)(2,1)S(1)}, bf16[128,512]{1,0:T(8,128)(2,1)S(1)}, u32[]{:S(2)}, u32[]{:S(2)}) collective-permute-start(bf16[128,512]{1,0:T(8,128)(2,1)S(1)} %get-tuple-element.38), channel_id=1, source_target_pairs={{0,4},{2,6},{4,0},{6,2},{8,12},{10,14},{12,8},{14,10},{1,5},{3,7},... | collective-permute-start | bytes 393224 | tf_op jit(solution)/shard_map/ppermute | solution.py:322
  110.7 10.8 %collective-permute-start.4 = (bf16[128,512]{1,0:T(8,128)(2,1)S(1)}, bf16[128,512]{1,0:T(8,128)(2,1)S(1)}, u32[]{:S(2)}, u32[]{:S(2)}) collective-permute-start(bf16[128,512]{1,0:T(8,128)(2,1)S(1)} %get-tuple-element.39), channel_id=1, source_target_pairs={{0,12},{2,14},{4,8},{6,10},{8,4},{10,6},{12,0},{14,2},{1,13},{3,15... | collective-permute-start | bytes 393224 | tf_op jit(solution)/shard_map/ppermute | solution.py:322

commit v8 on v7

--- a/solution.py
+++ b/solution.py
@@ -228,19 +228,16 @@
     layer_out_ref[...] = jnp.where(keep, own, received).astype(bf16)
 
 
-def slots_kernel(pieces_ref, copies_hbm, scale_grad_ref, by_slot, sems):
+def slots_kernel(pieces_ref, copies_ref, scale_grad_ref):
     total = pieces_ref[0].astype(f32)
     for piece in range(1, N_DP):
         total = total + pieces_ref[piece].astype(f32)
     for slot in range(HEADS):
-        by_slot[slot] = total[:, slot * ROWS : (slot + 1) * ROWS].astype(bf16)
-    copies = [
-        (by_slot, copies_hbm.at[pl.ds(z * HEADS, HEADS)]) for z in range(NZ)
-    ]
-    copies = start(sems, *copies)
+        part = total[:, slot * ROWS : (slot + 1) * ROWS].astype(bf16)
+        for z in range(NZ):
+            copies_ref[z * HEADS + slot] = part
     lines = total[0:2, D:] + total[2:4, D:]
     scale_grad_ref[...] = jnp.concatenate([lines[0:1, :], lines[1:2, : ROWS - HD]], axis=1)
-    wait(copies)
 
 
 def join_kernel(owned_ref, copies_hbm, joined, whole, sems):
@@ -322,25 +319,26 @@
     return lax.ppermute(array, axis, [(i, i ^ bit) for i in range(size)])
 
 
-EVEN = (0, 8, 4, 12, 2, 10, 6, 14)
-
-
-def add_kernel(*refs, parts):
-    in_refs, out_refs = refs[:-parts], refs[-parts:]
-    rows = in_refs[0].shape[0] // parts
-    for index, out_ref in enumerate(out_refs):
-        cut = pl.ds(index * rows, rows)
+EVEN = (0, 4, 8, 2, 6, 10, 12, 14)
+
+
+def add_kernel(*refs, blocks):
+    count = len(blocks)
+    in_refs, out_refs = refs[:-count], refs[-count:]
+    first = 0
+    for out_ref, size in zip(out_refs, blocks):
+        cut = pl.ds(first * HD, size * HD)
         total = in_refs[0][cut, :].astype(f32)
         for ref in in_refs[1:]:
             total = total + ref[cut, :].astype(f32)
         out_ref[...] = total.astype(bf16)
-
-
-def add(arrays, parts):
-    rows = arrays[0].shape[0] // parts
+        first += size
+
+
+def add(arrays, *blocks):
     return call(
-        functools.partial(add_kernel, parts=parts), "add", [V] * len(arrays), arrays,
-        [((rows, CAP_ROWS), bf16, V)] * parts, cost=FREE,
+        functools.partial(add_kernel, blocks=blocks), "add", [V] * len(arrays), arrays,
+        [((size * HD, CAP_ROWS), bf16, V) for size in blocks], cost=FREE,
     )
 
 
@@ -391,17 +389,16 @@
         [V((ROWS, CAP_ROWS), bf16), V((ROWS, CAP_ROWS), bf16), dma((2,))],
         FREE,
     )
-    left, other = add((even, crossed(odd, "c", NC, 1)), 2)
-    summed, _ = lax.optimization_barrier((summed, left))
+    left, near, *far = add((even, crossed(odd, "c", NC, 1)), 3, 3, 1, 1)
+    far = [crossed(other, "y", NY, step) for other, step in zip(far, (6, 7))]
+    left, *others = add((left, crossed(near, "y", NY, 1)), 1, 1, 1)
+    summed, _ = lax.optimization_barrier((summed, (left, far)))
     copies, scale_grad = call(
         slots_kernel, "slots", [V], (summed,),
-        [((NZ * HEADS, SHARE, ROWS), bf16, H), ((1, ROWS), f32, V)],
-        [V((HEADS, SHARE, ROWS), bf16), dma((NZ,))],
+        [((NZ * HEADS, SHARE, ROWS), bf16, V), ((1, ROWS), f32, V)],
     )
     owned = exchange(copies, ("z", "y", "c"))
-    left, *others = add((left, crossed(other, "y", NY, 1)), 4)
-    owned, _ = lax.optimization_barrier((owned, left))
-    others = [crossed(other, "y", NY, step) for other, step in zip(others, (4, 2, 6))]
+    far += [crossed(other, "y", NY, step) for other, step in zip(others, (2, 4))]
     (copies,) = call(
         join_kernel, "join", [V], (owned,),
         [((NX, BY_X, D), bf16, H)],
@@ -412,8 +409,8 @@
         ortho_kernel, "ortho", [V], (whole,), [((D, HD), bf16, H)],
         [V((D, HD), bf16), dma((PARTS,))],
     )
-    left, others, ortho_update = lax.optimization_barrier((left, others, ortho_update))
-    (input_grad,) = add((left, *others), 1)
+    left, far, ortho_update = lax.optimization_barrier((left, far, ortho_update))
+    (input_grad,) = add((left, *far), 1)
     return (layer_out, input_grad, scale_grad.reshape(ROWS), ortho_update[:, None, :])
 
 

time: 123 us -> 131 us (1.065)
  blocking collectives: 35.5 us -> 65.8 us
  starting transfers between devices: 42.5 us -> 29.5 us
  waiting for transfers between devices: 24.8 us -> 16.7 us
    all_to_all x2 -> x3, blocking collectives: 35.5 us -> 65.8 us  [exchange(): return lax.all_to_all(pieces, axes, split_axis=0, concat_axis=0, tiled=True)]
    all_to_all x3 -> x2, waiting for transfers between devices: 22.1 us -> 5.79 us  [exchange(): return lax.all_to_all(pieces, axes, split_axis=0, concat_axis=0, tiled=True)]
    all_to_all x3 -> x2, starting transfers between devices: 22.7 us -> 7.91 us  [exchange(): return lax.all_to_all(pieces, axes, split_axis=0, concat_axis=0, tiled=True)]
    ppermute x5 -> x6, waiting for transfers between devices: 2.67 us -> 10.9 us  [crossed(): return lax.ppermute(array, axis, [(i, i ^ bit) for i in range(size)])]
    ppermute x5 -> x6, starting transfers between devices: 19.8 us -> 21.6 us  [crossed(): return lax.ppermute(array, axis, [(i, i ^ bit) for i in range(size)])]
  transfers between devices with their start and end apart: 8 -> 8, of which waited for: 5 -> 5; matrix products, arithmetic and copies ran while one was open for 0% -> 0% of each run, Pallas kernels for 8% -> 6%
where the time goes in v8:
time: 131 us
  blocking collectives  65.8 us (50%)
  starting transfers between devices  29.5 us (23%)
  Pallas kernels  17.6 us (13%)
  waiting for transfers between devices  16.7 us (13%)
    all_to_all x3, blocking collectives, exchange(): return lax.all_to_all(pieces, axes, split_axis=0, concat_axis=0, tiled=True)  65.8 us
    ppermute x6, starting transfers between devices, crossed(): return lax.ppermute(array, axis, [(i, i ^ bit) for i in range(size)])  21.6 us
    pallas_call x10, Pallas kernels, call(): pl.pallas_call(kernel, out_shape=[H(shape, dtype) if place is H else jax....  17.6 us
    ppermute x6, waiting for transfers between devices, crossed(): return lax.ppermute(array, axis, [(i, i ^ bit) for i in range(size)])  10.9 us
    all_to_all x2, starting transfers between devices, exchange(): return lax.all_to_all(pieces, axes, split_axis=0, concat_axis=0, tiled=True)  7.91 us
    all_to_all x2, waiting for transfers between devices, exchange(): return lax.all_to_all(pieces, axes, split_axis=0, concat_axis=0, tiled=True)  5.79 us
  transfers between devices with their start and end apart: 8, of which 5 were waited for; matrix products, arithmetic and copies ran while one was open for 0% of the time, Pallas kernels for 6%

profile of v8, /device:TPU:1, one launch (start us, length us, event | category | flops | bytes accessed | tf_op | source)
XLA Modules:
  0.0 130.6 jit_solution(336182621532549470)
XLA Ops:
  0.6 0.0 copy-start.3
  0.6 0.0 copy-start.5
  0.7 0.0 copy-start.4
  0.7 0.0 copy-start.2
  0.7 0.0 copy-start
  0.7 0.0 copy-start.6
  0.7 0.0 copy-start.7
  0.7 3.6 %project.1 = (f32[200,512]{1,0:T(8,128)}, bf16[200,512]{1,0:T(8,128)(2,1)}, bf16[256,256]{1,0:T(8,128)(2,1)S(1)}) custom-call(s32[32]{0:T(128)} %frames_ref.3, s32[32]{0:T(128)} %partner_ref.5, s32[32]{0:T(128)} %moved_ref.3, bf16[2048,512]{1,0:T(8,128)(2,1)} %attended_ref.1, bf16[200,512]{1,0:T(8,128)(2,1)} %residual_hbm.1, bf16[200,384]{1,0:T(8,128)(2,1)} %grad_ref.1, ...), custom_call_target="tpu_custom_call" | custom-call | tf_op jit(solution)/shard_map/project/pallas_call | solution.py:299
  4.3 22.9 %all_to_all.25.pieces_ref = bf16[32,8,256]{2,1,0:T(8,128)(2,1)S(1)} all-to-all(bf16[32,8,256]{2,1,0:T(8,128)(2,1)S(1)} %bitcast.9), channel_id=1, replica_groups=mesh['z'=8,'x'=4,'y'=8,'c'=2] {'z','x'}, dimensions={0} | all-to-all | bytes 262144 | tf_op jit(solution)/shard_map/all_to_all | solution.py:315
  27.2 0.0 copy-done.3
  27.2 0.6 forward.1
  27.7 12.6 %all_to_all.26 = bf16[32,8,256]{2,1,0:T(8,128)(2,1)S(1)} all-to-all(bf16[32,8,256]{2,1,0:T(8,128)(2,1)S(1)} %forward.1), channel_id=1, replica_groups=mesh['z'=8,'x'=4,'y'=8,'c'=2] {'z','x'}, dimensions={0} | all-to-all | bytes 262144 | tf_op jit(solution)/shard_map/all_to_all | solution.py:315
  40.4 0.0 copy-done.5
  40.4 0.0 copy-done.4
  40.4 0.0 copy-done.2
  40.4 0.0 copy-done
  40.4 0.0 copy-done.6
  40.4 0.0 copy-done.7
  40.4 0.0 copy-start.1
  40.4 3.0 %weight_grad.1 = (bf16[200,512]{1,0:T(8,128)(2,1)}, bf16[32,4,3328]{2,1,0:T(4,128)(2,1)}) custom-call(s32[32]{0:T(128)S(1)} %copy-done.4, s32[32]{0:T(128)S(1)} %copy-done.3, s32[32]{0:T(128)S(1)} %copy-done.5, s32[16]{0:T(128)S(1)} %copy-done.7, bf16[2048,512]{1,0:T(8,128)(2,1)S(1)} %copy-done, bf16[200,384]{1,0:T(8,128)(2,1)S(1)} %copy-done.2, ...), custom_call_target="tpu_custom_call" | custom-call | tf_op jit(solution)/shard_map/weight_grad/pallas_call | solution.py:299
  43.4 3.9 %all-to-all-start.2 = ((bf16[32,4,3328]{2,1,0:T(4,128)(2,1)}), bf16[32,4,3328]{2,1,0:T(4,128)(2,1)S(1)}, u32[]{:S(2)}, u32[]{:S(2)}) async-start(bf16[32,4,3328]{2,1,0:T(4,128)(2,1)} %get-tuple-element.42), calls=%async_computation.2 | async-start | bytes 1703936 | tf_op jit(solution)/shard_map/all_to_all | solution.py:315
  47.4 0.0 copy-done.1
  47.4 3.2 %input_grad.1 = (bf16[1024,512]{1,0:T(8,128)(2,1)S(1)}, bf16[1024,512]{1,0:T(8,128)(2,1)S(1)}, bf16[200,384]{1,0:T(8,128)(2,1)}) custom-call(s32[32]{0:T(128)S(1)} %copy-done.4, s32[32]{0:T(128)S(1)} %copy-done.3, s32[32]{0:T(128)S(1)} %copy-done.5, bf16[200,2048]{1,0:T(8,128)(2,1)S(1)} %copy-done.1, bf16[256,256]{1,0:T(8,128)(2,1)S(1)} %bitcast.8, ...), custom_call_target="tpu_custom_call" | custom-call | tf_op jit(solution)/shard_map/input_grad/pallas_call | solution.py:299
  50.6 5.2 %collective-permute-start = (bf16[1024,512]{1,0:T(8,128)(2,1)S(1)}, bf16[1024,512]{1,0:T(8,128)(2,1)S(1)}, u32[]{:S(2)}, u32[]{:S(2)}) collective-permute-start(bf16[1024,512]{1,0:T(8,128)(2,1)S(1)} %get-tuple-element.34), channel_id=1, source_target_pairs={{0,1},{1,0},{2,3},{3,2},{4,5},{5,4},{6,7},{7,6},{8,9},{9,8},{10,11... | collective-permute-start | bytes 3145736 | tf_op jit(solution)/shard_map/ppermute | solution.py:319
  55.9 2.3 %collective-permute-done.refs_1_ = bf16[1024,512]{1,0:T(8,128)(2,1)S(1)} collective-permute-done((bf16[1024,512]{1,0:T(8,128)(2,1)S(1)}, bf16[1024,512]{1,0:T(8,128)(2,1)S(1)}, u32[]{:S(2)}, u32[]{:S(2)}) %collective-permute-start) | collective-permute-done | bytes 1048608 | tf_op jit(solution)/shard_map/ppermute | solution.py:319
  58.1 0.2 add.3
  58.4 3.2 %collective-permute-start.1 = (bf16[384,512]{1,0:T(8,128)(2,1)S(1)}, bf16[384,512]{1,0:T(8,128)(2,1)S(1)}, u32[]{:S(2)}, u32[]{:S(2)}) collective-permute-start(bf16[384,512]{1,0:T(8,128)(2,1)S(1)} %get-tuple-element.36), channel_id=1, source_target_pairs={{0,2},{2,0},{4,6},{6,4},{8,10},{10,8},{12,14},{14,12},{1,3},{3,1},... | collective-permute-start | bytes 1179656 | tf_op jit(solution)/shard_map/ppermute | solution.py:319
  61.6 5.0 %collective-permute-start.2 = (bf16[128,512]{1,0:T(8,128)(2,1)S(1)}, bf16[128,512]{1,0:T(8,128)(2,1)S(1)}, u32[]{:S(2)}, u32[]{:S(2)}) collective-permute-start(bf16[128,512]{1,0:T(8,128)(2,1)S(1)} %get-tuple-element.38), channel_id=1, source_target_pairs={{0,12},{2,14},{4,8},{6,10},{8,4},{10,6},{12,0},{14,2},{1,13},{3,15... | collective-permute-start | bytes 393224 | tf_op jit(solution)/shard_map/ppermute | solution.py:319
  66.6 1.9 %collective-permute-start.3 = (bf16[128,512]{1,0:T(8,128)(2,1)S(1)}, bf16[128,512]{1,0:T(8,128)(2,1)S(1)}, u32[]{:S(2)}, u32[]{:S(2)}) collective-permute-start(bf16[128,512]{1,0:T(8,128)(2,1)S(1)} %get-tuple-element.39), channel_id=1, source_target_pairs={{0,14},{2,12},{4,10},{6,8},{8,6},{10,4},{12,2},{14,0},{1,15},{3,13... | collective-permute-start | bytes 393224 | tf_op jit(solution)/shard_map/ppermute | solution.py:319
  68.5 4.0 %collective-permute-done.1.refs_1_ = bf16[384,512]{1,0:T(8,128)(2,1)S(1)} collective-permute-done((bf16[384,512]{1,0:T(8,128)(2,1)S(1)}, bf16[384,512]{1,0:T(8,128)(2,1)S(1)}, u32[]{:S(2)}, u32[]{:S(2)}) %collective-permute-start.1) | collective-permute-done | bytes 393248 | tf_op jit(solution)/shard_map/ppermute | solution.py:319
  72.5 0.1 add.4
  72.6 3.8 %collective-permute-done.2.refs_1_ = bf16[128,512]{1,0:T(8,128)(2,1)S(1)} collective-permute-done((bf16[128,512]{1,0:T(8,128)(2,1)S(1)}, bf16[128,512]{1,0:T(8,128)(2,1)S(1)}, u32[]{:S(2)}, u32[]{:S(2)}) %collective-permute-start.2) | collective-permute-done | bytes 131104 | tf_op jit(solution)/shard_map/ppermute | solution.py:319
  76.3 0.9 collective-permute-done.3.refs_2_
  77.2 0.0 all-to-all-done.2.pieces_ref
  77.2 0.7 slots.1
  77.9 30.3 %all_to_all.27.owned_ref = bf16[128,4,200]{2,1,0:T(4,128)(2,1)S(1)} all-to-all(bf16[128,4,200]{2,1,0:T(4,128)(2,1)S(1)} %get-tuple-element.44), channel_id=1, replica_groups=mesh['z'=8,'x'=4,'y'=8,'c'=2] {'z','y','c'}, dimensions={0} | all-to-all | bytes 409600 | tf_op jit(solution)/shard_map/all_to_all | solution.py:315
  108.2 1.2 join.1
  109.4 4.0 %all-to-all-start.4 = ((bf16[4,32,3200]{2,1,0:T(8,128)(2,1)}), bf16[4,32,3200]{2,1,0:T(8,128)(2,1)S(1)}, u32[]{:S(2)}, u32[]{:S(2)}) async-start(bf16[4,32,3200]{2,1,0:T(8,128)(2,1)} %join.1), calls=%async_computation.4 | async-start | bytes 1638400 | tf_op jit(solution)/shard_map/all_to_all | solution.py:315
  113.4 2.0 %collective-permute-start.4 = (bf16[128,512]{1,0:T(8,128)(2,1)S(1)}, bf16[128,512]{1,0:T(8,128)(2,1)S(1)}, u32[]{:S(2)}, u32[]{:S(2)}) collective-permute-start(bf16[128,512]{1,0:T(8,128)(2,1)S(1)} %get-tuple-element.40), channel_id=1, source_target_pairs={{0,4},{2,6},{4,0},{6,2},{8,12},{10,14},{12,8},{14,10},{1,5},{3,7},... | collective-permute-start | bytes 393224 | tf_op jit(solution)/shard_map/ppermute | solution.py:319
  115.4 4.3 %collective-permute-start.5 = (bf16[128,512]{1,0:T(8,128)(2,1)S(1)}, bf16[128,512]{1,0:T(8,128)(2,1)S(1)}, u32[]{:S(2)}, u32[]{:S(2)}) collective-permute-start(bf16[128,512]{1,0:T(8,128)(2,1)S(1)} %get-tuple-element.41), channel_id=1, source_target_pairs={{0,8},{2,10},{4,12},{6,14},{8,0},{10,2},{12,4},{14,6},{1,9},{3,11}... | collective-permute-start | bytes 393224 | tf_op jit(solution)/shard_map/ppermute | solution.py:319
  119.6 5.8 %all-to-all-done.4 = bf16[4,32,3200]{2,1,0:T(8,128)(2,1)S(1)} async-done(((bf16[4,32,3200]{2,1,0:T(8,128)(2,1)}), bf16[4,32,3200]{2,1,0:T(8,128)(2,1)S(1)}, u32[]{:S(2)}, u32[]{:S(2)}) %all-to-all-start.4) | async-done | bytes 819232 | tf_op jit(solution)/shard_map/all_to_all | solution.py:315
  125.4 4.4 %ortho.1 = bf16[3200,128]{1,0:T(8,128)(2,1)} custom-call(bf16[128,3200]{1,0:T(8,128)(2,1)S(1)} %bitcast.6), custom_call_target="tpu_custom_call" | custom-call | tf_op jit(solution)/shard_map/ortho/pallas_call | solution.py:299
  129.8 0.0 collective-permute-done.4.refs_3_
  129.8 0.0 collective-permute-done.5.refs_4_
  129.8 0.7 add.5
Async XLA Ops:
  0.6 26.5 %copy-start.3 = (s32[32]{0:T(128)S(1)}, s32[32]{0:T(128)}, u32[]{:S(2)}) copy-start(s32[32]{0:T(128)} %partner_ref.5) | copy-start | bytes 388
  0.6 39.8 %copy-start.5 = (s32[32]{0:T(128)S(1)}, s32[32]{0:T(128)}, u32[]{:S(2)}) copy-start(s32[32]{0:T(128)} %moved_ref.3) | copy-start | bytes 388
  0.7 39.7 %copy-start.4 = (s32[32]{0:T(128)S(1)}, s32[32]{0:T(128)}, u32[]{:S(2)}) copy-start(s32[32]{0:T(128)} %frames_ref.3) | copy-start | bytes 388
  0.7 39.7 %copy-start.2 = (bf16[200,384]{1,0:T(8,128)(2,1)S(1)}, bf16[200,384]{1,0:T(8,128)(2,1)}, u32[]{:S(2)}) copy-start(bf16[200,384]{1,0:T(8,128)(2,1)} %grad_ref.1) | copy-start | bytes 460804
  0.7 39.7 %copy-start = (bf16[2048,512]{1,0:T(8,128)(2,1)S(1)}, bf16[2048,512]{1,0:T(8,128)(2,1)}, u32[]{:S(2)}) copy-start(bf16[2048,512]{1,0:T(8,128)(2,1)} %attended_ref.1) | copy-start | bytes 6291460
  0.7 39.7 %copy-start.6 = (f32[200]{0:T(256)S(1)}, f32[200]{0:T(256)}, u32[]{:S(2)}) copy-start(f32[200]{0:T(256)} %param.13) | copy-start | bytes 2404
  0.7 39.7 %copy-start.7 = (s32[16]{0:T(128)S(1)}, s32[16]{0:T(128)}, u32[]{:S(2)}) copy-start(s32[16]{0:T(128)} %slot_ref.1) | copy-start | bytes 196
  40.4 6.9 %copy-start.1 = (bf16[200,2048]{1,0:T(8,128)(2,1)S(1)}, bf16[200,2048]{1,0:T(8,128)(2,1)}, u32[]{:S(2)}) copy-start(bf16[200,2048]{1,0:T(8,128)(2,1)} %weight_ref.1) | copy-start | bytes 2457604
  43.4 33.8 %all-to-all-start.2 = ((bf16[32,4,3328]{2,1,0:T(4,128)(2,1)}), bf16[32,4,3328]{2,1,0:T(4,128)(2,1)S(1)}, u32[]{:S(2)}, u32[]{:S(2)}) async-start(bf16[32,4,3328]{2,1,0:T(4,128)(2,1)} %get-tuple-element.42), calls=%async_computation.2 | async-start | bytes 1703936 | tf_op jit(solution)/shard_map/all_to_all | solution.py:315
  50.6 7.5 %collective-permute-start = (bf16[1024,512]{1,0:T(8,128)(2,1)S(1)}, bf16[1024,512]{1,0:T(8,128)(2,1)S(1)}, u32[]{:S(2)}, u32[]{:S(2)}) collective-permute-start(bf16[1024,512]{1,0:T(8,128)(2,1)S(1)} %get-tuple-element.34), channel_id=1, source_target_pairs={{0,1},{1,0},{2,3},{3,2},{4,5},{5,4},{6,7},{7,6},{8,9},{9,8},{10,11... | collective-permute-start | bytes 3145736 | tf_op jit(solution)/shard_map/ppermute | solution.py:319
  58.4 14.1 %collective-permute-start.1 = (bf16[384,512]{1,0:T(8,128)(2,1)S(1)}, bf16[384,512]{1,0:T(8,128)(2,1)S(1)}, u32[]{:S(2)}, u32[]{:S(2)}) collective-permute-start(bf16[384,512]{1,0:T(8,128)(2,1)S(1)} %get-tuple-element.36), channel_id=1, source_target_pairs={{0,2},{2,0},{4,6},{6,4},{8,10},{10,8},{12,14},{14,12},{1,3},{3,1},... | collective-permute-start | bytes 1179656 | tf_op jit(solution)/shard_map/ppermute | solution.py:319
  61.6 14.8 %collective-permute-start.2 = (bf16[128,512]{1,0:T(8,128)(2,1)S(1)}, bf16[128,512]{1,0:T(8,128)(2,1)S(1)}, u32[]{:S(2)}, u32[]{:S(2)}) collective-permute-start(bf16[128,512]{1,0:T(8,128)(2,1)S(1)} %get-tuple-element.38), channel_id=1, source_target_pairs={{0,12},{2,14},{4,8},{6,10},{8,4},{10,6},{12,0},{14,2},{1,13},{3,15... | collective-permute-start | bytes 393224 | tf_op jit(solution)/shard_map/ppermute | solution.py:319
  66.6 10.7 %collective-permute-start.3 = (bf16[128,512]{1,0:T(8,128)(2,1)S(1)}, bf16[128,512]{1,0:T(8,128)(2,1)S(1)}, u32[]{:S(2)}, u32[]{:S(2)}) collective-permute-start(bf16[128,512]{1,0:T(8,128)(2,1)S(1)} %get-tuple-element.39), channel_id=1, source_target_pairs={{0,14},{2,12},{4,10},{6,8},{8,6},{10,4},{12,2},{14,0},{1,15},{3,13... | collective-permute-start | bytes 393224 | tf_op jit(solution)/shard_map/ppermute | solution.py:319
  109.4 16.1 %all-to-all-start.4 = ((bf16[4,32,3200]{2,1,0:T(8,128)(2,1)}), bf16[4,32,3200]{2,1,0:T(8,128)(2,1)S(1)}, u32[]{:S(2)}, u32[]{:S(2)}) async-start(bf16[4,32,3200]{2,1,0:T(8,128)(2,1)} %join.1), calls=%async_computation.4 | async-start | bytes 1638400 | tf_op jit(solution)/shard_map/all_to_all | solution.py:315
  113.4 16.4 %collective-permute-start.4 = (bf16[128,512]{1,0:T(8,128)(2,1)S(1)}, bf16[128,512]{1,0:T(8,128)(2,1)S(1)}, u32[]{:S(2)}, u32[]{:S(2)}) collective-permute-start(bf16[128,512]{1,0:T(8,128)(2,1)S(1)} %get-tuple-element.40), channel_id=1, source_target_pairs={{0,4},{2,6},{4,0},{6,2},{8,12},{10,14},{12,8},{14,10},{1,5},{3,7},... | collective-permute-start | bytes 393224 | tf_op jit(solution)/shard_map/ppermute | solution.py:319
  115.4 14.4 %collective-permute-start.5 = (bf16[128,512]{1,0:T(8,128)(2,1)S(1)}, bf16[128,512]{1,0:T(8,128)(2,1)S(1)}, u32[]{:S(2)}, u32[]{:S(2)}) collective-permute-start(bf16[128,512]{1,0:T(8,128)(2,1)S(1)} %get-tuple-element.41), channel_id=1, source_target_pairs={{0,8},{2,10},{4,12},{6,14},{8,0},{10,2},{12,4},{14,6},{1,9},{3,11}... | collective-permute-start | bytes 393224 | tf_op jit(solution)/shard_map/ppermute | solution.py:319

commit v9 on v8

--- a/solution.py
+++ b/solution.py
@@ -213,12 +213,12 @@
 ):
     fetch = start(sems, (scaled_hbm, scaled_ref), (layer_hbm, layer_ref))
     kept, incoming, holds_two = my_counts(frames_ref, partner_ref, moved_ref)
-    block = lax.axis_index("y") * NC + lax.axis_index("c")
+    y, c = lax.axis_index("y"), lax.axis_index("c")
     fetch[0].wait()
     scaled = scaled_ref[...]
-    for index, other in enumerate(EVEN):
-        for ref, partner in ((even_ref, other), (odd_ref, other + 1)):
-            first = pl.multiple_of((block ^ partner) * HD, HD)
+    for index, step in enumerate(STEPS):
+        for ref, core in ((even_ref, c), (odd_ref, 1 - c)):
+            first = pl.multiple_of((lax.rem(y + step + NY, NY) * NC + core) * HD, HD)
             part = dot(weight_ref[:, pl.ds(first, HD)], scaled, ROWS_BY_COLS)
             ref[pl.ds(index * HD, HD), :] = part.astype(bf16)
     fetch[1].wait()
@@ -315,11 +315,11 @@
     return lax.all_to_all(pieces, axes, split_axis=0, concat_axis=0, tiled=True)
 
 
-def crossed(array, axis, size, bit):
-    return lax.ppermute(array, axis, [(i, i ^ bit) for i in range(size)])
-
-
-EVEN = (0, 4, 8, 2, 6, 10, 12, 14)
+def shifted(array, axis, size, step):
+    return lax.ppermute(array, axis, [(i, (i + step) % size) for i in range(size)])
+
+
+STEPS = (0, -3, 3, -1, -4, 2, 1, -2)
 
 
 def add_kernel(*refs, blocks):
@@ -329,10 +329,11 @@
     for out_ref, size in zip(out_refs, blocks):
         cut = pl.ds(first * HD, size * HD)
         total = in_refs[0][cut, :].astype(f32)
+        first += size
         for ref in in_refs[1:]:
-            total = total + ref[cut, :].astype(f32)
+            if ref.shape[0] >= first * HD:
+                total = total + ref[cut, :].astype(f32)
         out_ref[...] = total.astype(bf16)
-        first += size
 
 
 def add(arrays, *blocks):
@@ -389,28 +390,28 @@
         [V((ROWS, CAP_ROWS), bf16), V((ROWS, CAP_ROWS), bf16), dma((2,))],
         FREE,
     )
-    left, near, *far = add((even, crossed(odd, "c", NC, 1)), 3, 3, 1, 1)
-    far = [crossed(other, "y", NY, step) for other, step in zip(far, (6, 7))]
-    left, *others = add((left, crossed(near, "y", NY, 1)), 1, 1, 1)
-    summed, _ = lax.optimization_barrier((summed, (left, far)))
+    keep, below, above = add((even, shifted(odd, "c", NC, 1)), 3, 3, 2)
+    below, above = shifted(below, "y", NY, -1), shifted(above, "y", NY, 1)
+    keep, below, above = add((keep, below, above), 1, 1, 1)
+    summed, _ = lax.optimization_barrier((summed, keep))
     copies, scale_grad = call(
         slots_kernel, "slots", [V], (summed,),
         [((NZ * HEADS, SHARE, ROWS), bf16, V), ((1, ROWS), f32, V)],
     )
     owned = exchange(copies, ("z", "y", "c"))
-    far += [crossed(other, "y", NY, step) for other, step in zip(others, (2, 4))]
     (copies,) = call(
         join_kernel, "join", [V], (owned,),
         [((NX, BY_X, D), bf16, H)],
         [V((BY_X, D), f32), V((BY_X, D), bf16), dma((NX,))],
     )
+    below, above = shifted(below, "y", NY, -3), shifted(above, "y", NY, 3)
     whole = exchange(copies, "x").reshape(HD, D)
     (ortho_update,) = call(
         ortho_kernel, "ortho", [V], (whole,), [((D, HD), bf16, H)],
         [V((D, HD), bf16), dma((PARTS,))],
     )
-    left, far, ortho_update = lax.optimization_barrier((left, far, ortho_update))
-    (input_grad,) = add((left, *far), 1)
+    keep, below, above, ortho_update = lax.optimization_barrier((keep, below, above, ortho_update))
+    (input_grad,) = add((keep, below, above), 1)
     return (layer_out, input_grad, scale_grad.reshape(ROWS), ortho_update[:, None, :])
 
 

time: 131 us -> 126 us (0.962)
  blocking collectives: 65.8 us -> 62.7 us
  starting transfers between devices: 29.5 us -> 27.1 us
    all_to_all x3, blocking collectives: 65.8 us -> 62.7 us  [exchange(): return lax.all_to_all(pieces, axes, split_axis=0, concat_axis=0, tiled=True)]
    ppermute x6 -> x5, starting transfers between devices: 21.6 us -> 19.2 us  [shifted(): lax.ppermute(array, axis, [(i, (i + step) % size) for i in range(size)])]
    ppermute x6 -> x5, waiting for transfers between devices: 10.9 us -> 12.2 us  [shifted(): lax.ppermute(array, axis, [(i, (i + step) % size) for i in range(size)])]
  transfers between devices with their start and end apart: 8 -> 7, of which waited for: 5 -> 4; matrix products, arithmetic and copies ran while one was open for 0% -> 0% of each run, Pallas kernels for 6% -> 6%
where the time goes in v9:
time: 126 us
  blocking collectives  62.7 us (50%)
  starting transfers between devices  27.1 us (22%)
  Pallas kernels  17.7 us (14%)
  waiting for transfers between devices  17.2 us (14%)
    all_to_all x3, blocking collectives, exchange(): return lax.all_to_all(pieces, axes, split_axis=0, concat_axis=0, tiled=True)  62.7 us
    ppermute x5, starting transfers between devices, shifted(): lax.ppermute(array, axis, [(i, (i + step) % size) for i in range(size)])  19.2 us
    pallas_call x10, Pallas kernels, call(): pl.pallas_call(kernel, out_shape=[H(shape, dtype) if place is H else jax....  17.7 us
    ppermute x5, waiting for transfers between devices, shifted(): lax.ppermute(array, axis, [(i, (i + step) % size) for i in range(size)])  12.2 us
    all_to_all x2, starting transfers between devices, exchange(): return lax.all_to_all(pieces, axes, split_axis=0, concat_axis=0, tiled=True)  7.91 us
    all_to_all x2, waiting for transfers between devices, exchange(): return lax.all_to_all(pieces, axes, split_axis=0, concat_axis=0, tiled=True)  4.99 us
  transfers between devices with their start and end apart: 7, of which 4 were waited for; matrix products, arithmetic and copies ran while one was open for 0% of the time, Pallas kernels for 6%

profile of v9, /device:TPU:1, one launch (start us, length us, event | category | flops | bytes accessed | tf_op | source)
XLA Modules:
  0.0 125.6 jit_solution(13741407964719778570)
XLA Ops:
  0.6 0.0 copy-start.3
  0.6 0.0 copy-start.5
  0.7 0.0 copy-start.4
  0.7 0.0 copy-start.2
  0.7 0.0 copy-start
  0.7 0.0 copy-start.6
  0.7 0.0 copy-start.7
  0.7 3.6 %project.1 = (f32[200,512]{1,0:T(8,128)}, bf16[200,512]{1,0:T(8,128)(2,1)}, bf16[256,256]{1,0:T(8,128)(2,1)S(1)}) custom-call(s32[32]{0:T(128)} %frames_ref.3, s32[32]{0:T(128)} %partner_ref.5, s32[32]{0:T(128)} %moved_ref.3, bf16[2048,512]{1,0:T(8,128)(2,1)} %attended_ref.1, bf16[200,512]{1,0:T(8,128)(2,1)} %residual_hbm.1, bf16[200,384]{1,0:T(8,128)(2,1)} %grad_ref.1, ...), custom_call_target="tpu_custom_call" | custom-call | tf_op jit(solution)/shard_map/project/pallas_call | solution.py:299
  4.3 22.9 %all_to_all.25.pieces_ref = bf16[32,8,256]{2,1,0:T(8,128)(2,1)S(1)} all-to-all(bf16[32,8,256]{2,1,0:T(8,128)(2,1)S(1)} %bitcast.9), channel_id=1, replica_groups=mesh['z'=8,'x'=4,'y'=8,'c'=2] {'z','x'}, dimensions={0} | all-to-all | bytes 262144 | tf_op jit(solution)/shard_map/all_to_all | solution.py:315
  27.2 0.0 copy-done.3
  27.2 0.6 forward.1
  27.8 12.7 %all_to_all.26 = bf16[32,8,256]{2,1,0:T(8,128)(2,1)S(1)} all-to-all(bf16[32,8,256]{2,1,0:T(8,128)(2,1)S(1)} %forward.1), channel_id=1, replica_groups=mesh['z'=8,'x'=4,'y'=8,'c'=2] {'z','x'}, dimensions={0} | all-to-all | bytes 262144 | tf_op jit(solution)/shard_map/all_to_all | solution.py:315
  40.5 0.0 copy-done.5
  40.5 0.0 copy-done.4
  40.5 0.0 copy-done.2
  40.5 0.0 copy-done
  40.5 0.0 copy-done.6
  40.5 0.0 copy-done.7
  40.6 0.0 copy-start.1
  40.6 3.0 %weight_grad.1 = (bf16[200,512]{1,0:T(8,128)(2,1)}, bf16[32,4,3328]{2,1,0:T(4,128)(2,1)}) custom-call(s32[32]{0:T(128)S(1)} %copy-done.4, s32[32]{0:T(128)S(1)} %copy-done.3, s32[32]{0:T(128)S(1)} %copy-done.5, s32[16]{0:T(128)S(1)} %copy-done.7, bf16[2048,512]{1,0:T(8,128)(2,1)S(1)} %copy-done, bf16[200,384]{1,0:T(8,128)(2,1)S(1)} %copy-done.2, ...), custom_call_target="tpu_custom_call" | custom-call | tf_op jit(solution)/shard_map/weight_grad/pallas_call | solution.py:299
  43.6 3.9 %all-to-all-start.2 = ((bf16[32,4,3328]{2,1,0:T(4,128)(2,1)}), bf16[32,4,3328]{2,1,0:T(4,128)(2,1)S(1)}, u32[]{:S(2)}, u32[]{:S(2)}) async-start(bf16[32,4,3328]{2,1,0:T(4,128)(2,1)} %get-tuple-element.38), calls=%async_computation.2 | async-start | bytes 1703936 | tf_op jit(solution)/shard_map/all_to_all | solution.py:315
  47.5 0.0 copy-done.1
  47.5 3.2 %input_grad.1 = (bf16[1024,512]{1,0:T(8,128)(2,1)S(1)}, bf16[1024,512]{1,0:T(8,128)(2,1)S(1)}, bf16[200,384]{1,0:T(8,128)(2,1)}) custom-call(s32[32]{0:T(128)S(1)} %copy-done.4, s32[32]{0:T(128)S(1)} %copy-done.3, s32[32]{0:T(128)S(1)} %copy-done.5, bf16[200,2048]{1,0:T(8,128)(2,1)S(1)} %copy-done.1, bf16[256,256]{1,0:T(8,128)(2,1)S(1)} %bitcast.8, ...), custom_call_target="tpu_custom_call" | custom-call | tf_op jit(solution)/shard_map/input_grad/pallas_call | solution.py:299
  50.7 5.1 %collective-permute-start = (bf16[1024,512]{1,0:T(8,128)(2,1)S(1)}, bf16[1024,512]{1,0:T(8,128)(2,1)S(1)}, u32[]{:S(2)}, u32[]{:S(2)}) collective-permute-start(bf16[1024,512]{1,0:T(8,128)(2,1)S(1)} %get-tuple-element.31), channel_id=1, source_target_pairs={{0,1},{1,0},{2,3},{3,2},{4,5},{5,4},{6,7},{7,6},{8,9},{9,8},{10,11... | collective-permute-start | bytes 3145736 | tf_op jit(solution)/shard_map/ppermute | solution.py:319
  55.9 2.3 %collective-permute-done.refs_1_ = bf16[1024,512]{1,0:T(8,128)(2,1)S(1)} collective-permute-done((bf16[1024,512]{1,0:T(8,128)(2,1)S(1)}, bf16[1024,512]{1,0:T(8,128)(2,1)S(1)}, u32[]{:S(2)}, u32[]{:S(2)}) %collective-permute-start) | collective-permute-done | bytes 1048608 | tf_op jit(solution)/shard_map/ppermute | solution.py:319
  58.1 0.2 add.3
  58.4 5.1 %collective-permute-start.1 = (bf16[384,512]{1,0:T(8,128)(2,1)S(1)}, bf16[384,512]{1,0:T(8,128)(2,1)S(1)}, u32[]{:S(2)}, u32[]{:S(2)}) collective-permute-start(bf16[384,512]{1,0:T(8,128)(2,1)S(1)} %get-tuple-element.33), channel_id=1, source_target_pairs={{0,14},{2,0},{4,2},{6,4},{8,6},{10,8},{12,10},{14,12},{1,15},{3,1}... | collective-permute-start | bytes 1179656 | tf_op jit(solution)/shard_map/ppermute | solution.py:319
  63.5 1.9 %collective-permute-start.2 = (bf16[256,512]{1,0:T(8,128)(2,1)S(1)}, bf16[256,512]{1,0:T(8,128)(2,1)S(1)}, u32[]{:S(2)}, u32[]{:S(2)}) collective-permute-start(bf16[256,512]{1,0:T(8,128)(2,1)S(1)} %get-tuple-element.34), channel_id=1, source_target_pairs={{0,2},{2,4},{4,6},{6,8},{8,10},{10,12},{12,14},{14,0},{1,3},{3,5},... | collective-permute-start | bytes 786440 | tf_op jit(solution)/shard_map/ppermute | solution.py:319
  65.4 8.4 %collective-permute-done.2.refs_2_ = bf16[256,512]{1,0:T(8,128)(2,1)S(1)} collective-permute-done((bf16[256,512]{1,0:T(8,128)(2,1)S(1)}, bf16[256,512]{1,0:T(8,128)(2,1)S(1)}, u32[]{:S(2)}, u32[]{:S(2)}) %collective-permute-start.2) | collective-permute-done | bytes 262176 | tf_op jit(solution)/shard_map/ppermute | solution.py:319
  73.8 0.0 collective-permute-done.1.refs_1_
  73.8 0.1 add.4
  73.9 0.0 all-to-all-done.2.pieces_ref
  73.9 0.7 slots.1
  74.6 27.1 %all_to_all.27.owned_ref = bf16[128,4,200]{2,1,0:T(4,128)(2,1)S(1)} all-to-all(bf16[128,4,200]{2,1,0:T(4,128)(2,1)S(1)} %get-tuple-element.40), channel_id=1, replica_groups=mesh['z'=8,'x'=4,'y'=8,'c'=2] {'z','y','c'}, dimensions={0} | all-to-all | bytes 409600 | tf_op jit(solution)/shard_map/all_to_all | solution.py:315
  101.7 1.2 join.1
  102.9 4.0 %all-to-all-start.4 = ((bf16[4,32,3200]{2,1,0:T(8,128)(2,1)}), bf16[4,32,3200]{2,1,0:T(8,128)(2,1)S(1)}, u32[]{:S(2)}, u32[]{:S(2)}) async-start(bf16[4,32,3200]{2,1,0:T(8,128)(2,1)} %join.1), calls=%async_computation.4 | async-start | bytes 1638400 | tf_op jit(solution)/shard_map/all_to_all | solution.py:315
  106.9 3.2 %collective-permute-start.3 = (bf16[128,512]{1,0:T(8,128)(2,1)S(1)}, bf16[128,512]{1,0:T(8,128)(2,1)S(1)}, u32[]{:S(2)}, u32[]{:S(2)}) collective-permute-start(bf16[128,512]{1,0:T(8,128)(2,1)S(1)} %get-tuple-element.36), channel_id=1, source_target_pairs={{0,10},{2,12},{4,14},{6,0},{8,2},{10,4},{12,6},{14,8},{1,11},{3,13... | collective-permute-start | bytes 393224 | tf_op jit(solution)/shard_map/ppermute | solution.py:319
  110.1 3.9 %collective-permute-start.4 = (bf16[128,512]{1,0:T(8,128)(2,1)S(1)}, bf16[128,512]{1,0:T(8,128)(2,1)S(1)}, u32[]{:S(2)}, u32[]{:S(2)}) collective-permute-start(bf16[128,512]{1,0:T(8,128)(2,1)S(1)} %get-tuple-element.37), channel_id=1, source_target_pairs={{0,6},{2,8},{4,10},{6,12},{8,14},{10,0},{12,2},{14,4},{1,7},{3,9},... | collective-permute-start | bytes 393224 | tf_op jit(solution)/shard_map/ppermute | solution.py:319
  114.0 5.0 %all-to-all-done.4 = bf16[4,32,3200]{2,1,0:T(8,128)(2,1)S(1)} async-done(((bf16[4,32,3200]{2,1,0:T(8,128)(2,1)}), bf16[4,32,3200]{2,1,0:T(8,128)(2,1)S(1)}, u32[]{:S(2)}, u32[]{:S(2)}) %all-to-all-start.4) | async-done | bytes 819232 | tf_op jit(solution)/shard_map/all_to_all | solution.py:315
  119.0 4.4 %ortho.1 = bf16[3200,128]{1,0:T(8,128)(2,1)} custom-call(bf16[128,3200]{1,0:T(8,128)(2,1)S(1)} %bitcast.6), custom_call_target="tpu_custom_call" | custom-call | tf_op jit(solution)/shard_map/ortho/pallas_call | solution.py:299
  123.3 0.0 collective-permute-done.3.refs_1_
  123.3 1.6 %collective-permute-done.4.refs_2_ = bf16[128,512]{1,0:T(8,128)(2,1)S(1)} collective-permute-done((bf16[128,512]{1,0:T(8,128)(2,1)S(1)}, bf16[128,512]{1,0:T(8,128)(2,1)S(1)}, u32[]{:S(2)}, u32[]{:S(2)}) %collective-permute-start.4) | collective-permute-done | bytes 131104 | tf_op jit(solution)/shard_map/ppermute | solution.py:319
  124.9 0.7 add.5
Async XLA Ops:
  0.6 26.6 %copy-start.3 = (s32[32]{0:T(128)S(1)}, s32[32]{0:T(128)}, u32[]{:S(2)}) copy-start(s32[32]{0:T(128)} %partner_ref.5) | copy-start | bytes 388
  0.6 39.9 %copy-start.5 = (s32[32]{0:T(128)S(1)}, s32[32]{0:T(128)}, u32[]{:S(2)}) copy-start(s32[32]{0:T(128)} %moved_ref.3) | copy-start | bytes 388
  0.7 39.9 %copy-start.4 = (s32[32]{0:T(128)S(1)}, s32[32]{0:T(128)}, u32[]{:S(2)}) copy-start(s32[32]{0:T(128)} %frames_ref.3) | copy-start | bytes 388
  0.7 39.9 %copy-start.2 = (bf16[200,384]{1,0:T(8,128)(2,1)S(1)}, bf16[200,384]{1,0:T(8,128)(2,1)}, u32[]{:S(2)}) copy-start(bf16[200,384]{1,0:T(8,128)(2,1)} %grad_ref.1) | copy-start | bytes 460804
  0.7 39.9 %copy-start = (bf16[2048,512]{1,0:T(8,128)(2,1)S(1)}, bf16[2048,512]{1,0:T(8,128)(2,1)}, u32[]{:S(2)}) copy-start(bf16[2048,512]{1,0:T(8,128)(2,1)} %attended_ref.1) | copy-start | bytes 6291460
  0.7 39.9 %copy-start.6 = (f32[200]{0:T(256)S(1)}, f32[200]{0:T(256)}, u32[]{:S(2)}) copy-start(f32[200]{0:T(256)} %param.13) | copy-start | bytes 2404
  0.7 39.9 %copy-start.7 = (s32[16]{0:T(128)S(1)}, s32[16]{0:T(128)}, u32[]{:S(2)}) copy-start(s32[16]{0:T(128)} %slot_ref.1) | copy-start | bytes 196
  40.6 6.9 %copy-start.1 = (bf16[200,2048]{1,0:T(8,128)(2,1)S(1)}, bf16[200,2048]{1,0:T(8,128)(2,1)}, u32[]{:S(2)}) copy-start(bf16[200,2048]{1,0:T(8,128)(2,1)} %weight_ref.1) | copy-start | bytes 2457604
  43.6 30.4 %all-to-all-start.2 = ((bf16[32,4,3328]{2,1,0:T(4,128)(2,1)}), bf16[32,4,3328]{2,1,0:T(4,128)(2,1)S(1)}, u32[]{:S(2)}, u32[]{:S(2)}) async-start(bf16[32,4,3328]{2,1,0:T(4,128)(2,1)} %get-tuple-element.38), calls=%async_computation.2 | async-start | bytes 1703936 | tf_op jit(solution)/shard_map/all_to_all | solution.py:315
  50.7 7.4 %collective-permute-start = (bf16[1024,512]{1,0:T(8,128)(2,1)S(1)}, bf16[1024,512]{1,0:T(8,128)(2,1)S(1)}, u32[]{:S(2)}, u32[]{:S(2)}) collective-permute-start(bf16[1024,512]{1,0:T(8,128)(2,1)S(1)} %get-tuple-element.31), channel_id=1, source_target_pairs={{0,1},{1,0},{2,3},{3,2},{4,5},{5,4},{6,7},{7,6},{8,9},{9,8},{10,11... | collective-permute-start | bytes 3145736 | tf_op jit(solution)/shard_map/ppermute | solution.py:319
  58.4 15.4 %collective-permute-start.1 = (bf16[384,512]{1,0:T(8,128)(2,1)S(1)}, bf16[384,512]{1,0:T(8,128)(2,1)S(1)}, u32[]{:S(2)}, u32[]{:S(2)}) collective-permute-start(bf16[384,512]{1,0:T(8,128)(2,1)S(1)} %get-tuple-element.33), channel_id=1, source_target_pairs={{0,14},{2,0},{4,2},{6,4},{8,6},{10,8},{12,10},{14,12},{1,15},{3,1}... | collective-permute-start | bytes 1179656 | tf_op jit(solution)/shard_map/ppermute | solution.py:319
  63.5 10.3 %collective-permute-start.2 = (bf16[256,512]{1,0:T(8,128)(2,1)S(1)}, bf16[256,512]{1,0:T(8,128)(2,1)S(1)}, u32[]{:S(2)}, u32[]{:S(2)}) collective-permute-start(bf16[256,512]{1,0:T(8,128)(2,1)S(1)} %get-tuple-element.34), channel_id=1, source_target_pairs={{0,2},{2,4},{4,6},{6,8},{8,10},{10,12},{12,14},{14,0},{1,3},{3,5},... | collective-permute-start | bytes 786440 | tf_op jit(solution)/shard_map/ppermute | solution.py:319
  102.9 16.1 %all-to-all-start.4 = ((bf16[4,32,3200]{2,1,0:T(8,128)(2,1)}), bf16[4,32,3200]{2,1,0:T(8,128)(2,1)S(1)}, u32[]{:S(2)}, u32[]{:S(2)}) async-start(bf16[4,32,3200]{2,1,0:T(8,128)(2,1)} %join.1), calls=%async_computation.4 | async-start | bytes 1638400 | tf_op jit(solution)/shard_map/all_to_all | solution.py:315
  106.9 16.4 %collective-permute-start.3 = (bf16[128,512]{1,0:T(8,128)(2,1)S(1)}, bf16[128,512]{1,0:T(8,128)(2,1)S(1)}, u32[]{:S(2)}, u32[]{:S(2)}) collective-permute-start(bf16[128,512]{1,0:T(8,128)(2,1)S(1)} %get-tuple-element.36), channel_id=1, source_target_pairs={{0,10},{2,12},{4,14},{6,0},{8,2},{10,4},{12,6},{14,8},{1,11},{3,13... | collective-permute-start | bytes 393224 | tf_op jit(solution)/shard_map/ppermute | solution.py:319
  110.1 14.9 %collective-permute-start.4 = (bf16[128,512]{1,0:T(8,128)(2,1)S(1)}, bf16[128,512]{1,0:T(8,128)(2,1)S(1)}, u32[]{:S(2)}, u32[]{:S(2)}) collective-permute-start(bf16[128,512]{1,0:T(8,128)(2,1)S(1)} %get-tuple-element.37), channel_id=1, source_target_pairs={{0,6},{2,8},{4,10},{6,12},{8,14},{10,0},{12,2},{14,4},{1,7},{3,9},... | collective-permute-start | bytes 393224 | tf_op jit(solution)/shard_map/ppermute | solution.py:319

commit v10 on v7

--- a/solution.py
+++ b/solution.py
@@ -243,14 +243,13 @@
     wait(copies)
 
 
-def join_kernel(owned_ref, copies_hbm, joined, whole, sems):
+def join_kernel(owned_ref, whole_ref, joined):
     for z in range(NZ):
         for block in range(N_FSDP):
             joined[pl.ds(z * SHARE, SHARE), pl.ds(block * ROWS, ROWS)] = owned_ref[
                 z * N_FSDP + block
             ].astype(f32)
-    whole[...] = joined[...].astype(bf16)
-    wait(start(sems, *[(whole, copies_hbm.at[x]) for x in range(NX)]))
+    whole_ref[...] = joined[...].astype(bf16)
 
 
 def split(values):
@@ -404,10 +403,10 @@
     others = [crossed(other, "y", NY, step) for other, step in zip(others, (4, 2, 6))]
     (copies,) = call(
         join_kernel, "join", [V], (owned,),
-        [((NX, BY_X, D), bf16, H)],
-        [V((BY_X, D), f32), V((BY_X, D), bf16), dma((NX,))],
-    )
-    whole = exchange(copies, "x").reshape(HD, D)
+        [((BY_X, D), bf16, V)],
+        [V((BY_X, D), f32)],
+    )
+    whole = lax.all_gather(copies, "x", axis=0, tiled=True)
     (ortho_update,) = call(
         ortho_kernel, "ortho", [V], (whole,), [((D, HD), bf16, H)],
         [V((D, HD), bf16), dma((PARTS,))],

time: 123 us -> 119 us (0.967)
  waiting for transfers between devices: 24.8 us -> 12.4 us
  blocking collectives: 35.5 us -> 47.3 us
  starting transfers between devices: 42.5 us -> 38.9 us
    all_to_all x3 -> x2, waiting for transfers between devices: 22.1 us -> 10.1 us  [exchange(): return lax.all_to_all(pieces, axes, split_axis=0, concat_axis=0, tiled=True)]
    all_gather x0 -> x1, blocking collectives: none -> 11.8 us  [body(): whole = lax.all_gather(copies, 'x', axis=0, tiled=True)]
    all_to_all x3 -> x2, starting transfers between devices: 22.7 us -> 19.1 us  [exchange(): return lax.all_to_all(pieces, axes, split_axis=0, concat_axis=0, tiled=True)]
  transfers between devices with their start and end apart: 8 -> 7, of which waited for: 5 -> 3; matrix products, arithmetic and copies ran while one was open for 0% -> 0% of each run, Pallas kernels for 8% -> 8%
where the time goes in v10:
time: 119 us; the launch traced here: 117 us
  blocking collectives  47.3 us (40%)
  starting transfers between devices  38.9 us (33%)
  Pallas kernels  17.6 us (15%)
  waiting for transfers between devices  12.4 us (10%)
    all_to_all x2, blocking collectives, exchange(): return lax.all_to_all(pieces, axes, split_axis=0, concat_axis=0, tiled=True)  35.5 us
    ppermute x5, starting transfers between devices, crossed(): return lax.ppermute(array, axis, [(i, i ^ bit) for i in range(size)])  19.8 us
    all_to_all x2, starting transfers between devices, exchange(): return lax.all_to_all(pieces, axes, split_axis=0, concat_axis=0, tiled=True)  19.1 us
    pallas_call x10, Pallas kernels, call(): pl.pallas_call(kernel, out_shape=[H(shape, dtype) if place is H else jax....  17.6 us
    all_gather x1, blocking collectives, body(): whole = lax.all_gather(copies, 'x', axis=0, tiled=True)  11.8 us
    all_to_all x2, waiting for transfers between devices, exchange(): return lax.all_to_all(pieces, axes, split_axis=0, concat_axis=0, tiled=True)  10.1 us
  transfers between devices with their start and end apart: 7, of which 3 were waited for; matrix products, arithmetic and copies ran while one was open for 0% of the time, Pallas kernels for 8%

profile of v10, /device:TPU:1, one launch (start us, length us, event | category | flops | bytes accessed | tf_op | source)
XLA Modules:
  0.0 117.2 jit_solution(14385453850229361349)
XLA Ops:
  0.6 0.0 copy-start.3
  0.6 0.0 copy-start.5
  0.7 0.0 copy-start.4
  0.7 0.0 copy-start.2
  0.7 0.0 copy-start
  0.7 0.0 copy-start.6
  0.7 0.0 copy-start.7
  0.7 3.6 %project.1 = (f32[200,512]{1,0:T(8,128)}, bf16[200,512]{1,0:T(8,128)(2,1)}, bf16[256,256]{1,0:T(8,128)(2,1)S(1)}) custom-call(s32[32]{0:T(128)} %frames_ref.3, s32[32]{0:T(128)} %partner_ref.5, s32[32]{0:T(128)} %moved_ref.3, bf16[2048,512]{1,0:T(8,128)(2,1)} %attended_ref.1, bf16[200,512]{1,0:T(8,128)(2,1)} %residual_hbm.1, bf16[200,384]{1,0:T(8,128)(2,1)} %grad_ref.1, ...), custom_call_target="tpu_custom_call" | custom-call | tf_op jit(solution)/shard_map/project/pallas_call | solution.py:301
  4.3 22.9 %all_to_all.20.pieces_ref = bf16[32,8,256]{2,1,0:T(8,128)(2,1)S(1)} all-to-all(bf16[32,8,256]{2,1,0:T(8,128)(2,1)S(1)} %bitcast.7), channel_id=1, replica_groups=mesh['z'=8,'x'=4,'y'=8,'c'=2] {'z','x'}, dimensions={0} | all-to-all | bytes 262144 | tf_op jit(solution)/shard_map/all_to_all | solution.py:317
  27.2 0.0 copy-done.3
  27.2 0.6 forward.1
  27.8 12.6 %all_to_all.21 = bf16[32,8,256]{2,1,0:T(8,128)(2,1)S(1)} all-to-all(bf16[32,8,256]{2,1,0:T(8,128)(2,1)S(1)} %forward.1), channel_id=1, replica_groups=mesh['z'=8,'x'=4,'y'=8,'c'=2] {'z','x'}, dimensions={0} | all-to-all | bytes 262144 | tf_op jit(solution)/shard_map/all_to_all | solution.py:317
  40.4 0.0 copy-done.5
  40.4 0.0 copy-done.4
  40.4 0.0 copy-done.2
  40.4 0.0 copy-done
  40.4 0.0 copy-done.6
  40.4 0.0 copy-done.7
  40.5 0.0 copy-start.1
  40.5 3.0 %weight_grad.1 = (bf16[200,512]{1,0:T(8,128)(2,1)}, bf16[32,4,3328]{2,1,0:T(4,128)(2,1)}) custom-call(s32[32]{0:T(128)S(1)} %copy-done.4, s32[32]{0:T(128)S(1)} %copy-done.3, s32[32]{0:T(128)S(1)} %copy-done.5, s32[16]{0:T(128)S(1)} %copy-done.7, bf16[2048,512]{1,0:T(8,128)(2,1)S(1)} %copy-done, bf16[200,384]{1,0:T(8,128)(2,1)S(1)} %copy-done.2, ...), custom_call_target="tpu_custom_call" | custom-call | tf_op jit(solution)/shard_map/weight_grad/pallas_call | solution.py:301
  43.5 3.9 %all-to-all-start.2 = ((bf16[32,4,3328]{2,1,0:T(4,128)(2,1)}), bf16[32,4,3328]{2,1,0:T(4,128)(2,1)S(1)}, u32[]{:S(2)}, u32[]{:S(2)}) async-start(bf16[32,4,3328]{2,1,0:T(4,128)(2,1)} %get-tuple-element.40), calls=%async_computation.2 | async-start | bytes 1703936 | tf_op jit(solution)/shard_map/all_to_all | solution.py:317
  47.4 0.0 copy-done.1
  47.4 3.2 %input_grad.1 = (bf16[1024,512]{1,0:T(8,128)(2,1)S(1)}, bf16[1024,512]{1,0:T(8,128)(2,1)S(1)}, bf16[200,384]{1,0:T(8,128)(2,1)}) custom-call(s32[32]{0:T(128)S(1)} %copy-done.4, s32[32]{0:T(128)S(1)} %copy-done.3, s32[32]{0:T(128)S(1)} %copy-done.5, bf16[200,2048]{1,0:T(8,128)(2,1)S(1)} %copy-done.1, bf16[256,256]{1,0:T(8,128)(2,1)S(1)} %bitcast.6, ...), custom_call_target="tpu_custom_call" | custom-call | tf_op jit(solution)/shard_map/input_grad/pallas_call | solution.py:301
  50.6 5.2 %collective-permute-start = (bf16[1024,512]{1,0:T(8,128)(2,1)S(1)}, bf16[1024,512]{1,0:T(8,128)(2,1)S(1)}, u32[]{:S(2)}, u32[]{:S(2)}) collective-permute-start(bf16[1024,512]{1,0:T(8,128)(2,1)S(1)} %get-tuple-element.33), channel_id=1, source_target_pairs={{0,1},{1,0},{2,3},{3,2},{4,5},{5,4},{6,7},{7,6},{8,9},{9,8},{10,11... | collective-permute-start | bytes 3145736 | tf_op jit(solution)/shard_map/ppermute | solution.py:321
  55.9 2.3 %collective-permute-done.refs_1_ = bf16[1024,512]{1,0:T(8,128)(2,1)S(1)} collective-permute-done((bf16[1024,512]{1,0:T(8,128)(2,1)S(1)}, bf16[1024,512]{1,0:T(8,128)(2,1)S(1)}, u32[]{:S(2)}, u32[]{:S(2)}) %collective-permute-start) | collective-permute-done | bytes 1048608 | tf_op jit(solution)/shard_map/ppermute | solution.py:321
  58.2 0.2 add.3
  58.4 3.2 %collective-permute-start.1 = (bf16[512,512]{1,0:T(8,128)(2,1)S(1)}, bf16[512,512]{1,0:T(8,128)(2,1)S(1)}, u32[]{:S(2)}, u32[]{:S(2)}) collective-permute-start(bf16[512,512]{1,0:T(8,128)(2,1)S(1)} %get-tuple-element.35), channel_id=1, source_target_pairs={{0,2},{2,0},{4,6},{6,4},{8,10},{10,8},{12,14},{14,12},{1,3},{3,1},... | collective-permute-start | bytes 1572872 | tf_op jit(solution)/shard_map/ppermute | solution.py:321
  61.6 6.1 %all-to-all-done.2.pieces_ref = bf16[32,4,3328]{2,1,0:T(4,128)(2,1)S(1)} async-done(((bf16[32,4,3328]{2,1,0:T(4,128)(2,1)}), bf16[32,4,3328]{2,1,0:T(4,128)(2,1)S(1)}, u32[]{:S(2)}, u32[]{:S(2)}) %all-to-all-start.2) | async-done | bytes 852000 | tf_op jit(solution)/shard_map/all_to_all | solution.py:317
  67.6 1.5 %slots.1 = (bf16[128,4,200]{2,1,0:T(4,128)(2,1)}, f32[1,200]{1,0:T(1,128)}) custom-call(bf16[32,4,3328]{2,1,0:T(4,128)(2,1)S(1)} %all-to-all-done.2.pieces_ref), custom_call_target="tpu_custom_call" | custom-call | tf_op jit(solution)/shard_map/slots/pallas_call | solution.py:301
  69.2 15.2 %all-to-all-start.3 = ((bf16[128,4,200]{2,1,0:T(4,128)(2,1)}), bf16[128,4,200]{2,1,0:T(4,128)(2,1)S(1)}, u32[]{:S(2)}, u32[]{:S(2)}) async-start(bf16[128,4,200]{2,1,0:T(4,128)(2,1)} %get-tuple-element.42), calls=%async_computation.3 | async-start | bytes 524288 | tf_op jit(solution)/shard_map/all_to_all | solution.py:317
  84.4 0.0 collective-permute-done.1.refs_1_
  84.4 0.1 add.4
  84.6 7.2 %collective-permute-start.2 = (bf16[128,512]{1,0:T(8,128)(2,1)S(1)}, bf16[128,512]{1,0:T(8,128)(2,1)S(1)}, u32[]{:S(2)}, u32[]{:S(2)}) collective-permute-start(bf16[128,512]{1,0:T(8,128)(2,1)S(1)} %get-tuple-element.37), channel_id=1, source_target_pairs={{0,8},{2,10},{4,12},{6,14},{8,0},{10,2},{12,4},{14,6},{1,9},{3,11}... | collective-permute-start | bytes 393224 | tf_op jit(solution)/shard_map/ppermute | solution.py:321
  91.8 2.2 %collective-permute-start.3 = (bf16[128,512]{1,0:T(8,128)(2,1)S(1)}, bf16[128,512]{1,0:T(8,128)(2,1)S(1)}, u32[]{:S(2)}, u32[]{:S(2)}) collective-permute-start(bf16[128,512]{1,0:T(8,128)(2,1)S(1)} %get-tuple-element.38), channel_id=1, source_target_pairs={{0,4},{2,6},{4,0},{6,2},{8,12},{10,14},{12,8},{14,10},{1,5},{3,7},... | collective-permute-start | bytes 393224 | tf_op jit(solution)/shard_map/ppermute | solution.py:321
  94.0 2.0 %collective-permute-start.4 = (bf16[128,512]{1,0:T(8,128)(2,1)S(1)}, bf16[128,512]{1,0:T(8,128)(2,1)S(1)}, u32[]{:S(2)}, u32[]{:S(2)}) collective-permute-start(bf16[128,512]{1,0:T(8,128)(2,1)S(1)} %get-tuple-element.39), channel_id=1, source_target_pairs={{0,12},{2,14},{4,8},{6,10},{8,4},{10,6},{12,0},{14,2},{1,13},{3,15... | collective-permute-start | bytes 393224 | tf_op jit(solution)/shard_map/ppermute | solution.py:321
  96.0 4.1 %all-to-all-done.3.owned_ref = bf16[128,4,200]{2,1,0:T(4,128)(2,1)S(1)} async-done(((bf16[128,4,200]{2,1,0:T(4,128)(2,1)}), bf16[128,4,200]{2,1,0:T(4,128)(2,1)S(1)}, u32[]{:S(2)}, u32[]{:S(2)}) %all-to-all-start.3) | async-done | bytes 204832 | tf_op jit(solution)/shard_map/all_to_all | solution.py:317
  100.0 0.2 join.1
  100.3 11.8 %all_gather.3.grad_ref = bf16[128,3200]{1,0:T(8,128)(2,1)S(1)} all-gather(bf16[32,3200]{1,0:T(8,128)(2,1)S(1)} %join.1), channel_id=1, replica_groups=mesh['z'=8,'x'=4,'y'=8,'c'=2] {'x'}, dimensions={0}, use_global_device_ids=true | all-gather | bytes 1024000 | tf_op jit(solution)/shard_map/all_gather | solution.py:409
  112.1 4.4 %ortho.1 = bf16[3200,128]{1,0:T(8,128)(2,1)} custom-call(bf16[128,3200]{1,0:T(8,128)(2,1)S(1)} %all_gather.3.grad_ref), custom_call_target="tpu_custom_call" | custom-call | tf_op jit(solution)/shard_map/ortho/pallas_call | solution.py:301
  116.5 0.0 collective-permute-done.2.refs_1_
  116.5 0.0 collective-permute-done.3.refs_2_
  116.5 0.0 collective-permute-done.4.refs_3_
  116.5 0.7 add.5
Async XLA Ops:
  0.6 26.6 %copy-start.3 = (s32[32]{0:T(128)S(1)}, s32[32]{0:T(128)}, u32[]{:S(2)}) copy-start(s32[32]{0:T(128)} %partner_ref.5) | copy-start | bytes 388
  0.6 39.8 %copy-start.5 = (s32[32]{0:T(128)S(1)}, s32[32]{0:T(128)}, u32[]{:S(2)}) copy-start(s32[32]{0:T(128)} %moved_ref.3) | copy-start | bytes 388
  0.7 39.8 %copy-start.4 = (s32[32]{0:T(128)S(1)}, s32[32]{0:T(128)}, u32[]{:S(2)}) copy-start(s32[32]{0:T(128)} %frames_ref.3) | copy-start | bytes 388
  0.7 39.8 %copy-start.2 = (bf16[200,384]{1,0:T(8,128)(2,1)S(1)}, bf16[200,384]{1,0:T(8,128)(2,1)}, u32[]{:S(2)}) copy-start(bf16[200,384]{1,0:T(8,128)(2,1)} %grad_ref.1) | copy-start | bytes 460804
  0.7 39.8 %copy-start = (bf16[2048,512]{1,0:T(8,128)(2,1)S(1)}, bf16[2048,512]{1,0:T(8,128)(2,1)}, u32[]{:S(2)}) copy-start(bf16[2048,512]{1,0:T(8,128)(2,1)} %attended_ref.1) | copy-start | bytes 6291460
  0.7 39.8 %copy-start.6 = (f32[200]{0:T(256)S(1)}, f32[200]{0:T(256)}, u32[]{:S(2)}) copy-start(f32[200]{0:T(256)} %param.13) | copy-start | bytes 2404
  0.7 39.8 %copy-start.7 = (s32[16]{0:T(128)S(1)}, s32[16]{0:T(128)}, u32[]{:S(2)}) copy-start(s32[16]{0:T(128)} %slot_ref.1) | copy-start | bytes 196
  40.5 6.9 %copy-start.1 = (bf16[200,2048]{1,0:T(8,128)(2,1)S(1)}, bf16[200,2048]{1,0:T(8,128)(2,1)}, u32[]{:S(2)}) copy-start(bf16[200,2048]{1,0:T(8,128)(2,1)} %weight_ref.1) | copy-start | bytes 2457604
  43.5 24.2 %all-to-all-start.2 = ((bf16[32,4,3328]{2,1,0:T(4,128)(2,1)}), bf16[32,4,3328]{2,1,0:T(4,128)(2,1)S(1)}, u32[]{:S(2)}, u32[]{:S(2)}) async-start(bf16[32,4,3328]{2,1,0:T(4,128)(2,1)} %get-tuple-element.40), calls=%async_computation.2 | async-start | bytes 1703936 | tf_op jit(solution)/shard_map/all_to_all | solution.py:317
  50.6 7.5 %collective-permute-start = (bf16[1024,512]{1,0:T(8,128)(2,1)S(1)}, bf16[1024,512]{1,0:T(8,128)(2,1)S(1)}, u32[]{:S(2)}, u32[]{:S(2)}) collective-permute-start(bf16[1024,512]{1,0:T(8,128)(2,1)S(1)} %get-tuple-element.33), channel_id=1, source_target_pairs={{0,1},{1,0},{2,3},{3,2},{4,5},{5,4},{6,7},{7,6},{8,9},{9,8},{10,11... | collective-permute-start | bytes 3145736 | tf_op jit(solution)/shard_map/ppermute | solution.py:321
  58.4 26.0 %collective-permute-start.1 = (bf16[512,512]{1,0:T(8,128)(2,1)S(1)}, bf16[512,512]{1,0:T(8,128)(2,1)S(1)}, u32[]{:S(2)}, u32[]{:S(2)}) collective-permute-start(bf16[512,512]{1,0:T(8,128)(2,1)S(1)} %get-tuple-element.35), channel_id=1, source_target_pairs={{0,2},{2,0},{4,6},{6,4},{8,10},{10,8},{12,14},{14,12},{1,3},{3,1},... | collective-permute-start | bytes 1572872 | tf_op jit(solution)/shard_map/ppermute | solution.py:321
  69.2 30.8 %all-to-all-start.3 = ((bf16[128,4,200]{2,1,0:T(4,128)(2,1)}), bf16[128,4,200]{2,1,0:T(4,128)(2,1)S(1)}, u32[]{:S(2)}, u32[]{:S(2)}) async-start(bf16[128,4,200]{2,1,0:T(4,128)(2,1)} %get-tuple-element.42), calls=%async_computation.3 | async-start | bytes 524288 | tf_op jit(solution)/shard_map/all_to_all | solution.py:317
  84.6 31.9 %collective-permute-start.2 = (bf16[128,512]{1,0:T(8,128)(2,1)S(1)}, bf16[128,512]{1,0:T(8,128)(2,1)S(1)}, u32[]{:S(2)}, u32[]{:S(2)}) collective-permute-start(bf16[128,512]{1,0:T(8,128)(2,1)S(1)} %get-tuple-element.37), channel_id=1, source_target_pairs={{0,8},{2,10},{4,12},{6,14},{8,0},{10,2},{12,4},{14,6},{1,9},{3,11}... | collective-permute-start | bytes 393224 | tf_op jit(solution)/shard_map/ppermute | solution.py:321
  91.8 24.7 %collective-permute-start.3 = (bf16[128,512]{1,0:T(8,128)(2,1)S(1)}, bf16[128,512]{1,0:T(8,128)(2,1)S(1)}, u32[]{:S(2)}, u32[]{:S(2)}) collective-permute-start(bf16[128,512]{1,0:T(8,128)(2,1)S(1)} %get-tuple-element.38), channel_id=1, source_target_pairs={{0,4},{2,6},{4,0},{6,2},{8,12},{10,14},{12,8},{14,10},{1,5},{3,7},... | collective-permute-start | bytes 393224 | tf_op jit(solution)/shard_map/ppermute | solution.py:321
  94.0 22.5 %collective-permute-start.4 = (bf16[128,512]{1,0:T(8,128)(2,1)S(1)}, bf16[128,512]{1,0:T(8,128)(2,1)S(1)}, u32[]{:S(2)}, u32[]{:S(2)}) collective-permute-start(bf16[128,512]{1,0:T(8,128)(2,1)S(1)} %get-tuple-element.39), channel_id=1, source_target_pairs={{0,12},{2,14},{4,8},{6,10},{8,4},{10,6},{12,0},{14,2},{1,13},{3,15... | collective-permute-start | bytes 393224 | tf_op jit(solution)/shard_map/ppermute | solution.py:321

commit v11 on v10

--- a/solution.py
+++ b/solution.py
@@ -97,12 +97,12 @@
 def project_kernel(
     frames_hbm, partner_hbm, moved_hbm,
     attended_hbm, residual_hbm, grad_hbm, weight_hbm, scale_hbm,
-    projected_hbm, layer_hbm, window_ref,
+    window_ref,
     frames_ref, partner_ref, moved_ref,
     attended_ref, residual_ref, grad_ref, weight_ref, scale_ref,
-    projected_ref, layer_ref,
-    small_sems, attended_sems, weight_sems, out_sems,
+    small_sems, attended_sems, weight_sems,
 ):
+    late = pl.ds(CAP_ROWS - MOVE_ROWS, MOVE_ROWS)
     small = start(
         small_sems,
         (frames_hbm, frames_ref),
@@ -110,11 +110,11 @@
         (moved_hbm, moved_ref),
         (scale_hbm, scale_ref),
         (grad_hbm, grad_ref),
-        (residual_hbm, residual_ref),
+        (residual_hbm.at[:, late], residual_ref),
     )
     cuts = [pl.ds(first, CHUNK) for first in range(0, A, CHUNK)]
     attended = start(
-        attended_sems, *[(attended_hbm.at[cut, :], attended_ref.at[cut, :]) for cut in cuts]
+        attended_sems, *[(attended_hbm.at[cut, late], attended_ref.at[cut, :]) for cut in cuts]
     )
     weight = start(
         weight_sems, *[(weight_hbm.at[:, cut], weight_ref.at[:, cut]) for cut in cuts]
@@ -132,15 +132,10 @@
         weight[index].wait()
         part = dot(weight_ref[:, cut], attended_ref[cut, :])
         projected = part if projected is None else projected + part
-    projected_ref[...] = projected
-    out = start(out_sems, (projected_ref, projected_hbm))
     small[5].wait()
     layer = (residual_ref[...].astype(f32) + gains * projected).astype(bf16)
-    layer_ref[...] = layer
-    out += start(out_sems.at[pl.ds(1, 1)], (layer_ref, layer_hbm))
-    layer_win = layer[:, MOVE_ROWS:].astype(f32)
+    layer_win = layer.astype(f32)
     window_ref[pl.ds(0, ROWS), :] = jnp.where(holds_two == 1, layer_win, grad_win).astype(bf16)
-    wait(out)
 
 
 def forward_kernel(partner_ref, pieces_ref, out_ref):
@@ -157,11 +152,10 @@
 
 def weight_grad_kernel(
     frames_ref, partner_ref, moved_ref, slot_ref,
-    attended_ref, grad_ref, scale_ref, got_ref, projected_hbm,
+    attended_ref, grad_ref, weight_ref, scale_ref, got_ref,
     scaled_hbm, pieces_hbm,
-    head_of, wide, projected_ref, scaled_ref, pieces_ref, sems,
+    head_of, wide, scaled_ref, pieces_ref, sems,
 ):
-    (fetch,) = start(sems, (projected_hbm, projected_ref))
     kept, incoming, holds_two = my_counts(frames_ref, partner_ref, moved_ref)
     for head in range(HEADS):
         head_of[slot_ref[head]] = head
@@ -186,8 +180,8 @@
                 pl.ds((piece % NX * NZ + piece // NX) * SHARE, SHARE), lanes
             ].astype(bf16), pieces_ref, pieces_hbm, sems.at[pl.ds(2 + slot // 4, 1)])
             done = full
-    fetch.wait()
-    part = jnp.sum(grad * projected_ref[...], axis=1, keepdims=True) * INVERSE_ROOT
+    projected = dot(weight_ref[...], attended_ref[...])
+    part = jnp.sum(grad * projected, axis=1, keepdims=True) * INVERSE_ROOT
     part = to_row(part)
     high = part.astype(bf16).astype(f32)
     low = part - high
@@ -207,11 +201,17 @@
 
 def input_kernel(
     frames_ref, partner_ref, moved_ref,
-    weight_ref, got_ref, scaled_hbm, layer_hbm,
+    weight_ref, scale_ref, got_ref, scaled_hbm, attended_hbm, residual_hbm,
     even_ref, odd_ref, layer_out_ref,
-    scaled_ref, layer_ref, sems,
+    scaled_ref, attended_ref, residual_ref, sems,
 ):
-    fetch = start(sems, (scaled_hbm, scaled_ref), (layer_hbm, layer_ref))
+    balanced = pl.ds(0, BAL_ROWS)
+    fetch = start(
+        sems,
+        (scaled_hbm, scaled_ref),
+        (residual_hbm.at[:, balanced], residual_ref),
+        (attended_hbm.at[:, balanced], attended_ref),
+    )
     kept, incoming, holds_two = my_counts(frames_ref, partner_ref, moved_ref)
     block = lax.axis_index("y") * NC + lax.axis_index("c")
     fetch[0].wait()
@@ -221,9 +221,10 @@
             first = pl.multiple_of((block ^ partner) * HD, HD)
             part = dot(weight_ref[:, pl.ds(first, HD)], scaled, ROWS_BY_COLS)
             ref[pl.ds(index * HD, HD), :] = part.astype(bf16)
-    fetch[1].wait()
     received = dot(got_ref[pl.ds(0, ROWS), :], light_places(kept, incoming), COLS_BY_COLS)
-    own = layer_ref[:, pl.ds(0, BAL_ROWS)].astype(f32)
+    wait(fetch[1:])
+    own = to_column(scale_ref[...]) * dot(weight_ref[...], attended_ref[...])
+    own = (residual_ref[...].astype(f32) + own).astype(bf16).astype(f32)
     keep = positions((ROWS, BAL_ROWS), 1) < kept
     layer_out_ref[...] = jnp.where(keep, own, received).astype(bf16)
 
@@ -266,7 +267,16 @@
     )
 
 
-def ortho_kernel(grad_ref, out_hbm, out_ref, sems):
+def ortho_kernel(
+    grad_ref, left_ref, first_ref, second_ref, third_ref,
+    out_hbm, input_grad_hbm,
+    out_ref, input_grad_ref, sems,
+):
+    total = left_ref[...].astype(f32)
+    for ref in (first_ref, second_ref, third_ref):
+        total = total + ref[...].astype(f32)
+    input_grad_ref[...] = total.astype(bf16)
+    stores = start(sems.at[pl.ds(PARTS, 1)], (input_grad_ref, input_grad_hbm))
     grad = grad_ref[...]
     gram = dot(grad, grad, COLS_BY_COLS)
     eye = jnp.where(same(HD), 1.0, 0.0).astype(f32)
@@ -280,7 +290,6 @@
         if sweep < ITERS - 1:
             gram = mul(mul(step, gram), step)
     total = jnp.concatenate(split(total * (0.2 * math.sqrt(D) / norm)), axis=1)
-    stores = []
     for index, first in enumerate(range(0, D, D // PARTS)):
         cut = pl.ds(first, D // PARTS)
         out = dot(grad_ref[:, cut], total, ROWS_BY_COLS)
@@ -350,16 +359,15 @@
     ints = pltpu.SMEM((N_DP,), jnp.int32)
     dma = pltpu.SemaphoreType.DMA
 
-    projected, layer_own, window = call(
+    (window,) = call(
         project_kernel, "project", [H] * 8,
         (frames, partner, moved_tiles, attended, residual, grad_out, out_weight, scale_row),
-        [((ROWS, CAP_ROWS), f32, H), ((ROWS, CAP_ROWS), bf16, H), ((PAD_ROWS, MOVE_ROWS), bf16, V)],
+        [((PAD_ROWS, MOVE_ROWS), bf16, V)],
         [
             ints, ints, ints,
-            V((A, CAP_ROWS), bf16), V((ROWS, CAP_ROWS), bf16), V((ROWS, BAL_ROWS), bf16),
+            V((A, MOVE_ROWS), bf16), V((ROWS, MOVE_ROWS), bf16), V((ROWS, BAL_ROWS), bf16),
             V((ROWS, A), bf16), V((1, ROWS), f32),
-            V((ROWS, CAP_ROWS), f32), V((ROWS, CAP_ROWS), bf16),
-            dma((6,)), dma((A // CHUNK,)), dma((A // CHUNK,)), dma((2,)),
+            dma((6,)), dma((A // CHUNK,)), dma((A // CHUNK,)),
         ],
     )
     pieces = exchange(window.reshape(N_DP, PAD_ROWS // N_DP, MOVE_ROWS), ("z", "x"))
@@ -371,23 +379,31 @@
     got = pieces.reshape(PAD_ROWS, MOVE_ROWS)
 
     scaled, pieces = call(
-        weight_grad_kernel, "weight_grad", [S] * 4 + [V] * 4 + [H],
-        (frames, partner, moved_tiles, owner_slot, attended, grad_out, scale_row, got, projected),
+        weight_grad_kernel, "weight_grad", [S] * 4 + [V] * 5,
+        (
+            frames, partner, moved_tiles, owner_slot,
+            attended, grad_out, out_weight, scale_row, got,
+        ),
         [((ROWS, CAP_ROWS), bf16, H), ((N_DP, SHARE, WIDE), bf16, H)],
         [
             pltpu.SMEM((HEADS,), jnp.int32), V((HD, D), f32),
-            V((ROWS, CAP_ROWS), f32), V((ROWS, CAP_ROWS), bf16),
-            V((N_DP, SHARE, WIDE), bf16), dma((7,)),
+            V((ROWS, CAP_ROWS), bf16), V((N_DP, SHARE, WIDE), bf16), dma((7,)),
         ],
     )
     summed = exchange(pieces, ("z", "x"))
 
     half = ((A // 2, CAP_ROWS), bf16, V)
     even, odd, layer_out = call(
-        input_kernel, "input_grad", [S] * 3 + [V] * 2 + [H] * 2,
-        (frames, partner, moved_tiles, out_weight, got, scaled, layer_own),
+        input_kernel, "input_grad", [S] * 3 + [V] * 3 + [H] * 3,
+        (
+            frames, partner, moved_tiles,
+            out_weight, scale_row, got, scaled, attended, residual,
+        ),
         [half, half, ((ROWS, BAL_ROWS), bf16, V)],
-        [V((ROWS, CAP_ROWS), bf16), V((ROWS, CAP_ROWS), bf16), dma((2,))],
+        [
+            V((ROWS, CAP_ROWS), bf16), V((A, BAL_ROWS), bf16), V((ROWS, BAL_ROWS), bf16),
+            dma((3,)),
+        ],
         FREE,
     )
     left, other = add((even, crossed(odd, "c", NC, 1)), 2)
@@ -407,12 +423,11 @@
         [V((BY_X, D), f32)],
     )
     whole = lax.all_gather(copies, "x", axis=0, tiled=True)
-    (ortho_update,) = call(
-        ortho_kernel, "ortho", [V], (whole,), [((D, HD), bf16, H)],
-        [V((D, HD), bf16), dma((PARTS,))],
-    )
-    left, others, ortho_update = lax.optimization_barrier((left, others, ortho_update))
-    (input_grad,) = add((left, *others), 1)
+    ortho_update, input_grad = call(
+        ortho_kernel, "ortho", [V] * 5, (whole, left, *others),
+        [((D, HD), bf16, H), ((HD, CAP_ROWS), bf16, H)],
+        [V((D, HD), bf16), V((HD, CAP_ROWS), bf16), dma((PARTS + 1,))],
+    )
     return (layer_out, input_grad, scale_grad.reshape(ROWS), ortho_update[:, None, :])
 
 

time: 119 us -> 118 us (level)
    pallas_call x10 -> x9, Pallas kernels: 17.6 us -> 16.8 us  [call(): pl.pallas_call(kernel, out_shape=[H(shape, dtype) if place is H else jax....]
  transfers between devices with their start and end apart: 7 -> 7, of which waited for: 3 -> 3; matrix products, arithmetic and copies ran while one was open for 0% -> 0% of each run, Pallas kernels for 8% -> 5%
where the time goes in v11:
time: 118 us; the launch traced here: 116 us
  blocking collectives  47.3 us (40%)
  starting transfers between devices  38.9 us (33%)
  Pallas kernels  16.8 us (14%)
  waiting for transfers between devices  12 us (10%)
    all_to_all x2, blocking collectives, exchange(): return lax.all_to_all(pieces, axes, split_axis=0, concat_axis=0, tiled=True)  35.5 us
    ppermute x5, starting transfers between devices, crossed(): return lax.ppermute(array, axis, [(i, i ^ bit) for i in range(size)])  19.8 us
    all_to_all x2, starting transfers between devices, exchange(): return lax.all_to_all(pieces, axes, split_axis=0, concat_axis=0, tiled=True)  19.1 us
    pallas_call x9, Pallas kernels, call(): pl.pallas_call(kernel, out_shape=[H(shape, dtype) if place is H else jax....  16.8 us
    all_gather x1, blocking collectives, body(): whole = lax.all_gather(copies, 'x', axis=0, tiled=True)  11.8 us
    all_to_all x2, waiting for transfers between devices, exchange(): return lax.all_to_all(pieces, axes, split_axis=0, concat_axis=0, tiled=True)  9.71 us
  transfers between devices with their start and end apart: 7, of which 3 were waited for; matrix products, arithmetic and copies ran while one was open for 0% of the time, Pallas kernels for 5%

profile of v11, /device:TPU:1, one launch (start us, length us, event | category | flops | bytes accessed | tf_op | source)
XLA Modules:
  0.0 115.9 jit_solution(16456011258811869426)
XLA Ops:
  0.6 0.0 copy-start.4
  0.6 0.0 copy-start
  0.7 0.0 copy-start.1
  0.7 0.0 copy-start.2
  0.7 0.0 copy-start.3
  0.7 0.0 copy-start.5
  0.7 0.0 copy-start.6
  0.7 0.0 copy-start.7
  0.7 2.6 %project.1 = bf16[256,256]{1,0:T(8,128)(2,1)S(1)} custom-call(s32[32]{0:T(128)} %frames_ref.3, s32[32]{0:T(128)} %partner_ref.5, s32[32]{0:T(128)} %moved_ref.3, bf16[2048,512]{1,0:T(8,128)(2,1)} %attended_hbm.3, bf16[200,512]{1,0:T(8,128)(2,1)} %residual_hbm.3, bf16[200,384]{1,0:T(8,128)(2,1)} %grad_ref.1, bf16[200,2048]{1,0:T(8,128)(2,1)} %weight_ref.3, ...), custom_call_target="tpu_custom_call" | custom-call | tf_op jit(solution)/shard_map/project/pallas_call | solution.py:310
  3.3 22.9 %all_to_all.20.pieces_ref = bf16[32,8,256]{2,1,0:T(8,128)(2,1)S(1)} all-to-all(bf16[32,8,256]{2,1,0:T(8,128)(2,1)S(1)} %bitcast.7), channel_id=1, replica_groups=mesh['z'=8,'x'=4,'y'=8,'c'=2] {'z','x'}, dimensions={0} | all-to-all | bytes 262144 | tf_op jit(solution)/shard_map/all_to_all | solution.py:326
  26.2 0.0 copy-done.4
  26.2 0.6 forward.1
  26.7 12.6 %all_to_all.21 = bf16[32,8,256]{2,1,0:T(8,128)(2,1)S(1)} all-to-all(bf16[32,8,256]{2,1,0:T(8,128)(2,1)S(1)} %forward.1), channel_id=1, replica_groups=mesh['z'=8,'x'=4,'y'=8,'c'=2] {'z','x'}, dimensions={0} | all-to-all | bytes 262144 | tf_op jit(solution)/shard_map/all_to_all | solution.py:326
  39.4 0.0 copy-done
  39.4 0.0 copy-done.1
  39.4 0.0 copy-done.2
  39.4 0.0 copy-done.3
  39.4 0.0 copy-done.5
  39.4 0.0 copy-done.6
  39.4 0.0 copy-done.7
  39.4 3.4 %weight_grad.1 = (bf16[200,512]{1,0:T(8,128)(2,1)}, bf16[32,4,3328]{2,1,0:T(4,128)(2,1)}) custom-call(s32[32]{0:T(128)S(1)} %copy-done.5, s32[32]{0:T(128)S(1)} %copy-done.4, s32[32]{0:T(128)S(1)} %copy-done.6, s32[16]{0:T(128)S(1)} %copy-done.7, bf16[2048,512]{1,0:T(8,128)(2,1)S(1)} %copy-done, bf16[200,384]{1,0:T(8,128)(2,1)S(1)} %copy-done.2, ...), custom_call_target="tpu_custom_call" | custom-call | tf_op jit(solution)/shard_map/weight_grad/pallas_call | solution.py:310
  42.9 3.9 %all-to-all-start.2 = ((bf16[32,4,3328]{2,1,0:T(4,128)(2,1)}), bf16[32,4,3328]{2,1,0:T(4,128)(2,1)S(1)}, u32[]{:S(2)}, u32[]{:S(2)}) async-start(bf16[32,4,3328]{2,1,0:T(4,128)(2,1)} %get-tuple-element.23), calls=%async_computation.2 | async-start | bytes 1703936 | tf_op jit(solution)/shard_map/all_to_all | solution.py:326
  46.8 3.7 %input_grad.1 = (bf16[1024,512]{1,0:T(8,128)(2,1)S(1)}, bf16[1024,512]{1,0:T(8,128)(2,1)S(1)}, bf16[200,384]{1,0:T(8,128)(2,1)}) custom-call(s32[32]{0:T(128)S(1)} %copy-done.5, s32[32]{0:T(128)S(1)} %copy-done.4, s32[32]{0:T(128)S(1)} %copy-done.6, bf16[200,2048]{1,0:T(8,128)(2,1)S(1)} %copy-done.1, f32[1,200]{1,0:T(1,128)S(1)} %bitcast.10, ...), custom_call_target="tpu_custom_call" | custom-call | tf_op jit(solution)/shard_map/input_grad/pallas_call | solution.py:310
  50.5 5.2 %collective-permute-start = (bf16[1024,512]{1,0:T(8,128)(2,1)S(1)}, bf16[1024,512]{1,0:T(8,128)(2,1)S(1)}, u32[]{:S(2)}, u32[]{:S(2)}) collective-permute-start(bf16[1024,512]{1,0:T(8,128)(2,1)S(1)} %get-tuple-element.25), channel_id=1, source_target_pairs={{0,1},{1,0},{2,3},{3,2},{4,5},{5,4},{6,7},{7,6},{8,9},{9,8},{10,11... | collective-permute-start | bytes 3145736 | tf_op jit(solution)/shard_map/ppermute | solution.py:330
  55.7 2.3 %collective-permute-done.refs_1_ = bf16[1024,512]{1,0:T(8,128)(2,1)S(1)} collective-permute-done((bf16[1024,512]{1,0:T(8,128)(2,1)S(1)}, bf16[1024,512]{1,0:T(8,128)(2,1)S(1)}, u32[]{:S(2)}, u32[]{:S(2)}) %collective-permute-start) | collective-permute-done | bytes 1048608 | tf_op jit(solution)/shard_map/ppermute | solution.py:330
  58.0 0.2 add.2
  58.2 3.2 %collective-permute-start.1 = (bf16[512,512]{1,0:T(8,128)(2,1)S(1)}, bf16[512,512]{1,0:T(8,128)(2,1)S(1)}, u32[]{:S(2)}, u32[]{:S(2)}) collective-permute-start(bf16[512,512]{1,0:T(8,128)(2,1)S(1)} %get-tuple-element.29), channel_id=1, source_target_pairs={{0,2},{2,0},{4,6},{6,4},{8,10},{10,8},{12,14},{14,12},{1,3},{3,1},... | collective-permute-start | bytes 1572872 | tf_op jit(solution)/shard_map/ppermute | solution.py:330
  61.4 5.7 %all-to-all-done.2.pieces_ref = bf16[32,4,3328]{2,1,0:T(4,128)(2,1)S(1)} async-done(((bf16[32,4,3328]{2,1,0:T(4,128)(2,1)}), bf16[32,4,3328]{2,1,0:T(4,128)(2,1)S(1)}, u32[]{:S(2)}, u32[]{:S(2)}) %all-to-all-start.2) | async-done | bytes 852000 | tf_op jit(solution)/shard_map/all_to_all | solution.py:326
  67.1 1.5 %slots.1 = (bf16[128,4,200]{2,1,0:T(4,128)(2,1)}, f32[1,200]{1,0:T(1,128)}) custom-call(bf16[32,4,3328]{2,1,0:T(4,128)(2,1)S(1)} %all-to-all-done.2.pieces_ref), custom_call_target="tpu_custom_call" | custom-call | tf_op jit(solution)/shard_map/slots/pallas_call | solution.py:310
  68.6 15.2 %all-to-all-start.3 = ((bf16[128,4,200]{2,1,0:T(4,128)(2,1)}), bf16[128,4,200]{2,1,0:T(4,128)(2,1)S(1)}, u32[]{:S(2)}, u32[]{:S(2)}) async-start(bf16[128,4,200]{2,1,0:T(4,128)(2,1)} %get-tuple-element.28), calls=%async_computation.3 | async-start | bytes 524288 | tf_op jit(solution)/shard_map/all_to_all | solution.py:326
  83.8 0.0 collective-permute-done.1.refs_1_
  83.8 0.1 add.3
  84.0 7.2 %collective-permute-start.2 = (bf16[128,512]{1,0:T(8,128)(2,1)S(1)}, bf16[128,512]{1,0:T(8,128)(2,1)S(1)}, u32[]{:S(2)}, u32[]{:S(2)}) collective-permute-start(bf16[128,512]{1,0:T(8,128)(2,1)S(1)} %get-tuple-element.32), channel_id=1, source_target_pairs={{0,8},{2,10},{4,12},{6,14},{8,0},{10,2},{12,4},{14,6},{1,9},{3,11}... | collective-permute-start | bytes 393224 | tf_op jit(solution)/shard_map/ppermute | solution.py:330
  91.2 2.2 %collective-permute-start.3 = (bf16[128,512]{1,0:T(8,128)(2,1)S(1)}, bf16[128,512]{1,0:T(8,128)(2,1)S(1)}, u32[]{:S(2)}, u32[]{:S(2)}) collective-permute-start(bf16[128,512]{1,0:T(8,128)(2,1)S(1)} %get-tuple-element.33), channel_id=1, source_target_pairs={{0,4},{2,6},{4,0},{6,2},{8,12},{10,14},{12,8},{14,10},{1,5},{3,7},... | collective-permute-start | bytes 393224 | tf_op jit(solution)/shard_map/ppermute | solution.py:330
  93.4 2.0 %collective-permute-start.4 = (bf16[128,512]{1,0:T(8,128)(2,1)S(1)}, bf16[128,512]{1,0:T(8,128)(2,1)S(1)}, u32[]{:S(2)}, u32[]{:S(2)}) collective-permute-start(bf16[128,512]{1,0:T(8,128)(2,1)S(1)} %get-tuple-element.34), channel_id=1, source_target_pairs={{0,12},{2,14},{4,8},{6,10},{8,4},{10,6},{12,0},{14,2},{1,13},{3,15... | collective-permute-start | bytes 393224 | tf_op jit(solution)/shard_map/ppermute | solution.py:330
  95.4 4.1 %all-to-all-done.3.owned_ref = bf16[128,4,200]{2,1,0:T(4,128)(2,1)S(1)} async-done(((bf16[128,4,200]{2,1,0:T(4,128)(2,1)}), bf16[128,4,200]{2,1,0:T(4,128)(2,1)S(1)}, u32[]{:S(2)}, u32[]{:S(2)}) %all-to-all-start.3) | async-done | bytes 204832 | tf_op jit(solution)/shard_map/all_to_all | solution.py:326
  99.4 0.2 join.1
  99.7 11.8 %all_gather.3.grad_ref = bf16[128,3200]{1,0:T(8,128)(2,1)S(1)} all-gather(bf16[32,3200]{1,0:T(8,128)(2,1)S(1)} %join.1), channel_id=1, replica_groups=mesh['z'=8,'x'=4,'y'=8,'c'=2] {'x'}, dimensions={0}, use_global_device_ids=true | all-gather | bytes 1024000 | tf_op jit(solution)/shard_map/all_gather | solution.py:425
  111.5 0.0 collective-permute-done.2.first_ref
  111.5 0.0 collective-permute-done.3.second_ref
  111.5 0.0 collective-permute-done.4.third_ref
  111.5 4.4 %ortho.1 = (bf16[3200,128]{1,0:T(8,128)(2,1)}, bf16[128,512]{1,0:T(8,128)(2,1)}) custom-call(bf16[128,3200]{1,0:T(8,128)(2,1)S(1)} %all_gather.3.grad_ref, bf16[128,512]{1,0:T(8,128)(2,1)S(1)} %get-tuple-element.30.left_ref, bf16[128,512]{1,0:T(8,128)(2,1)S(1)} %collective-permute-done.2.first_ref, bf16[128,512]{1,0:T(8,128)(2,1)S(1)} %collective-permute-done.3.second_ref, ...), custom_call_target="tpu_custom_call" | custom-call | tf_op jit(solution)/shard_map/ortho/pallas_call | solution.py:310
Async XLA Ops:
  0.6 25.5 %copy-start.4 = (s32[32]{0:T(128)S(1)}, s32[32]{0:T(128)}, u32[]{:S(2)}) copy-start(s32[32]{0:T(128)} %partner_ref.5) | copy-start | bytes 388
  0.6 38.7 %copy-start = (bf16[2048,512]{1,0:T(8,128)(2,1)S(1)}, bf16[2048,512]{1,0:T(8,128)(2,1)}, u32[]{:S(2)}) copy-start(bf16[2048,512]{1,0:T(8,128)(2,1)} %attended_hbm.3) | copy-start | bytes 6291460
  0.7 38.7 %copy-start.1 = (bf16[200,2048]{1,0:T(8,128)(2,1)S(1)}, bf16[200,2048]{1,0:T(8,128)(2,1)}, u32[]{:S(2)}) copy-start(bf16[200,2048]{1,0:T(8,128)(2,1)} %weight_ref.3) | copy-start | bytes 2457604
  0.7 38.7 %copy-start.2 = (bf16[200,384]{1,0:T(8,128)(2,1)S(1)}, bf16[200,384]{1,0:T(8,128)(2,1)}, u32[]{:S(2)}) copy-start(bf16[200,384]{1,0:T(8,128)(2,1)} %grad_ref.1) | copy-start | bytes 460804
  0.7 38.7 %copy-start.3 = (f32[200]{0:T(256)S(1)}, f32[200]{0:T(256)}, u32[]{:S(2)}) copy-start(f32[200]{0:T(256)} %param.13) | copy-start | bytes 2404
  0.7 38.7 %copy-start.5 = (s32[32]{0:T(128)S(1)}, s32[32]{0:T(128)}, u32[]{:S(2)}) copy-start(s32[32]{0:T(128)} %frames_ref.3) | copy-start | bytes 388
  0.7 38.7 %copy-start.6 = (s32[32]{0:T(128)S(1)}, s32[32]{0:T(128)}, u32[]{:S(2)}) copy-start(s32[32]{0:T(128)} %moved_ref.3) | copy-start | bytes 388
  0.7 38.7 %copy-start.7 = (s32[16]{0:T(128)S(1)}, s32[16]{0:T(128)}, u32[]{:S(2)}) copy-start(s32[16]{0:T(128)} %slot_ref.1) | copy-start | bytes 196
  42.9 24.2 %all-to-all-start.2 = ((bf16[32,4,3328]{2,1,0:T(4,128)(2,1)}), bf16[32,4,3328]{2,1,0:T(4,128)(2,1)S(1)}, u32[]{:S(2)}, u32[]{:S(2)}) async-start(bf16[32,4,3328]{2,1,0:T(4,128)(2,1)} %get-tuple-element.23), calls=%async_computation.2 | async-start | bytes 1703936 | tf_op jit(solution)/shard_map/all_to_all | solution.py:326
  50.5 7.5 %collective-permute-start = (bf16[1024,512]{1,0:T(8,128)(2,1)S(1)}, bf16[1024,512]{1,0:T(8,128)(2,1)S(1)}, u32[]{:S(2)}, u32[]{:S(2)}) collective-permute-start(bf16[1024,512]{1,0:T(8,128)(2,1)S(1)} %get-tuple-element.25), channel_id=1, source_target_pairs={{0,1},{1,0},{2,3},{3,2},{4,5},{5,4},{6,7},{7,6},{8,9},{9,8},{10,11... | collective-permute-start | bytes 3145736 | tf_op jit(solution)/shard_map/ppermute | solution.py:330
  58.2 25.6 %collective-permute-start.1 = (bf16[512,512]{1,0:T(8,128)(2,1)S(1)}, bf16[512,512]{1,0:T(8,128)(2,1)S(1)}, u32[]{:S(2)}, u32[]{:S(2)}) collective-permute-start(bf16[512,512]{1,0:T(8,128)(2,1)S(1)} %get-tuple-element.29), channel_id=1, source_target_pairs={{0,2},{2,0},{4,6},{6,4},{8,10},{10,8},{12,14},{14,12},{1,3},{3,1},... | collective-permute-start | bytes 1572872 | tf_op jit(solution)/shard_map/ppermute | solution.py:330
  68.6 30.8 %all-to-all-start.3 = ((bf16[128,4,200]{2,1,0:T(4,128)(2,1)}), bf16[128,4,200]{2,1,0:T(4,128)(2,1)S(1)}, u32[]{:S(2)}, u32[]{:S(2)}) async-start(bf16[128,4,200]{2,1,0:T(4,128)(2,1)} %get-tuple-element.28), calls=%async_computation.3 | async-start | bytes 524288 | tf_op jit(solution)/shard_map/all_to_all | solution.py:326
  84.0 27.5 %collective-permute-start.2 = (bf16[128,512]{1,0:T(8,128)(2,1)S(1)}, bf16[128,512]{1,0:T(8,128)(2,1)S(1)}, u32[]{:S(2)}, u32[]{:S(2)}) collective-permute-start(bf16[128,512]{1,0:T(8,128)(2,1)S(1)} %get-tuple-element.32), channel_id=1, source_target_pairs={{0,8},{2,10},{4,12},{6,14},{8,0},{10,2},{12,4},{14,6},{1,9},{3,11}... | collective-permute-start | bytes 393224 | tf_op jit(solution)/shard_map/ppermute | solution.py:330
  91.2 20.3 %collective-permute-start.3 = (bf16[128,512]{1,0:T(8,128)(2,1)S(1)}, bf16[128,512]{1,0:T(8,128)(2,1)S(1)}, u32[]{:S(2)}, u32[]{:S(2)}) collective-permute-start(bf16[128,512]{1,0:T(8,128)(2,1)S(1)} %get-tuple-element.33), channel_id=1, source_target_pairs={{0,4},{2,6},{4,0},{6,2},{8,12},{10,14},{12,8},{14,10},{1,5},{3,7},... | collective-permute-start | bytes 393224 | tf_op jit(solution)/shard_map/ppermute | solution.py:330
  93.4 18.1 %collective-permute-start.4 = (bf16[128,512]{1,0:T(8,128)(2,1)S(1)}, bf16[128,512]{1,0:T(8,128)(2,1)S(1)}, u32[]{:S(2)}, u32[]{:S(2)}) collective-permute-start(bf16[128,512]{1,0:T(8,128)(2,1)S(1)} %get-tuple-element.34), channel_id=1, source_target_pairs={{0,12},{2,14},{4,8},{6,10},{8,4},{10,6},{12,0},{14,2},{1,13},{3,15... | collective-permute-start | bytes 393224 | tf_op jit(solution)/shard_map/ppermute | solution.py:330

commit v12 on v11

--- a/solution.py
+++ b/solution.py
@@ -27,7 +27,7 @@
 SHARE = HD // N_DP
 WIDE = D + HD
 PAD_ROWS = 256
-CHUNK = 512
+CHUNK = 1024
 PARTS = 5
 
 coeff_linear = 3.4445
@@ -168,18 +168,6 @@
     scaled = (grad * to_column(scale_ref[...])).astype(bf16)
     scaled_ref[...] = scaled
     (store,) = start(sems.at[pl.ds(1, 1)], (scaled_ref, scaled_hbm))
-    stores, done = [store], 0
-    for slot in range(HEADS):
-        first = pl.multiple_of(head_of[slot] * HD, HD)
-        wide[:, pl.ds(slot * ROWS, ROWS)] = dot(
-            attended_ref[pl.ds(first, HD), :], scaled, COLS_BY_COLS
-        )
-        if (slot + 1) % 4 == 0:
-            full = (slot + 1) * ROWS // HD * HD
-            stores += send_lanes(done, full, lambda piece, lanes: wide[
-                pl.ds((piece % NX * NZ + piece // NX) * SHARE, SHARE), lanes
-            ].astype(bf16), pieces_ref, pieces_hbm, sems.at[pl.ds(2 + slot // 4, 1)])
-            done = full
     projected = dot(weight_ref[...], attended_ref[...])
     part = jnp.sum(grad * projected, axis=1, keepdims=True) * INVERSE_ROOT
     part = to_row(part)
@@ -193,9 +181,22 @@
         jnp.concatenate([low[:, HD:], zeros], axis=1),
     ]
     lines = jnp.concatenate(lines, axis=0).astype(bf16)
+    stores = [store]
     stores += send_lanes(
         D, WIDE, lambda piece, lanes: lines, pieces_ref, pieces_hbm, sems.at[pl.ds(6, 1)]
     )
+    done = 0
+    for slot in range(HEADS):
+        first = pl.multiple_of(head_of[slot] * HD, HD)
+        wide[:, pl.ds(slot * ROWS, ROWS)] = dot(
+            attended_ref[pl.ds(first, HD), :], scaled, COLS_BY_COLS
+        )
+        if (slot + 1) % 4 == 0:
+            full = (slot + 1) * ROWS // HD * HD
+            stores += send_lanes(done, full, lambda piece, lanes: wide[
+                pl.ds((piece % NX * NZ + piece // NX) * SHARE, SHARE), lanes
+            ].astype(bf16), pieces_ref, pieces_hbm, sems.at[pl.ds(2 + slot // 4, 1)])
+            done = full
     wait(stores)
 
 
@@ -416,7 +417,7 @@
     owned = exchange(copies, ("z", "y", "c"))
     left, *others = add((left, crossed(other, "y", NY, 1)), 4)
     owned, _ = lax.optimization_barrier((owned, left))
-    others = [crossed(other, "y", NY, step) for other, step in zip(others, (4, 2, 6))]
+    others = [crossed(other, "y", NY, step) for other, step in zip(others[1:] + others[:1], (2, 6, 4))]
     (copies,) = call(
         join_kernel, "join", [V], (owned,),
         [((BY_X, D), bf16, V)],

time: 118 us -> 117 us (level)
  no operation moved by 1% of the time
where the time goes in v12:
time: 117 us; the launch traced here: 116 us
  blocking collectives  47.3 us (40%)
  starting transfers between devices  39 us (33%)
  Pallas kernels  16.4 us (14%)
  waiting for transfers between devices  12 us (10%)
    all_to_all x2, blocking collectives, exchange(): return lax.all_to_all(pieces, axes, split_axis=0, concat_axis=0, tiled=True)  35.5 us
    ppermute x5, starting transfers between devices, crossed(): return lax.ppermute(array, axis, [(i, i ^ bit) for i in range(size)])  19.8 us
    all_to_all x2, starting transfers between devices, exchange(): return lax.all_to_all(pieces, axes, split_axis=0, concat_axis=0, tiled=True)  19.1 us
    pallas_call x9, Pallas kernels, call(): pl.pallas_call(kernel, out_shape=[H(shape, dtype) if place is H else jax....  16.4 us
    all_gather x1, blocking collectives, body(): whole = lax.all_gather(copies, 'x', axis=0, tiled=True)  11.8 us
    all_to_all x2, waiting for transfers between devices, exchange(): return lax.all_to_all(pieces, axes, split_axis=0, concat_axis=0, tiled=True)  9.68 us
  transfers between devices with their start and end apart: 7, of which 3 were waited for; matrix products, arithmetic and copies ran while one was open for 0% of the time, Pallas kernels for 5%

profile of v12, /device:TPU:1, one launch (start us, length us, event | category | flops | bytes accessed | tf_op | source)
XLA Modules:
  0.0 115.6 jit_solution(11492447685996107468)
XLA Ops:
  0.6 0.0 copy-start.4
  0.6 0.0 copy-start
  0.7 0.0 copy-start.1
  0.7 0.0 copy-start.2
  0.7 0.0 copy-start.3
  0.7 0.0 copy-start.5
  0.7 0.0 copy-start.6
  0.7 0.0 copy-start.7
  0.7 2.3 %project.1 = bf16[256,256]{1,0:T(8,128)(2,1)S(1)} custom-call(s32[32]{0:T(128)} %frames_ref.3, s32[32]{0:T(128)} %partner_ref.5, s32[32]{0:T(128)} %moved_ref.3, bf16[2048,512]{1,0:T(8,128)(2,1)} %attended_hbm.3, bf16[200,512]{1,0:T(8,128)(2,1)} %residual_hbm.3, bf16[200,384]{1,0:T(8,128)(2,1)} %grad_ref.1, bf16[200,2048]{1,0:T(8,128)(2,1)} %weight_ref.3, ...), custom_call_target="tpu_custom_call" | custom-call | tf_op jit(solution)/shard_map/project/pallas_call | solution.py:311
  3.0 22.9 %all_to_all.20.pieces_ref = bf16[32,8,256]{2,1,0:T(8,128)(2,1)S(1)} all-to-all(bf16[32,8,256]{2,1,0:T(8,128)(2,1)S(1)} %bitcast.7), channel_id=1, replica_groups=mesh['z'=8,'x'=4,'y'=8,'c'=2] {'z','x'}, dimensions={0} | all-to-all | bytes 262144 | tf_op jit(solution)/shard_map/all_to_all | solution.py:327
  25.9 0.0 copy-done.4
  25.9 0.6 forward.1
  26.4 12.6 %all_to_all.21 = bf16[32,8,256]{2,1,0:T(8,128)(2,1)S(1)} all-to-all(bf16[32,8,256]{2,1,0:T(8,128)(2,1)S(1)} %forward.1), channel_id=1, replica_groups=mesh['z'=8,'x'=4,'y'=8,'c'=2] {'z','x'}, dimensions={0} | all-to-all | bytes 262144 | tf_op jit(solution)/shard_map/all_to_all | solution.py:327
  39.1 0.0 copy-done
  39.1 0.0 copy-done.1
  39.1 0.0 copy-done.2
  39.1 0.0 copy-done.3
  39.1 0.0 copy-done.5
  39.1 0.0 copy-done.6
  39.1 0.0 copy-done.7
  39.1 3.3 %weight_grad.1 = (bf16[200,512]{1,0:T(8,128)(2,1)}, bf16[32,4,3328]{2,1,0:T(4,128)(2,1)}) custom-call(s32[32]{0:T(128)S(1)} %copy-done.5, s32[32]{0:T(128)S(1)} %copy-done.4, s32[32]{0:T(128)S(1)} %copy-done.6, s32[16]{0:T(128)S(1)} %copy-done.7, bf16[2048,512]{1,0:T(8,128)(2,1)S(1)} %copy-done, bf16[200,384]{1,0:T(8,128)(2,1)S(1)} %copy-done.2, ...), custom_call_target="tpu_custom_call" | custom-call | tf_op jit(solution)/shard_map/weight_grad/pallas_call | solution.py:311
  42.5 3.9 %all-to-all-start.2 = ((bf16[32,4,3328]{2,1,0:T(4,128)(2,1)}), bf16[32,4,3328]{2,1,0:T(4,128)(2,1)S(1)}, u32[]{:S(2)}, u32[]{:S(2)}) async-start(bf16[32,4,3328]{2,1,0:T(4,128)(2,1)} %get-tuple-element.23), calls=%async_computation.2 | async-start | bytes 1703936 | tf_op jit(solution)/shard_map/all_to_all | solution.py:327
  46.4 3.7 %input_grad.1 = (bf16[1024,512]{1,0:T(8,128)(2,1)S(1)}, bf16[1024,512]{1,0:T(8,128)(2,1)S(1)}, bf16[200,384]{1,0:T(8,128)(2,1)}) custom-call(s32[32]{0:T(128)S(1)} %copy-done.5, s32[32]{0:T(128)S(1)} %copy-done.4, s32[32]{0:T(128)S(1)} %copy-done.6, bf16[200,2048]{1,0:T(8,128)(2,1)S(1)} %copy-done.1, f32[1,200]{1,0:T(1,128)S(1)} %bitcast.10, ...), custom_call_target="tpu_custom_call" | custom-call | tf_op jit(solution)/shard_map/input_grad/pallas_call | solution.py:311
  50.1 5.2 %collective-permute-start = (bf16[1024,512]{1,0:T(8,128)(2,1)S(1)}, bf16[1024,512]{1,0:T(8,128)(2,1)S(1)}, u32[]{:S(2)}, u32[]{:S(2)}) collective-permute-start(bf16[1024,512]{1,0:T(8,128)(2,1)S(1)} %get-tuple-element.25), channel_id=1, source_target_pairs={{0,1},{1,0},{2,3},{3,2},{4,5},{5,4},{6,7},{7,6},{8,9},{9,8},{10,11... | collective-permute-start | bytes 3145736 | tf_op jit(solution)/shard_map/ppermute | solution.py:331
  55.3 2.3 %collective-permute-done.refs_1_ = bf16[1024,512]{1,0:T(8,128)(2,1)S(1)} collective-permute-done((bf16[1024,512]{1,0:T(8,128)(2,1)S(1)}, bf16[1024,512]{1,0:T(8,128)(2,1)S(1)}, u32[]{:S(2)}, u32[]{:S(2)}) %collective-permute-start) | collective-permute-done | bytes 1048608 | tf_op jit(solution)/shard_map/ppermute | solution.py:331
  57.6 0.2 add.2
  57.9 3.2 %collective-permute-start.1 = (bf16[512,512]{1,0:T(8,128)(2,1)S(1)}, bf16[512,512]{1,0:T(8,128)(2,1)S(1)}, u32[]{:S(2)}, u32[]{:S(2)}) collective-permute-start(bf16[512,512]{1,0:T(8,128)(2,1)S(1)} %get-tuple-element.29), channel_id=1, source_target_pairs={{0,2},{2,0},{4,6},{6,4},{8,10},{10,8},{12,14},{14,12},{1,3},{3,1},... | collective-permute-start | bytes 1572872 | tf_op jit(solution)/shard_map/ppermute | solution.py:331
  61.1 5.6 %all-to-all-done.2.pieces_ref = bf16[32,4,3328]{2,1,0:T(4,128)(2,1)S(1)} async-done(((bf16[32,4,3328]{2,1,0:T(4,128)(2,1)}), bf16[32,4,3328]{2,1,0:T(4,128)(2,1)S(1)}, u32[]{:S(2)}, u32[]{:S(2)}) %all-to-all-start.2) | async-done | bytes 852000 | tf_op jit(solution)/shard_map/all_to_all | solution.py:327
  66.7 1.5 %slots.1 = (bf16[128,4,200]{2,1,0:T(4,128)(2,1)}, f32[1,200]{1,0:T(1,128)}) custom-call(bf16[32,4,3328]{2,1,0:T(4,128)(2,1)S(1)} %all-to-all-done.2.pieces_ref), custom_call_target="tpu_custom_call" | custom-call | tf_op jit(solution)/shard_map/slots/pallas_call | solution.py:311
  68.2 15.2 %all-to-all-start.3 = ((bf16[128,4,200]{2,1,0:T(4,128)(2,1)}), bf16[128,4,200]{2,1,0:T(4,128)(2,1)S(1)}, u32[]{:S(2)}, u32[]{:S(2)}) async-start(bf16[128,4,200]{2,1,0:T(4,128)(2,1)} %get-tuple-element.28), calls=%async_computation.3 | async-start | bytes 524288 | tf_op jit(solution)/shard_map/all_to_all | solution.py:327
  83.4 0.0 collective-permute-done.1.refs_1_
  83.4 0.1 add.3
  83.6 4.2 %collective-permute-start.2 = (bf16[128,512]{1,0:T(8,128)(2,1)S(1)}, bf16[128,512]{1,0:T(8,128)(2,1)S(1)}, u32[]{:S(2)}, u32[]{:S(2)}) collective-permute-start(bf16[128,512]{1,0:T(8,128)(2,1)S(1)} %get-tuple-element.32), channel_id=1, source_target_pairs={{0,4},{2,6},{4,0},{6,2},{8,12},{10,14},{12,8},{14,10},{1,5},{3,7},... | collective-permute-start | bytes 393224 | tf_op jit(solution)/shard_map/ppermute | solution.py:331
  87.8 5.2 %collective-permute-start.3 = (bf16[128,512]{1,0:T(8,128)(2,1)S(1)}, bf16[128,512]{1,0:T(8,128)(2,1)S(1)}, u32[]{:S(2)}, u32[]{:S(2)}) collective-permute-start(bf16[128,512]{1,0:T(8,128)(2,1)S(1)} %get-tuple-element.33), channel_id=1, source_target_pairs={{0,12},{2,14},{4,8},{6,10},{8,4},{10,6},{12,0},{14,2},{1,13},{3,15... | collective-permute-start | bytes 393224 | tf_op jit(solution)/shard_map/ppermute | solution.py:331
  93.0 2.0 %collective-permute-start.4 = (bf16[128,512]{1,0:T(8,128)(2,1)S(1)}, bf16[128,512]{1,0:T(8,128)(2,1)S(1)}, u32[]{:S(2)}, u32[]{:S(2)}) collective-permute-start(bf16[128,512]{1,0:T(8,128)(2,1)S(1)} %get-tuple-element.34), channel_id=1, source_target_pairs={{0,8},{2,10},{4,12},{6,14},{8,0},{10,2},{12,4},{14,6},{1,9},{3,11}... | collective-permute-start | bytes 393224 | tf_op jit(solution)/shard_map/ppermute | solution.py:331
  95.0 4.1 %all-to-all-done.3.owned_ref = bf16[128,4,200]{2,1,0:T(4,128)(2,1)S(1)} async-done(((bf16[128,4,200]{2,1,0:T(4,128)(2,1)}), bf16[128,4,200]{2,1,0:T(4,128)(2,1)S(1)}, u32[]{:S(2)}, u32[]{:S(2)}) %all-to-all-start.3) | async-done | bytes 204832 | tf_op jit(solution)/shard_map/all_to_all | solution.py:327
  99.0 0.2 join.1
  99.3 11.8 %all_gather.3.grad_ref = bf16[128,3200]{1,0:T(8,128)(2,1)S(1)} all-gather(bf16[32,3200]{1,0:T(8,128)(2,1)S(1)} %join.1), channel_id=1, replica_groups=mesh['z'=8,'x'=4,'y'=8,'c'=2] {'x'}, dimensions={0}, use_global_device_ids=true | all-gather | bytes 1024000 | tf_op jit(solution)/shard_map/all_gather | solution.py:426
  111.1 0.0 collective-permute-done.2.first_ref
  111.1 0.0 collective-permute-done.3.second_ref
  111.1 0.0 collective-permute-done.4.third_ref
  111.1 4.4 %ortho.1 = (bf16[3200,128]{1,0:T(8,128)(2,1)}, bf16[128,512]{1,0:T(8,128)(2,1)}) custom-call(bf16[128,3200]{1,0:T(8,128)(2,1)S(1)} %all_gather.3.grad_ref, bf16[128,512]{1,0:T(8,128)(2,1)S(1)} %get-tuple-element.30.left_ref, bf16[128,512]{1,0:T(8,128)(2,1)S(1)} %collective-permute-done.2.first_ref, bf16[128,512]{1,0:T(8,128)(2,1)S(1)} %collective-permute-done.3.second_ref, ...), custom_call_target="tpu_custom_call" | custom-call | tf_op jit(solution)/shard_map/ortho/pallas_call | solution.py:311
Async XLA Ops:
  0.6 25.2 %copy-start.4 = (s32[32]{0:T(128)S(1)}, s32[32]{0:T(128)}, u32[]{:S(2)}) copy-start(s32[32]{0:T(128)} %partner_ref.5) | copy-start | bytes 388
  0.6 38.5 %copy-start = (bf16[2048,512]{1,0:T(8,128)(2,1)S(1)}, bf16[2048,512]{1,0:T(8,128)(2,1)}, u32[]{:S(2)}) copy-start(bf16[2048,512]{1,0:T(8,128)(2,1)} %attended_hbm.3) | copy-start | bytes 6291460
  0.7 38.4 %copy-start.1 = (bf16[200,2048]{1,0:T(8,128)(2,1)S(1)}, bf16[200,2048]{1,0:T(8,128)(2,1)}, u32[]{:S(2)}) copy-start(bf16[200,2048]{1,0:T(8,128)(2,1)} %weight_ref.3) | copy-start | bytes 2457604
  0.7 38.4 %copy-start.2 = (bf16[200,384]{1,0:T(8,128)(2,1)S(1)}, bf16[200,384]{1,0:T(8,128)(2,1)}, u32[]{:S(2)}) copy-start(bf16[200,384]{1,0:T(8,128)(2,1)} %grad_ref.1) | copy-start | bytes 460804
  0.7 38.4 %copy-start.3 = (f32[200]{0:T(256)S(1)}, f32[200]{0:T(256)}, u32[]{:S(2)}) copy-start(f32[200]{0:T(256)} %param.13) | copy-start | bytes 2404
  0.7 38.4 %copy-start.5 = (s32[32]{0:T(128)S(1)}, s32[32]{0:T(128)}, u32[]{:S(2)}) copy-start(s32[32]{0:T(128)} %frames_ref.3) | copy-start | bytes 388
  0.7 38.4 %copy-start.6 = (s32[32]{0:T(128)S(1)}, s32[32]{0:T(128)}, u32[]{:S(2)}) copy-start(s32[32]{0:T(128)} %moved_ref.3) | copy-start | bytes 388
  0.7 38.4 %copy-start.7 = (s32[16]{0:T(128)S(1)}, s32[16]{0:T(128)}, u32[]{:S(2)}) copy-start(s32[16]{0:T(128)} %slot_ref.1) | copy-start | bytes 196
  42.5 24.2 %all-to-all-start.2 = ((bf16[32,4,3328]{2,1,0:T(4,128)(2,1)}), bf16[32,4,3328]{2,1,0:T(4,128)(2,1)S(1)}, u32[]{:S(2)}, u32[]{:S(2)}) async-start(bf16[32,4,3328]{2,1,0:T(4,128)(2,1)} %get-tuple-element.23), calls=%async_computation.2 | async-start | bytes 1703936 | tf_op jit(solution)/shard_map/all_to_all | solution.py:327
  50.1 7.5 %collective-permute-start = (bf16[1024,512]{1,0:T(8,128)(2,1)S(1)}, bf16[1024,512]{1,0:T(8,128)(2,1)S(1)}, u32[]{:S(2)}, u32[]{:S(2)}) collective-permute-start(bf16[1024,512]{1,0:T(8,128)(2,1)S(1)} %get-tuple-element.25), channel_id=1, source_target_pairs={{0,1},{1,0},{2,3},{3,2},{4,5},{5,4},{6,7},{7,6},{8,9},{9,8},{10,11... | collective-permute-start | bytes 3145736 | tf_op jit(solution)/shard_map/ppermute | solution.py:331
  57.9 25.6 %collective-permute-start.1 = (bf16[512,512]{1,0:T(8,128)(2,1)S(1)}, bf16[512,512]{1,0:T(8,128)(2,1)S(1)}, u32[]{:S(2)}, u32[]{:S(2)}) collective-permute-start(bf16[512,512]{1,0:T(8,128)(2,1)S(1)} %get-tuple-element.29), channel_id=1, source_target_pairs={{0,2},{2,0},{4,6},{6,4},{8,10},{10,8},{12,14},{14,12},{1,3},{3,1},... | collective-permute-start | bytes 1572872 | tf_op jit(solution)/shard_map/ppermute | solution.py:331
  68.2 30.8 %all-to-all-start.3 = ((bf16[128,4,200]{2,1,0:T(4,128)(2,1)}), bf16[128,4,200]{2,1,0:T(4,128)(2,1)S(1)}, u32[]{:S(2)}, u32[]{:S(2)}) async-start(bf16[128,4,200]{2,1,0:T(4,128)(2,1)} %get-tuple-element.28), calls=%async_computation.3 | async-start | bytes 524288 | tf_op jit(solution)/shard_map/all_to_all | solution.py:327
  83.6 27.5 %collective-permute-start.2 = (bf16[128,512]{1,0:T(8,128)(2,1)S(1)}, bf16[128,512]{1,0:T(8,128)(2,1)S(1)}, u32[]{:S(2)}, u32[]{:S(2)}) collective-permute-start(bf16[128,512]{1,0:T(8,128)(2,1)S(1)} %get-tuple-element.32), channel_id=1, source_target_pairs={{0,4},{2,6},{4,0},{6,2},{8,12},{10,14},{12,8},{14,10},{1,5},{3,7},... | collective-permute-start | bytes 393224 | tf_op jit(solution)/shard_map/ppermute | solution.py:331
  87.8 23.3 %collective-permute-start.3 = (bf16[128,512]{1,0:T(8,128)(2,1)S(1)}, bf16[128,512]{1,0:T(8,128)(2,1)S(1)}, u32[]{:S(2)}, u32[]{:S(2)}) collective-permute-start(bf16[128,512]{1,0:T(8,128)(2,1)S(1)} %get-tuple-element.33), channel_id=1, source_target_pairs={{0,12},{2,14},{4,8},{6,10},{8,4},{10,6},{12,0},{14,2},{1,13},{3,15... | collective-permute-start | bytes 393224 | tf_op jit(solution)/shard_map/ppermute | solution.py:331
  93.0 18.1 %collective-permute-start.4 = (bf16[128,512]{1,0:T(8,128)(2,1)S(1)}, bf16[128,512]{1,0:T(8,128)(2,1)S(1)}, u32[]{:S(2)}, u32[]{:S(2)}) collective-permute-start(bf16[128,512]{1,0:T(8,128)(2,1)S(1)} %get-tuple-element.34), channel_id=1, source_target_pairs={{0,8},{2,10},{4,12},{6,14},{8,0},{10,2},{12,4},{14,6},{1,9},{3,11}... | collective-permute-start | bytes 393224 | tf_op jit(solution)/shard_map/ppermute | solution.py:331

commit v13 on v12

--- a/solution.py
+++ b/solution.py
@@ -200,10 +200,23 @@
     wait(stores)
 
 
-def input_kernel(
+def blocks_of(weight_ref, scaled, odd, out_ref):
+    block = lax.axis_index("y") * NC + lax.axis_index("c")
+    for index, other in enumerate(EVEN):
+        first = pl.multiple_of((block ^ (other + odd)) * HD, HD)
+        part = dot(weight_ref[:, pl.ds(first, HD)], scaled, ROWS_BY_COLS)
+        out_ref[pl.ds(index * HD, HD), :] = part.astype(bf16)
+
+
+def odd_kernel(weight_ref, scaled_hbm, odd_ref, scaled_ref, sems):
+    wait(start(sems, (scaled_hbm, scaled_ref)))
+    blocks_of(weight_ref, scaled_ref[...], 1, odd_ref)
+
+
+def even_kernel(
     frames_ref, partner_ref, moved_ref,
     weight_ref, scale_ref, got_ref, scaled_hbm, attended_hbm, residual_hbm,
-    even_ref, odd_ref, layer_out_ref,
+    even_ref, layer_out_ref,
     scaled_ref, attended_ref, residual_ref, sems,
 ):
     balanced = pl.ds(0, BAL_ROWS)
@@ -214,14 +227,8 @@
         (attended_hbm.at[:, balanced], attended_ref),
     )
     kept, incoming, holds_two = my_counts(frames_ref, partner_ref, moved_ref)
-    block = lax.axis_index("y") * NC + lax.axis_index("c")
     fetch[0].wait()
-    scaled = scaled_ref[...]
-    for index, other in enumerate(EVEN):
-        for ref, partner in ((even_ref, other), (odd_ref, other + 1)):
-            first = pl.multiple_of((block ^ partner) * HD, HD)
-            part = dot(weight_ref[:, pl.ds(first, HD)], scaled, ROWS_BY_COLS)
-            ref[pl.ds(index * HD, HD), :] = part.astype(bf16)
+    blocks_of(weight_ref, scaled_ref[...], 0, even_ref)
     received = dot(got_ref[pl.ds(0, ROWS), :], light_places(kept, incoming), COLS_BY_COLS)
     wait(fetch[1:])
     own = to_column(scale_ref[...]) * dot(weight_ref[...], attended_ref[...])
@@ -394,20 +401,26 @@
     summed = exchange(pieces, ("z", "x"))
 
     half = ((A // 2, CAP_ROWS), bf16, V)
-    even, odd, layer_out = call(
-        input_kernel, "input_grad", [S] * 3 + [V] * 3 + [H] * 3,
+    (odd,) = call(
+        odd_kernel, "input_grad_odd", [V, H], (out_weight, scaled), [half],
+        [V((ROWS, CAP_ROWS), bf16), dma((1,))],
+        FREE,
+    )
+    odd = crossed(odd, "c", NC, 1)
+    even, layer_out = call(
+        even_kernel, "input_grad_even", [S] * 3 + [V] * 3 + [H] * 3,
         (
             frames, partner, moved_tiles,
             out_weight, scale_row, got, scaled, attended, residual,
         ),
-        [half, half, ((ROWS, BAL_ROWS), bf16, V)],
+        [half, ((ROWS, BAL_ROWS), bf16, V)],
         [
             V((ROWS, CAP_ROWS), bf16), V((A, BAL_ROWS), bf16), V((ROWS, BAL_ROWS), bf16),
             dma((3,)),
         ],
         FREE,
     )
-    left, other = add((even, crossed(odd, "c", NC, 1)), 2)
+    left, other = add((even, odd), 2)
     summed, _ = lax.optimization_barrier((summed, left))
     copies, scale_grad = call(
         slots_kernel, "slots", [V], (summed,),

time: 117 us -> 117 us (level)
  Pallas kernels: 16.4 us -> 17.7 us
  waiting for transfers between devices: 12 us -> 10.7 us
    ppermute x5, waiting for transfers between devices: 2.28 us -> 0.01 us  [crossed(): return lax.ppermute(array, axis, [(i, i ^ bit) for i in range(size)])]
    pallas_call x9 -> x10, Pallas kernels: 16.4 us -> 17.7 us  [call(): pl.pallas_call(kernel, out_shape=[H(shape, dtype) if place is H else jax....]
  transfers between devices with their start and end apart: 7 -> 7, of which waited for: 3 -> 2; matrix products, arithmetic and copies ran while one was open for 0% -> 0% of each run, Pallas kernels for 5% -> 6%
where the time goes in v13:
time: 117 us; the launch traced here: 116 us
  blocking collectives  47.3 us (40%)
  starting transfers between devices  39 us (33%)
  Pallas kernels  17.7 us (15%)
  waiting for transfers between devices  10.7 us (9%)
    all_to_all x2, blocking collectives, exchange(): return lax.all_to_all(pieces, axes, split_axis=0, concat_axis=0, tiled=True)  35.5 us
    ppermute x5, starting transfers between devices, crossed(): return lax.ppermute(array, axis, [(i, i ^ bit) for i in range(size)])  19.8 us
    all_to_all x2, starting transfers between devices, exchange(): return lax.all_to_all(pieces, axes, split_axis=0, concat_axis=0, tiled=True)  19.2 us
    pallas_call x10, Pallas kernels, call(): pl.pallas_call(kernel, out_shape=[H(shape, dtype) if place is H else jax....  17.7 us
    all_gather x1, blocking collectives, body(): whole = lax.all_gather(copies, 'x', axis=0, tiled=True)  11.8 us
    all_to_all x2, waiting for transfers between devices, exchange(): return lax.all_to_all(pieces, axes, split_axis=0, concat_axis=0, tiled=True)  10.7 us
  transfers between devices with their start and end apart: 7, of which 2 were waited for; matrix products, arithmetic and copies ran while one was open for 0% of the time, Pallas kernels for 6%

profile of v13, /device:TPU:1, one launch (start us, length us, event | category | flops | bytes accessed | tf_op | source)
XLA Modules:
  0.0 115.6 jit_solution(12153337103795251525)
XLA Ops:
  0.6 0.0 copy-start.4
  0.6 0.0 copy-start
  0.7 0.0 copy-start.1
  0.7 0.0 copy-start.2
  0.7 0.0 copy-start.3
  0.7 0.0 copy-start.5
  0.7 0.0 copy-start.6
  0.7 0.0 copy-start.7
  0.7 2.3 %project.1 = bf16[256,256]{1,0:T(8,128)(2,1)S(1)} custom-call(s32[32]{0:T(128)} %frames_ref.3, s32[32]{0:T(128)} %partner_ref.5, s32[32]{0:T(128)} %moved_ref.3, bf16[2048,512]{1,0:T(8,128)(2,1)} %attended_hbm.3, bf16[200,512]{1,0:T(8,128)(2,1)} %residual_hbm.3, bf16[200,384]{1,0:T(8,128)(2,1)} %grad_ref.1, bf16[200,2048]{1,0:T(8,128)(2,1)} %weight_ref.5, ...), custom_call_target="tpu_custom_call" | custom-call | tf_op jit(solution)/shard_map/project/pallas_call | solution.py:318
  3.0 22.9 %all_to_all.20.pieces_ref = bf16[32,8,256]{2,1,0:T(8,128)(2,1)S(1)} all-to-all(bf16[32,8,256]{2,1,0:T(8,128)(2,1)S(1)} %bitcast.7), channel_id=1, replica_groups=mesh['z'=8,'x'=4,'y'=8,'c'=2] {'z','x'}, dimensions={0} | all-to-all | bytes 262144 | tf_op jit(solution)/shard_map/all_to_all | solution.py:334
  25.9 0.0 copy-done.4
  25.9 0.6 forward.1
  26.4 12.6 %all_to_all.21 = bf16[32,8,256]{2,1,0:T(8,128)(2,1)S(1)} all-to-all(bf16[32,8,256]{2,1,0:T(8,128)(2,1)S(1)} %forward.1), channel_id=1, replica_groups=mesh['z'=8,'x'=4,'y'=8,'c'=2] {'z','x'}, dimensions={0} | all-to-all | bytes 262144 | tf_op jit(solution)/shard_map/all_to_all | solution.py:334
  39.1 0.0 copy-done
  39.1 0.0 copy-done.1
  39.1 0.0 copy-done.2
  39.1 0.0 copy-done.3
  39.1 0.0 copy-done.5
  39.1 0.0 copy-done.6
  39.1 0.0 copy-done.7
  39.1 3.3 %weight_grad.1 = (bf16[200,512]{1,0:T(8,128)(2,1)}, bf16[32,4,3328]{2,1,0:T(4,128)(2,1)}) custom-call(s32[32]{0:T(128)S(1)} %copy-done.5, s32[32]{0:T(128)S(1)} %copy-done.4, s32[32]{0:T(128)S(1)} %copy-done.6, s32[16]{0:T(128)S(1)} %copy-done.7, bf16[2048,512]{1,0:T(8,128)(2,1)S(1)} %copy-done, bf16[200,384]{1,0:T(8,128)(2,1)S(1)} %copy-done.2, ...), custom_call_target="tpu_custom_call" | custom-call | tf_op jit(solution)/shard_map/weight_grad/pallas_call | solution.py:318
  42.5 3.9 %all-to-all-start.2 = ((bf16[32,4,3328]{2,1,0:T(4,128)(2,1)}), bf16[32,4,3328]{2,1,0:T(4,128)(2,1)S(1)}, u32[]{:S(2)}, u32[]{:S(2)}) async-start(bf16[32,4,3328]{2,1,0:T(4,128)(2,1)} %get-tuple-element.22), calls=%async_computation.2 | async-start | bytes 1703936 | tf_op jit(solution)/shard_map/all_to_all | solution.py:334
  46.4 1.4 %input_grad_odd.1 = bf16[1024,512]{1,0:T(8,128)(2,1)S(1)} custom-call(bf16[200,2048]{1,0:T(8,128)(2,1)S(1)} %copy-done.1, bf16[200,512]{1,0:T(8,128)(2,1)} %get-tuple-element.20.scaled_hbm), custom_call_target="tpu_custom_call" | custom-call | tf_op jit(solution)/shard_map/input_grad_odd/pallas_call | solution.py:318
  47.9 5.2 %collective-permute-start = (bf16[1024,512]{1,0:T(8,128)(2,1)S(1)}, bf16[1024,512]{1,0:T(8,128)(2,1)S(1)}, u32[]{:S(2)}, u32[]{:S(2)}) collective-permute-start(bf16[1024,512]{1,0:T(8,128)(2,1)S(1)} %input_grad_odd.1), channel_id=1, source_target_pairs={{0,1},{1,0},{2,3},{3,2},{4,5},{5,4},{6,7},{7,6},{8,9},{9,8},{10,11... | collective-permute-start | bytes 3145736 | tf_op jit(solution)/shard_map/ppermute | solution.py:338
  53.1 3.5 %input_grad_even.1 = (bf16[1024,512]{1,0:T(8,128)(2,1)S(1)}, bf16[200,384]{1,0:T(8,128)(2,1)}) custom-call(s32[32]{0:T(128)S(1)} %copy-done.5, s32[32]{0:T(128)S(1)} %copy-done.4, s32[32]{0:T(128)S(1)} %copy-done.6, bf16[200,2048]{1,0:T(8,128)(2,1)S(1)} %copy-done.1, f32[1,200]{1,0:T(1,128)S(1)} %bitcast.10, bf16[256,256]{1,0:T(8,128)(2,1)S(1)} %bitcast.6, ...), custom_call_target="tpu_custom_call" | custom-call | tf_op jit(solution)/shard_map/input_grad_even/pallas_call | solution.py:318
  56.6 0.0 collective-permute-done.refs_1_
  56.6 0.2 add.2
  56.9 3.2 %collective-permute-start.1 = (bf16[512,512]{1,0:T(8,128)(2,1)S(1)}, bf16[512,512]{1,0:T(8,128)(2,1)S(1)}, u32[]{:S(2)}, u32[]{:S(2)}) collective-permute-start(bf16[512,512]{1,0:T(8,128)(2,1)S(1)} %get-tuple-element.27), channel_id=1, source_target_pairs={{0,2},{2,0},{4,6},{6,4},{8,10},{10,8},{12,14},{14,12},{1,3},{3,1},... | collective-permute-start | bytes 1572872 | tf_op jit(solution)/shard_map/ppermute | solution.py:338
  60.1 6.6 %all-to-all-done.2.pieces_ref = bf16[32,4,3328]{2,1,0:T(4,128)(2,1)S(1)} async-done(((bf16[32,4,3328]{2,1,0:T(4,128)(2,1)}), bf16[32,4,3328]{2,1,0:T(4,128)(2,1)S(1)}, u32[]{:S(2)}, u32[]{:S(2)}) %all-to-all-start.2) | async-done | bytes 852000 | tf_op jit(solution)/shard_map/all_to_all | solution.py:334
  66.7 1.5 %slots.1 = (bf16[128,4,200]{2,1,0:T(4,128)(2,1)}, f32[1,200]{1,0:T(1,128)}) custom-call(bf16[32,4,3328]{2,1,0:T(4,128)(2,1)S(1)} %all-to-all-done.2.pieces_ref), custom_call_target="tpu_custom_call" | custom-call | tf_op jit(solution)/shard_map/slots/pallas_call | solution.py:318
  68.2 15.2 %all-to-all-start.3 = ((bf16[128,4,200]{2,1,0:T(4,128)(2,1)}), bf16[128,4,200]{2,1,0:T(4,128)(2,1)S(1)}, u32[]{:S(2)}, u32[]{:S(2)}) async-start(bf16[128,4,200]{2,1,0:T(4,128)(2,1)} %get-tuple-element.26), calls=%async_computation.3 | async-start | bytes 524288 | tf_op jit(solution)/shard_map/all_to_all | solution.py:334
  83.4 0.0 collective-permute-done.1.refs_1_
  83.5 0.1 add.3
  83.6 4.2 %collective-permute-start.2 = (bf16[128,512]{1,0:T(8,128)(2,1)S(1)}, bf16[128,512]{1,0:T(8,128)(2,1)S(1)}, u32[]{:S(2)}, u32[]{:S(2)}) collective-permute-start(bf16[128,512]{1,0:T(8,128)(2,1)S(1)} %get-tuple-element.30), channel_id=1, source_target_pairs={{0,4},{2,6},{4,0},{6,2},{8,12},{10,14},{12,8},{14,10},{1,5},{3,7},... | collective-permute-start | bytes 393224 | tf_op jit(solution)/shard_map/ppermute | solution.py:338
  87.8 5.2 %collective-permute-start.3 = (bf16[128,512]{1,0:T(8,128)(2,1)S(1)}, bf16[128,512]{1,0:T(8,128)(2,1)S(1)}, u32[]{:S(2)}, u32[]{:S(2)}) collective-permute-start(bf16[128,512]{1,0:T(8,128)(2,1)S(1)} %get-tuple-element.31), channel_id=1, source_target_pairs={{0,12},{2,14},{4,8},{6,10},{8,4},{10,6},{12,0},{14,2},{1,13},{3,15... | collective-permute-start | bytes 393224 | tf_op jit(solution)/shard_map/ppermute | solution.py:338
  93.0 2.0 %collective-permute-start.4 = (bf16[128,512]{1,0:T(8,128)(2,1)S(1)}, bf16[128,512]{1,0:T(8,128)(2,1)S(1)}, u32[]{:S(2)}, u32[]{:S(2)}) collective-permute-start(bf16[128,512]{1,0:T(8,128)(2,1)S(1)} %get-tuple-element.32), channel_id=1, source_target_pairs={{0,8},{2,10},{4,12},{6,14},{8,0},{10,2},{12,4},{14,6},{1,9},{3,11}... | collective-permute-start | bytes 393224 | tf_op jit(solution)/shard_map/ppermute | solution.py:338
  95.0 4.1 %all-to-all-done.3.owned_ref = bf16[128,4,200]{2,1,0:T(4,128)(2,1)S(1)} async-done(((bf16[128,4,200]{2,1,0:T(4,128)(2,1)}), bf16[128,4,200]{2,1,0:T(4,128)(2,1)S(1)}, u32[]{:S(2)}, u32[]{:S(2)}) %all-to-all-start.3) | async-done | bytes 204832 | tf_op jit(solution)/shard_map/all_to_all | solution.py:334
  99.1 0.2 join.1
  99.3 11.8 %all_gather.3.grad_ref = bf16[128,3200]{1,0:T(8,128)(2,1)S(1)} all-gather(bf16[32,3200]{1,0:T(8,128)(2,1)S(1)} %join.1), channel_id=1, replica_groups=mesh['z'=8,'x'=4,'y'=8,'c'=2] {'x'}, dimensions={0}, use_global_device_ids=true | all-gather | bytes 1024000 | tf_op jit(solution)/shard_map/all_gather | solution.py:439
  111.1 0.0 collective-permute-done.2.first_ref
  111.1 0.0 collective-permute-done.3.second_ref
  111.1 0.0 collective-permute-done.4.third_ref
  111.1 4.4 %ortho.1 = (bf16[3200,128]{1,0:T(8,128)(2,1)}, bf16[128,512]{1,0:T(8,128)(2,1)}) custom-call(bf16[128,3200]{1,0:T(8,128)(2,1)S(1)} %all_gather.3.grad_ref, bf16[128,512]{1,0:T(8,128)(2,1)S(1)} %get-tuple-element.28.left_ref, bf16[128,512]{1,0:T(8,128)(2,1)S(1)} %collective-permute-done.2.first_ref, bf16[128,512]{1,0:T(8,128)(2,1)S(1)} %collective-permute-done.3.second_ref, ...), custom_call_target="tpu_custom_call" | custom-call | tf_op jit(solution)/shard_map/ortho/pallas_call | solution.py:318
Async XLA Ops:
  0.6 25.2 %copy-start.4 = (s32[32]{0:T(128)S(1)}, s32[32]{0:T(128)}, u32[]{:S(2)}) copy-start(s32[32]{0:T(128)} %partner_ref.5) | copy-start | bytes 388
  0.6 38.5 %copy-start = (bf16[2048,512]{1,0:T(8,128)(2,1)S(1)}, bf16[2048,512]{1,0:T(8,128)(2,1)}, u32[]{:S(2)}) copy-start(bf16[2048,512]{1,0:T(8,128)(2,1)} %attended_hbm.3) | copy-start | bytes 6291460
  0.7 38.4 %copy-start.1 = (bf16[200,2048]{1,0:T(8,128)(2,1)S(1)}, bf16[200,2048]{1,0:T(8,128)(2,1)}, u32[]{:S(2)}) copy-start(bf16[200,2048]{1,0:T(8,128)(2,1)} %weight_ref.5) | copy-start | bytes 2457604
  0.7 38.4 %copy-start.2 = (bf16[200,384]{1,0:T(8,128)(2,1)S(1)}, bf16[200,384]{1,0:T(8,128)(2,1)}, u32[]{:S(2)}) copy-start(bf16[200,384]{1,0:T(8,128)(2,1)} %grad_ref.1) | copy-start | bytes 460804
  0.7 38.4 %copy-start.3 = (f32[200]{0:T(256)S(1)}, f32[200]{0:T(256)}, u32[]{:S(2)}) copy-start(f32[200]{0:T(256)} %param.13) | copy-start | bytes 2404
  0.7 38.4 %copy-start.5 = (s32[32]{0:T(128)S(1)}, s32[32]{0:T(128)}, u32[]{:S(2)}) copy-start(s32[32]{0:T(128)} %frames_ref.3) | copy-start | bytes 388
  0.7 38.4 %copy-start.6 = (s32[32]{0:T(128)S(1)}, s32[32]{0:T(128)}, u32[]{:S(2)}) copy-start(s32[32]{0:T(128)} %moved_ref.3) | copy-start | bytes 388
  0.7 38.4 %copy-start.7 = (s32[16]{0:T(128)S(1)}, s32[16]{0:T(128)}, u32[]{:S(2)}) copy-start(s32[16]{0:T(128)} %slot_ref.1) | copy-start | bytes 196
  42.5 24.2 %all-to-all-start.2 = ((bf16[32,4,3328]{2,1,0:T(4,128)(2,1)}), bf16[32,4,3328]{2,1,0:T(4,128)(2,1)S(1)}, u32[]{:S(2)}, u32[]{:S(2)}) async-start(bf16[32,4,3328]{2,1,0:T(4,128)(2,1)} %get-tuple-element.22), calls=%async_computation.2 | async-start | bytes 1703936 | tf_op jit(solution)/shard_map/all_to_all | solution.py:334
  47.9 8.8 %collective-permute-start = (bf16[1024,512]{1,0:T(8,128)(2,1)S(1)}, bf16[1024,512]{1,0:T(8,128)(2,1)S(1)}, u32[]{:S(2)}, u32[]{:S(2)}) collective-permute-start(bf16[1024,512]{1,0:T(8,128)(2,1)S(1)} %input_grad_odd.1), channel_id=1, source_target_pairs={{0,1},{1,0},{2,3},{3,2},{4,5},{5,4},{6,7},{7,6},{8,9},{9,8},{10,11... | collective-permute-start | bytes 3145736 | tf_op jit(solution)/shard_map/ppermute | solution.py:338
  56.9 26.6 %collective-permute-start.1 = (bf16[512,512]{1,0:T(8,128)(2,1)S(1)}, bf16[512,512]{1,0:T(8,128)(2,1)S(1)}, u32[]{:S(2)}, u32[]{:S(2)}) collective-permute-start(bf16[512,512]{1,0:T(8,128)(2,1)S(1)} %get-tuple-element.27), channel_id=1, source_target_pairs={{0,2},{2,0},{4,6},{6,4},{8,10},{10,8},{12,14},{14,12},{1,3},{3,1},... | collective-permute-start | bytes 1572872 | tf_op jit(solution)/shard_map/ppermute | solution.py:338
  68.2 30.9 %all-to-all-start.3 = ((bf16[128,4,200]{2,1,0:T(4,128)(2,1)}), bf16[128,4,200]{2,1,0:T(4,128)(2,1)S(1)}, u32[]{:S(2)}, u32[]{:S(2)}) async-start(bf16[128,4,200]{2,1,0:T(4,128)(2,1)} %get-tuple-element.26), calls=%async_computation.3 | async-start | bytes 524288 | tf_op jit(solution)/shard_map/all_to_all | solution.py:334
  83.6 27.5 %collective-permute-start.2 = (bf16[128,512]{1,0:T(8,128)(2,1)S(1)}, bf16[128,512]{1,0:T(8,128)(2,1)S(1)}, u32[]{:S(2)}, u32[]{:S(2)}) collective-permute-start(bf16[128,512]{1,0:T(8,128)(2,1)S(1)} %get-tuple-element.30), channel_id=1, source_target_pairs={{0,4},{2,6},{4,0},{6,2},{8,12},{10,14},{12,8},{14,10},{1,5},{3,7},... | collective-permute-start | bytes 393224 | tf_op jit(solution)/shard_map/ppermute | solution.py:338
  87.8 23.3 %collective-permute-start.3 = (bf16[128,512]{1,0:T(8,128)(2,1)S(1)}, bf16[128,512]{1,0:T(8,128)(2,1)S(1)}, u32[]{:S(2)}, u32[]{:S(2)}) collective-permute-start(bf16[128,512]{1,0:T(8,128)(2,1)S(1)} %get-tuple-element.31), channel_id=1, source_target_pairs={{0,12},{2,14},{4,8},{6,10},{8,4},{10,6},{12,0},{14,2},{1,13},{3,15... | collective-permute-start | bytes 393224 | tf_op jit(solution)/shard_map/ppermute | solution.py:338
  93.0 18.1 %collective-permute-start.4 = (bf16[128,512]{1,0:T(8,128)(2,1)S(1)}, bf16[128,512]{1,0:T(8,128)(2,1)S(1)}, u32[]{:S(2)}, u32[]{:S(2)}) collective-permute-start(bf16[128,512]{1,0:T(8,128)(2,1)S(1)} %get-tuple-element.32), channel_id=1, source_target_pairs={{0,8},{2,10},{4,12},{6,14},{8,0},{10,2},{12,4},{14,6},{1,9},{3,11}... | collective-permute-start | bytes 393224 | tf_op jit(solution)/shard_map/ppermute | solution.py:338

commit v14 on v12

--- a/solution.py
+++ b/solution.py
@@ -230,19 +230,16 @@
     layer_out_ref[...] = jnp.where(keep, own, received).astype(bf16)
 
 
-def slots_kernel(pieces_ref, copies_hbm, scale_grad_ref, by_slot, sems):
+def slots_kernel(pieces_ref, copies_ref, scale_grad_ref):
     total = pieces_ref[0].astype(f32)
     for piece in range(1, N_DP):
         total = total + pieces_ref[piece].astype(f32)
     for slot in range(HEADS):
-        by_slot[slot] = total[:, slot * ROWS : (slot + 1) * ROWS].astype(bf16)
-    copies = [
-        (by_slot, copies_hbm.at[pl.ds(z * HEADS, HEADS)]) for z in range(NZ)
-    ]
-    copies = start(sems, *copies)
+        part = total[:, slot * ROWS : (slot + 1) * ROWS].astype(bf16)
+        for z in range(NZ):
+            copies_ref[z * HEADS + slot] = part
     lines = total[0:2, D:] + total[2:4, D:]
     scale_grad_ref[...] = jnp.concatenate([lines[0:1, :], lines[1:2, : ROWS - HD]], axis=1)
-    wait(copies)
 
 
 def join_kernel(owned_ref, whole_ref, joined):
@@ -411,8 +408,7 @@
     summed, _ = lax.optimization_barrier((summed, left))
     copies, scale_grad = call(
         slots_kernel, "slots", [V], (summed,),
-        [((NZ * HEADS, SHARE, ROWS), bf16, H), ((1, ROWS), f32, V)],
-        [V((HEADS, SHARE, ROWS), bf16), dma((NZ,))],
+        [((NZ * HEADS, SHARE, ROWS), bf16, V), ((1, ROWS), f32, V)],
     )
     owned = exchange(copies, ("z", "y", "c"))
     left, *others = add((left, crossed(other, "y", NY, 1)), 4)

time: 117 us -> 117 us (level)
  no operation moved by 1% of the time
where the time goes in v14:
time: 117 us; the launch traced here: 115 us
  blocking collectives  47.3 us (40%)
  starting transfers between devices  38.9 us (33%)
  Pallas kernels  15.8 us (14%)
  waiting for transfers between devices  12 us (10%)
    all_to_all x2, blocking collectives, exchange(): return lax.all_to_all(pieces, axes, split_axis=0, concat_axis=0, tiled=True)  35.5 us
    ppermute x5, starting transfers between devices, crossed(): return lax.ppermute(array, axis, [(i, i ^ bit) for i in range(size)])  19.8 us
    all_to_all x2, starting transfers between devices, exchange(): return lax.all_to_all(pieces, axes, split_axis=0, concat_axis=0, tiled=True)  19.1 us
    pallas_call x9, Pallas kernels, call(): pl.pallas_call(kernel, out_shape=[H(shape, dtype) if place is H else jax....  15.8 us
    all_gather x1, blocking collectives, body(): whole = lax.all_gather(copies, 'x', axis=0, tiled=True)  11.8 us
    all_to_all x2, waiting for transfers between devices, exchange(): return lax.all_to_all(pieces, axes, split_axis=0, concat_axis=0, tiled=True)  9.68 us
  transfers between devices with their start and end apart: 7, of which 3 were waited for; matrix products, arithmetic and copies ran while one was open for 0% of the time, Pallas kernels for 5%

profile of v14, /device:TPU:1, one launch (start us, length us, event | category | flops | bytes accessed | tf_op | source)
XLA Modules:
  0.0 114.9 jit_solution(3397497542094119179)
XLA Ops:
  0.6 0.0 copy-start.4
  0.6 0.0 copy-start
  0.7 0.0 copy-start.1
  0.7 0.0 copy-start.2
  0.7 0.0 copy-start.3
  0.7 0.0 copy-start.5
  0.7 0.0 copy-start.6
  0.7 0.0 copy-start.7
  0.7 2.3 %project.1 = bf16[256,256]{1,0:T(8,128)(2,1)S(1)} custom-call(s32[32]{0:T(128)} %frames_ref.3, s32[32]{0:T(128)} %partner_ref.5, s32[32]{0:T(128)} %moved_ref.3, bf16[2048,512]{1,0:T(8,128)(2,1)} %attended_hbm.3, bf16[200,512]{1,0:T(8,128)(2,1)} %residual_hbm.3, bf16[200,384]{1,0:T(8,128)(2,1)} %grad_ref.1, bf16[200,2048]{1,0:T(8,128)(2,1)} %weight_ref.3, ...), custom_call_target="tpu_custom_call" | custom-call | tf_op jit(solution)/shard_map/project/pallas_call | solution.py:308
  3.0 22.9 %all_to_all.20.pieces_ref = bf16[32,8,256]{2,1,0:T(8,128)(2,1)S(1)} all-to-all(bf16[32,8,256]{2,1,0:T(8,128)(2,1)S(1)} %bitcast.7), channel_id=1, replica_groups=mesh['z'=8,'x'=4,'y'=8,'c'=2] {'z','x'}, dimensions={0} | all-to-all | bytes 262144 | tf_op jit(solution)/shard_map/all_to_all | solution.py:324
  25.9 0.0 copy-done.4
  25.9 0.6 forward.1
  26.4 12.6 %all_to_all.21 = bf16[32,8,256]{2,1,0:T(8,128)(2,1)S(1)} all-to-all(bf16[32,8,256]{2,1,0:T(8,128)(2,1)S(1)} %forward.1), channel_id=1, replica_groups=mesh['z'=8,'x'=4,'y'=8,'c'=2] {'z','x'}, dimensions={0} | all-to-all | bytes 262144 | tf_op jit(solution)/shard_map/all_to_all | solution.py:324
  39.1 0.0 copy-done
  39.1 0.0 copy-done.1
  39.1 0.0 copy-done.2
  39.1 0.0 copy-done.3
  39.1 0.0 copy-done.5
  39.1 0.0 copy-done.6
  39.1 0.0 copy-done.7
  39.1 3.3 %weight_grad.1 = (bf16[200,512]{1,0:T(8,128)(2,1)}, bf16[32,4,3328]{2,1,0:T(4,128)(2,1)}) custom-call(s32[32]{0:T(128)S(1)} %copy-done.5, s32[32]{0:T(128)S(1)} %copy-done.4, s32[32]{0:T(128)S(1)} %copy-done.6, s32[16]{0:T(128)S(1)} %copy-done.7, bf16[2048,512]{1,0:T(8,128)(2,1)S(1)} %copy-done, bf16[200,384]{1,0:T(8,128)(2,1)S(1)} %copy-done.2, ...), custom_call_target="tpu_custom_call" | custom-call | tf_op jit(solution)/shard_map/weight_grad/pallas_call | solution.py:308
  42.5 3.9 %all-to-all-start.2 = ((bf16[32,4,3328]{2,1,0:T(4,128)(2,1)}), bf16[32,4,3328]{2,1,0:T(4,128)(2,1)S(1)}, u32[]{:S(2)}, u32[]{:S(2)}) async-start(bf16[32,4,3328]{2,1,0:T(4,128)(2,1)} %get-tuple-element.23), calls=%async_computation.2 | async-start | bytes 1703936 | tf_op jit(solution)/shard_map/all_to_all | solution.py:324
  46.4 3.7 %input_grad.1 = (bf16[1024,512]{1,0:T(8,128)(2,1)S(1)}, bf16[1024,512]{1,0:T(8,128)(2,1)S(1)}, bf16[200,384]{1,0:T(8,128)(2,1)}) custom-call(s32[32]{0:T(128)S(1)} %copy-done.5, s32[32]{0:T(128)S(1)} %copy-done.4, s32[32]{0:T(128)S(1)} %copy-done.6, bf16[200,2048]{1,0:T(8,128)(2,1)S(1)} %copy-done.1, f32[1,200]{1,0:T(1,128)S(1)} %bitcast.10, ...), custom_call_target="tpu_custom_call" | custom-call | tf_op jit(solution)/shard_map/input_grad/pallas_call | solution.py:308
  50.1 5.2 %collective-permute-start = (bf16[1024,512]{1,0:T(8,128)(2,1)S(1)}, bf16[1024,512]{1,0:T(8,128)(2,1)S(1)}, u32[]{:S(2)}, u32[]{:S(2)}) collective-permute-start(bf16[1024,512]{1,0:T(8,128)(2,1)S(1)} %get-tuple-element.25), channel_id=1, source_target_pairs={{0,1},{1,0},{2,3},{3,2},{4,5},{5,4},{6,7},{7,6},{8,9},{9,8},{10,11... | collective-permute-start | bytes 3145736 | tf_op jit(solution)/shard_map/ppermute | solution.py:328
  55.3 2.3 %collective-permute-done.refs_1_ = bf16[1024,512]{1,0:T(8,128)(2,1)S(1)} collective-permute-done((bf16[1024,512]{1,0:T(8,128)(2,1)S(1)}, bf16[1024,512]{1,0:T(8,128)(2,1)S(1)}, u32[]{:S(2)}, u32[]{:S(2)}) %collective-permute-start) | collective-permute-done | bytes 1048608 | tf_op jit(solution)/shard_map/ppermute | solution.py:328
  57.6 0.2 add.2
  57.9 3.2 %collective-permute-start.1 = (bf16[512,512]{1,0:T(8,128)(2,1)S(1)}, bf16[512,512]{1,0:T(8,128)(2,1)S(1)}, u32[]{:S(2)}, u32[]{:S(2)}) collective-permute-start(bf16[512,512]{1,0:T(8,128)(2,1)S(1)} %get-tuple-element.29), channel_id=1, source_target_pairs={{0,2},{2,0},{4,6},{6,4},{8,10},{10,8},{12,14},{14,12},{1,3},{3,1},... | collective-permute-start | bytes 1572872 | tf_op jit(solution)/shard_map/ppermute | solution.py:328
  61.1 5.6 %all-to-all-done.2.pieces_ref = bf16[32,4,3328]{2,1,0:T(4,128)(2,1)S(1)} async-done(((bf16[32,4,3328]{2,1,0:T(4,128)(2,1)}), bf16[32,4,3328]{2,1,0:T(4,128)(2,1)S(1)}, u32[]{:S(2)}, u32[]{:S(2)}) %all-to-all-start.2) | async-done | bytes 852000 | tf_op jit(solution)/shard_map/all_to_all | solution.py:324
  66.7 0.9 slots.1
  67.6 15.2 %all-to-all-start.3 = ((bf16[128,4,200]{2,1,0:T(4,128)(2,1)}), bf16[128,4,200]{2,1,0:T(4,128)(2,1)S(1)}, u32[]{:S(2)}, u32[]{:S(2)}) async-start(bf16[128,4,200]{2,1,0:T(4,128)(2,1)} %get-tuple-element.28), calls=%async_computation.3 | async-start | bytes 524288 | tf_op jit(solution)/shard_map/all_to_all | solution.py:324
  82.8 0.0 collective-permute-done.1.refs_1_
  82.8 0.1 add.3
  82.9 4.2 %collective-permute-start.2 = (bf16[128,512]{1,0:T(8,128)(2,1)S(1)}, bf16[128,512]{1,0:T(8,128)(2,1)S(1)}, u32[]{:S(2)}, u32[]{:S(2)}) collective-permute-start(bf16[128,512]{1,0:T(8,128)(2,1)S(1)} %get-tuple-element.32), channel_id=1, source_target_pairs={{0,4},{2,6},{4,0},{6,2},{8,12},{10,14},{12,8},{14,10},{1,5},{3,7},... | collective-permute-start | bytes 393224 | tf_op jit(solution)/shard_map/ppermute | solution.py:328
  87.1 5.2 %collective-permute-start.3 = (bf16[128,512]{1,0:T(8,128)(2,1)S(1)}, bf16[128,512]{1,0:T(8,128)(2,1)S(1)}, u32[]{:S(2)}, u32[]{:S(2)}) collective-permute-start(bf16[128,512]{1,0:T(8,128)(2,1)S(1)} %get-tuple-element.33), channel_id=1, source_target_pairs={{0,12},{2,14},{4,8},{6,10},{8,4},{10,6},{12,0},{14,2},{1,13},{3,15... | collective-permute-start | bytes 393224 | tf_op jit(solution)/shard_map/ppermute | solution.py:328
  92.4 2.0 %collective-permute-start.4 = (bf16[128,512]{1,0:T(8,128)(2,1)S(1)}, bf16[128,512]{1,0:T(8,128)(2,1)S(1)}, u32[]{:S(2)}, u32[]{:S(2)}) collective-permute-start(bf16[128,512]{1,0:T(8,128)(2,1)S(1)} %get-tuple-element.34), channel_id=1, source_target_pairs={{0,8},{2,10},{4,12},{6,14},{8,0},{10,2},{12,4},{14,6},{1,9},{3,11}... | collective-permute-start | bytes 393224 | tf_op jit(solution)/shard_map/ppermute | solution.py:328
  94.4 4.1 %all-to-all-done.3.owned_ref = bf16[128,4,200]{2,1,0:T(4,128)(2,1)S(1)} async-done(((bf16[128,4,200]{2,1,0:T(4,128)(2,1)}), bf16[128,4,200]{2,1,0:T(4,128)(2,1)S(1)}, u32[]{:S(2)}, u32[]{:S(2)}) %all-to-all-start.3) | async-done | bytes 204832 | tf_op jit(solution)/shard_map/all_to_all | solution.py:324
  98.4 0.2 join.1
  98.7 11.8 %all_gather.3.grad_ref = bf16[128,3200]{1,0:T(8,128)(2,1)S(1)} all-gather(bf16[32,3200]{1,0:T(8,128)(2,1)S(1)} %join.1), channel_id=1, replica_groups=mesh['z'=8,'x'=4,'y'=8,'c'=2] {'x'}, dimensions={0}, use_global_device_ids=true | all-gather | bytes 1024000 | tf_op jit(solution)/shard_map/all_gather | solution.py:422
  110.5 0.0 collective-permute-done.2.first_ref
  110.5 0.0 collective-permute-done.3.second_ref
  110.5 0.0 collective-permute-done.4.third_ref
  110.5 4.4 %ortho.1 = (bf16[3200,128]{1,0:T(8,128)(2,1)}, bf16[128,512]{1,0:T(8,128)(2,1)}) custom-call(bf16[128,3200]{1,0:T(8,128)(2,1)S(1)} %all_gather.3.grad_ref, bf16[128,512]{1,0:T(8,128)(2,1)S(1)} %get-tuple-element.30.left_ref, bf16[128,512]{1,0:T(8,128)(2,1)S(1)} %collective-permute-done.2.first_ref, bf16[128,512]{1,0:T(8,128)(2,1)S(1)} %collective-permute-done.3.second_ref, ...), custom_call_target="tpu_custom_call" | custom-call | tf_op jit(solution)/shard_map/ortho/pallas_call | solution.py:308
Async XLA Ops:
  0.6 25.2 %copy-start.4 = (s32[32]{0:T(128)S(1)}, s32[32]{0:T(128)}, u32[]{:S(2)}) copy-start(s32[32]{0:T(128)} %partner_ref.5) | copy-start | bytes 388
  0.6 38.5 %copy-start = (bf16[2048,512]{1,0:T(8,128)(2,1)S(1)}, bf16[2048,512]{1,0:T(8,128)(2,1)}, u32[]{:S(2)}) copy-start(bf16[2048,512]{1,0:T(8,128)(2,1)} %attended_hbm.3) | copy-start | bytes 6291460
  0.7 38.4 %copy-start.1 = (bf16[200,2048]{1,0:T(8,128)(2,1)S(1)}, bf16[200,2048]{1,0:T(8,128)(2,1)}, u32[]{:S(2)}) copy-start(bf16[200,2048]{1,0:T(8,128)(2,1)} %weight_ref.3) | copy-start | bytes 2457604
  0.7 38.4 %copy-start.2 = (bf16[200,384]{1,0:T(8,128)(2,1)S(1)}, bf16[200,384]{1,0:T(8,128)(2,1)}, u32[]{:S(2)}) copy-start(bf16[200,384]{1,0:T(8,128)(2,1)} %grad_ref.1) | copy-start | bytes 460804
  0.7 38.4 %copy-start.3 = (f32[200]{0:T(256)S(1)}, f32[200]{0:T(256)}, u32[]{:S(2)}) copy-start(f32[200]{0:T(256)} %param.13) | copy-start | bytes 2404
  0.7 38.4 %copy-start.5 = (s32[32]{0:T(128)S(1)}, s32[32]{0:T(128)}, u32[]{:S(2)}) copy-start(s32[32]{0:T(128)} %frames_ref.3) | copy-start | bytes 388
  0.7 38.4 %copy-start.6 = (s32[32]{0:T(128)S(1)}, s32[32]{0:T(128)}, u32[]{:S(2)}) copy-start(s32[32]{0:T(128)} %moved_ref.3) | copy-start | bytes 388
  0.7 38.4 %copy-start.7 = (s32[16]{0:T(128)S(1)}, s32[16]{0:T(128)}, u32[]{:S(2)}) copy-start(s32[16]{0:T(128)} %slot_ref.1) | copy-start | bytes 196
  42.5 24.2 %all-to-all-start.2 = ((bf16[32,4,3328]{2,1,0:T(4,128)(2,1)}), bf16[32,4,3328]{2,1,0:T(4,128)(2,1)S(1)}, u32[]{:S(2)}, u32[]{:S(2)}) async-start(bf16[32,4,3328]{2,1,0:T(4,128)(2,1)} %get-tuple-element.23), calls=%async_computation.2 | async-start | bytes 1703936 | tf_op jit(solution)/shard_map/all_to_all | solution.py:324
  50.1 7.5 %collective-permute-start = (bf16[1024,512]{1,0:T(8,128)(2,1)S(1)}, bf16[1024,512]{1,0:T(8,128)(2,1)S(1)}, u32[]{:S(2)}, u32[]{:S(2)}) collective-permute-start(bf16[1024,512]{1,0:T(8,128)(2,1)S(1)} %get-tuple-element.25), channel_id=1, source_target_pairs={{0,1},{1,0},{2,3},{3,2},{4,5},{5,4},{6,7},{7,6},{8,9},{9,8},{10,11... | collective-permute-start | bytes 3145736 | tf_op jit(solution)/shard_map/ppermute | solution.py:328
  57.9 25.0 %collective-permute-start.1 = (bf16[512,512]{1,0:T(8,128)(2,1)S(1)}, bf16[512,512]{1,0:T(8,128)(2,1)S(1)}, u32[]{:S(2)}, u32[]{:S(2)}) collective-permute-start(bf16[512,512]{1,0:T(8,128)(2,1)S(1)} %get-tuple-element.29), channel_id=1, source_target_pairs={{0,2},{2,0},{4,6},{6,4},{8,10},{10,8},{12,14},{14,12},{1,3},{3,1},... | collective-permute-start | bytes 1572872 | tf_op jit(solution)/shard_map/ppermute | solution.py:328
  67.6 30.8 %all-to-all-start.3 = ((bf16[128,4,200]{2,1,0:T(4,128)(2,1)}), bf16[128,4,200]{2,1,0:T(4,128)(2,1)S(1)}, u32[]{:S(2)}, u32[]{:S(2)}) async-start(bf16[128,4,200]{2,1,0:T(4,128)(2,1)} %get-tuple-element.28), calls=%async_computation.3 | async-start | bytes 524288 | tf_op jit(solution)/shard_map/all_to_all | solution.py:324
  82.9 27.5 %collective-permute-start.2 = (bf16[128,512]{1,0:T(8,128)(2,1)S(1)}, bf16[128,512]{1,0:T(8,128)(2,1)S(1)}, u32[]{:S(2)}, u32[]{:S(2)}) collective-permute-start(bf16[128,512]{1,0:T(8,128)(2,1)S(1)} %get-tuple-element.32), channel_id=1, source_target_pairs={{0,4},{2,6},{4,0},{6,2},{8,12},{10,14},{12,8},{14,10},{1,5},{3,7},... | collective-permute-start | bytes 393224 | tf_op jit(solution)/shard_map/ppermute | solution.py:328
  87.1 23.3 %collective-permute-start.3 = (bf16[128,512]{1,0:T(8,128)(2,1)S(1)}, bf16[128,512]{1,0:T(8,128)(2,1)S(1)}, u32[]{:S(2)}, u32[]{:S(2)}) collective-permute-start(bf16[128,512]{1,0:T(8,128)(2,1)S(1)} %get-tuple-element.33), channel_id=1, source_target_pairs={{0,12},{2,14},{4,8},{6,10},{8,4},{10,6},{12,0},{14,2},{1,13},{3,15... | collective-permute-start | bytes 393224 | tf_op jit(solution)/shard_map/ppermute | solution.py:328
  92.4 18.1 %collective-permute-start.4 = (bf16[128,512]{1,0:T(8,128)(2,1)S(1)}, bf16[128,512]{1,0:T(8,128)(2,1)S(1)}, u32[]{:S(2)}, u32[]{:S(2)}) collective-permute-start(bf16[128,512]{1,0:T(8,128)(2,1)S(1)} %get-tuple-element.34), channel_id=1, source_target_pairs={{0,8},{2,10},{4,12},{6,14},{8,0},{10,2},{12,4},{14,6},{1,9},{3,11}... | collective-permute-start | bytes 393224 | tf_op jit(solution)/shard_map/ppermute | solution.py:328
